TPU v7x, 32 devices: a whole 2x2x4 slice. The times are simulated.
32 devices in a mesh: dp: 8 (over y, x, core), tp: 4 (over z).
Axes of the slice: x: 2, y: 2, z: 4, core: 2. Of those that a mesh axis runs over, the one named last changes fastest.
Arguments:
- tokens: bfloat16 [8192, 1536], P(('dp', 'tp')), may hold values from -6 to 6
- out_grad: bfloat16 [8192, 1536], P(('dp', 'tp')), may hold values from -6 to 6
- segment_ids: int32 [8192], replicated, may hold values from 0 to 3, never falling along the last dimension, each value on 1 to 4096 neighbouring positions
- attn_gain: bfloat16 [1536], replicated, may hold values from 0.5 to 1.5
- query_weight: bfloat16 [1536, 1536], P(None, 'tp'), may hold values from -0.15625 to 0.15625
- key_matrix: bfloat16 [1536, 768], P(None, 'tp'), may hold values from -0.15625 to 0.15625
- value_matrix: bfloat16 [1536, 768], P(None, 'tp'), may hold values from -0.15625 to 0.15625
- output_weight: bfloat16 [1536, 1536], P('tp'), may hold values from -2.5 to 2.5
- mlp_gain: bfloat16 [1536], replicated, may hold values from 0.5 to 1.5
- gate_weight: bfloat16 [1536, 4096], P(None, 'tp'), may hold values from -0.15625 to 0.15625
- up_weight: bfloat16 [1536, 4096], P(None, 'tp'), may hold values from -0.15625 to 0.15625
- down_weight: bfloat16 [4096, 1536], P('tp'), may hold values from -0.09375 to 0.09375
Outputs:
- output: bfloat16 [8192, 1536], P(('dp', 'tp'))
- input_grad: float32 [8192, 1536], P(('dp', 'tp'))
- attn_gain_grad: float32 [1536], P('dp')
- query_weight_grad: float32 [1536, 1536], P('dp', 'tp')
- key_weight_grad: float32 [1536, 768], P('dp', 'tp')
- value_weight_grad: float32 [1536, 768], P('dp', 'tp')
- output_weight_grad: float32 [1536, 1536], P('tp', 'dp')
- mlp_gain_grad: float32 [1536], P('dp')
- gate_weight_grad: float32 [1536, 4096], P('dp', 'tp')
- up_weight_grad: float32 [1536, 4096], P('dp', 'tp')
- down_weight_grad: float32 [4096, 1536], P('tp', 'dp')
Inputs may be any that keep to these rules, and one draw needn't show every extreme that they name: segment_ids never fall along the packed batch; every item has 1 to 4096 tokens and the longest has exactly 4096, so the keys of a token lie in its own row or the 4 rows before it.
All inputs are finite; a program needn't handle non-finite values.
Results may differ from a plain program's by a relative error of at most 0.025.
Values may be sent and summed in bfloat16 or wider, within the bound.
A program may use at most 192 MiB of HBM per device.

v0:
```python
import jax
import jax.numpy as jnp
from jax import lax
from jax.sharding import PartitionSpec as P

HEAD_WIDTH = 96


eps_norm = 1e-05
rope_base = 100000.0
reach_limit = 8


def shifted(block, axis, distance):
    devices = range(lax.axis_size(axis))
    route = [(i - distance, i) for i in devices if i - distance in devices]
    return lax.ppermute(block, axis, route)


def rms_scale(value_vectors, gain_vec):
    return (
        value_vectors
        * lax.rsqrt(jnp.mean(value_vectors * value_vectors, axis=-1, keepdims=True) + eps_norm)
        * gain_vec
    )


def rotary_turn(value_vectors, token_positions, heads):
    half_width = HEAD_WIDTH // 2
    inverse = 1.0 / rope_base ** (jnp.arange(half_width, dtype=jnp.float32) * 2.0 / HEAD_WIDTH)
    angles = token_positions.astype(jnp.float32)[:, None] * inverse[None, :]
    cosine = jnp.cos(angles)[:, None, :]
    sine_part = jnp.sin(angles)[:, None, :]
    shaped = value_vectors.reshape(value_vectors.shape[0], heads, HEAD_WIDTH)
    first_half = shaped[..., :half_width]
    second = shaped[..., half_width:]
    turned = jnp.concatenate(
        [first_half * cosine - second * sine_part, second * cosine + first_half * sine_part],
        axis=-1,
    )
    return turned.reshape(value_vectors.shape)


def swiglu(gate_pre, up_pre):
    return jax.nn.silu(gate_pre) * up_pre


def contract_rows(left_side, right_side):
    return lax.dot_general(
        left_side, right_side, (((0,), (0,)), ((), ())), preferred_element_type=jnp.float32
    )


def contract_cols(left_side, right_side):
    return lax.dot_general(
        left_side, right_side, (((1,), (1,)), ((), ())), preferred_element_type=jnp.float32
    )


def local(
    tokens,
    out_grad,
    segment_ids,
    attn_gain,
    query_weight,
    key_matrix,
    value_matrix,
    output_weight,
    mlp_gain,
    gate_weight,
    up_weight,
    down_weight,
):
    floats = jnp.float32
    halves = jnp.bfloat16
    shard_rows = tokens.shape[0]
    row_len = shard_rows * lax.axis_size("tp")
    row_index = lax.axis_index("dp")
    reach = min(reach_limit, lax.axis_size("dp") // 2)
    heads_q = query_weight.shape[1] // HEAD_WIDTH
    heads_kv = key_matrix.shape[1] // HEAD_WIDTH
    group_width = heads_q // heads_kv
    q_cols = heads_q * HEAD_WIDTH
    kv_cols = heads_kv * HEAD_WIDTH
    score_scale = HEAD_WIDTH ** (-0.5)
    row_first = row_index * row_len
    seg_row = lax.dynamic_slice_in_dim(segment_ids, row_first, row_len)
    index_row = row_first + jnp.arange(row_len, dtype=jnp.int32)
    previous = jnp.where(row_first > 0, segment_ids[jnp.maximum(row_first - 1, 0)], -1)
    before = jnp.concatenate([previous[None], seg_row[:-1]])
    starts = jnp.where(seg_row != before, index_row, 0)
    first_start = jnp.sum((segment_ids < seg_row[0]).astype(jnp.int32))
    token_positions = index_row - jnp.maximum(lax.cummax(starts), first_start)
    tokens32 = tokens.astype(floats)
    gain_attn = attn_gain.astype(floats)
    gain_mlp = mlp_gain.astype(floats)
    normed = rms_scale(tokens32, gain_attn).astype(halves)
    normed_full = lax.all_gather(normed, "tp", axis=0, tiled=True)
    joined = jnp.concatenate([query_weight, key_matrix, value_matrix], axis=1)
    projected = jnp.dot(normed_full, joined, preferred_element_type=floats)
    q_linear = projected[:, :q_cols]
    key_linear_out = projected[:, q_cols : q_cols + kv_cols]
    query_vectors = rotary_turn(q_linear, token_positions, heads_q).astype(halves)
    key_vectors = rotary_turn(key_linear_out, token_positions, heads_kv).astype(halves)
    value_vectors = projected[:, q_cols + kv_cols :].astype(halves)
    query_heads = query_vectors.reshape(row_len, heads_kv, group_width, HEAD_WIDTH)
    held_blocks = [(key_vectors, value_vectors)]
    moving = (key_vectors, value_vectors)
    for step_hop in range(reach):
        moving = shifted((moving[0], moving[1]), "dp", 1)
        held_blocks.append(moving)

    def block_mask(step_hop):
        key_row = row_index - step_hop
        seg_keys = lax.dynamic_slice_in_dim(segment_ids, jnp.maximum(key_row, 0) * row_len, row_len)
        key_index = key_row * row_len + jnp.arange(row_len, dtype=jnp.int32)
        return (seg_keys[None, :] == seg_row[:, None]) & (key_index[None, :] <= index_row[:, None])

    def block_needed(step_hop):
        last_key = jnp.maximum((row_index - step_hop + 1) * row_len - 1, 0)
        return (row_index >= step_hop) & (segment_ids[last_key] == seg_row[0])

    block_masks = [block_mask(step_hop) for step_hop in range(reach + 1)]

    def apply_block(step_hop, update, state_in):
        key_block, value_block = held_blocks[step_hop]
        if step_hop == 0:
            return update(state_in, key_block, value_block, block_masks[0])
        return lax.cond(
            block_needed(step_hop),
            update,
            lambda state_kept, key_skip, value_skip, mask_skip: state_kept,
            state_in,
            key_block,
            value_block,
            block_masks[step_hop],
        )

    def scores(key_block, allowed):
        raw_scores = jnp.einsum(
            "qhgd,khd->hgqk",
            query_heads,
            key_block.reshape(row_len, heads_kv, HEAD_WIDTH),
            preferred_element_type=floats,
        )
        return jnp.where(allowed, raw_scores * score_scale, -jnp.inf)

    def add_online(state_in, key_block, value_block, allowed):
        run_max, run_total, run_sum = state_in
        block_scores = scores(key_block, allowed)
        new_max = jnp.maximum(run_max, jnp.max(block_scores, axis=-1))
        factor = jnp.exp(run_max - new_max)
        weights = jnp.exp(block_scores - new_max[..., None])
        run_total = run_total * factor + jnp.sum(weights, axis=-1)
        run_sum = run_sum * jnp.moveaxis(factor, 2, 0)[..., None] + jnp.einsum(
            "hgqk,khd->qhgd",
            weights.astype(halves),
            value_block.reshape(row_len, heads_kv, HEAD_WIDTH),
            preferred_element_type=floats,
        )
        return (new_max, run_total, run_sum)

    online = (
        jnp.full((heads_kv, group_width, row_len), -jnp.inf, floats),
        jnp.zeros((heads_kv, group_width, row_len), floats),
        jnp.zeros((row_len, heads_kv, group_width, HEAD_WIDTH), floats),
    )
    for step_hop in range(reach + 1):
        online = apply_block(step_hop, add_online, online)
    run_max, run_total, run_sum = online
    log_total = (run_max + jnp.log(run_total))[..., None]
    context_heads = (run_sum / jnp.moveaxis(run_total, 2, 0)[..., None]).astype(halves)
    context = context_heads.reshape(row_len, q_cols)
    residual = tokens32 + lax.psum_scatter(
        jnp.dot(context, output_weight, preferred_element_type=floats).astype(jnp.bfloat16),
        "tp",
        scatter_dimension=0,
        tiled=True,
    ).astype(jnp.float32)
    mlp_normed = rms_scale(residual, gain_mlp).astype(halves)
    mlp_full = lax.all_gather(mlp_normed, "tp", axis=0, tiled=True)
    gate_pre = jnp.dot(mlp_full, gate_weight, preferred_element_type=floats)
    up_pre = jnp.dot(mlp_full, up_weight, preferred_element_type=floats)
    hidden = swiglu(gate_pre, up_pre).astype(halves)
    output = residual + lax.psum_scatter(
        jnp.dot(hidden, down_weight, preferred_element_type=floats).astype(jnp.bfloat16),
        "tp",
        scatter_dimension=0,
        tiled=True,
    ).astype(jnp.float32)
    grad_full = lax.all_gather(out_grad, "tp", axis=0, tiled=True)
    grad_hidden = contract_cols(grad_full, down_weight)
    down_grad = contract_rows(grad_full, hidden)
    silu_back = jax.vjp(swiglu, gate_pre, up_pre)[1]
    grad_gate, grad_up = silu_back(grad_hidden)
    grad_gate = grad_gate.astype(halves)
    grad_up = grad_up.astype(halves)
    gate_grad = contract_rows(mlp_full, grad_gate)
    up_grad = contract_rows(mlp_full, grad_up)
    grad_mlp_normed = lax.psum_scatter(
        (contract_cols(grad_gate, gate_weight) + contract_cols(grad_up, up_weight)).astype(
            jnp.bfloat16
        ),
        "tp",
        scatter_dimension=0,
        tiled=True,
    ).astype(jnp.float32)
    mlp_norm_back = jax.vjp(rms_scale, residual, gain_mlp)[1]
    grad_residual_part, mlp_gain_part = mlp_norm_back(grad_mlp_normed)
    grad_residual = out_grad.astype(floats) + grad_residual_part
    attn_grad_full = lax.all_gather(grad_residual.astype(halves), "tp", axis=0, tiled=True)
    output_grad = contract_rows(attn_grad_full, context)
    grad_context = (
        contract_cols(attn_grad_full, output_weight)
        .astype(halves)
        .reshape(row_len, heads_kv, group_width, HEAD_WIDTH)
    )
    delta_col = jnp.einsum(
        "qhgd,qhgd->hgq", grad_context, context_heads, preferred_element_type=floats
    )[..., None]

    def add_grads(state_in, key_block, value_block, allowed):
        query_acc, key_acc, value_acc = state_in
        probabilities = jnp.exp(scores(key_block, allowed) - log_total)
        grad_probs = jnp.einsum(
            "qhgd,khd->hgqk",
            grad_context,
            value_block.reshape(row_len, heads_kv, HEAD_WIDTH),
            preferred_element_type=floats,
        )
        grad_scores = (probabilities * (grad_probs - delta_col)).astype(halves)
        key_heads = key_block.reshape(row_len, heads_kv, HEAD_WIDTH)
        query_acc = (
            query_acc
            + jnp.einsum("hgqk,khd->qhgd", grad_scores, key_heads, preferred_element_type=floats)
            * score_scale
        )
        key_acc = (
            key_acc
            + jnp.einsum(
                "hgqk,qhgd->khd", grad_scores, query_heads, preferred_element_type=floats
            ).reshape(row_len, kv_cols)
            * score_scale
        )
        value_acc = value_acc + jnp.einsum(
            "hgqk,qhgd->khd",
            probabilities.astype(halves),
            grad_context,
            preferred_element_type=floats,
        ).reshape(row_len, kv_cols)
        return (query_acc, key_acc, value_acc)

    query_acc = jnp.zeros((row_len, heads_kv, group_width, HEAD_WIDTH), floats)
    carried = (jnp.zeros((row_len, kv_cols), floats), jnp.zeros((row_len, kv_cols), floats))
    for step_hop in range(reach, 0, -1):
        query_acc, key_acc, value_acc = apply_block(
            step_hop, add_grads, (query_acc, carried[0], carried[1])
        )
        carried = (
            shifted(key_acc.astype(jnp.bfloat16), "dp", -1).astype(key_acc.dtype),
            shifted(value_acc.astype(jnp.bfloat16), "dp", -1).astype(value_acc.dtype),
        )
    query_acc, key_total, value_total = apply_block(
        0, add_grads, (query_acc, carried[0], carried[1])
    )
    query_back = jax.vjp(lambda linear: rotary_turn(linear, token_positions, heads_q), q_linear)[1]
    key_back = jax.vjp(
        lambda linear: rotary_turn(linear, token_positions, heads_kv), key_linear_out
    )[1]
    grad_q_linear = query_back(query_acc.reshape(row_len, q_cols))[0]
    grad_k_linear = key_back(key_total)[0]
    grads_joined = jnp.concatenate([grad_q_linear, grad_k_linear, value_total], axis=1).astype(
        halves
    )
    proj_grad = contract_rows(normed_full, grads_joined)
    query_grad = proj_grad[:, :q_cols]
    key_grad = proj_grad[:, q_cols : q_cols + kv_cols]
    value_grad = proj_grad[:, q_cols + kv_cols :]
    grad_normed = lax.psum_scatter(
        contract_cols(grads_joined, joined).astype(jnp.bfloat16),
        "tp",
        scatter_dimension=0,
        tiled=True,
    ).astype(jnp.float32)
    attn_norm_back = jax.vjp(rms_scale, tokens32, gain_attn)[1]
    grad_tokens_part, attn_gain_part = attn_norm_back(grad_normed)
    input_grad = grad_residual + grad_tokens_part
    (
        query_sum,
        key_sum,
        value_sum,
        output_sum,
        gate_sum,
        up_sum,
        down_sum,
        attn_gain_sum,
        mlp_gain_sum,
    ) = (
        lax.psum_scatter(query_grad, "dp", scatter_dimension=0, tiled=True),
        lax.psum_scatter(key_grad, "dp", scatter_dimension=0, tiled=True),
        lax.psum_scatter(value_grad, "dp", scatter_dimension=0, tiled=True),
        lax.psum_scatter(output_grad, "dp", scatter_dimension=0, tiled=True),
        lax.psum_scatter(gate_grad, "dp", scatter_dimension=0, tiled=True),
        lax.psum_scatter(up_grad, "dp", scatter_dimension=0, tiled=True),
        lax.psum_scatter(down_grad, "dp", scatter_dimension=0, tiled=True),
        lax.psum_scatter(attn_gain_part, "dp", scatter_dimension=0, tiled=True),
        lax.psum_scatter(mlp_gain_part, "dp", scatter_dimension=0, tiled=True),
    )
    attn_gain_total, mlp_gain_total = lax.psum((attn_gain_sum, mlp_gain_sum), "tp")
    return (
        output.astype(halves),
        input_grad,
        attn_gain_total,
        query_sum,
        key_sum,
        value_sum,
        output_sum.T,
        mlp_gain_total,
        gate_sum,
        up_sum,
        down_sum.T,
    )


def solution(mesh):
    return jax.shard_map(
        local,
        mesh=mesh,
        in_specs=(
            P(("dp", "tp"), None),
            P(("dp", "tp"), None),
            P(),
            P(),
            P(None, "tp"),
            P(None, "tp"),
            P(None, "tp"),
            P("tp", None),
            P(),
            P(None, "tp"),
            P(None, "tp"),
            P("tp", None),
        ),
        out_specs=(
            P(("dp", "tp"), None),
            P(("dp", "tp"), None),
            P("dp"),
            P("dp", "tp"),
            P("dp", "tp"),
            P("dp", "tp"),
            P("tp", "dp"),
            P("dp"),
            P("dp", "tp"),
            P("dp", "tp"),
            P("tp", "dp"),
        ),
        check_vma=False,
    )
```

profile of v0, /device:TPU:3, one launch (start us, length us, event | category | flops | bytes accessed | tf_op | source)
XLA Modules:
  0.0 1271.0 jit_solution(12487312107339645841)
XLA Ops:
  30.0 7.3 compare_and_fusion
  37.4 40.4 %all-gather.5.cloned.1.call-done = bf16[1024,1536]{1,0:T(8,128)(2,1)} async-done(((bf16[256,1536]{1,0:T(8,128)(2,1)}), bf16[1024,1536]{1,0:T(8,128)(2,1)}) %all-gather.5.cloned.1.call-update) | async-done | bytes 3145744 | tf_op jit(solution)/shard_map/all_gather | solution.py:98
  127.6 15.9 %conditional.8 = ((f32[2,2,1024]{2,1,0:T(2,128)S(1)}, f32[2,2,1024]{2,1,0:T(2,128)S(1)}, f32[1024,2,2,96]{0,3,2,1:T(8,128)})) conditional(s32[]{:T(128)} %convert_element_type.203, (f32[2,2,1024]{2,1,0:T(2,128)S(1)}, f32[2,2,1024]{2,1,0:T(2,128)S(1)}, f32[1024,2,2,96]{0,3,2,1:T(8,128)}) %tuple.74, (pred[1024,1024]{0,1:T(8,128)(4,1)}, ...), branch_computations={%region_6.7_spmd, %region_7.10_spmd} | conditional | flops 1657548800 | bytes 78381224 | solution.py:129
  133.8 6.0 bitcast_add_fusion
  143.5 15.3 %conditional.9 = ((f32[2,2,1024]{2,1,0:T(2,128)S(1)}, f32[2,2,1024]{2,1,0:T(2,128)S(1)}, f32[1024,2,2,96]{0,3,2,1:T(8,128)})) conditional(s32[]{:T(128)} %convert_element_type.202, (f32[2,2,1024]{2,1,0:T(2,128)S(1)}, f32[2,2,1024]{2,1,0:T(2,128)S(1)}, f32[1024,2,2,96]{0,3,2,1:T(8,128)}) %get-tuple-element.491, (pred[1024,1024]{0,1:T(8,128)(4,1)}, ...), branch_computations={%region_10.11_spmd, %region_11.14_spmd} | conditional | flops 1657548800 | bytes 75235448 | solution.py:129
  149.1 6.0 bitcast_add_fusion.1
  158.8 15.3 %conditional.10 = ((f32[2,2,1024]{2,1,0:T(2,128)S(1)}, f32[2,2,1024]{2,1,0:T(2,128)S(1)}, f32[1024,2,2,96]{0,3,2,1:T(8,128)})) conditional(s32[]{:T(128)} %convert_element_type.201, (f32[2,2,1024]{2,1,0:T(2,128)S(1)}, f32[2,2,1024]{2,1,0:T(2,128)S(1)}, f32[1024,2,2,96]{0,3,2,1:T(8,128)}) %get-tuple-element.492, (pred[1024,1024]{0,1:T(8,128)(4,1)}, ...), branch_computations={%region_14.15_spmd, %region_15.18_spmd} | conditional | flops 1657548800 | bytes 75235448 | solution.py:129
  164.4 6.0 bitcast_add_fusion.2
  183.9 63.1 %reduce-scatter.20.cloned.1.call-done = bf16[256,1536]{1,0:T(8,128)(2,1)} async-done(((bf16[1024,1536]{1,0:T(8,128)(2,1)}), bf16[256,1536]{1,0:T(8,128)(2,1)}) %reduce-scatter.20.cloned.1.call-update) | async-done | bytes 786448 | tf_op jit(solution)/shard_map/reduce_scatter | solution.py:174
  252.0 63.0 %all-gather.7.cloned.1.call-done = bf16[1024,1536]{1,0:T(8,128)(2,1)} async-done(((bf16[256,1536]{1,0:T(8,128)(2,1)}), bf16[1024,1536]{1,0:T(8,128)(2,1)}) %all-gather.7.cloned.1.call-update) | async-done | bytes 3145744 | tf_op jit(solution)/shard_map/all_gather | solution.py:181
  315.0 8.4 fusion.148
  328.4 50.2 %all-gather.9.cloned.1.call-done = bf16[1024,1536]{1,0:T(8,128)(2,1)} async-done(((bf16[256,1536]{1,0:T(8,128)(2,1)}), bf16[1024,1536]{1,0:T(8,128)(2,1)}) %all-gather.9.cloned.1.call-update) | async-done | bytes 3145744 | tf_op jit(solution)/shard_map/all_gather | solution.py:191
  378.6 9.6 multiply_convert_fusion
  396.9 58.9 %reduce-scatter.24.cloned.1.call-done = bf16[256,1536]{1,0:T(8,128)(2,1)} async-done(((bf16[1024,1536]{1,0:T(8,128)(2,1)}), bf16[256,1536]{1,0:T(8,128)(2,1)}) %reduce-scatter.24.cloned.1.call-update) | async-done | bytes 786448 | tf_op jit(solution)/shard_map/reduce_scatter | solution.py:200
  462.3 63.5 %all-gather.11.cloned.1.call-done = bf16[1024,1536]{1,0:T(8,128)(2,1)} async-done(((bf16[256,1536]{1,0:T(8,128)(2,1)}), bf16[1024,1536]{1,0:T(8,128)(2,1)}) %all-gather.11.cloned.1.call-update) | async-done | bytes 3145744 | tf_op jit(solution)/shard_map/all_gather | solution.py:211
  539.7 13.5 %fusion.89 = bf16[2,2,1024,1024]{2,3,1,0:T(8,128)(2,1)} fusion(f32[2,1024,1024,2]{2,1,3,0:T(8,128)} %copy-done.8, f32[2,2,1024]{2,1,0:T(2,128)S(1)} %fusion.116, f32[2,2,1024]{2,1,0:T(2,128)} %get-tuple-element.314, pred[1024,1024]{0,1:T(8,128)(4,1)} %get-tuple-element.429, bf16[1024,2,96,1]{0,2,3,1:T(8,128)(2,1)S(1)} %bitcast.496, ...), kind=kOutput, calls=%fused_computation.118 | convolution fusion | flops 830472192 | bytes 27426816 | tf_op jit(solution)/shard_map/qhgd,khd->hgqk/dot_general | solution.py:225
  553.2 11.3 fusion.96
  566.4 40.9 %conditional.13 = ((f32[1024,2,2,96]{0,3,2,1:T(8,128)}, f32[1024,192]{0,1:T(8,128)}, f32[1024,192]{0,1:T(8,128)})) conditional(s32[]{:T(128)} %convert_element_type.201, (f32[1024,2,2,96]{0,3,2,1:T(8,128)}, f32[1024,192]{0,1:T(8,128)}, f32[1024,192]{0,1:T(8,128)}) %tuple.81, (pred[1024,1024]{0,1:T(8,128)(4,1)}, bf16[1024,192]{0,1:T(8,128)(2,1)}, ...), branch_computations={%region_29.30_spmd, %region_30.31_spmd} | conditional | flops 4069851136 | bytes 97697880 | solution.py:129
  566.6 9.5 fusion.144
  576.1 11.6 fusion.49
  587.6 9.5 fusion.45
  613.6 7.2 fusion.119
  624.9 41.0 %conditional.14 = ((f32[1024,2,2,96]{0,3,2,1:T(8,128)}, f32[1024,192]{0,1:T(8,128)}, f32[1024,192]{0,1:T(8,128)})) conditional(s32[]{:T(128)} %convert_element_type.202, (f32[1024,2,2,96]{0,3,2,1:T(8,128)}, f32[1024,192]{0,1:T(8,128)}, f32[1024,192]{0,1:T(8,128)}) %tuple.83, (pred[1024,1024]{0,1:T(8,128)(4,1)}, bf16[1024,192]{0,1:T(8,128)(2,1)}, ...), branch_computations={%region_31.32_spmd, %region_32.33_spmd} | conditional | flops 4069851136 | bytes 99270776 | solution.py:129
  624.9 9.5 fusion.145
  634.4 11.6 fusion.60
  646.0 9.6 fusion.56
  672.2 6.0 fusion.123
  683.5 40.5 %conditional.15 = ((f32[1024,2,2,96]{0,3,2,1:T(8,128)}, f32[1024,192]{0,1:T(8,128)}, f32[1024,192]{0,1:T(8,128)})) conditional(s32[]{:T(128)} %convert_element_type.203, (f32[1024,2,2,96]{0,3,2,1:T(8,128)}, f32[1024,192]{0,1:T(8,128)}, f32[1024,192]{0,1:T(8,128)}) %tuple.85, (pred[1024,1024]{0,1:T(8,128)(4,1)}, bf16[1024,192]{0,1:T(8,128)(2,1)}, ...), branch_computations={%region_33.34_spmd, %region_34.35_spmd} | conditional | flops 4069851136 | bytes 99270776 | solution.py:129
  683.5 9.5 fusion.146
  692.9 11.6 fusion.71
  704.5 9.5 fusion.67
  733.0 7.7 collective-permute-done.14
  746.7 6.5 convolution_convert_fusion.2
  753.3 8.7 convolution_bitcast_fusion.4
  762.0 6.6 copy.162
  768.9 8.7 fusion.152
  777.7 8.6 fusion.151
  814.1 11.2 reduce-scatter.26.cloned.1.call-done
  827.4 31.1 %all-reduce.6 = (f32[1536]{0:T(1024)S(1)}, f32[1536]{0:T(1024)S(1)}) all-reduce(f32[1536]{0:T(1024)S(1)} %get-tuple-element.369, f32[1536]{0:T(1024)S(1)} %copy-done.55), channel_id=6, replica_groups=mesh['dp'=8,'tp'=4] {'dp'}, use_global_device_ids=true, to_apply=%region_38.39.clone | all-reduce | flops 3072 | bytes 24576
  858.7 9.8 all-reduce.7
  868.6 19.6 %reduce-scatter.22.cloned.1.call-done = bf16[256,1536]{1,0:T(8,128)(2,1)} async-done(((bf16[1024,1536]{1,0:T(8,128)(2,1)}), bf16[256,1536]{1,0:T(8,128)(2,1)}) %reduce-scatter.22.cloned.1.call-update) | async-done | bytes 786448 | tf_op jit(solution)/shard_map/reduce_scatter | solution.py:185
  893.0 61.0 %reduce-scatter.40.cloned.1.call-done = f32[192,1024]{1,0:T(8,128)} async-done(((f32[1536,1024]{1,0:T(8,128)}), f32[192,1024]{1,0:T(8,128)}) %reduce-scatter.40.cloned.1.call-update) | async-done | bytes 786448
  954.0 65.9 %reduce-scatter.32.cloned.1.call-done = f32[192,1024]{1,0:T(8,128)} async-done(((f32[1536,1024]{1,0:T(8,128)}), f32[192,1024]{1,0:T(8,128)}) %reduce-scatter.32.cloned.1.call-update) | async-done | bytes 786448 | tf_op jit(solution)/shard_map/reduce_scatter | solution.py:304
  1020.0 65.7 %reduce-scatter.30.cloned.1.call-done = f32[192,1024]{1,0:T(8,128)} async-done(((f32[1536,1024]{1,0:T(8,128)}), f32[192,1024]{1,0:T(8,128)}) %reduce-scatter.30.cloned.1.call-update) | async-done | bytes 786448 | tf_op jit(solution)/shard_map/reduce_scatter | solution.py:303
  1085.7 42.6 %reduce-scatter.38.cloned.1.call-done = f32[192,192]{1,0:T(8,128)} async-done(((f32[1536,192]{1,0:T(8,128)}), f32[192,192]{1,0:T(8,128)}) %reduce-scatter.38.cloned.1.call-update) | async-done | bytes 147472
  1128.3 42.7 %reduce-scatter.36.cloned.1.call-done = f32[192,192]{1,0:T(8,128)} async-done(((f32[1536,192]{1,0:T(8,128)}), f32[192,192]{1,0:T(8,128)}) %reduce-scatter.36.cloned.1.call-update) | async-done | bytes 147472
  1171.0 46.7 %reduce-scatter.28.cloned.1.call-done = f32[192,384]{1,0:T(8,128)} async-done(((f32[1536,384]{1,0:T(8,128)}), f32[192,384]{1,0:T(8,128)}) %reduce-scatter.28.cloned.1.call-update) | async-done | bytes 294928 | tf_op jit(solution)/shard_map/reduce_scatter | solution.py:302
  1217.7 46.3 %reduce-scatter.34.cloned.1.call-done = f32[192,384]{1,0:T(8,128)} async-done(((f32[1536,384]{1,0:T(8,128)}), f32[192,384]{1,0:T(8,128)}) %reduce-scatter.34.cloned.1.call-update) | async-done | bytes 294928
  (313 shorter events, 250.2 us)
Async XLA Ops:
  7.2 371.5 %copy-start = (bf16[1024,1536]{1,0:T(8,128)(2,1)S(1)}, bf16[1024,1536]{1,0:T(8,128)(2,1)}, u32[]{:S(2)}) copy-start(bf16[1024,1536]{1,0:T(8,128)(2,1)} %param.39) | copy-start | bytes 9437188
  7.2 20.0 %copy-start.54 = (s32[8192]{0:T(1024)S(1)}, s32[8192]{0:T(1024)}, u32[]{:S(2)}) copy-start(s32[8192]{0:T(1024)} %param.30) | copy-start | bytes 98308
  7.2 70.6 %all-gather.5.cloned.1.call-start = ((), (), s32[]{:S(2)}) async-start(), calls=%async_computation.11 | async-start | bytes 3932160 | tf_op jit(solution)/shard_map/all_gather | solution.py:98
  12.9 234.0 %reduce-scatter.20.cloned.1.call-start = ((), (), s32[]{:S(2)}) async-start(), calls=%async_computation.12 | async-start | bytes 3932160 | tf_op jit(solution)/shard_map/reduce_scatter | solution.py:174
  30.0 59.4 %copy-start.18 = (f32[1024,48]{0,1:T(8,128)}, f32[1024,48]{0,1:T(8,128)S(1)}, u32[]{:S(2)}) copy-start(f32[1024,48]{0,1:T(8,128)S(1)} %get-tuple-element.431) | copy-start | bytes 589828
  30.0 59.4 %copy-start.20 = (f32[1024,48]{0,1:T(8,128)}, f32[1024,48]{0,1:T(8,128)S(1)}, u32[]{:S(2)}) copy-start(f32[1024,48]{0,1:T(8,128)S(1)} %get-tuple-element.432) | copy-start | bytes 589828
  83.3 38.5 %copy-start.47 = (bf16[1024,192]{0,1:T(8,128)(2,1)}, bf16[1024,192]{0,1:T(8,128)(2,1)S(1)}, u32[]{:S(2)}) copy-start(bf16[1024,192]{0,1:T(8,128)(2,1)S(1)} %slice.87) | copy-start | bytes 1179652
  83.5 8.5 collective-permute-start.1
  87.5 9.8 collective-permute-start
  89.8 25.4 %copy-start.1 = (bf16[1024,4,96]{0,2,1:T(8,128)(2,1)}, bf16[1024,4,96]{0,2,1:T(8,128)(2,1)S(1)}, u32[]{:S(2)}) copy-start(bf16[1024,4,96]{0,2,1:T(8,128)(2,1)S(1)} %pad_maximum_fusion.2) | copy-start | bytes 2359300
  92.0 35.6 %copy-start.70 = (bf16[1024,192]{0,1:T(8,128)(2,1)}, bf16[1024,192]{0,1:T(8,128)(2,1)S(1)}, u32[]{:S(2)}) copy-start(bf16[1024,192]{0,1:T(8,128)(2,1)S(1)} %collective-permute-done.1) | copy-start | bytes 1179652
  92.0 12.7 collective-permute-start.3
  97.3 30.3 %copy-start.34 = (bf16[1024,192]{0,1:T(8,128)(2,1)}, bf16[1024,192]{0,1:T(8,128)(2,1)S(1)}, u32[]{:S(2)}) copy-start(bf16[1024,192]{0,1:T(8,128)(2,1)S(1)} %collective-permute-done) | copy-start | bytes 1179652
  97.3 10.0 collective-permute-start.2
  104.7 10.5 collective-permute-start.5
  107.3 10.1 collective-permute-start.4
  115.2 58.9 %collective-permute-start.7 = (bf16[1024,192]{0,1:T(8,128)(2,1)}, bf16[1024,192]{0,1:T(8,128)(2,1)}, u32[]{:S(2)}, u32[]{:S(2)}) collective-permute-start(bf16[1024,192]{0,1:T(8,128)(2,1)} %collective-permute-done.5), channel_id=1, source_target_pairs={{0,4},{4,8},{8,12},{12,16},{16,20},{20,24},{24,28},{1,5},{5,9},{9,... | collective-permute-start | bytes 1179656 | tf_op jit(solution)/shard_map/ppermute | solution.py:17
  117.4 56.8 %collective-permute-start.6 = (bf16[1024,192]{0,1:T(8,128)(2,1)}, bf16[1024,192]{0,1:T(8,128)(2,1)}, u32[]{:S(2)}, u32[]{:S(2)}) collective-permute-start(bf16[1024,192]{0,1:T(8,128)(2,1)} %collective-permute-done.4), channel_id=1, source_target_pairs={{0,4},{4,8},{8,12},{12,16},{16,20},{20,24},{24,28},{1,5},{5,9},{9,... | collective-permute-start | bytes 1179656 | tf_op jit(solution)/shard_map/ppermute | solution.py:17
  183.8 131.2 %all-gather.7.cloned.1.call-start = ((), (), s32[]{:S(2)}) async-start(), calls=%async_computation.13 | async-start | bytes 3932160 | tf_op jit(solution)/shard_map/all_gather | solution.py:181
  183.9 274.8 %copy-start.50 = (f32[1536]{0:T(1024)}, f32[1536]{0:T(1024)S(1)}, u32[]{:S(2)}) copy-start(f32[1536]{0:T(1024)S(1)} %convert_element_type.215) | copy-start | bytes 18436
  248.7 210.0 %copy-start.56 = (f32[256]{0:T(256)}, f32[256]{0:T(256)S(1)}, u32[]{:S(2)}) copy-start(f32[256]{0:T(256)S(1)} %fusion.131) | copy-start | bytes 3076
  251.2 127.4 %all-gather.9.cloned.1.call-start = ((), (), s32[]{:S(2)}) async-start(), calls=%async_computation.15 | async-start | bytes 3932160 | tf_op jit(solution)/shard_map/all_gather | solution.py:191
  251.8 203.9 %reduce-scatter.24.cloned.1.call-start = ((), (), s32[]{:S(2)}) async-start(), calls=%async_computation.16 | async-start | bytes 3932160 | tf_op jit(solution)/shard_map/reduce_scatter | solution.py:200
  396.8 129.0 %all-gather.11.cloned.1.call-start = ((), (), s32[]{:S(2)}) async-start(), calls=%async_computation.17 | async-start | bytes 3932160 | tf_op jit(solution)/shard_map/all_gather | solution.py:211
  458.7 71.8 %copy-start.60 = (f32[256]{0:T(256)}, f32[256]{0:T(256)S(1)}, u32[]{:S(2)}) copy-start(f32[256]{0:T(256)S(1)} %multiply_multiply_fusion.1) | copy-start | bytes 3076
  462.1 363.3 %reduce-scatter.26.cloned.1.call-start = ((), (), s32[]{:S(2)}) async-start(), calls=%async_computation.18 | async-start | bytes 3932160 | tf_op jit(solution)/shard_map/reduce_scatter | solution.py:279
  535.3 29.2 %collective-permute-start.8 = (bf16[1024,192]{0,1:T(8,128)(2,1)}, bf16[1024,192]{0,1:T(8,128)(2,1)S(1)}, u32[]{:S(2)}, u32[]{:S(2)}) collective-permute-start(bf16[1024,192]{0,1:T(8,128)(2,1)} %get-tuple-element.299), channel_id=1, source_target_pairs={{4,0},{8,4},{12,8},{16,12},{20,16},{24,20},{28,24},{5,1},{9,5},{13... | collective-permute-start | bytes 1179656 | tf_op jit(solution)/shard_map/ppermute | solution.py:17
  537.8 27.7 %collective-permute-start.9 = (bf16[1024,192]{0,1:T(8,128)(2,1)}, bf16[1024,192]{0,1:T(8,128)(2,1)S(1)}, u32[]{:S(2)}, u32[]{:S(2)}) collective-permute-start(bf16[1024,192]{0,1:T(8,128)(2,1)} %get-tuple-element.300), channel_id=1, source_target_pairs={{4,0},{8,4},{12,8},{16,12},{20,16},{24,20},{28,24},{5,1},{9,5},{13... | collective-permute-start | bytes 1179656 | tf_op jit(solution)/shard_map/ppermute | solution.py:17
  609.7 11.1 collective-permute-start.11
  611.6 12.3 collective-permute-start.10
  624.9 47.2 %copy-start.31 = (bf16[1024,2,48]{0,2,1:T(8,128)(2,1)S(1)}, bf16[1024,2,48]{0,2,1:T(8,128)(2,1)}, u32[]{:S(2)}) copy-start(bf16[1024,2,48]{0,2,1:T(8,128)(2,1)} %copy-done.30) | copy-start | bytes 589828
  624.9 47.3 %copy-start.33 = (bf16[1024,2,48]{0,2,1:T(8,128)(2,1)S(1)}, bf16[1024,2,48]{0,2,1:T(8,128)(2,1)}, u32[]{:S(2)}) copy-start(bf16[1024,2,48]{0,2,1:T(8,128)(2,1)} %copy-done.32) | copy-start | bytes 589828
  668.3 10.0 collective-permute-start.13
  670.2 12.3 collective-permute-start.12
  726.5 14.5 %collective-permute-start.15 = (bf16[1024,192]{0,1:T(8,128)(2,1)S(1)}, bf16[1024,192]{0,1:T(8,128)(2,1)S(1)}, u32[]{:S(2)}, u32[]{:S(2)}) collective-permute-start(bf16[1024,192]{0,1:T(8,128)(2,1)S(1)} %convert_element_type.243), channel_id=1, source_target_pairs={{4,0},{8,4},{12,8},{16,12},{20,16},{24,20},{28,24},{5,1},{9,5},{13... | collective-permute-start | bytes 1179656 | tf_op jit(solution)/shard_map/ppermute | solution.py:17
  728.4 12.3 collective-permute-start.14
  746.6 141.6 %reduce-scatter.22.cloned.1.call-start = ((), (), s32[]{:S(2)}) async-start(), calls=%async_computation.14 | async-start | bytes 3932160 | tf_op jit(solution)/shard_map/reduce_scatter | solution.py:185
  753.2 200.8 %reduce-scatter.40.cloned.1.call-start = ((), (), s32[]{:S(2)}) async-start(), calls=%async_computation.25 | async-start | bytes 7077888
  768.6 251.4 %reduce-scatter.32.cloned.1.call-start = ((), (), s32[]{:S(2)}) async-start(), calls=%async_computation.21 | async-start | bytes 7077888 | tf_op jit(solution)/shard_map/reduce_scatter | solution.py:304
  777.7 308.0 %reduce-scatter.30.cloned.1.call-start = ((), (), s32[]{:S(2)}) async-start(), calls=%async_computation.20 | async-start | bytes 7077888 | tf_op jit(solution)/shard_map/reduce_scatter | solution.py:303
  786.4 341.9 %reduce-scatter.38.cloned.1.call-start = ((), (), s32[]{:S(2)}) async-start(), calls=%async_computation.24 | async-start | bytes 1769472
  798.0 373.0 %reduce-scatter.36.cloned.1.call-start = ((), (), s32[]{:S(2)}) async-start(), calls=%async_computation.23 | async-start | bytes 1769472
  801.0 416.7 %reduce-scatter.28.cloned.1.call-start = ((), (), s32[]{:S(2)}) async-start(), calls=%async_computation.19 | async-start | bytes 2654208 | tf_op jit(solution)/shard_map/reduce_scatter | solution.py:302
  806.4 457.6 %reduce-scatter.34.cloned.1.call-start = ((), (), s32[]{:S(2)}) async-start(), calls=%async_computation.22 | async-start | bytes 2654208
  809.7 58.9 %copy-start.63 = (f32[256]{0:T(256)S(1)}, f32[256]{0:T(256)}, u32[]{:S(2)}) copy-start(f32[256]{0:T(256)} %copy-done.62) | copy-start | bytes 3076
  809.7 78.5 %copy-start.51 = (f32[1536]{0:T(1024)S(1)}, f32[1536]{0:T(1024)}, u32[]{:S(2)}) copy-start(f32[1536]{0:T(1024)} %copy-done.50) | copy-start | bytes 18436
  809.7 78.5 %copy-start.57 = (f32[256]{0:T(256)S(1)}, f32[256]{0:T(256)}, u32[]{:S(2)}) copy-start(f32[256]{0:T(256)} %copy-done.56) | copy-start | bytes 3076
  809.7 78.5 %copy-start.61 = (f32[256]{0:T(256)S(1)}, f32[256]{0:T(256)}, u32[]{:S(2)}) copy-start(f32[256]{0:T(256)} %copy-done.60) | copy-start | bytes 3076
  (54 other events, 375.3 us)
Sparse Core Ops, SparseCore 0:
  13.1 64.6 all-gather.4
  183.9 62.9 reduce-scatter.19
  251.4 63.6 all-gather.6
  316.5 62.1 all-gather.8
  396.9 58.7 reduce-scatter.23
  462.2 63.6 all-gather.10
  746.7 78.5 reduce-scatter.25
  827.6 60.4 reduce-scatter.21
  892.1 61.8 reduce-scatter.39
  958.2 61.7 reduce-scatter.31
  1023.9 61.7 reduce-scatter.29
  1089.8 38.4 reduce-scatter.37
  1132.5 38.4 reduce-scatter.35
  1175.1 42.5 reduce-scatter.27
  1221.5 42.4 reduce-scatter.33
where the time goes:
time: 1270 us
  waiting for transfers between devices  757 us (60%)
  matrix products  286 us (23%)
  other arithmetic  77.4 us (6%)
  starting transfers between devices  45.6 us (4%)
  blocking collectives  41 us (3%)
  local copies, waits for them, and re-layouts  39.5 us (3%)
  between operations  22 us (2%)
    unnamed x19, waiting for transfers between devices  193 us
    reduce_scatter x1, waiting for transfers between devices, local(): lax.psum_scatter(up_grad, 'dp', scatter_dimension=0, tiled=True)  65.9 us
    reduce_scatter x1, waiting for transfers between devices, local(): lax.psum_scatter(gate_grad, 'dp', scatter_dimension=0, tiled=True)  65.7 us
    all_gather x1, waiting for transfers between devices, local(): lax.all_gather(grad_residual.astype(halves), 'tp', axis=0, tiled=True)  63.5 us
    reduce_scatter x1, waiting for transfers between devices, local(): lax.psum_scatter(jnp.dot(context, output_weight, preferred_element_type=f...  63.1 us
    all_gather x1, waiting for transfers between devices, local(): mlp_full = lax.all_gather(mlp_normed, 'tp', axis=0, tiled=True)  63 us
    reduce_scatter x1, waiting for transfers between devices, local(): lax.psum_scatter((contract_cols(grad_gate, gate_weight) + contract_cols(g...  58.9 us
    all_gather x1, waiting for transfers between devices, local(): grad_full = lax.all_gather(out_grad, 'tp', axis=0, tiled=True)  50.2 us
  transfers between devices with their start and end apart: 31, of which 20 were waited for; matrix products, arithmetic and copies ran while one was open for 16% of the time, Pallas kernels for 0%

commit v1 on v0

--- a/solution.py
+++ b/solution.py
@@ -86,11 +86,11 @@
     row_first = row_index * row_len
     seg_row = lax.dynamic_slice_in_dim(segment_ids, row_first, row_len)
     index_row = row_first + jnp.arange(row_len, dtype=jnp.int32)
-    previous = jnp.where(row_first > 0, segment_ids[jnp.maximum(row_first - 1, 0)], -1)
-    before = jnp.concatenate([previous[None], seg_row[:-1]])
-    starts = jnp.where(seg_row != before, index_row, 0)
-    first_start = jnp.sum((segment_ids < seg_row[0]).astype(jnp.int32))
-    token_positions = index_row - jnp.maximum(lax.cummax(starts), first_start)
+    every_index = jnp.arange(segment_ids.shape[0], dtype=jnp.int32)
+    marks = (segment_ids[1:] != segment_ids[:-1]).astype(jnp.int32)
+    starts = jnp.concatenate([jnp.zeros((1,), jnp.int32), marks * every_index[1:]])
+    is_at = (starts[None, :] <= index_row[:, None]).astype(jnp.int32)
+    token_positions = index_row - jnp.max(is_at * starts[None, :], axis=1)
     tokens32 = tokens.astype(floats)
     gain_attn = attn_gain.astype(floats)
     gain_mlp = mlp_gain.astype(floats)
@@ -273,9 +273,6 @@
         halves
     )
     proj_grad = contract_rows(normed_full, grads_joined)
-    query_grad = proj_grad[:, :q_cols]
-    key_grad = proj_grad[:, q_cols : q_cols + kv_cols]
-    value_grad = proj_grad[:, q_cols + kv_cols :]
     grad_normed = lax.psum_scatter(
         contract_cols(grads_joined, joined).astype(jnp.bfloat16),
         "tp",
@@ -285,27 +282,23 @@
     attn_norm_back = jax.vjp(rms_scale, tokens32, gain_attn)[1]
     grad_tokens_part, attn_gain_part = attn_norm_back(grad_normed)
     input_grad = grad_residual + grad_tokens_part
-    (
-        query_sum,
-        key_sum,
-        value_sum,
-        output_sum,
-        gate_sum,
-        up_sum,
-        down_sum,
-        attn_gain_sum,
-        mlp_gain_sum,
-    ) = (
-        lax.psum_scatter(query_grad, "dp", scatter_dimension=0, tiled=True),
-        lax.psum_scatter(key_grad, "dp", scatter_dimension=0, tiled=True),
-        lax.psum_scatter(value_grad, "dp", scatter_dimension=0, tiled=True),
-        lax.psum_scatter(output_grad, "dp", scatter_dimension=0, tiled=True),
-        lax.psum_scatter(gate_grad, "dp", scatter_dimension=0, tiled=True),
-        lax.psum_scatter(up_grad, "dp", scatter_dimension=0, tiled=True),
-        lax.psum_scatter(down_grad, "dp", scatter_dimension=0, tiled=True),
-        lax.psum_scatter(attn_gain_part, "dp", scatter_dimension=0, tiled=True),
-        lax.psum_scatter(mlp_gain_part, "dp", scatter_dimension=0, tiled=True),
-    )
+    def scatter_rows(grad):
+        return lax.psum_scatter(
+            grad.astype(halves), "dp", scatter_dimension=0, tiled=True
+        ).astype(floats)
+
+    mlp_sums = scatter_rows(jnp.concatenate([gate_grad, up_grad, down_grad], axis=1))
+    ff_cols = gate_weight.shape[1]
+    gate_sum = mlp_sums[:, :ff_cols]
+    up_sum = mlp_sums[:, ff_cols : 2 * ff_cols]
+    down_sum = mlp_sums[:, 2 * ff_cols :]
+    attn_sums = scatter_rows(jnp.concatenate([proj_grad, output_grad], axis=1))
+    query_sum = attn_sums[:, :q_cols]
+    key_sum = attn_sums[:, q_cols : q_cols + kv_cols]
+    value_sum = attn_sums[:, q_cols + kv_cols : q_cols + 2 * kv_cols]
+    output_sum = attn_sums[:, q_cols + 2 * kv_cols :]
+    attn_gain_sum = lax.psum_scatter(attn_gain_part, "dp", scatter_dimension=0, tiled=True)
+    mlp_gain_sum = lax.psum_scatter(mlp_gain_part, "dp", scatter_dimension=0, tiled=True)
     attn_gain_total, mlp_gain_total = lax.psum((attn_gain_sum, mlp_gain_sum), "tp")
     return (
         output.astype(halves),

time: 1270 us -> 950 us (0.75)
  waiting for transfers between devices: 757 us -> 440 us
  matrix products: 286 us -> 269 us
  local copies, waits for them, and re-layouts: 39.5 us -> 56.2 us
  other arithmetic: 77.4 us -> 93.9 us
    reduce_scatter x3 -> x0, waiting for transfers between devices: 178 us -> none  [the longest x1 65.9 us: local(): lax.psum_scatter(up_grad, 'dp', scatter_dimension=0, tiled=True)]
    unnamed x19 -> x12, waiting for transfers between devices: 193 us -> 37.4 us
    reduce_scatter x1, waiting for transfers between devices: 11.2 us -> 51.8 us  [local(): lax.psum_scatter(contract_cols(grads_joined, joined).astype(jnp.bfloat16)...]
    all_gather x1, waiting for transfers between devices: 63.5 us -> 32.2 us  [local(): lax.all_gather(grad_residual.astype(halves), 'tp', axis=0, tiled=True)]
    unnamed x113 -> x124, local copies, waits for them, and re-layouts: 25.9 us -> 42 us
    dot_general x5, matrix products: 36.4 us -> 22.2 us  [contract_rows(): lax.dot_general(left_side, right_side, (((0,), (0,)), ((), ())), preferre...]
  transfers between devices with their start and end apart: 31 -> 26, of which waited for: 20 -> 15; matrix products, arithmetic and copies ran while one was open for 16% -> 38% of each run, Pallas kernels for 0% -> 0%
where the time goes in v1:
time: 950 us; the launch traced here: 963 us
  waiting for transfers between devices  440 us (46%)
  matrix products  269 us (28%)
  other arithmetic  93.9 us (10%)
  local copies, waits for them, and re-layouts  56.2 us (6%)
  starting transfers between devices  45.7 us (5%)
  blocking collectives  33.1 us (3%)
  between operations  21.7 us (2%)
    reduce_scatter x1, waiting for transfers between devices, local(): lax.psum_scatter(jnp.dot(context, output_weight, preferred_element_type=f...  63 us
    all_gather x1, waiting for transfers between devices, local(): mlp_full = lax.all_gather(mlp_normed, 'tp', axis=0, tiled=True)  63 us
    reduce_scatter x1, waiting for transfers between devices, local(): lax.psum_scatter((contract_cols(grad_gate, gate_weight) + contract_cols(g...  58.9 us
    reduce_scatter x1, waiting for transfers between devices, local(): lax.psum_scatter(contract_cols(grads_joined, joined).astype(jnp.bfloat16)...  51.8 us
    all_gather x1, waiting for transfers between devices, local(): grad_full = lax.all_gather(out_grad, 'tp', axis=0, tiled=True)  50.2 us
    dot_general x4, matrix products, add_grads(): jnp.einsum('hgqk,qhgd->khd', probabilities.astype(halves), grad_context,...  49.2 us
    dot_general x7, matrix products, scores(): jnp.einsum('qhgd,khd->hgqk', query_heads, key_block.reshape(row_len, head...  45.2 us
    ppermute x16, starting transfers between devices, shifted(): return lax.ppermute(block, axis, route)  44.7 us
  transfers between devices with their start and end apart: 26, of which 15 were waited for; matrix products, arithmetic and copies ran while one was open for 38% of the time, Pallas kernels for 0%

profile of v1, /device:TPU:3, one launch (start us, length us, event | category | flops | bytes accessed | tf_op | source)
XLA Modules:
  0.0 963.2 jit_solution(15515510477019249277)
XLA Ops:
  31.7 7.1 compare_and_fusion
  38.8 39.0 %all-gather.5.cloned.1.call-done = bf16[1024,1536]{1,0:T(8,128)(2,1)} async-done(((bf16[256,1536]{1,0:T(8,128)(2,1)}), bf16[1024,1536]{1,0:T(8,128)(2,1)}) %all-gather.5.cloned.1.call-update) | async-done | bytes 3145744 | tf_op jit(solution)/shard_map/all_gather | solution.py:98
  77.8 5.4 fusion.122
  92.0 5.3 collective-permute-start.3
  121.6 5.8 bitcast_add_fusion.14
  127.4 16.1 %conditional.8 = ((f32[2,2,1024]{2,1,0:T(2,128)S(1)}, f32[2,2,1024]{2,1,0:T(2,128)S(1)}, f32[1024,2,2,96]{0,3,2,1:T(8,128)})) conditional(s32[]{:T(128)} %convert_element_type.210, (f32[2,2,1024]{2,1,0:T(2,128)S(1)}, f32[2,2,1024]{2,1,0:T(2,128)S(1)}, f32[1024,2,2,96]{0,3,2,1:T(8,128)}) %tuple.74, (pred[1024,1024]{0,1:T(8,128)(4,1)}, ...), branch_computations={%region_4.5_spmd, %region_5.8_spmd} | conditional | flops 1657548800 | bytes 78381224 | solution.py:129
  133.7 6.0 bitcast_add_fusion
  143.4 15.3 %conditional.9 = ((f32[2,2,1024]{2,1,0:T(2,128)S(1)}, f32[2,2,1024]{2,1,0:T(2,128)S(1)}, f32[1024,2,2,96]{0,3,2,1:T(8,128)})) conditional(s32[]{:T(128)} %convert_element_type.209, (f32[2,2,1024]{2,1,0:T(2,128)S(1)}, f32[2,2,1024]{2,1,0:T(2,128)S(1)}, f32[1024,2,2,96]{0,3,2,1:T(8,128)}) %get-tuple-element.492, (pred[1024,1024]{0,1:T(8,128)(4,1)}, ...), branch_computations={%region_8.9_spmd, %region_9.12_spmd} | conditional | flops 1657548800 | bytes 75235448 | solution.py:129
  149.0 6.0 bitcast_add_fusion.1
  158.7 15.3 %conditional.10 = ((f32[2,2,1024]{2,1,0:T(2,128)S(1)}, f32[2,2,1024]{2,1,0:T(2,128)S(1)}, f32[1024,2,2,96]{0,3,2,1:T(8,128)})) conditional(s32[]{:T(128)} %convert_element_type.208, (f32[2,2,1024]{2,1,0:T(2,128)S(1)}, f32[2,2,1024]{2,1,0:T(2,128)S(1)}, f32[1024,2,2,96]{0,3,2,1:T(8,128)}) %get-tuple-element.493, (pred[1024,1024]{0,1:T(8,128)(4,1)}, ...), branch_computations={%region_12.13_spmd, %region_13.16_spmd} | conditional | flops 1657548800 | bytes 75235448 | solution.py:129
  164.3 6.0 bitcast_add_fusion.2
  179.0 4.8 convolution_convert_fusion.1
  183.8 63.0 %reduce-scatter.11.cloned.1.call-done = bf16[256,1536]{1,0:T(8,128)(2,1)} async-done(((bf16[1024,1536]{1,0:T(8,128)(2,1)}), bf16[256,1536]{1,0:T(8,128)(2,1)}) %reduce-scatter.11.cloned.1.call-update) | async-done | bytes 786448 | tf_op jit(solution)/shard_map/reduce_scatter | solution.py:174
  252.0 63.0 %all-gather.7.cloned.1.call-done = bf16[1024,1536]{1,0:T(8,128)(2,1)} async-done(((bf16[256,1536]{1,0:T(8,128)(2,1)}), bf16[1024,1536]{1,0:T(8,128)(2,1)}) %all-gather.7.cloned.1.call-update) | async-done | bytes 3145744 | tf_op jit(solution)/shard_map/all_gather | solution.py:181
  315.0 8.4 fusion.148
  323.4 5.0 fusion.147
  328.4 50.2 %all-gather.9.cloned.1.call-done = bf16[1024,1536]{1,0:T(8,128)(2,1)} async-done(((bf16[256,1536]{1,0:T(8,128)(2,1)}), bf16[1024,1536]{1,0:T(8,128)(2,1)}) %all-gather.9.cloned.1.call-update) | async-done | bytes 3145744 | tf_op jit(solution)/shard_map/all_gather | solution.py:191
  378.6 9.6 %multiply_convert_fusion = (bf16[1024,1024]{1,0:T(8,128)(2,1)S(1)}, bf16[1024,1024]{1,0:T(8,128)(2,1)S(1)}, bf16[1024,1024]{1,0:T(8,128)(2,1)}) fusion(f32[1024,1024]{1,0:T(8,128)} %fusion.147, f32[1024,1024]{1,0:T(8,128)} %fusion.148, bf16[1024,1536]{1,0:T(8,128)(2,1)} %all-gather.9.cloned.1.call-done, bf16[1024,1536]{1,0:T(8,128)(2,1)S(1)} %copy-done), kind=kOutput, calls=%fused_computation.137 | convolution fusion | flops 3238002688 | bytes 20971520 | tf_op jit(solution)/shard_map/dot_general | solution.py:55
  391.8 5.0 add_convert_fusion
  396.8 58.9 %reduce-scatter.15.cloned.1.call-done = bf16[256,1536]{1,0:T(8,128)(2,1)} async-done(((bf16[1024,1536]{1,0:T(8,128)(2,1)}), bf16[256,1536]{1,0:T(8,128)(2,1)}) %reduce-scatter.15.cloned.1.call-update) | async-done | bytes 786448 | tf_op jit(solution)/shard_map/reduce_scatter | solution.py:200
  462.5 6.2 convolution_convert_fusion.3
  480.8 12.7 %copy.167 = bf16[1536,3072]{1,0:T(8,128)(2,1)} copy(bf16[1536,3072]{0,1:T(8,128)(2,1)} %pad_maximum_fusion) | data formatting | bytes 18874368
  493.6 32.2 %all-gather.11.cloned.1.call-done = bf16[1024,1536]{1,0:T(8,128)(2,1)} async-done(((bf16[256,1536]{1,0:T(8,128)(2,1)}), bf16[1024,1536]{1,0:T(8,128)(2,1)}) %all-gather.11.cloned.1.call-update) | async-done | bytes 3145744 | tf_op jit(solution)/shard_map/all_gather | solution.py:211
  539.1 14.2 %fusion.96 = f32[2,96,1024,1]{2,1,3,0:T(8,128)} fusion(bf16[1024,2,2,96]{0,3,2,1:T(8,128)(2,1)} %bitcast.123, f32[2,1024,1024,2]{2,1,3,0:T(8,128)} %copy-done.12, f32[2,2,1024]{2,1,0:T(2,128)} %get-tuple-element.314, pred[1024,1024]{0,1:T(8,128)(4,1)} %get-tuple-element.431), kind=kOutput, calls=%fused_computation.129 | convolution fusion | flops 822083584 | bytes 19415040 | tf_op jit(solution)/shard_map/hgqk,qhgd->khd/dot_general | solution.py:245
  553.3 10.1 %fusion.89 = bf16[2,2,1024,1024]{2,3,1,0:T(8,128)(2,1)S(1)} fusion(f32[2,1024,1024,2]{2,1,3,0:T(8,128)} %copy-done.12, f32[2,2,1024]{2,1,0:T(2,128)S(1)} %fusion.117, f32[2,2,1024]{2,1,0:T(2,128)} %get-tuple-element.314, pred[1024,1024]{0,1:T(8,128)(4,1)S(1)} %copy-done.30, bf16[1024,2,96,1]{0,2,3,1:T(8,128)(2,1)S(1)} %bitcast.486, ...), kind=kOutput, calls=%fused_computation.119 | convolution fusion | flops 830472192 | bytes 27426816 | tf_op jit(solution)/shard_map/qhgd,khd->hgqk/dot_general | solution.py:225
  569.1 42.1 %conditional.13 = ((f32[1024,2,2,96]{0,3,2,1:T(8,128)}, f32[1024,192]{0,1:T(8,128)}, f32[1024,192]{0,1:T(8,128)})) conditional(s32[]{:T(128)} %convert_element_type.208, (f32[1024,2,2,96]{0,3,2,1:T(8,128)}, f32[1024,192]{0,1:T(8,128)}, f32[1024,192]{0,1:T(8,128)}) %tuple.81, (pred[1024,1024]{0,1:T(8,128)(4,1)}, bf16[1024,192]{0,1:T(8,128)(2,1)}, ...), branch_computations={%region_27.28_spmd, %region_28.29_spmd} | conditional | flops 4069851136 | bytes 100843640 | solution.py:129
  570.1 9.2 fusion.144
  579.4 11.7 %fusion.49 = f32[2,1024,96,1]{1,2,3,0:T(8,128)} fusion(bf16[1024,2,2,96]{0,3,2,1:T(8,128)(2,1)} %get-tuple-element.227, f32[2,1024,1024,2]{2,1,3,0:T(8,128)} %fusion.144, f32[2,2,1024]{2,1,0:T(2,128)} %bitcast.52, pred[1024,1024]{0,1:T(8,128)(4,1)} %get-tuple-element.222), kind=kOutput, calls=%fused_computation.60 | convolution fusion | flops 822083584 | bytes 19415040 | tf_op jit(solution)/shard_map/cond/branch_1_fun/hgqk,qhgd->khd/dot_general | solution.py:245
  591.1 9.6 fusion.45
  617.4 6.0 fusion.123
  628.7 40.6 %conditional.14 = ((f32[1024,2,2,96]{0,3,2,1:T(8,128)}, f32[1024,192]{0,1:T(8,128)}, f32[1024,192]{0,1:T(8,128)})) conditional(s32[]{:T(128)} %convert_element_type.209, (f32[1024,2,2,96]{0,3,2,1:T(8,128)}, f32[1024,192]{0,1:T(8,128)}, f32[1024,192]{0,1:T(8,128)}) %tuple.83, (pred[1024,1024]{0,1:T(8,128)(4,1)}, bf16[1024,192]{0,1:T(8,128)(2,1)}, ...), branch_computations={%region_29.30_spmd, %region_30.31_spmd} | conditional | flops 4069851136 | bytes 99270776 | solution.py:129
  628.7 9.5 fusion.145
  638.2 11.6 %fusion.60 = f32[2,1024,96,1]{1,2,3,0:T(8,128)} fusion(bf16[1024,2,2,96]{0,3,2,1:T(8,128)(2,1)} %get-tuple-element.237, f32[2,1024,1024,2]{2,1,3,0:T(8,128)} %fusion.145, f32[2,2,1024]{2,1,0:T(2,128)} %bitcast.71, pred[1024,1024]{0,1:T(8,128)(4,1)} %get-tuple-element.232), kind=kOutput, calls=%fused_computation.76 | convolution fusion | flops 822083584 | bytes 19415040 | tf_op jit(solution)/shard_map/cond/branch_1_fun/hgqk,qhgd->khd/dot_general | solution.py:245
  649.8 9.5 fusion.56
  687.0 40.6 %conditional.15 = ((f32[1024,2,2,96]{0,3,2,1:T(8,128)}, f32[1024,192]{0,1:T(8,128)}, f32[1024,192]{0,1:T(8,128)})) conditional(s32[]{:T(128)} %convert_element_type.210, (f32[1024,2,2,96]{0,3,2,1:T(8,128)}, f32[1024,192]{0,1:T(8,128)}, f32[1024,192]{0,1:T(8,128)}) %tuple.85, (pred[1024,1024]{0,1:T(8,128)(4,1)}, bf16[1024,192]{0,1:T(8,128)(2,1)S(1)}, ...), branch_computations={%region_31.32_spmd, %region_32.33_spmd} | conditional | flops 4069851136 | bytes 97697880 | solution.py:129
  687.0 9.4 fusion.146
  696.4 11.6 %fusion.71 = f32[2,1024,96,1]{1,2,3,0:T(8,128)} fusion(bf16[1024,2,2,96]{0,3,2,1:T(8,128)(2,1)} %get-tuple-element.247, f32[2,1024,1024,2]{2,1,3,0:T(8,128)} %fusion.146, f32[2,2,1024]{2,1,0:T(2,128)} %bitcast.90, pred[1024,1024]{0,1:T(8,128)(4,1)} %get-tuple-element.242), kind=kOutput, calls=%fused_computation.92 | convolution fusion | flops 822083584 | bytes 19415040 | tf_op jit(solution)/shard_map/cond/branch_1_fun/hgqk,qhgd->khd/dot_general | solution.py:245
  708.0 9.5 fusion.67
  736.6 7.7 collective-permute-done.14
  751.4 5.8 copy.165
  757.3 6.8 convolution_convert_fusion
  764.2 6.4 convolution_convert_fusion.5
  789.1 36.7 %reduce-scatter.19.cloned.1.call-done = bf16[192,1152]{1,0:T(8,128)(2,1)} async-done(((bf16[1536,1152]{1,0:T(8,128)(2,1)}), bf16[192,1152]{1,0:T(8,128)(2,1)}) %reduce-scatter.19.cloned.1.call-update) | async-done | bytes 442384
  836.4 51.8 %reduce-scatter.17.cloned.1.call-done = bf16[256,1536]{1,0:T(8,128)(2,1)} async-done(((bf16[1024,1536]{1,0:T(8,128)(2,1)}), bf16[256,1536]{1,0:T(8,128)(2,1)}) %reduce-scatter.17.cloned.1.call-update) | async-done | bytes 786448 | tf_op jit(solution)/shard_map/reduce_scatter | solution.py:276
  890.3 22.2 %all-reduce.6 = (f32[1536]{0:T(1024)S(1)}, f32[1536]{0:T(1024)S(1)}) all-reduce(f32[1536]{0:T(1024)S(1)} %get-tuple-element.369, f32[1536]{0:T(1024)} %get-tuple-element.367), channel_id=6, replica_groups=mesh['dp'=8,'tp'=4] {'dp'}, use_global_device_ids=true, to_apply=%region_36.37.clone | all-reduce | flops 3072 | bytes 24576
  912.7 10.9 %all-reduce.7 = (f32[192]{0:T(256)}, f32[192]{0:T(256)}) all-reduce(f32[192]{0:T(256)S(1)} %dynamic-slice.1, f32[192]{0:T(256)S(1)} %dynamic-slice.3), channel_id=1, replica_groups=mesh['dp'=8,'tp'=4] {'tp'}, use_global_device_ids=true, to_apply=%region_37.38 | all-reduce | flops 384 | bytes 3072 | tf_op jit(solution)/shard_map/psum | solution.py:302
  924.2 26.7 %reduce-scatter.13.cloned.1.call-done = bf16[256,1536]{1,0:T(8,128)(2,1)} async-done(((bf16[1024,1536]{1,0:T(8,128)(2,1)}), bf16[256,1536]{1,0:T(8,128)(2,1)}) %reduce-scatter.13.cloned.1.call-update) | async-done | bytes 786448 | tf_op jit(solution)/shard_map/reduce_scatter | solution.py:185
  950.9 4.9 fusion.114
  (313 shorter events, 242.0 us)
Async XLA Ops:
  7.2 371.4 %copy-start = (bf16[1024,1536]{1,0:T(8,128)(2,1)S(1)}, bf16[1024,1536]{1,0:T(8,128)(2,1)}, u32[]{:S(2)}) copy-start(bf16[1024,1536]{1,0:T(8,128)(2,1)} %param.39) | copy-start | bytes 9437188
  7.2 18.9 %copy-start.52 = (s32[8192]{0:T(1024)S(1)}, s32[8192]{0:T(1024)}, u32[]{:S(2)}) copy-start(s32[8192]{0:T(1024)} %param.30) | copy-start | bytes 98308
  7.2 70.6 %all-gather.5.cloned.1.call-start = ((), (), s32[]{:S(2)}) async-start(), calls=%async_computation.6 | async-start | bytes 3932160 | tf_op jit(solution)/shard_map/all_gather | solution.py:98
  12.9 234.0 %reduce-scatter.11.cloned.1.call-start = ((), (), s32[]{:S(2)}) async-start(), calls=%async_computation.7 | async-start | bytes 3932160 | tf_op jit(solution)/shard_map/reduce_scatter | solution.py:174
  14.4 16.5 %copy-start.58 = (s32[1024]{0:T(1024)}, s32[1024]{0:T(1024)S(1)}, u32[]{:S(2)}) copy-start(s32[1024]{0:T(1024)S(1)} %get-tuple-element.420) | copy-start | bytes 12292
  31.6 57.7 %copy-start.22 = (f32[1024,48]{0,1:T(8,128)}, f32[1024,48]{0,1:T(8,128)S(1)}, u32[]{:S(2)}) copy-start(f32[1024,48]{0,1:T(8,128)S(1)} %get-tuple-element.433) | copy-start | bytes 589828
  31.7 57.7 %copy-start.24 = (f32[1024,48]{0,1:T(8,128)}, f32[1024,48]{0,1:T(8,128)S(1)}, u32[]{:S(2)}) copy-start(f32[1024,48]{0,1:T(8,128)S(1)} %get-tuple-element.434) | copy-start | bytes 589828
  83.2 38.3 %copy-start.49 = (bf16[1024,192]{0,1:T(8,128)(2,1)}, bf16[1024,192]{0,1:T(8,128)(2,1)S(1)}, u32[]{:S(2)}) copy-start(bf16[1024,192]{0,1:T(8,128)(2,1)S(1)} %slice.111) | copy-start | bytes 1179652
  83.3 18.6 %copy-start.29 = (pred[1024,1024]{0,1:T(8,128)(4,1)S(1)}, pred[1024,1024]{0,1:T(8,128)(4,1)}, u32[]{:S(2)}) copy-start(pred[1024,1024]{0,1:T(8,128)(4,1)} %get-tuple-element.431) | copy-start | bytes 3145732
  83.4 8.5 collective-permute-start.1
  87.4 17.7 %copy-start.33 = (bf16[1024,2,48]{0,2,1:T(8,128)(2,1)}, bf16[1024,2,48]{0,2,1:T(8,128)(2,1)S(1)}, u32[]{:S(2)}) copy-start(bf16[1024,2,48]{0,2,1:T(8,128)(2,1)S(1)} %get-tuple-element.412) | copy-start | bytes 589828
  87.4 17.7 %copy-start.35 = (bf16[1024,2,48]{0,2,1:T(8,128)(2,1)}, bf16[1024,2,48]{0,2,1:T(8,128)(2,1)S(1)}, u32[]{:S(2)}) copy-start(bf16[1024,2,48]{0,2,1:T(8,128)(2,1)S(1)} %get-tuple-element.413) | copy-start | bytes 589828
  87.5 9.8 %collective-permute-start = (bf16[1024,192]{0,1:T(8,128)(2,1)S(1)}, bf16[1024,192]{0,1:T(8,128)(2,1)S(1)}, u32[]{:S(2)}, u32[]{:S(2)}) collective-permute-start(bf16[1024,192]{0,1:T(8,128)(2,1)S(1)} %bitcast.487), channel_id=1, source_target_pairs={{0,4},{4,8},{8,12},{12,16},{16,20},{20,24},{24,28},{1,5},{5,9},{9,... | collective-permute-start | bytes 1179656 | tf_op jit(solution)/shard_map/ppermute | solution.py:17
  89.7 25.4 %copy-start.1 = (bf16[1024,4,96]{0,2,1:T(8,128)(2,1)}, bf16[1024,4,96]{0,2,1:T(8,128)(2,1)S(1)}, u32[]{:S(2)}) copy-start(bf16[1024,4,96]{0,2,1:T(8,128)(2,1)S(1)} %pad_maximum_fusion.4) | copy-start | bytes 2359300
  92.0 35.4 %copy-start.70 = (bf16[1024,192]{0,1:T(8,128)(2,1)}, bf16[1024,192]{0,1:T(8,128)(2,1)S(1)}, u32[]{:S(2)}) copy-start(bf16[1024,192]{0,1:T(8,128)(2,1)S(1)} %collective-permute-done.1) | copy-start | bytes 1179652
  92.0 13.1 %collective-permute-start.3 = (bf16[1024,192]{0,1:T(8,128)(2,1)S(1)}, bf16[1024,192]{0,1:T(8,128)(2,1)S(1)}, u32[]{:S(2)}, u32[]{:S(2)}) collective-permute-start(bf16[1024,192]{0,1:T(8,128)(2,1)S(1)} %collective-permute-done.1), channel_id=1, source_target_pairs={{0,4},{4,8},{8,12},{12,16},{16,20},{20,24},{24,28},{1,5},{5,9},{9,... | collective-permute-start | bytes 1179656 | tf_op jit(solution)/shard_map/ppermute | solution.py:17
  97.3 30.1 %copy-start.37 = (bf16[1024,192]{0,1:T(8,128)(2,1)}, bf16[1024,192]{0,1:T(8,128)(2,1)S(1)}, u32[]{:S(2)}) copy-start(bf16[1024,192]{0,1:T(8,128)(2,1)S(1)} %collective-permute-done) | copy-start | bytes 1179652
  97.3 10.0 %collective-permute-start.2 = (bf16[1024,192]{0,1:T(8,128)(2,1)S(1)}, bf16[1024,192]{0,1:T(8,128)(2,1)S(1)}, u32[]{:S(2)}, u32[]{:S(2)}) collective-permute-start(bf16[1024,192]{0,1:T(8,128)(2,1)S(1)} %collective-permute-done), channel_id=1, source_target_pairs={{0,4},{4,8},{8,12},{12,16},{16,20},{20,24},{24,28},{1,5},{5,9},{9,... | collective-permute-start | bytes 1179656 | tf_op jit(solution)/shard_map/ppermute | solution.py:17
  105.1 16.5 %copy-start.12 = (f32[2,1024,1024,2]{2,1,3,0:T(8,128)}, f32[2,1024,1024,2]{2,1,3,0:T(8,128)S(1)}, u32[]{:S(2)}) copy-start(f32[2,1024,1024,2]{2,1,3,0:T(8,128)S(1)} %get-tuple-element.436) | copy-start | bytes 50331652
  105.1 10.1 %collective-permute-start.5 = (bf16[1024,192]{0,1:T(8,128)(2,1)S(1)}, bf16[1024,192]{0,1:T(8,128)(2,1)}, u32[]{:S(2)}, u32[]{:S(2)}) collective-permute-start(bf16[1024,192]{0,1:T(8,128)(2,1)S(1)} %collective-permute-done.3), channel_id=1, source_target_pairs={{0,4},{4,8},{8,12},{12,16},{16,20},{20,24},{24,28},{1,5},{5,9},{9,... | collective-permute-start | bytes 1179656 | tf_op jit(solution)/shard_map/ppermute | solution.py:17
  107.3 10.1 %collective-permute-start.4 = (bf16[1024,192]{0,1:T(8,128)(2,1)S(1)}, bf16[1024,192]{0,1:T(8,128)(2,1)}, u32[]{:S(2)}, u32[]{:S(2)}) collective-permute-start(bf16[1024,192]{0,1:T(8,128)(2,1)S(1)} %collective-permute-done.2), channel_id=1, source_target_pairs={{0,4},{4,8},{8,12},{12,16},{16,20},{20,24},{24,28},{1,5},{5,9},{9,... | collective-permute-start | bytes 1179656 | tf_op jit(solution)/shard_map/ppermute | solution.py:17
  115.2 58.9 %collective-permute-start.7 = (bf16[1024,192]{0,1:T(8,128)(2,1)}, bf16[1024,192]{0,1:T(8,128)(2,1)}, u32[]{:S(2)}, u32[]{:S(2)}) collective-permute-start(bf16[1024,192]{0,1:T(8,128)(2,1)} %collective-permute-done.5), channel_id=1, source_target_pairs={{0,4},{4,8},{8,12},{12,16},{16,20},{20,24},{24,28},{1,5},{5,9},{9,... | collective-permute-start | bytes 1179656 | tf_op jit(solution)/shard_map/ppermute | solution.py:17
  117.3 56.7 %collective-permute-start.6 = (bf16[1024,192]{0,1:T(8,128)(2,1)}, bf16[1024,192]{0,1:T(8,128)(2,1)}, u32[]{:S(2)}, u32[]{:S(2)}) collective-permute-start(bf16[1024,192]{0,1:T(8,128)(2,1)} %collective-permute-done.4), channel_id=1, source_target_pairs={{0,4},{4,8},{8,12},{12,16},{16,20},{20,24},{24,28},{1,5},{5,9},{9,... | collective-permute-start | bytes 1179656 | tf_op jit(solution)/shard_map/ppermute | solution.py:17
  183.8 131.2 %all-gather.7.cloned.1.call-start = ((), (), s32[]{:S(2)}) async-start(), calls=%async_computation.8 | async-start | bytes 3932160 | tf_op jit(solution)/shard_map/all_gather | solution.py:181
  183.8 274.8 %copy-start.53 = (f32[1536]{0:T(1024)}, f32[1536]{0:T(1024)S(1)}, u32[]{:S(2)}) copy-start(f32[1536]{0:T(1024)S(1)} %convert_element_type.221) | copy-start | bytes 18436
  248.6 210.0 %copy-start.57 = (f32[256]{0:T(256)}, f32[256]{0:T(256)S(1)}, u32[]{:S(2)}) copy-start(f32[256]{0:T(256)S(1)} %fusion.130) | copy-start | bytes 3076
  251.2 127.4 %all-gather.9.cloned.1.call-start = ((), (), s32[]{:S(2)}) async-start(), calls=%async_computation.10 | async-start | bytes 3932160 | tf_op jit(solution)/shard_map/all_gather | solution.py:191
  251.8 203.9 %reduce-scatter.15.cloned.1.call-start = ((), (), s32[]{:S(2)}) async-start(), calls=%async_computation.11 | async-start | bytes 3932160 | tf_op jit(solution)/shard_map/reduce_scatter | solution.py:200
  396.7 129.1 %all-gather.11.cloned.1.call-start = ((), (), s32[]{:S(2)}) async-start(), calls=%async_computation.12 | async-start | bytes 3932160 | tf_op jit(solution)/shard_map/all_gather | solution.py:211
  462.0 309.9 %reduce-scatter.21.cloned.1.call-start = ((), (), s32[]{:S(2)}) async-start(), calls=%async_computation.15 | async-start | bytes 10616832
  493.6 332.3 %reduce-scatter.19.cloned.1.call-start = ((), (), s32[]{:S(2)}) async-start(), calls=%async_computation.14 | async-start | bytes 3981312
  534.3 32.8 %collective-permute-start.8 = (bf16[1024,192]{0,1:T(8,128)(2,1)}, bf16[1024,192]{0,1:T(8,128)(2,1)S(1)}, u32[]{:S(2)}, u32[]{:S(2)}) collective-permute-start(bf16[1024,192]{0,1:T(8,128)(2,1)} %get-tuple-element.299), channel_id=1, source_target_pairs={{4,0},{8,4},{12,8},{16,12},{20,16},{24,20},{28,24},{5,1},{9,5},{13... | collective-permute-start | bytes 1179656 | tf_op jit(solution)/shard_map/ppermute | solution.py:17
  537.1 30.9 %collective-permute-start.9 = (bf16[1024,192]{0,1:T(8,128)(2,1)S(1)}, bf16[1024,192]{0,1:T(8,128)(2,1)S(1)}, u32[]{:S(2)}, u32[]{:S(2)}) collective-permute-start(bf16[1024,192]{0,1:T(8,128)(2,1)S(1)} %get-tuple-element.300), channel_id=1, source_target_pairs={{4,0},{8,4},{12,8},{16,12},{20,16},{24,20},{28,24},{5,1},{9,5},{13... | collective-permute-start | bytes 1179656 | tf_op jit(solution)/shard_map/ppermute | solution.py:17
  539.1 14.3 %copy-start.30 = (pred[1024,1024]{0,1:T(8,128)(4,1)S(1)}, pred[1024,1024]{0,1:T(8,128)(4,1)}, u32[]{:S(2)}) copy-start(pred[1024,1024]{0,1:T(8,128)(4,1)} %get-tuple-element.431) | copy-start | bytes 3145732
  539.1 14.3 %copy-start.50 = (bf16[1024,192]{0,1:T(8,128)(2,1)S(1)}, bf16[1024,192]{0,1:T(8,128)(2,1)}, u32[]{:S(2)}) copy-start(bf16[1024,192]{0,1:T(8,128)(2,1)} %copy-done.49) | copy-start | bytes 1179652
  569.1 48.3 %copy-start.34 = (bf16[1024,2,48]{0,2,1:T(8,128)(2,1)S(1)}, bf16[1024,2,48]{0,2,1:T(8,128)(2,1)}, u32[]{:S(2)}) copy-start(bf16[1024,2,48]{0,2,1:T(8,128)(2,1)} %copy-done.33) | copy-start | bytes 589828
  569.1 48.3 %copy-start.36 = (bf16[1024,2,48]{0,2,1:T(8,128)(2,1)S(1)}, bf16[1024,2,48]{0,2,1:T(8,128)(2,1)}, u32[]{:S(2)}) copy-start(bf16[1024,2,48]{0,2,1:T(8,128)(2,1)} %copy-done.35) | copy-start | bytes 589828
  613.5 10.0 %collective-permute-start.11 = (bf16[1024,192]{0,1:T(8,128)(2,1)S(1)}, bf16[1024,192]{0,1:T(8,128)(2,1)S(1)}, u32[]{:S(2)}, u32[]{:S(2)}) collective-permute-start(bf16[1024,192]{0,1:T(8,128)(2,1)S(1)} %convert_element_type.240), channel_id=1, source_target_pairs={{4,0},{8,4},{12,8},{16,12},{20,16},{24,20},{28,24},{5,1},{9,5},{13... | collective-permute-start | bytes 1179656 | tf_op jit(solution)/shard_map/ppermute | solution.py:17
  615.5 12.3 %collective-permute-start.10 = (bf16[1024,192]{0,1:T(8,128)(2,1)S(1)}, bf16[1024,192]{0,1:T(8,128)(2,1)S(1)}, u32[]{:S(2)}, u32[]{:S(2)}) collective-permute-start(bf16[1024,192]{0,1:T(8,128)(2,1)S(1)} %convert_element_type.238), channel_id=1, source_target_pairs={{4,0},{8,4},{12,8},{16,12},{20,16},{24,20},{28,24},{5,1},{9,5},{13... | collective-permute-start | bytes 1179656 | tf_op jit(solution)/shard_map/ppermute | solution.py:17
  671.7 15.4 %copy-start.38 = (bf16[1024,192]{0,1:T(8,128)(2,1)S(1)}, bf16[1024,192]{0,1:T(8,128)(2,1)}, u32[]{:S(2)}) copy-start(bf16[1024,192]{0,1:T(8,128)(2,1)} %copy-done.37) | copy-start | bytes 1179652
  671.7 10.1 %collective-permute-start.13 = (bf16[1024,192]{0,1:T(8,128)(2,1)S(1)}, bf16[1024,192]{0,1:T(8,128)(2,1)S(1)}, u32[]{:S(2)}, u32[]{:S(2)}) collective-permute-start(bf16[1024,192]{0,1:T(8,128)(2,1)S(1)} %convert_element_type.244), channel_id=1, source_target_pairs={{4,0},{8,4},{12,8},{16,12},{20,16},{24,20},{28,24},{5,1},{9,5},{13... | collective-permute-start | bytes 1179656 | tf_op jit(solution)/shard_map/ppermute | solution.py:17
  673.7 12.3 %collective-permute-start.12 = (bf16[1024,192]{0,1:T(8,128)(2,1)S(1)}, bf16[1024,192]{0,1:T(8,128)(2,1)S(1)}, u32[]{:S(2)}, u32[]{:S(2)}) collective-permute-start(bf16[1024,192]{0,1:T(8,128)(2,1)S(1)} %convert_element_type.242), channel_id=1, source_target_pairs={{4,0},{8,4},{12,8},{16,12},{20,16},{24,20},{28,24},{5,1},{9,5},{13... | collective-permute-start | bytes 1179656 | tf_op jit(solution)/shard_map/ppermute | solution.py:17
  730.1 14.5 %collective-permute-start.15 = (bf16[1024,192]{0,1:T(8,128)(2,1)S(1)}, bf16[1024,192]{0,1:T(8,128)(2,1)S(1)}, u32[]{:S(2)}, u32[]{:S(2)}) collective-permute-start(bf16[1024,192]{0,1:T(8,128)(2,1)S(1)} %convert_element_type.249), channel_id=1, source_target_pairs={{4,0},{8,4},{12,8},{16,12},{20,16},{24,20},{28,24},{5,1},{9,5},{13... | collective-permute-start | bytes 1179656 | tf_op jit(solution)/shard_map/ppermute | solution.py:17
  732.1 12.3 %collective-permute-start.14 = (bf16[1024,192]{0,1:T(8,128)(2,1)S(1)}, bf16[1024,192]{0,1:T(8,128)(2,1)S(1)}, u32[]{:S(2)}, u32[]{:S(2)}) collective-permute-start(bf16[1024,192]{0,1:T(8,128)(2,1)S(1)} %convert_element_type.247), channel_id=1, source_target_pairs={{4,0},{8,4},{12,8},{16,12},{20,16},{24,20},{28,24},{5,1},{9,5},{13... | collective-permute-start | bytes 1179656 | tf_op jit(solution)/shard_map/ppermute | solution.py:17
  757.2 131.1 %reduce-scatter.17.cloned.1.call-start = ((), (), s32[]{:S(2)}) async-start(), calls=%async_computation.13 | async-start | bytes 3932160 | tf_op jit(solution)/shard_map/reduce_scatter | solution.py:276
  764.1 186.8 %reduce-scatter.13.cloned.1.call-start = ((), (), s32[]{:S(2)}) async-start(), calls=%async_computation.9 | async-start | bytes 3932160 | tf_op jit(solution)/shard_map/reduce_scatter | solution.py:185
  786.5 101.7 %copy-start.56 = (f32[1536]{0:T(1024)S(1)}, f32[1536]{0:T(1024)}, u32[]{:S(2)}) copy-start(f32[1536]{0:T(1024)} %copy-done.55) | copy-start | bytes 18436
  827.9 123.1 %copy-start.54 = (f32[1536]{0:T(1024)S(1)}, f32[1536]{0:T(1024)}, u32[]{:S(2)}) copy-start(f32[1536]{0:T(1024)} %copy-done.53) | copy-start | bytes 18436
  (51 other events, 260.7 us)
Sparse Core Ops, SparseCore 0:
  13.0 64.6 all-gather.4
  183.9 62.9 reduce-scatter.10
  251.3 63.6 all-gather.6
  316.4 62.1 all-gather.8
  396.9 58.7 reduce-scatter.14
  462.1 63.6 all-gather.10
  529.3 75.0 reduce-scatter.20
  757.3 68.4 reduce-scatter.18
  828.1 60.1 reduce-scatter.16
  890.4 60.4 reduce-scatter.12

commit v2 on v1

--- a/solution.py
+++ b/solution.py
@@ -1,9 +1,273 @@
+import functools
+
 import jax
 import jax.numpy as jnp
 from jax import lax
+from jax.experimental import pallas as pl
+from jax.experimental.pallas import tpu as pltpu
 from jax.sharding import PartitionSpec as P
 
 HEAD_WIDTH = 96
+BLK = 256
+LOG2E = 1.4426950408889634
+SCORE = LOG2E * HEAD_WIDTH ** (-0.5)
+VSCALE = 2.0 ** -9
+floats = jnp.float32
+halves = jnp.bfloat16
+
+
+def dot_nn(a, b):
+    return jnp.dot(a, b, preferred_element_type=floats)
+
+
+def dot_nt(a, b):
+    return lax.dot_general(a, b, (((1,), (1,)), ((), ())), preferred_element_type=floats)
+
+
+def pair_state(sc, kb, qb):
+    key_base = sc[0, kb]
+    q_base, least, most = sc[1, qb], sc[2, qb], sc[3, qb]
+    needed = (key_base <= q_base + (BLK - 1)) & (key_base + (BLK - 1) >= least)
+    whole = (key_base + (BLK - 1) <= q_base) & (key_base >= most)
+    return key_base, needed, whole
+
+
+def allowed_mask(key_base, tok_ref, start_ref, lanes):
+    keys = key_base + lax.broadcasted_iota(jnp.int32, (BLK, BLK), 0)
+    return (keys <= tok_ref[0:1, lanes]) & (keys >= start_ref[0:1, lanes])
+
+
+def fwd_kernel(n, width, first, last, sc, q_ref, tok_ref, start_ref, *refs):
+    pieces = refs[:n]
+    refs = refs[n:]
+    if not first:
+        acc_in, sum_in = refs[:2]
+        refs = refs[2:]
+    out_acc, out_sum = refs[:2]
+    kv, keys_nat, acc, total, q_wide, sem = refs[2:]
+    per = width // BLK
+    for i in range(n):
+        pltpu.make_async_copy(pieces[i], kv.at[i], sem.at[i]).start()
+    if first:
+        acc[...] = jnp.zeros_like(acc)
+        total[...] = jnp.zeros_like(total)
+    else:
+        acc[...] = acc_in[...]
+        total[...] = sum_in[...]
+    for i in range(n):
+        pltpu.make_async_copy(pieces[i], kv.at[i], sem.at[i]).wait()
+    heads_kv = pieces[0].shape[0] // (2 * HEAD_WIDTH)
+    group = q_ref.shape[0] // (heads_kv * HEAD_WIDTH)
+    v_off = heads_kv * HEAD_WIDTH
+    places = [
+        (h, slice((h * group + g) * HEAD_WIDTH, (h * group + g + 1) * HEAD_WIDTH), slice(qb * BLK, (qb + 1) * BLK),
+         slice(h * HEAD_WIDTH, (h + 1) * HEAD_WIDTH), slice((qb * group + g) * BLK, (qb * group + g + 1) * BLK), h * group + g)
+        for h in range(heads_kv) for g in range(group) for qb in range(q_ref.shape[1] // BLK)
+    ]
+    for h, rows, lanes, wrows, wlanes, hd in places:
+        q_wide[wrows, wlanes] = q_ref[rows, lanes]
+
+    def key_block(kb, carry):
+        piece = kb // per
+        klanes = pl.ds(pl.multiple_of((kb % per) * BLK, BLK), BLK)
+        for h in range(heads_kv):
+            keys_nat[h] = kv[piece, h * HEAD_WIDTH : (h + 1) * HEAD_WIDTH, klanes].T
+
+        def query_block(qb, carry):
+            key_base, needed, whole = pair_state(sc, kb, qb)
+            lanes = pl.ds(pl.multiple_of(qb * BLK, BLK), BLK)
+
+            def unit(masked):
+                wide = pl.ds(pl.multiple_of(qb * (group * BLK), group * BLK), group * BLK)
+                if masked:
+                    allowed = allowed_mask(key_base, tok_ref, start_ref, lanes)
+                    allowed = jnp.concatenate([allowed] * group, axis=1)
+                scores = [
+                    dot_nn(keys_nat[h], q_wide[h * HEAD_WIDTH : (h + 1) * HEAD_WIDTH, wide])
+                    for h in range(heads_kv)
+                ]
+                weights = [jnp.exp2(s * SCORE) for s in scores]
+                if masked:
+                    weights = [jnp.where(allowed, w, 0.0) for w in weights]
+                sums = [jnp.sum(w, axis=0, keepdims=True) for w in weights]
+                parts = [
+                    dot_nn(
+                        kv[piece, v_off + h * HEAD_WIDTH : v_off + (h + 1) * HEAD_WIDTH, klanes],
+                        weights[h].astype(halves),
+                    )
+                    for h in range(heads_kv)
+                ]
+                for h in range(heads_kv):
+                    total[h : h + 1, wide] += sums[h]
+                    acc[h * HEAD_WIDTH : (h + 1) * HEAD_WIDTH, wide] += parts[h]
+
+            pl.when(needed & whole)(lambda: unit(False))
+            pl.when(needed & jnp.logical_not(whole))(lambda: unit(True))
+            return carry
+
+        return lax.fori_loop(0, q_ref.shape[1] // BLK, query_block, carry)
+
+    lax.fori_loop(0, n * per, key_block, 0)
+    if last:
+        for h, rows, lanes, wrows, wlanes, hd in places:
+            row = total[h : h + 1, wlanes]
+            out_acc[rows, lanes] = (acc[wrows, wlanes] * ((1.0 / VSCALE) / row)).astype(halves)
+            out_sum[hd : hd + 1, lanes] = jnp.log2(row)
+    else:
+        out_acc[...] = acc[...]
+        out_sum[...] = total[...]
+
+
+VM = pl.BlockSpec(memory_space=pltpu.VMEM)
+SM = pl.BlockSpec(memory_space=pltpu.SMEM)
+HB = pl.BlockSpec(memory_space=pl.ANY)
+
+
+def attend_forward(sc, q_t, tok, start, pieces, state=None, last=True):
+    n, width = len(pieces), pieces[0].shape[1]
+    heads = q_t.shape[0] // HEAD_WIDTH
+    heads_kv = pieces[0].shape[0] // (2 * HEAD_WIDTH)
+    first = state is None
+    tokens = q_t.shape[1]
+    out_shape = (
+        jax.ShapeDtypeStruct(q_t.shape, halves if last else floats),
+        jax.ShapeDtypeStruct((heads, tokens), floats),
+    )
+    return pl.pallas_call(
+        functools.partial(fwd_kernel, n, width, first, last),
+        out_shape=out_shape,
+        in_specs=[SM, VM, VM, VM] + [HB] * n + ([] if first else [VM, VM]),
+        out_specs=(VM, VM),
+        scratch_shapes=[
+            pltpu.VMEM((n,) + pieces[0].shape, halves),
+            pltpu.VMEM((heads_kv, BLK, HEAD_WIDTH), halves),
+            pltpu.VMEM((heads_kv * HEAD_WIDTH, tokens * heads // heads_kv), floats),
+            pltpu.VMEM((heads_kv, tokens * heads // heads_kv), floats),
+            pltpu.VMEM((heads_kv * HEAD_WIDTH, tokens * heads // heads_kv), halves),
+            pltpu.SemaphoreType.DMA((n,)),
+        ],
+        compiler_params=pltpu.CompilerParams(vmem_limit_bytes=40 << 20),
+        name="attend_forward",
+    )(sc, q_t, tok, start, *pieces, *(() if first else state))
+
+
+def bwd_kernel(n, width, first, sc, q_ref, do_ref, log_ref, delta_ref, tok_ref, start_ref, *refs):
+    pieces = refs[:n]
+    refs = refs[n:]
+    if not first:
+        dq_in = refs[0]
+        refs = refs[1:]
+    dq_out = refs[0]
+    douts = refs[1 : 1 + n]
+    kv, dkv, keys_nat, vals_nat, acc, q_wide, do_wide, log_wide, delta_wide, dq_wide, sem, osem = refs[1 + n :]
+    per = width // BLK
+    for i in range(n):
+        pltpu.make_async_copy(pieces[i], kv.at[i], sem.at[i]).start()
+    for i in range(n):
+        pltpu.make_async_copy(pieces[i], kv.at[i], sem.at[i]).wait()
+    heads_kv = pieces[0].shape[0] // (2 * HEAD_WIDTH)
+    group = q_ref.shape[0] // (heads_kv * HEAD_WIDTH)
+    v_off = heads_kv * HEAD_WIDTH
+    places = [
+        (h, slice((h * group + g) * HEAD_WIDTH, (h * group + g + 1) * HEAD_WIDTH), slice(qb * BLK, (qb + 1) * BLK),
+         slice(h * HEAD_WIDTH, (h + 1) * HEAD_WIDTH), slice((qb * group + g) * BLK, (qb * group + g + 1) * BLK), h * group + g)
+        for h in range(heads_kv) for g in range(group) for qb in range(q_ref.shape[1] // BLK)
+    ]
+    for h, rows, lanes, wrows, wlanes, hd in places:
+        q_wide[wrows, wlanes] = q_ref[rows, lanes]
+        do_wide[wrows, wlanes] = do_ref[rows, lanes]
+        log_wide[h : h + 1, wlanes] = log_ref[hd : hd + 1, lanes]
+        delta_wide[h : h + 1, wlanes] = delta_ref[hd : hd + 1, lanes]
+        dq_wide[wrows, wlanes] = jnp.zeros((HEAD_WIDTH, BLK), floats) if first else dq_in[rows, lanes]
+    out_scale = (1.0 / VSCALE) * HEAD_WIDTH ** (-0.5)
+
+    def key_block(kb, carry):
+        piece = kb // per
+        klanes = pl.ds(pl.multiple_of((kb % per) * BLK, BLK), BLK)
+        for h in range(heads_kv):
+            keys_nat[h] = kv[piece, h * HEAD_WIDTH : (h + 1) * HEAD_WIDTH, klanes].T
+            vals_nat[h] = kv[piece, v_off + h * HEAD_WIDTH : v_off + (h + 1) * HEAD_WIDTH, klanes].T
+        acc[...] = jnp.zeros_like(acc)
+
+        def query_block(qb, carry):
+            key_base, needed, whole = pair_state(sc, kb, qb)
+            lanes = pl.ds(pl.multiple_of(qb * BLK, BLK), BLK)
+
+            def unit(masked):
+                wide = pl.ds(pl.multiple_of(qb * (group * BLK), group * BLK), group * BLK)
+                if masked:
+                    allowed = allowed_mask(key_base, tok_ref, start_ref, lanes)
+                    allowed = jnp.concatenate([allowed] * group, axis=1)
+                heads = range(heads_kv)
+                krows = [slice(h * HEAD_WIDTH, (h + 1) * HEAD_WIDTH) for h in heads]
+                vrows = [slice(v_off + h * HEAD_WIDTH, v_off + (h + 1) * HEAD_WIDTH) for h in heads]
+                qt = [q_wide[krows[h], wide] for h in heads]
+                dot = [do_wide[krows[h], wide] for h in heads]
+                scores = [dot_nn(keys_nat[h], qt[h]) for h in heads]
+                dprobs = [dot_nn(vals_nat[h], dot[h]) for h in heads]
+                weights = [
+                    jnp.exp2(scores[h] * SCORE - log_wide[h : h + 1, wide]) for h in heads
+                ]
+                if masked:
+                    weights = [jnp.where(allowed, w, 0.0) for w in weights]
+                ds = [
+                    (weights[h] * (dprobs[h] - delta_wide[h : h + 1, wide])).astype(halves)
+                    for h in heads
+                ]
+                dv = [dot_nt(dot[h], weights[h].astype(halves)) for h in heads]
+                dk = [dot_nt(qt[h], ds[h]) for h in heads]
+                dq = [dot_nn(kv[piece, krows[h], klanes], ds[h]) for h in heads]
+                for h in heads:
+                    acc[vrows[h], :] += dv[h]
+                    acc[krows[h], :] += dk[h]
+                    dq_wide[krows[h], wide] += dq[h]
+
+            pl.when(needed & whole)(lambda: unit(False))
+            pl.when(needed & jnp.logical_not(whole))(lambda: unit(True))
+            return carry
+
+        carry = lax.fori_loop(0, q_ref.shape[1] // BLK, query_block, carry)
+        dkv[piece, 0:v_off, klanes] = (acc[0:v_off, :] * out_scale).astype(halves)
+        dkv[piece, v_off:, klanes] = acc[v_off:, :].astype(halves)
+        return carry
+
+    lax.fori_loop(0, n * per, key_block, 0)
+    for i in range(n):
+        pltpu.make_async_copy(dkv.at[i], douts[i], osem.at[i]).start()
+    for h, rows, lanes, wrows, wlanes, hd in places:
+        dq_out[rows, lanes] = dq_wide[wrows, wlanes] * out_scale
+    for i in range(n):
+        pltpu.make_async_copy(dkv.at[i], douts[i], osem.at[i]).wait()
+
+
+def attend_backward(sc, q_t, do_t, log_total, delta, tok, start, pieces):
+    n, width = len(pieces), pieces[0].shape[1]
+    heads_kv = pieces[0].shape[0] // (2 * HEAD_WIDTH)
+    wide = q_t.shape[0] // (heads_kv * HEAD_WIDTH) * q_t.shape[1]
+    outs = pl.pallas_call(
+        functools.partial(bwd_kernel, n, width, True),
+        out_shape=(jax.ShapeDtypeStruct(q_t.shape, floats),)
+        + tuple(jax.ShapeDtypeStruct(p.shape, halves) for p in pieces),
+        in_specs=[SM] + [VM] * 6 + [HB] * n,
+        out_specs=(VM,) + (HB,) * n,
+        scratch_shapes=[
+            pltpu.VMEM((n,) + pieces[0].shape, halves),
+            pltpu.VMEM((n,) + pieces[0].shape, halves),
+            pltpu.VMEM((heads_kv, BLK, HEAD_WIDTH), halves),
+            pltpu.VMEM((heads_kv, BLK, HEAD_WIDTH), halves),
+            pltpu.VMEM((pieces[0].shape[0], BLK), floats),
+            pltpu.VMEM((heads_kv * HEAD_WIDTH, wide), halves),
+            pltpu.VMEM((heads_kv * HEAD_WIDTH, wide), halves),
+            pltpu.VMEM((heads_kv, wide), floats),
+            pltpu.VMEM((heads_kv, wide), floats),
+            pltpu.VMEM((heads_kv * HEAD_WIDTH, wide), floats),
+            pltpu.SemaphoreType.DMA((n,)),
+            pltpu.SemaphoreType.DMA((n,)),
+        ],
+        compiler_params=pltpu.CompilerParams(vmem_limit_bytes=44 << 20),
+        name="attend_backward",
+    )(sc, q_t, do_t, log_total, delta, tok, start, *pieces)
+    return outs[0], list(outs[1:])
 
 
 eps_norm = 1e-05
@@ -315,9 +579,374 @@
     )
 
 
+def routes(target):
+    pairs = []
+    for index in range(32):
+        dp, z = divmod(index, 4)
+        there = target(dp // 4, dp // 2 % 2, dp % 2, z)
+        if there is not None:
+            y, x, c, z = there
+            pairs.append((index, (y * 4 + x * 2 + c) * 4 + z))
+    return pairs
+
+
+ROUTES = {
+    "core": routes(lambda y, x, c, z: (y, x, 1 - c, z)),
+    "x": routes(lambda y, x, c, z: (y, 1 - x, c, z)),
+    "y": routes(lambda y, x, c, z: (1 - y, x, c, z)),
+    "near": routes(lambda y, x, c, z: (y, x, c, z ^ 1)),
+    "far": routes(lambda y, x, c, z: (y, x, c, z ^ 2)),
+    "cross": routes(lambda y, x, c, z: (y, x, 1 - c, z ^ 2)),
+    "odd_far": routes(lambda y, x, c, z: (y, x, c, z ^ 2) if c else None),
+    "odd_x": routes(lambda y, x, c, z: (y, 1 - x, c, z) if c else None),
+    "odd_y": routes(lambda y, x, c, z: (1 - y, x, c, z) if c else None),
+    "odd_xy": routes(lambda y, x, c, z: (1 - y, 1 - x, c, z) if c else None),
+    "home": routes(lambda y, x, c, z: (y, x, 0, z ^ 2) if c else (y, x, 1, z)),
+    "x_up": routes(lambda y, x, c, z: None if x else (y, 1, c, z)),
+    "y_up": routes(lambda y, x, c, z: None if y else (1, x, c, z)),
+    "x_down": routes(lambda y, x, c, z: (y, 0, c, z) if x else None),
+    "y_down": routes(lambda y, x, c, z: (0, x, c, z) if y else None),
+    "relay": routes(lambda y, x, c, z: (1, 0, c, z) if x and y else None),
+    "unrelay": routes(lambda y, x, c, z: (1, 1, c, z) if y and not x else None),
+}
+FAR_BASE = 1 << 24
+
+
+def send(block, way):
+    return lax.ppermute(block, ("dp", "tp"), ROUTES[way])
+
+
+def assemble_kernel(where, own_ref, a_ref, x_ref, y_ref, xy_ref, out_ref, sem):
+    odd, y, x = where[0], where[1], where[2]
+    rows = a_ref.shape[0]
+
+    @pl.when(odd == 0)
+    def _():
+        copy = pltpu.make_async_copy(own_ref, out_ref, sem.at[0])
+        copy.start()
+        copy.wait()
+
+    @pl.when(odd != 0)
+    def _():
+        copies = []
+        for i, (ref, slot) in enumerate(
+            (
+                (a_ref, 2 * y + x),
+                (x_ref, 2 * y + (1 - x)),
+                (y_ref, 2 * (1 - y) + x),
+                (xy_ref, 2 * (1 - y) + (1 - x)),
+            )
+        ):
+            copies.append(
+                pltpu.make_async_copy(ref, out_ref.at[pl.ds(slot * rows, rows)], sem.at[i])
+            )
+        for copy in copies:
+            copy.start()
+        for copy in copies:
+            copy.wait()
+
+
+def fetch_quarter(weight, where, slot):
+    rows = weight.shape[0] // 4
+    part = send(lax.dynamic_slice_in_dim(weight, slot * rows, rows), "odd_far")
+    pieces = (part, send(part, "odd_x"), send(part, "odd_y"), send(part, "odd_xy"))
+    return pl.pallas_call(
+        assemble_kernel,
+        out_shape=jax.ShapeDtypeStruct(weight.shape, weight.dtype),
+        in_specs=[SM] + [HB] * 5,
+        out_specs=HB,
+        scratch_shapes=[pltpu.SemaphoreType.DMA((4,))],
+        compiler_params=pltpu.CompilerParams(vmem_limit_bytes=4 << 20),
+        name="assemble",
+    )(where, weight, *pieces)
+
+
+def gather_group(block):
+    near = send(block, "near")
+    beside = send(block, "core")
+    return jnp.concatenate([block, beside]), jnp.concatenate([near, send(near, "core")])
+
+
+def scatter_group(here, there):
+    rows = here.shape[0] // 2
+    there_sum = there[:rows] + send(there[rows:].astype(halves), "core").astype(floats)
+    here_sum = here[:rows] + send(here[rows:].astype(halves), "core").astype(floats)
+    return here_sum + send(there_sum.astype(halves), "near").astype(floats)
+
+
+def dot_tt(a, b):
+    return lax.dot_general(a, b, (((0,), (1,)), ((), ())), preferred_element_type=floats)
+
+
+def rope_tables(positions):
+    half_width = HEAD_WIDTH // 2
+    inverse = 1.0 / rope_base ** (jnp.arange(half_width, dtype=floats) * 2.0 / HEAD_WIDTH)
+    angles = inverse[:, None] * positions.astype(floats)[None, :]
+    return jnp.cos(angles), jnp.sin(angles)
+
+
+def turn(linear, cosine, sine):
+    shaped = linear.reshape(-1, 2, HEAD_WIDTH // 2, linear.shape[-1])
+    one, two = shaped[:, 0], shaped[:, 1]
+    turned = jnp.stack([one * cosine - two * sine, two * cosine + one * sine], axis=1)
+    return turned.reshape(linear.shape)
+
+
+def norm_back(vectors, gain, grad):
+    root = lax.rsqrt(jnp.mean(vectors * vectors, axis=-1, keepdims=True) + eps_norm)
+    weighted = grad * gain
+    slope = jnp.mean(weighted * vectors, axis=-1, keepdims=True)
+    back = root * weighted - vectors * (root * root * root * slope)
+    return back, jnp.sum(grad * vectors * root, axis=0)
+
+
+def sum_rows_over_plane(grad, x, y, x_first):
+    shaped = grad.reshape(2, 2, -1, grad.shape[-1])
+
+    def pick(array, at, axis):
+        return lax.dynamic_index_in_dim(array, at, axis, keepdims=False)
+
+    axes = (("x", x, 1), ("y", y, 0)) if x_first else (("y", y, 0), ("x", x, 1))
+    (way, at, axis), (way_two, at_two, _) = axes
+    come = send(pick(shaped, 1 - at, axis), way)
+    half = pick(shaped, at, axis).astype(floats) + come.astype(floats)
+    come = send(pick(half, 1 - at_two, 0).astype(halves), way_two)
+    return pick(half, at_two, 0) + come.astype(floats)
+
+
+def sum_rows_home(part, odd):
+    rows = part.shape[0] // 2
+    first, second = part[:rows], part[rows:]
+    one = send(jnp.where(odd, first, second).astype(halves), "home").astype(floats)
+    two = send(second.astype(halves), "odd_far").astype(floats)
+    return jnp.where(odd, one + two, first + one)
+
+
+def local_regrouped(
+    tokens,
+    out_grad,
+    segment_ids,
+    attn_gain,
+    query_weight,
+    key_matrix,
+    value_matrix,
+    output_weight,
+    mlp_gain,
+    gate_weight,
+    up_weight,
+    down_weight,
+):
+    block = tokens.shape[0]
+    row_len = 4 * block
+    dp, z = lax.axis_index("dp"), lax.axis_index("tp")
+    y, x, c = dp // 4, dp // 2 % 2, dp % 2
+    j = dp // 2
+    odd = c == 1
+    pair, side = z // 2, z % 2
+    q_cols, kv_cols = query_weight.shape[1], key_matrix.shape[1]
+    heads = q_cols // HEAD_WIDTH
+    group_width = q_cols // kv_cols
+    ff_cols = gate_weight.shape[1]
+    gain_attn, gain_mlp = attn_gain.astype(floats), mlp_gain.astype(floats)
+
+    def base(j_of, core, pair_of, side_of):
+        return (2 * j_of + core) * row_len + (2 * pair_of + side_of) * block
+
+    where = jnp.stack([c, y, x]).astype(jnp.int32)
+    slot = 2 * y + x
+    joined = fetch_quarter(
+        jnp.concatenate([query_weight, key_matrix, value_matrix], axis=1), where, slot
+    )
+    weight_o = fetch_quarter(output_weight, where, slot)
+    weight_gate = fetch_quarter(gate_weight, where, slot)
+    weight_up = fetch_quarter(up_weight, where, slot)
+    weight_down = fetch_quarter(down_weight, where, slot)
+
+    bases = [
+        base(j, c, pair, side),
+        base(j, 1 - c, pair, side),
+        base(j, c, pair, 1 - side),
+        base(j, 1 - c, pair, 1 - side),
+    ]
+    counts = [jnp.sum((segment_ids < item).astype(jnp.int32)) for item in range(1, 4)]
+    segs = jnp.concatenate([lax.dynamic_slice_in_dim(segment_ids, b, block) for b in bases])
+    index = jnp.concatenate([b + jnp.arange(block, dtype=jnp.int32) for b in bases])
+    start = jnp.zeros_like(segs)
+    for item in range(1, 4):
+        start = jnp.where(segs == item, counts[item - 1], start)
+    cosine, sine = rope_tables(index - start)
+    index_row, start_row = index[None, :], start[None, :]
+    starts4 = start.reshape(4, block)
+
+    tokens32 = tokens.astype(floats)
+    normed = rms_scale(tokens32, gain_attn).astype(halves)
+    here_n, there_n = gather_group(normed)
+    qs, kvs = [], []
+    for n, part in enumerate((here_n, there_n)):
+        lanes = slice(2 * n * block, 2 * (n + 1) * block)
+        linear = dot_tt(joined, part)
+        cos_n, sin_n = cosine[:, lanes], sine[:, lanes]
+        turned = turn(linear[: q_cols + kv_cols], cos_n, sin_n)
+        qs.append(turned[:q_cols].astype(halves))
+        kvs.append(
+            jnp.concatenate(
+                [
+                    turned[q_cols:].astype(halves),
+                    (linear[q_cols + kv_cols :].astype(halves) * VSCALE).astype(halves),
+                ]
+            )
+        )
+    q_t = jnp.concatenate(qs, axis=1)
+
+    pieces, piece_bases = [], []
+
+    def there_or_far(present, value):
+        return jnp.where(present, value, FAR_BASE)
+
+    for n in range(2):
+        side_n = side if n == 0 else 1 - side
+        for cross in range(2):
+            block_kv = kvs[n] if cross == 0 else send(kvs[n], "cross")
+            from_x = send(block_kv, "x_up")
+            from_y = send(block_kv, "y_up")
+            from_relay = send(from_y, "relay")
+            cores = (c, 1 - c) if cross == 0 else (1 - c, c)
+            pair_of = pair if cross == 0 else 1 - pair
+            for piece, j_of, present in (
+                (block_kv, j, None),
+                (from_x, j - 1, x == 1),
+                (from_y, j - 2, y == 1),
+                (from_relay, j - 1, (y == 1) & (x == 0)),
+            ):
+                pieces.append(piece)
+                for core in cores:
+                    where_from = base(j_of, core, pair_of, side_n)
+                    piece_bases.append(
+                        where_from if present is None else there_or_far(present, where_from)
+                    )
+    total_blocks = len(piece_bases)
+
+    def padded(values):
+        values = jnp.stack(values).astype(jnp.int32)
+        return jnp.pad(values, (0, total_blocks - values.shape[0]))
+
+    sc = jnp.stack(
+        [
+            padded(piece_bases),
+            padded(bases),
+            jnp.pad(starts4[:, 0], (0, total_blocks - 4)),
+            jnp.pad(starts4[:, -1], (0, total_blocks - 4)),
+        ]
+    )
+    context_t, log_total = attend_forward(sc, q_t, index_row, start_row, pieces)
+
+    def halves_of(product):
+        return product(slice(0, 2 * block)), product(slice(2 * block, 4 * block))
+
+    here_o, there_o = halves_of(
+        lambda lanes: lax.dot_general(
+            context_t[:, lanes], weight_o, (((0,), (0,)), ((), ())), preferred_element_type=floats
+        )
+    )
+    residual = tokens32 + scatter_group(here_o, there_o)
+
+    mlp_normed = rms_scale(residual, gain_mlp).astype(halves)
+    here_m, there_m = gather_group(mlp_normed)
+    here_g, there_g = gather_group(out_grad)
+    hiddens, d_gates, d_ups, outs, d_norms = [], [], [], [], []
+    for part, grad in ((here_m, here_g), (there_m, there_g)):
+        gate_pre = jnp.dot(part, weight_gate, preferred_element_type=floats)
+        up_pre = jnp.dot(part, weight_up, preferred_element_type=floats)
+        d_hidden = contract_cols(grad, weight_down)
+        sigma = jax.nn.sigmoid(gate_pre)
+        silu = gate_pre * sigma
+        hiddens.append((silu * up_pre).astype(halves))
+        d_gates.append(
+            (d_hidden * up_pre * (sigma * (1.0 + gate_pre * (1.0 - sigma)))).astype(halves)
+        )
+        d_ups.append((d_hidden * silu).astype(halves))
+    for n in range(2):
+        d_norms.append(contract_cols(d_gates[n], weight_gate) + contract_cols(d_ups[n], weight_up))
+    for n in range(2):
+        outs.append(jnp.dot(hiddens[n], weight_down, preferred_element_type=floats))
+    grad_mlp_normed = scatter_group(*d_norms)
+    output = residual + scatter_group(*outs)
+    mlp_full = jnp.concatenate([here_m, there_m])
+    grad_full = jnp.concatenate([here_g, there_g])
+    gate_grad = contract_rows(mlp_full, jnp.concatenate(d_gates)).astype(halves)
+    up_grad = contract_rows(mlp_full, jnp.concatenate(d_ups)).astype(halves)
+    down_grad = contract_rows(grad_full, jnp.concatenate(hiddens)).astype(halves)
+    gate_sum = sum_rows_home(sum_rows_over_plane(gate_grad, x, y, True), odd)
+    up_sum = sum_rows_home(sum_rows_over_plane(up_grad, x, y, False), odd)
+    down_sum = sum_rows_home(sum_rows_over_plane(down_grad, x, y, True), odd)
+
+    grad_part, mlp_gain_part = norm_back(residual, gain_mlp, grad_mlp_normed)
+    grad_residual = out_grad.astype(floats) + grad_part
+    here_e, there_e = gather_group(grad_residual.astype(halves))
+
+    d_context_t = jnp.concatenate(
+        [contract_cols(weight_o, here_e), contract_cols(weight_o, there_e)], axis=1
+    ).astype(halves)
+    attn_grad_full = jnp.concatenate([here_e, there_e])
+    output_grad = dot_tt(attn_grad_full, context_t).astype(halves)
+    output_sum = sum_rows_home(sum_rows_over_plane(output_grad, x, y, False), odd)
+    delta = jnp.sum(
+        (d_context_t.astype(floats) * context_t.astype(floats)).reshape(heads, HEAD_WIDTH, -1), axis=1
+    )
+    d_query_t, d_pieces = attend_backward(
+        sc, q_t, d_context_t, log_total, delta * VSCALE, index_row, start_row, pieces
+    )
+    d_halves = []
+    for n in range(2):
+        sums = []
+        for cross in range(2):
+            own, from_x, from_y, from_relay = d_pieces[8 * n + 4 * cross : 8 * n + 4 * cross + 4]
+            back = send(from_relay, "unrelay").astype(floats)
+            from_y = (from_y.astype(floats) + back).astype(halves)
+            sums.append(
+                own.astype(floats)
+                + send(from_x, "x_down").astype(floats)
+                + send(from_y, "y_down").astype(floats)
+            )
+        d_halves.append(sums[0] + send(sums[1].astype(halves), "cross").astype(floats))
+    d_kv = jnp.concatenate(d_halves, axis=1)
+    d_turned = turn(jnp.concatenate([d_query_t, d_kv[:kv_cols]]), cosine, -sine)
+    d_linear = jnp.concatenate([d_turned, d_kv[kv_cols:]]).astype(halves)
+    normed_full = jnp.concatenate([here_n, there_n])
+    here_d, there_d = halves_of(lambda lanes: dot_tt(d_linear[:, lanes], joined))
+    grad_normed = scatter_group(here_d, there_d)
+    proj_grad = lax.dot_general(
+        normed_full, d_linear, (((0,), (1,)), ((), ())), preferred_element_type=floats
+    ).astype(halves)
+    proj_sum = sum_rows_home(sum_rows_over_plane(proj_grad, x, y, True), odd)
+    grad_tokens_part, attn_gain_part = norm_back(tokens32, gain_attn, grad_normed)
+    input_grad = grad_residual + grad_tokens_part
+
+    gains = jnp.stack([attn_gain_part, mlp_gain_part])
+    for way in ("core", "x", "y", "near", "far"):
+        gains = gains + send(gains, way)
+    per = gains.shape[1] // 8
+    gains = lax.dynamic_slice_in_dim(gains, dp * per, per, axis=1)
+    return (
+        output.astype(halves),
+        input_grad,
+        gains[0],
+        proj_sum[:, :q_cols],
+        proj_sum[:, q_cols : q_cols + kv_cols],
+        proj_sum[:, q_cols + kv_cols :],
+        output_sum.T,
+        gains[1],
+        gate_sum,
+        up_sum,
+        down_sum.T,
+    )
+
+
 def solution(mesh):
+    regroup = mesh.shape["dp"] == 8 and mesh.shape["tp"] == 4
+    chosen = local_regrouped if regroup else local
     return jax.shard_map(
-        local,
+        chosen,
         mesh=mesh,
         in_specs=(
             P(("dp", "tp"), None),

time: 950 us -> 674 us (0.71); the launches traced: 963 us -> 663 us
  matrix products: 269 us -> 57.8 us
  waiting for transfers between devices: 440 us -> 244 us
  starting transfers between devices: 45.7 us -> 189 us
  Pallas kernels: 0 us -> 77.4 us
  other arithmetic: 93.9 us -> 44.7 us
  blocking collectives: 33.1 us -> 0 us
  between operations: 21.7 us -> 3.74 us
  local copies, waits for them, and re-layouts: 56.2 us -> 46.7 us
    ppermute x16 -> x97, waiting for transfers between devices: 18.2 us -> 244 us  [send(): return lax.ppermute(block, ('dp', 'tp'), ROUTES[way])]
    reduce_scatter x4 -> x0, waiting for transfers between devices: 200 us -> none  [the longest x1 63 us: local(): lax.psum_scatter(jnp.dot(context, output_weight, preferred_element_type=f...]
    dot_general x32 -> x14, matrix products: 218 us -> 30.7 us  [the longest x5 10.4 us: dot_tt(): lax.dot_general(a, b, (((0,), (1,)), ((), ())), preferred_element_type=fl...]
    all_gather x4 -> x0, waiting for transfers between devices: 184 us -> none  [the longest x1 63 us: local(): mlp_full = lax.all_gather(mlp_normed, 'tp', axis=0, tiled=True)]
    ppermute x16 -> x97, starting transfers between devices: 44.7 us -> 189 us  [send(): return lax.ppermute(block, ('dp', 'tp'), ROUTES[way])]
    pallas_call x0 -> x7, Pallas kernels: none -> 77.4 us  [the longest x1 44.6 us: attend_backward(): pl.pallas_call(functools.partial(bwd_kernel, n, width, True), out_shape=(...]
    unnamed x12 -> x0, waiting for transfers between devices: 37.4 us -> none
    unnamed x1 -> x0, blocking collectives: 22.2 us -> none
  transfers between devices with their start and end apart: 26 -> 97, of which waited for: 15 -> 30; matrix products, arithmetic and copies ran while one was open for 38% -> 17% of each run, Pallas kernels for 0% -> 5%
where the time goes in v2:
time: 674 us; the launch traced here: 663 us
  waiting for transfers between devices  244 us (36%)
  starting transfers between devices  189 us (28%)
  Pallas kernels  77.4 us (11%)
  matrix products  57.8 us (9%)
  local copies, waits for them, and re-layouts  46.7 us (7%)
  other arithmetic  44.7 us (7%)
    ppermute x97, waiting for transfers between devices, send(): return lax.ppermute(block, ('dp', 'tp'), ROUTES[way])  244 us
    ppermute x97, starting transfers between devices, send(): return lax.ppermute(block, ('dp', 'tp'), ROUTES[way])  189 us
    pallas_call x1, Pallas kernels, attend_backward(): pl.pallas_call(functools.partial(bwd_kernel, n, width, True), out_shape=(...  44.6 us
    unnamed x247, local copies, waits for them, and re-layouts  28.2 us
    pallas_call x1, Pallas kernels, attend_forward(): pl.pallas_call(functools.partial(fwd_kernel, n, width, first, last), out_...  26.1 us
    dot_general x3, matrix products, contract_rows(): lax.dot_general(left_side, right_side, (((0,), (0,)), ((), ())), preferre...  14.4 us
  transfers between devices with their start and end apart: 97, of which 30 were waited for; matrix products, arithmetic and copies ran while one was open for 17% of the time, Pallas kernels for 5%

profile of v2, /device:TPU:3, one launch (start us, length us, event | category | flops | bytes accessed | tf_op | source)
XLA Modules:
  0.0 663.3 jit_solution(3168810729231221623)
XLA Ops:
  9.6 4.2 collective-permute-start.21
  24.5 14.8 %collective-permute-done.a_ref = bf16[384,768]{1,0:T(8,128)(2,1)S(1)} collective-permute-done((bf16[384,768]{1,0:T(8,128)(2,1)}, bf16[384,768]{1,0:T(8,128)(2,1)S(1)}, u32[]{:S(2)}, u32[]{:S(2)}) %collective-permute-start) | collective-permute-done | bytes 589856 | tf_op jit(solution)/shard_map/ppermute | solution.py:616
  41.5 3.1 collective-permute-start.2
  51.9 6.6 collective-permute-done.2.y_ref
  58.5 3.1 collective-permute-start.22
  61.6 3.1 collective-permute-start.23
  77.8 3.2 collective-permute-start.8
  87.2 21.3 %collective-permute-done.10.refs_4_ = bf16[384,512]{1,0:T(8,128)(2,1)S(1)} collective-permute-done((bf16[384,512]{1,0:T(8,128)(2,1)S(1)}, bf16[384,512]{1,0:T(8,128)(2,1)S(1)}, u32[]{:S(2)}, u32[]{:S(2)}) %collective-permute-start.10) | collective-permute-done | bytes 393248 | tf_op jit(solution)/shard_map/ppermute | solution.py:616
  112.6 4.4 collective-permute-done.17.refs_12_
  135.0 3.9 collective-permute-done.14.refs_9_
  139.0 3.9 collective-permute-start.33
  149.5 26.1 %attend_forward.1 = (bf16[384,1024]{1,0:T(8,128)(2,1)S(1)}, f32[4,1024]{1,0:T(4,128)S(1)}) custom-call(s32[4,32]{1,0:T(4,128)S(1)} %pad_add_fusion.2.sc, bf16[384,1024]{1,0:T(8,128)(2,1)S(1)} %pad_maximum_fusion.10.q_ref, s32[1,1024]{1,0:T(1,128)S(1)} %bitcast.147, s32[1,1024]{1,0:T(1,128)S(1)} %compare_select_fusion.2.start_ref, ...), custom_call_target="tpu_custom_call" | custom-call | tf_op jit(solution)/shard_map/attend_forward/pallas_call | solution.py:136
  176.9 8.4 %collective-permute-start.39 = (bf16[256,1536]{1,0:T(8,128)(2,1)S(1)}, bf16[256,1536]{1,0:T(8,128)(2,1)S(1)}, u32[]{:S(2)}, u32[]{:S(2)}) collective-permute-start(bf16[256,1536]{1,0:T(8,128)(2,1)S(1)} %copy-done.28), channel_id=1, source_target_pairs={{4,20},{5,21},{6,22},{7,23},{12,28},{13,29},{14,30},{15,31},{20,4}... | collective-permute-start | bytes 2359304 | tf_op jit(solution)/shard_map/ppermute | solution.py:616
  185.4 7.1 %collective-permute-start.40 = (bf16[256,1536]{1,0:T(8,128)(2,1)S(1)}, bf16[256,1536]{1,0:T(8,128)(2,1)S(1)}, u32[]{:S(2)}, u32[]{:S(2)}) collective-permute-start(bf16[256,1536]{1,0:T(8,128)(2,1)S(1)} %copy-done.28), channel_id=1, source_target_pairs={{4,28},{5,29},{6,30},{7,31},{12,20},{13,21},{14,22},{15,23},{20,12... | collective-permute-start | bytes 2359304 | tf_op jit(solution)/shard_map/ppermute | solution.py:616
  205.1 6.3 collective-permute-start.30
  212.3 3.4 collective-permute-start.31
  233.9 3.3 collective-permute-done.31.y_ref
  254.5 12.7 %collective-permute-done.42 = bf16[256,1536]{1,0:T(8,128)(2,1)S(1)} collective-permute-done((bf16[256,1536]{1,0:T(8,128)(2,1)S(1)}, bf16[256,1536]{1,0:T(8,128)(2,1)S(1)}, u32[]{:S(2)}, u32[]{:S(2)}) %collective-permute-start.42) | collective-permute-done | bytes 786464 | tf_op jit(solution)/shard_map/ppermute | solution.py:616
  276.1 4.1 multiply_convert_fusion.1
  285.0 14.1 %collective-permute-start.50 = (bf16[256,1536]{1,0:T(8,128)(2,1)}, bf16[256,1536]{1,0:T(8,128)(2,1)}, u32[]{:S(2)}, u32[]{:S(2)}) collective-permute-start(bf16[256,1536]{1,0:T(8,128)(2,1)} %slice.420), channel_id=1, source_target_pairs={{0,4},{1,5},{2,6},{3,7},{4,0},{5,1},{6,2},{7,3},{8,12},{9,13},{10,... | collective-permute-start | bytes 2359304 | tf_op jit(solution)/shard_map/ppermute | solution.py:616
  302.2 3.5 convolution_convert_fusion.2
  307.1 5.1 convolution_convert_fusion.1
  312.2 5.7 convolution_convert_fusion
  324.0 13.9 %collective-permute-done.51 = bf16[256,1536]{1,0:T(8,128)(2,1)S(1)} collective-permute-done((bf16[256,1536]{1,0:T(8,128)(2,1)S(1)}, bf16[256,1536]{1,0:T(8,128)(2,1)S(1)}, u32[]{:S(2)}, u32[]{:S(2)}) %collective-permute-start.51) | collective-permute-done | bytes 786464 | tf_op jit(solution)/shard_map/ppermute | solution.py:616
  338.0 8.0 %collective-permute-start.93 = (bf16[2,384,1024]{2,1,0:T(8,128)(2,1)S(1)}, bf16[2,384,1024]{2,1,0:T(8,128)(2,1)S(1)}, u32[]{:S(2)}, u32[]{:S(2)}) collective-permute-start(bf16[2,384,1024]{2,1,0:T(8,128)(2,1)S(1)} %dynamic-slice_bitcast_fusion), channel_id=1, source_target_pairs={{0,8},{1,9},{2,10},{3,11},{4,12},{5,13},{6,14},{7,15},{8,0},{9,1},... | collective-permute-start | bytes 4718600 | tf_op jit(solution)/shard_map/ppermute | solution.py:616
  346.8 8.1 %collective-permute-done.45 = bf16[256,1536]{1,0:T(8,128)(2,1)} collective-permute-done((bf16[256,1536]{1,0:T(8,128)(2,1)S(1)}, bf16[256,1536]{1,0:T(8,128)(2,1)}, u32[]{:S(2)}, u32[]{:S(2)}) %collective-permute-start.45) | collective-permute-done | bytes 786464 | tf_op jit(solution)/shard_map/ppermute | solution.py:616
  354.9 4.0 fusion.132
  366.0 14.7 %collective-permute-done.93 = bf16[2,384,1024]{2,1,0:T(8,128)(2,1)S(1)} collective-permute-done((bf16[2,384,1024]{2,1,0:T(8,128)(2,1)S(1)}, bf16[2,384,1024]{2,1,0:T(8,128)(2,1)S(1)}, u32[]{:S(2)}, u32[]{:S(2)}) %collective-permute-start.93) | collective-permute-done | bytes 1572896 | tf_op jit(solution)/shard_map/ppermute | solution.py:616
  383.7 3.7 collective-permute-start.87
  387.4 10.2 %collective-permute-done.90 = bf16[384,1024]{1,0:T(8,128)(2,1)S(1)} collective-permute-done((bf16[384,1024]{1,0:T(8,128)(2,1)S(1)}, bf16[384,1024]{1,0:T(8,128)(2,1)S(1)}, u32[]{:S(2)}, u32[]{:S(2)}) %collective-permute-start.90) | collective-permute-done | bytes 786464 | tf_op jit(solution)/shard_map/ppermute | solution.py:616
  397.5 4.0 collective-permute-start.88
  402.0 5.5 collective-permute-start.91
  407.8 4.0 collective-permute-start.92
  414.8 13.2 %collective-permute-done.92 = bf16[192,1024]{1,0:T(8,128)(2,1)S(1)} collective-permute-done((bf16[192,1024]{1,0:T(8,128)(2,1)S(1)}, bf16[192,1024]{1,0:T(8,128)(2,1)S(1)}, u32[]{:S(2)}, u32[]{:S(2)}) %collective-permute-start.92) | collective-permute-done | bytes 393248 | tf_op jit(solution)/shard_map/ppermute | solution.py:616
  437.9 44.6 %attend_backward.1 = (f32[384,1024]{1,0:T(8,128)}, bf16[384,512]{1,0:T(8,128)(2,1)S(1)}, bf16[384,512]{1,0:T(8,128)(2,1)S(1)}, bf16[384,512]{1,0:T(8,128)(2,1)S(...) custom-call(s32[4,32]{1,0:T(4,128)S(1)} %pad_add_fusion.2.sc, ...), custom_call_target="tpu_custom_call" | custom-call | tf_op jit(solution)/shard_map/attend_backward/pallas_call | solution.py:247
  490.5 12.9 %collective-permute-start.81 = (bf16[2,384,384]{2,1,0:T(8,128)(2,1)S(1)}, bf16[2,384,384]{2,1,0:T(8,128)(2,1)S(1)}, u32[]{:S(2)}, u32[]{:S(2)}) collective-permute-start(bf16[2,384,384]{2,1,0:T(8,128)(2,1)S(1)} %dynamic-slice_bitcast_fusion.4), channel_id=1, source_target_pairs={{0,16},{1,17},{2,18},{3,19},{4,20},{5,21},{6,22},{7,23},{8,24},{9,... | collective-permute-start | bytes 1769480 | tf_op jit(solution)/shard_map/ppermute | solution.py:616
  506.4 6.3 collective-permute-done.81
  515.7 12.9 %collective-permute-done.60 = bf16[384,512]{1,0:T(8,128)(2,1)S(1)} collective-permute-done((bf16[384,512]{1,0:T(8,128)(2,1)S(1)}, bf16[384,512]{1,0:T(8,128)(2,1)S(1)}, u32[]{:S(2)}, u32[]{:S(2)}) %collective-permute-start.60) | collective-permute-done | bytes 393248 | tf_op jit(solution)/shard_map/ppermute | solution.py:616
  530.1 6.8 %collective-permute-done.67 = bf16[384,512]{1,0:T(8,128)(2,1)S(1)} collective-permute-done((bf16[384,512]{1,0:T(8,128)(2,1)S(1)}, bf16[384,512]{1,0:T(8,128)(2,1)S(1)}, u32[]{:S(2)}, u32[]{:S(2)}) %collective-permute-start.67) | collective-permute-done | bytes 393248 | tf_op jit(solution)/shard_map/ppermute | solution.py:616
  543.7 27.0 %collective-permute-done.61 = bf16[384,512]{1,0:T(8,128)(2,1)S(1)} collective-permute-done((bf16[384,512]{1,0:T(8,128)(2,1)S(1)}, bf16[384,512]{1,0:T(8,128)(2,1)S(1)}, u32[]{:S(2)}, u32[]{:S(2)}) %collective-permute-start.61) | collective-permute-done | bytes 393248 | tf_op jit(solution)/shard_map/ppermute | solution.py:616
  572.8 10.5 %collective-permute-done.68 = bf16[384,512]{1,0:T(8,128)(2,1)S(1)} collective-permute-done((bf16[384,512]{1,0:T(8,128)(2,1)S(1)}, bf16[384,512]{1,0:T(8,128)(2,1)S(1)}, u32[]{:S(2)}, u32[]{:S(2)}) %collective-permute-start.68) | collective-permute-done | bytes 393248 | tf_op jit(solution)/shard_map/ppermute | solution.py:616
  591.8 4.3 convolution_convert_fusion.3
  597.7 3.5 collective-permute-start.84
  602.2 13.1 %collective-permute-done.83 = bf16[192,384]{1,0:T(8,128)(2,1)S(1)} collective-permute-done((bf16[192,384]{1,0:T(8,128)(2,1)S(1)}, bf16[192,384]{1,0:T(8,128)(2,1)S(1)}, u32[]{:S(2)}, u32[]{:S(2)}) %collective-permute-start.83) | collective-permute-done | bytes 147488 | tf_op jit(solution)/shard_map/ppermute | solution.py:616
  620.4 3.8 collective-permute-done.77
  627.2 11.9 %collective-permute-done.74 = f32[2,1536]{1,0:T(2,128)S(1)} collective-permute-done((f32[2,1536]{1,0:T(2,128)S(1)}, f32[2,1536]{1,0:T(2,128)S(1)}, u32[]{:S(2)}, u32[]{:S(2)}) %collective-permute-start.74) | collective-permute-done | bytes 12320 | tf_op jit(solution)/shard_map/ppermute | solution.py:616
  642.2 5.3 collective-permute-start.79
  651.2 10.2 %collective-permute-done.80 = bf16[192,768]{1,0:T(8,128)(2,1)S(1)} collective-permute-done((bf16[192,768]{1,0:T(8,128)(2,1)S(1)}, bf16[192,768]{1,0:T(8,128)(2,1)S(1)}, u32[]{:S(2)}, u32[]{:S(2)}) %collective-permute-start.80) | collective-permute-done | bytes 294944 | tf_op jit(solution)/shard_map/ppermute | solution.py:616
  (551 shorter events, 225.8 us)
Async XLA Ops:
  5.6 60.3 %collective-permute-start.5 = (bf16[256,1536]{1,0:T(8,128)(2,1)}, bf16[256,1536]{1,0:T(8,128)(2,1)}, u32[]{:S(2)}, u32[]{:S(2)}) collective-permute-start(bf16[256,1536]{1,0:T(8,128)(2,1)} %fusion.38), channel_id=1, source_target_pairs={{0,1},{1,0},{2,3},{3,2},{4,5},{5,4},{6,7},{7,6},{8,9},{9,8},{10,11... | collective-permute-start | bytes 2359304 | tf_op jit(solution)/shard_map/ppermute | solution.py:616
  6.9 61.1 %collective-permute-start.4 = (bf16[256,1536]{1,0:T(8,128)(2,1)}, bf16[256,1536]{1,0:T(8,128)(2,1)}, u32[]{:S(2)}, u32[]{:S(2)}) collective-permute-start(bf16[256,1536]{1,0:T(8,128)(2,1)} %fusion.38), channel_id=1, source_target_pairs={{0,4},{1,5},{2,6},{3,7},{4,0},{5,1},{6,2},{7,3},{8,12},{9,13},{10,... | collective-permute-start | bytes 2359304 | tf_op jit(solution)/shard_map/ppermute | solution.py:616
  9.6 35.1 %collective-permute-start.21 = (bf16[96,1536]{1,0:T(8,128)(2,1)}, bf16[96,1536]{1,0:T(8,128)(2,1)}, u32[]{:S(2)}, u32[]{:S(2)}) collective-permute-start(bf16[96,1536]{1,0:T(8,128)(2,1)} %constant_dynamic-slice_fusion.5), channel_id=1, source_target_pairs={{4,6},{5,7},{6,4},{7,5},{12,14},{13,15},{14,12},{15,13},{20,22},{2... | collective-permute-start | bytes 884744 | tf_op jit(solution)/shard_map/ppermute | solution.py:616
  18.1 21.2 %collective-permute-start = (bf16[384,768]{1,0:T(8,128)(2,1)}, bf16[384,768]{1,0:T(8,128)(2,1)S(1)}, u32[]{:S(2)}, u32[]{:S(2)}) collective-permute-start(bf16[384,768]{1,0:T(8,128)(2,1)} %constant_dynamic-slice_fusion.6), channel_id=1, source_target_pairs={{4,6},{5,7},{6,4},{7,5},{12,14},{13,15},{14,12},{15,13},{20,22},{2... | collective-permute-start | bytes 1769480 | tf_op jit(solution)/shard_map/ppermute | solution.py:616
  50.0 35.9 %collective-permute-start.37 = (bf16[256,1536]{1,0:T(8,128)(2,1)S(1)}, bf16[256,1536]{1,0:T(8,128)(2,1)S(1)}, u32[]{:S(2)}, u32[]{:S(2)}) collective-permute-start(bf16[256,1536]{1,0:T(8,128)(2,1)S(1)} %constant_dynamic-slice_fusion.2), channel_id=1, source_target_pairs={{4,6},{5,7},{6,4},{7,5},{12,14},{13,15},{14,12},{15,13},{20,22},{2... | collective-permute-start | bytes 2359304 | tf_op jit(solution)/shard_map/ppermute | solution.py:616
  72.1 37.8 %collective-permute-start.7 = (bf16[384,512]{1,0:T(8,128)(2,1)S(1)}, bf16[384,512]{1,0:T(8,128)(2,1)S(1)}, u32[]{:S(2)}, u32[]{:S(2)}) collective-permute-start(bf16[384,512]{1,0:T(8,128)(2,1)S(1)} %pad_maximum_fusion.14.refs_0_), channel_id=1, source_target_pairs={{0,8},{1,9},{2,10},{3,11},{4,12},{5,13},{6,14},{7,15},{16,24},{17,... | collective-permute-start | bytes 1179656 | tf_op jit(solution)/shard_map/ppermute | solution.py:616
  77.8 34.2 %collective-permute-start.8 = (bf16[384,512]{1,0:T(8,128)(2,1)S(1)}, bf16[384,512]{1,0:T(8,128)(2,1)S(1)}, u32[]{:S(2)}, u32[]{:S(2)}) collective-permute-start(bf16[384,512]{1,0:T(8,128)(2,1)S(1)} %pad_maximum_fusion.14.refs_0_), channel_id=1, source_target_pairs={{0,16},{1,17},{2,18},{3,19},{4,20},{5,21},{6,22},{7,23},{8,24},{9,... | collective-permute-start | bytes 1179656 | tf_op jit(solution)/shard_map/ppermute | solution.py:616
  81.7 26.9 %collective-permute-start.10 = (bf16[384,512]{1,0:T(8,128)(2,1)S(1)}, bf16[384,512]{1,0:T(8,128)(2,1)S(1)}, u32[]{:S(2)}, u32[]{:S(2)}) collective-permute-start(bf16[384,512]{1,0:T(8,128)(2,1)S(1)} %pad_maximum_fusion.14.refs_0_), channel_id=1, source_target_pairs={{0,6},{1,7},{2,4},{3,5},{4,2},{5,3},{6,0},{7,1},{8,14},{9,15},{10,... | collective-permute-start | bytes 1179656 | tf_op jit(solution)/shard_map/ppermute | solution.py:616
  82.7 34.3 %collective-permute-start.17 = (bf16[384,512]{1,0:T(8,128)(2,1)S(1)}, bf16[384,512]{1,0:T(8,128)(2,1)S(1)}, u32[]{:S(2)}, u32[]{:S(2)}) collective-permute-start(bf16[384,512]{1,0:T(8,128)(2,1)S(1)} %pad_maximum_fusion.15.refs_8_), channel_id=1, source_target_pairs={{0,6},{1,7},{2,4},{3,5},{4,2},{5,3},{6,0},{7,1},{8,14},{9,15},{10,... | collective-permute-start | bytes 1179656 | tf_op jit(solution)/shard_map/ppermute | solution.py:616
  85.9 44.3 %collective-permute-start.15 = (bf16[384,512]{1,0:T(8,128)(2,1)S(1)}, bf16[384,512]{1,0:T(8,128)(2,1)S(1)}, u32[]{:S(2)}, u32[]{:S(2)}) collective-permute-start(bf16[384,512]{1,0:T(8,128)(2,1)S(1)} %pad_maximum_fusion.15.refs_8_), channel_id=1, source_target_pairs={{0,16},{1,17},{2,18},{3,19},{4,20},{5,21},{6,22},{7,23},{8,24},{9,... | collective-permute-start | bytes 1179656 | tf_op jit(solution)/shard_map/ppermute | solution.py:616
  138.9 38.0 %collective-permute-start.48 = (bf16[256,1536]{1,0:T(8,128)(2,1)S(1)}, bf16[256,1536]{1,0:T(8,128)(2,1)S(1)}, u32[]{:S(2)}, u32[]{:S(2)}) collective-permute-start(bf16[256,1536]{1,0:T(8,128)(2,1)S(1)} %copy-done.70), channel_id=1, source_target_pairs={{0,1},{1,0},{2,3},{3,2},{4,5},{5,4},{6,7},{7,6},{8,9},{9,8},{10,11... | collective-permute-start | bytes 2359304 | tf_op jit(solution)/shard_map/ppermute | solution.py:616
  139.0 46.4 %collective-permute-start.33 = (bf16[384,1024]{1,0:T(8,128)(2,1)S(1)}, bf16[384,1024]{1,0:T(8,128)(2,1)S(1)}, u32[]{:S(2)}, u32[]{:S(2)}) collective-permute-start(bf16[384,1024]{1,0:T(8,128)(2,1)S(1)} %constant_dynamic-slice_fusion.3), channel_id=1, source_target_pairs={{4,6},{5,7},{6,4},{7,5},{12,14},{13,15},{14,12},{15,13},{20,22},{2... | collective-permute-start | bytes 2359304 | tf_op jit(solution)/shard_map/ppermute | solution.py:616
  142.9 49.5 %collective-permute-start.29 = (bf16[384,1024]{1,0:T(8,128)(2,1)S(1)}, bf16[384,1024]{1,0:T(8,128)(2,1)}, u32[]{:S(2)}, u32[]{:S(2)}) collective-permute-start(bf16[384,1024]{1,0:T(8,128)(2,1)S(1)} %constant_dynamic-slice_fusion.4), channel_id=1, source_target_pairs={{4,6},{5,7},{6,4},{7,5},{12,14},{13,15},{14,12},{15,13},{20,22},{2... | collective-permute-start | bytes 2359304 | tf_op jit(solution)/shard_map/ppermute | solution.py:616
  147.4 47.3 %collective-permute-start.38 = (bf16[256,1536]{1,0:T(8,128)(2,1)S(1)}, bf16[256,1536]{1,0:T(8,128)(2,1)S(1)}, u32[]{:S(2)}, u32[]{:S(2)}) collective-permute-start(bf16[256,1536]{1,0:T(8,128)(2,1)S(1)} %copy-done.28), channel_id=1, source_target_pairs={{4,12},{5,13},{6,14},{7,15},{12,4},{13,5},{14,6},{15,7},{20,28},{2... | collective-permute-start | bytes 2359304 | tf_op jit(solution)/shard_map/ppermute | solution.py:616
  176.8 21.0 %collective-permute-start.26 = (bf16[256,1536]{1,0:T(8,128)(2,1)S(1)}, bf16[256,1536]{1,0:T(8,128)(2,1)S(1)}, u32[]{:S(2)}, u32[]{:S(2)}) collective-permute-start(bf16[256,1536]{1,0:T(8,128)(2,1)S(1)} %slice.424), channel_id=1, source_target_pairs={{0,4},{1,5},{2,6},{3,7},{4,0},{5,1},{6,2},{7,3},{8,12},{9,13},{10,... | collective-permute-start | bytes 2359304 | tf_op jit(solution)/shard_map/ppermute | solution.py:616
  176.9 27.3 %collective-permute-start.39 = (bf16[256,1536]{1,0:T(8,128)(2,1)S(1)}, bf16[256,1536]{1,0:T(8,128)(2,1)S(1)}, u32[]{:S(2)}, u32[]{:S(2)}) collective-permute-start(bf16[256,1536]{1,0:T(8,128)(2,1)S(1)} %copy-done.28), channel_id=1, source_target_pairs={{4,20},{5,21},{6,22},{7,23},{12,28},{13,29},{14,30},{15,31},{20,4}... | collective-permute-start | bytes 2359304 | tf_op jit(solution)/shard_map/ppermute | solution.py:616
  185.4 26.0 %collective-permute-start.40 = (bf16[256,1536]{1,0:T(8,128)(2,1)S(1)}, bf16[256,1536]{1,0:T(8,128)(2,1)S(1)}, u32[]{:S(2)}, u32[]{:S(2)}) collective-permute-start(bf16[256,1536]{1,0:T(8,128)(2,1)S(1)} %copy-done.28), channel_id=1, source_target_pairs={{4,28},{5,29},{6,30},{7,31},{12,20},{13,21},{14,22},{15,23},{20,12... | collective-permute-start | bytes 2359304 | tf_op jit(solution)/shard_map/ppermute | solution.py:616
  192.5 23.2 %collective-permute-start.34 = (bf16[384,1024]{1,0:T(8,128)(2,1)S(1)}, bf16[384,1024]{1,0:T(8,128)(2,1)S(1)}, u32[]{:S(2)}, u32[]{:S(2)}) collective-permute-start(bf16[384,1024]{1,0:T(8,128)(2,1)S(1)} %collective-permute-done.33.a_ref), channel_id=1, source_target_pairs={{4,12},{5,13},{6,14},{7,15},{12,4},{13,5},{14,6},{15,7},{20,28},{2... | collective-permute-start | bytes 2359304 | tf_op jit(solution)/shard_map/ppermute | solution.py:616
  194.7 25.3 %collective-permute-start.35 = (bf16[384,1024]{1,0:T(8,128)(2,1)S(1)}, bf16[384,1024]{1,0:T(8,128)(2,1)S(1)}, u32[]{:S(2)}, u32[]{:S(2)}) collective-permute-start(bf16[384,1024]{1,0:T(8,128)(2,1)S(1)} %collective-permute-done.33.a_ref), channel_id=1, source_target_pairs={{4,20},{5,21},{6,22},{7,23},{12,28},{13,29},{14,30},{15,31},{20,4}... | collective-permute-start | bytes 2359304 | tf_op jit(solution)/shard_map/ppermute | solution.py:616
  197.8 23.1 %collective-permute-start.36 = (bf16[384,1024]{1,0:T(8,128)(2,1)S(1)}, bf16[384,1024]{1,0:T(8,128)(2,1)S(1)}, u32[]{:S(2)}, u32[]{:S(2)}) collective-permute-start(bf16[384,1024]{1,0:T(8,128)(2,1)S(1)} %collective-permute-done.33.a_ref), channel_id=1, source_target_pairs={{4,28},{5,29},{6,30},{7,31},{12,20},{13,21},{14,22},{15,23},{20,12... | collective-permute-start | bytes 2359304 | tf_op jit(solution)/shard_map/ppermute | solution.py:616
  205.1 28.1 %collective-permute-start.30 = (bf16[384,1024]{1,0:T(8,128)(2,1)}, bf16[384,1024]{1,0:T(8,128)(2,1)}, u32[]{:S(2)}, u32[]{:S(2)}) collective-permute-start(bf16[384,1024]{1,0:T(8,128)(2,1)} %collective-permute-done.29.a_ref), channel_id=1, source_target_pairs={{4,12},{5,13},{6,14},{7,15},{12,4},{13,5},{14,6},{15,7},{20,28},{2... | collective-permute-start | bytes 2359304 | tf_op jit(solution)/shard_map/ppermute | solution.py:616
  212.3 25.0 %collective-permute-start.31 = (bf16[384,1024]{1,0:T(8,128)(2,1)}, bf16[384,1024]{1,0:T(8,128)(2,1)}, u32[]{:S(2)}, u32[]{:S(2)}) collective-permute-start(bf16[384,1024]{1,0:T(8,128)(2,1)} %collective-permute-done.29.a_ref), channel_id=1, source_target_pairs={{4,20},{5,21},{6,22},{7,23},{12,28},{13,29},{14,30},{15,31},{20,4}... | collective-permute-start | bytes 2359304 | tf_op jit(solution)/shard_map/ppermute | solution.py:616
  270.8 51.7 %collective-permute-start.47 = (bf16[256,1536]{1,0:T(8,128)(2,1)}, bf16[256,1536]{1,0:T(8,128)(2,1)S(1)}, u32[]{:S(2)}, u32[]{:S(2)}) collective-permute-start(bf16[256,1536]{1,0:T(8,128)(2,1)} %slice.421), channel_id=1, source_target_pairs={{0,4},{1,5},{2,6},{3,7},{4,0},{5,1},{6,2},{7,3},{8,12},{9,13},{10,... | collective-permute-start | bytes 2359304 | tf_op jit(solution)/shard_map/ppermute | solution.py:616
  273.6 73.2 %collective-permute-start.41 = (bf16[256,1536]{1,0:T(8,128)(2,1)}, bf16[256,1536]{1,0:T(8,128)(2,1)}, u32[]{:S(2)}, u32[]{:S(2)}) collective-permute-start(bf16[256,1536]{1,0:T(8,128)(2,1)} %slice.423), channel_id=1, source_target_pairs={{0,4},{1,5},{2,6},{3,7},{4,0},{5,1},{6,2},{7,3},{8,12},{9,13},{10,... | collective-permute-start | bytes 2359304 | tf_op jit(solution)/shard_map/ppermute | solution.py:616
  285.0 32.9 %collective-permute-start.50 = (bf16[256,1536]{1,0:T(8,128)(2,1)}, bf16[256,1536]{1,0:T(8,128)(2,1)}, u32[]{:S(2)}, u32[]{:S(2)}) collective-permute-start(bf16[256,1536]{1,0:T(8,128)(2,1)} %slice.420), channel_id=1, source_target_pairs={{0,4},{1,5},{2,6},{3,7},{4,0},{5,1},{6,2},{7,3},{8,12},{9,13},{10,... | collective-permute-start | bytes 2359304 | tf_op jit(solution)/shard_map/ppermute | solution.py:616
  307.1 54.9 %collective-permute-start.85 = (bf16[2,384,1024]{2,1,0:T(8,128)(2,1)}, bf16[2,384,1024]{2,1,0:T(8,128)(2,1)S(1)}, u32[]{:S(2)}, u32[]{:S(2)}) collective-permute-start(bf16[2,384,1024]{2,1,0:T(8,128)(2,1)} %dynamic-slice_bitcast_fusion.2), channel_id=1, source_target_pairs={{0,8},{1,9},{2,10},{3,11},{4,12},{5,13},{6,14},{7,15},{8,0},{9,1},... | collective-permute-start | bytes 4718600 | tf_op jit(solution)/shard_map/ppermute | solution.py:616
  322.2 32.7 %collective-permute-start.45 = (bf16[256,1536]{1,0:T(8,128)(2,1)S(1)}, bf16[256,1536]{1,0:T(8,128)(2,1)}, u32[]{:S(2)}, u32[]{:S(2)}) collective-permute-start(bf16[256,1536]{1,0:T(8,128)(2,1)S(1)} %fusion.48), channel_id=1, source_target_pairs={{0,1},{1,0},{2,3},{3,2},{4,5},{5,4},{6,7},{7,6},{8,9},{9,8},{10,11... | collective-permute-start | bytes 2359304 | tf_op jit(solution)/shard_map/ppermute | solution.py:616
  322.5 41.5 %collective-permute-start.89 = (bf16[2,384,1024]{2,1,0:T(8,128)(2,1)S(1)}, bf16[2,384,1024]{2,1,0:T(8,128)(2,1)S(1)}, u32[]{:S(2)}, u32[]{:S(2)}) collective-permute-start(bf16[2,384,1024]{2,1,0:T(8,128)(2,1)S(1)} %dynamic-slice_bitcast_fusion.1), channel_id=1, source_target_pairs={{0,16},{1,17},{2,18},{3,19},{4,20},{5,21},{6,22},{7,23},{8,24},{9,... | collective-permute-start | bytes 4718600 | tf_op jit(solution)/shard_map/ppermute | solution.py:616
  338.0 42.7 %collective-permute-start.93 = (bf16[2,384,1024]{2,1,0:T(8,128)(2,1)S(1)}, bf16[2,384,1024]{2,1,0:T(8,128)(2,1)S(1)}, u32[]{:S(2)}, u32[]{:S(2)}) collective-permute-start(bf16[2,384,1024]{2,1,0:T(8,128)(2,1)S(1)} %dynamic-slice_bitcast_fusion), channel_id=1, source_target_pairs={{0,8},{1,9},{2,10},{3,11},{4,12},{5,13},{6,14},{7,15},{8,0},{9,1},... | collective-permute-start | bytes 4718600 | tf_op jit(solution)/shard_map/ppermute | solution.py:616
  358.9 48.9 %collective-permute-start.53 = (bf16[256,1536]{1,0:T(8,128)(2,1)S(1)}, bf16[256,1536]{1,0:T(8,128)(2,1)S(1)}, u32[]{:S(2)}, u32[]{:S(2)}) collective-permute-start(bf16[256,1536]{1,0:T(8,128)(2,1)S(1)} %get-tuple-element.58), channel_id=1, source_target_pairs={{0,1},{1,0},{2,3},{3,2},{4,5},{5,4},{6,7},{7,6},{8,9},{9,8},{10,11... | collective-permute-start | bytes 2359304 | tf_op jit(solution)/shard_map/ppermute | solution.py:616
  360.4 51.4 %collective-permute-start.52 = (bf16[256,1536]{1,0:T(8,128)(2,1)S(1)}, bf16[256,1536]{1,0:T(8,128)(2,1)S(1)}, u32[]{:S(2)}, u32[]{:S(2)}) collective-permute-start(bf16[256,1536]{1,0:T(8,128)(2,1)S(1)} %get-tuple-element.58), channel_id=1, source_target_pairs={{0,4},{1,5},{2,6},{3,7},{4,0},{5,1},{6,2},{7,3},{8,12},{9,13},{10,... | collective-permute-start | bytes 2359304 | tf_op jit(solution)/shard_map/ppermute | solution.py:616
  364.8 32.8 %collective-permute-start.90 = (bf16[384,1024]{1,0:T(8,128)(2,1)S(1)}, bf16[384,1024]{1,0:T(8,128)(2,1)S(1)}, u32[]{:S(2)}, u32[]{:S(2)}) collective-permute-start(bf16[384,1024]{1,0:T(8,128)(2,1)S(1)} %fusion.91), channel_id=1, source_target_pairs={{0,8},{1,9},{2,10},{3,11},{4,12},{5,13},{6,14},{7,15},{8,0},{9,1},... | collective-permute-start | bytes 2359304 | tf_op jit(solution)/shard_map/ppermute | solution.py:616
  383.7 30.0 %collective-permute-start.87 = (bf16[192,1024]{1,0:T(8,128)(2,1)S(1)}, bf16[192,1024]{1,0:T(8,128)(2,1)S(1)}, u32[]{:S(2)}, u32[]{:S(2)}) collective-permute-start(bf16[192,1024]{1,0:T(8,128)(2,1)S(1)} %get-tuple-element.77), channel_id=1, source_target_pairs={{0,4},{1,5},{2,6},{3,7},{4,2},{5,3},{6,0},{7,1},{8,12},{9,13},{10,... | collective-permute-start | bytes 1179656 | tf_op jit(solution)/shard_map/ppermute | solution.py:616
  483.2 30.9 %collective-permute-start.58 = (bf16[384,512]{1,0:T(8,128)(2,1)S(1)}, bf16[384,512]{1,0:T(8,128)(2,1)S(1)}, u32[]{:S(2)}, u32[]{:S(2)}) collective-permute-start(bf16[384,512]{1,0:T(8,128)(2,1)S(1)} %get-tuple-element.38), channel_id=1, source_target_pairs={{8,0},{9,1},{10,2},{11,3},{12,4},{13,5},{14,6},{15,7},{24,16},{25,... | collective-permute-start | bytes 1179656 | tf_op jit(solution)/shard_map/ppermute | solution.py:616
  485.3 51.9 %collective-permute-start.55 = (bf16[384,512]{1,0:T(8,128)(2,1)S(1)}, bf16[384,512]{1,0:T(8,128)(2,1)S(1)}, u32[]{:S(2)}, u32[]{:S(2)}) collective-permute-start(bf16[384,512]{1,0:T(8,128)(2,1)S(1)} %get-tuple-element.34), channel_id=1, source_target_pairs={{8,0},{9,1},{10,2},{11,3},{12,4},{13,5},{14,6},{15,7},{24,16},{25,... | collective-permute-start | bytes 1179656 | tf_op jit(solution)/shard_map/ppermute | solution.py:616
  490.5 22.2 %collective-permute-start.81 = (bf16[2,384,384]{2,1,0:T(8,128)(2,1)S(1)}, bf16[2,384,384]{2,1,0:T(8,128)(2,1)S(1)}, u32[]{:S(2)}, u32[]{:S(2)}) collective-permute-start(bf16[2,384,384]{2,1,0:T(8,128)(2,1)S(1)} %dynamic-slice_bitcast_fusion.4), channel_id=1, source_target_pairs={{0,16},{1,17},{2,18},{3,19},{4,20},{5,21},{6,22},{7,23},{8,24},{9,... | collective-permute-start | bytes 1769480 | tf_op jit(solution)/shard_map/ppermute | solution.py:616
  503.5 25.2 %collective-permute-start.65 = (bf16[384,512]{1,0:T(8,128)(2,1)S(1)}, bf16[384,512]{1,0:T(8,128)(2,1)S(1)}, u32[]{:S(2)}, u32[]{:S(2)}) collective-permute-start(bf16[384,512]{1,0:T(8,128)(2,1)S(1)} %get-tuple-element.46), channel_id=1, source_target_pairs={{8,0},{9,1},{10,2},{11,3},{12,4},{13,5},{14,6},{15,7},{24,16},{25,... | collective-permute-start | bytes 1179656 | tf_op jit(solution)/shard_map/ppermute | solution.py:616
  505.0 23.6 %collective-permute-start.60 = (bf16[384,512]{1,0:T(8,128)(2,1)S(1)}, bf16[384,512]{1,0:T(8,128)(2,1)S(1)}, u32[]{:S(2)}, u32[]{:S(2)}) collective-permute-start(bf16[384,512]{1,0:T(8,128)(2,1)S(1)} %add_convert_fusion.5), channel_id=1, source_target_pairs={{16,0},{17,1},{18,2},{19,3},{20,4},{21,5},{22,6},{23,7},{24,8},{25... | collective-permute-start | bytes 1179656 | tf_op jit(solution)/shard_map/ppermute | solution.py:616
  512.7 24.3 %collective-permute-start.67 = (bf16[384,512]{1,0:T(8,128)(2,1)S(1)}, bf16[384,512]{1,0:T(8,128)(2,1)S(1)}, u32[]{:S(2)}, u32[]{:S(2)}) collective-permute-start(bf16[384,512]{1,0:T(8,128)(2,1)S(1)} %add_convert_fusion.2), channel_id=1, source_target_pairs={{16,0},{17,1},{18,2},{19,3},{20,4},{21,5},{22,6},{23,7},{24,8},{25... | collective-permute-start | bytes 1179656 | tf_op jit(solution)/shard_map/ppermute | solution.py:616
  514.2 58.7 %collective-permute-start.62 = (bf16[384,512]{1,0:T(8,128)(2,1)S(1)}, bf16[384,512]{1,0:T(8,128)(2,1)S(1)}, u32[]{:S(2)}, u32[]{:S(2)}) collective-permute-start(bf16[384,512]{1,0:T(8,128)(2,1)S(1)} %get-tuple-element.42), channel_id=1, source_target_pairs={{8,0},{9,1},{10,2},{11,3},{12,4},{13,5},{14,6},{15,7},{24,16},{25,... | collective-permute-start | bytes 1179656 | tf_op jit(solution)/shard_map/ppermute | solution.py:616
  537.0 33.7 %collective-permute-start.61 = (bf16[384,512]{1,0:T(8,128)(2,1)S(1)}, bf16[384,512]{1,0:T(8,128)(2,1)S(1)}, u32[]{:S(2)}, u32[]{:S(2)}) collective-permute-start(bf16[384,512]{1,0:T(8,128)(2,1)S(1)} %add_convert_fusion.4), channel_id=1, source_target_pairs={{0,6},{1,7},{2,4},{3,5},{4,2},{5,3},{6,0},{7,1},{8,14},{9,15},{10,... | collective-permute-start | bytes 1179656 | tf_op jit(solution)/shard_map/ppermute | solution.py:616
  537.1 35.7 %collective-permute-start.64 = (bf16[384,512]{1,0:T(8,128)(2,1)S(1)}, bf16[384,512]{1,0:T(8,128)(2,1)S(1)}, u32[]{:S(2)}, u32[]{:S(2)}) collective-permute-start(bf16[384,512]{1,0:T(8,128)(2,1)S(1)} %add_convert_fusion.3), channel_id=1, source_target_pairs={{16,0},{17,1},{18,2},{19,3},{20,4},{21,5},{22,6},{23,7},{24,8},{25... | collective-permute-start | bytes 1179656 | tf_op jit(solution)/shard_map/ppermute | solution.py:616
  538.4 44.9 %collective-permute-start.68 = (bf16[384,512]{1,0:T(8,128)(2,1)S(1)}, bf16[384,512]{1,0:T(8,128)(2,1)S(1)}, u32[]{:S(2)}, u32[]{:S(2)}) collective-permute-start(bf16[384,512]{1,0:T(8,128)(2,1)S(1)} %add_convert_fusion.1), channel_id=1, source_target_pairs={{0,6},{1,7},{2,4},{3,5},{4,2},{5,3},{6,0},{7,1},{8,14},{9,15},{10,... | collective-permute-start | bytes 1179656 | tf_op jit(solution)/shard_map/ppermute | solution.py:616
  543.7 52.9 %collective-permute-start.95 = (bf16[192,1024]{1,0:T(8,128)(2,1)S(1)}, bf16[192,1024]{1,0:T(8,128)(2,1)S(1)}, u32[]{:S(2)}, u32[]{:S(2)}) collective-permute-start(bf16[192,1024]{1,0:T(8,128)(2,1)S(1)} %copy-done.78), channel_id=1, source_target_pairs={{0,4},{1,5},{2,6},{3,7},{4,2},{5,3},{6,0},{7,1},{8,12},{9,13},{10,... | collective-permute-start | bytes 1179656 | tf_op jit(solution)/shard_map/ppermute | solution.py:616
  570.7 27.0 %collective-permute-start.96 = (bf16[192,1024]{1,0:T(8,128)(2,1)S(1)}, bf16[192,1024]{1,0:T(8,128)(2,1)S(1)}, u32[]{:S(2)}, u32[]{:S(2)}) collective-permute-start(bf16[192,1024]{1,0:T(8,128)(2,1)S(1)} %copy-done.77), channel_id=1, source_target_pairs={{4,6},{5,7},{6,4},{7,5},{12,14},{13,15},{14,12},{15,13},{20,22},{2... | collective-permute-start | bytes 1179656 | tf_op jit(solution)/shard_map/ppermute | solution.py:616
  591.2 26.5 %collective-permute-start.69 = (bf16[256,1536]{1,0:T(8,128)(2,1)S(1)}, bf16[256,1536]{1,0:T(8,128)(2,1)S(1)}, u32[]{:S(2)}, u32[]{:S(2)}) collective-permute-start(bf16[256,1536]{1,0:T(8,128)(2,1)S(1)} %slice.419), channel_id=1, source_target_pairs={{0,4},{1,5},{2,6},{3,7},{4,0},{5,1},{6,2},{7,3},{8,12},{9,13},{10,... | collective-permute-start | bytes 2359304 | tf_op jit(solution)/shard_map/ppermute | solution.py:616
  596.3 22.4 %collective-permute-start.71 = (bf16[256,1536]{1,0:T(8,128)(2,1)S(1)}, bf16[256,1536]{1,0:T(8,128)(2,1)S(1)}, u32[]{:S(2)}, u32[]{:S(2)}) collective-permute-start(bf16[256,1536]{1,0:T(8,128)(2,1)S(1)} %fusion.44), channel_id=1, source_target_pairs={{0,1},{1,0},{2,3},{3,2},{4,5},{5,4},{6,7},{7,6},{8,9},{9,8},{10,11... | collective-permute-start | bytes 2359304 | tf_op jit(solution)/shard_map/ppermute | solution.py:616
  596.5 27.6 %collective-permute-start.77 = (bf16[2,384,768]{2,1,0:T(8,128)(2,1)S(1)}, bf16[2,384,768]{2,1,0:T(8,128)(2,1)S(1)}, u32[]{:S(2)}, u32[]{:S(2)}) collective-permute-start(bf16[2,384,768]{2,1,0:T(8,128)(2,1)S(1)} %dynamic-slice_bitcast_fusion.3), channel_id=1, source_target_pairs={{0,8},{1,9},{2,10},{3,11},{4,12},{5,13},{6,14},{7,15},{8,0},{9,1},... | collective-permute-start | bytes 3538952 | tf_op jit(solution)/shard_map/ppermute | solution.py:616
  (171 other events, 1975.2 us)

commit v3 on v2

--- a/solution.py
+++ b/solution.py
@@ -579,6 +579,370 @@
     )
 
 
+MESH = pl.DeviceIdType.MESH
+
+
+def group_devices():
+    dp, z = lax.axis_index("dp"), lax.axis_index("tp")
+    beside = (dp + 1 - 2 * lax.rem(dp, 2), z)
+    near = (dp, z + 1 - 2 * lax.rem(z, 2))
+    return beside, near
+
+
+def meet(devices):
+    barrier = pltpu.get_barrier_semaphore()
+    for device in devices:
+        pl.semaphore_signal(barrier, inc=1, device_id=device, device_id_type=MESH)
+    pl.semaphore_wait(barrier, len(devices))
+
+
+def tiles(total, step, body):
+    def one(i, carry):
+        body(pl.ds(pl.multiple_of(i * step, step), step))
+        return carry
+
+    lax.fori_loop(0, total // step, one, 0)
+
+
+CHUNKS = 4
+
+
+class GroupSum:
+    copies = 2 + CHUNKS
+
+    def __init__(self, first, sems, bufs, devices):
+        self.first, (self.ss, self.rs), self.bufs = first, sems, bufs
+        self.beside, self.near = devices
+
+    def remote(self, i, src, dst, device):
+        i = self.first + i
+        return pltpu.make_async_remote_copy(
+            src_ref=src, dst_ref=dst, send_sem=self.ss.at[i], recv_sem=self.rs.at[i],
+            device_id=device, device_id_type=MESH,
+        )
+
+    def run(self, product):
+        part_near, part_own, out_far, out_beside, out_near, in_near, in_own, in_sum = self.bufs
+
+        def put_there(cols, value):
+            rows = value.shape[0] // 2
+            part_near[:, cols] = value[:rows]
+            out_far[:, cols] = value[rows:].astype(halves)
+
+        def put_here(cols, value):
+            rows = value.shape[0] // 2
+            part_own[:, cols] = value[:rows]
+            out_beside[:, cols] = value[rows:].astype(halves)
+
+        product(1, put_there)
+        self.far = self.remote(0, out_far, in_near, self.beside)
+        self.far.start()
+        product(0, put_here)
+        self.side = self.remote(1, out_beside, in_own, self.beside)
+        self.side.start()
+        self.far.wait_recv()
+        rows = part_near.shape[0] // CHUNKS
+        self.sums = []
+        for k in range(CHUNKS):
+            at = pl.ds(k * rows, rows)
+            out_near[at, :] = (part_near[at, :] + in_near[at, :].astype(floats)).astype(halves)
+            copy = self.remote(2 + k, out_near.at[at], in_sum.at[at], self.near)
+            copy.start()
+            self.sums.append(copy)
+
+    def take(self, k):
+        part_near, part_own, out_far, out_beside, out_near, in_near, in_own, in_sum = self.bufs
+        if k == 0:
+            self.side.wait_recv()
+        self.sums[k].wait_recv()
+        rows = part_own.shape[0] // CHUNKS
+        at = pl.ds(k * rows, rows)
+        return part_own[at, :] + in_own[at, :].astype(floats) + in_sum[at, :].astype(floats)
+
+    def finish(self):
+        for copy in (self.far, self.side, *self.sums):
+            copy.wait_send()
+
+
+class GroupGather:
+    copies = 3 * CHUNKS
+
+    def __init__(self, first, sems, full, block, devices):
+        self.first, (self.ss, self.rs), self.full, self.block = first, sems, full, block
+        self.beside, self.near = devices
+        self.sent = []
+
+    def remote(self, i, src, dst, device):
+        i = self.first + i
+        return pltpu.make_async_remote_copy(
+            src_ref=src, dst_ref=dst, send_sem=self.ss.at[i], recv_sem=self.rs.at[i],
+            device_id=device, device_id_type=MESH,
+        )
+
+    def slot(self, n, k):
+        rows = self.block // CHUNKS
+        return self.full.at[pl.ds(n * self.block + k * rows, rows)]
+
+    def put(self, k):
+        for i, (n, device) in enumerate(((2, self.near), (1, self.beside))):
+            copy = self.remote(i * CHUNKS + k, self.slot(0, k), self.slot(n, k), device)
+            copy.start()
+            self.sent.append((i, copy))
+
+    def wait_here(self):
+        for i, copy in self.sent:
+            if i == 1:
+                copy.wait_recv()
+
+    def wait_there(self):
+        relays = []
+        k = 0
+        for i, copy in self.sent:
+            if i == 0:
+                copy.wait_recv()
+                relay = self.remote(2 * CHUNKS + k, self.slot(2, k), self.slot(3, k), self.beside)
+                relay.start()
+                relays.append(relay)
+                k += 1
+        for relay in relays:
+            relay.wait_recv()
+        self.sent += [(2, relay) for relay in relays]
+
+    def finish(self):
+        for _, copy in self.sent:
+            copy.wait_send()
+
+
+def start_weight(odd, slots, own, pieces, out, sem):
+    rows = pieces[0].shape[0]
+
+    @pl.when(odd == 0)
+    def _():
+        pltpu.make_async_copy(own, out, sem.at[0]).start()
+
+    @pl.when(odd != 0)
+    def _():
+        for i in range(4):
+            pltpu.make_async_copy(pieces[i], out.at[pl.ds(slots[i] * rows, rows)], sem.at[i]).start()
+
+
+def wait_weight(odd, slots, own, pieces, out, sem):
+    rows = pieces[0].shape[0]
+
+    @pl.when(odd == 0)
+    def _():
+        pltpu.make_async_copy(own, out, sem.at[0]).wait()
+
+    @pl.when(odd != 0)
+    def _():
+        for i in range(4):
+            pltpu.make_async_copy(pieces[i], out.at[pl.ds(slots[i] * rows, rows)], sem.at[i]).wait()
+
+
+def mid_kernel(ctx_ref, tok_ref, gain_ref, grad_refs, weight_refs, outs, scratch):
+    (res_out, gres_out, e_full, part_out, gate_out, up_out, down_out, dctx_out, delta_out, gain_out) = outs
+    (ctx, g_full, m_full, dh, hid, dgate, dup, w_o, w_g, w_u, w_d, *bufs, ss, rs, wsem, gsem) = scratch
+    dp = lax.axis_index("dp")
+    odd = lax.rem(dp, 2)
+    x, y = lax.rem(dp // 2, 2), dp // 4
+    slots = (2 * y + x, 2 * y + 1 - x, 2 - 2 * y + x, 3 - 2 * y - x)
+    devices = group_devices()
+    block, width = tok_ref.shape
+    two = 2 * block
+    hidden = w_g.shape[1]
+    weights = [
+        (odd, slots, weight_refs[5 * i], weight_refs[5 * i + 1 : 5 * i + 5], out, wsem.at[i])
+        for i, out in enumerate((w_o, w_d, w_g, w_u))
+    ]
+    start_weight(*weights[0])
+    grads = [
+        pltpu.make_async_copy(grad_refs[i], g_full.at[pl.ds(i * block, block)], gsem.at[i])
+        for i in range(4)
+    ]
+    for copy in grads:
+        copy.start()
+    for weight in weights[1:]:
+        start_weight(*weight)
+    ctx[...] = ctx_ref[...].T
+    meet(devices)
+
+    sum_one = GroupSum(0, (ss, rs), bufs, devices)
+    first = GroupSum.copies
+    gather_one = GroupGather(first, (ss, rs), m_full, block, devices)
+    first += GroupGather.copies
+    sum_two = GroupSum(first, (ss, rs), bufs, devices)
+    first += GroupSum.copies
+    gather_two = GroupGather(first, (ss, rs), e_full, block, devices)
+
+    def project(k, put):
+        rows = slice(k * two, (k + 1) * two)
+        tiles(width, 256, lambda cols: put(cols, dot_nn(ctx[rows, :], w_o[:, cols])))
+
+    wait_weight(*weights[0])
+    sum_one.run(project)
+    wait_weight(*weights[1])
+    for copy in grads:
+        copy.wait()
+
+    def back_hidden(cols):
+        for rows in (slice(0, two), slice(two, 2 * two)):
+            dh[rows, cols] = dot_nt(g_full[rows, :], w_d[cols, :]).astype(halves)
+
+    tiles(hidden, 256, back_hidden)
+    chunk = block // CHUNKS
+    for k in range(CHUNKS):
+        at = pl.ds(k * chunk, chunk)
+        res = tok_ref[at, :].astype(floats) + sum_one.take(k)
+        res_out[at, :] = res
+        root = lax.rsqrt(jnp.mean(res * res, axis=-1, keepdims=True) + eps_norm)
+        m_full[at, :] = (res * root * gain_ref[...]).astype(halves)
+        gather_one.put(k)
+    sum_one.finish()
+
+    def activate(k):
+        rows = slice(k * two, (k + 1) * two)
+
+        def one(cols):
+            gate_pre = dot_nn(m_full[rows, :], w_g[:, cols])
+            up_pre = dot_nn(m_full[rows, :], w_u[:, cols])
+            back = dh[rows, cols].astype(floats)
+            sigma = 1.0 / (1.0 + jnp.exp(-gate_pre))
+            silu = gate_pre * sigma
+            hid[rows, cols] = (silu * up_pre).astype(halves)
+            dgate[rows, cols] = (back * up_pre * (sigma + silu * (1.0 - sigma))).astype(halves)
+            dup[rows, cols] = (back * silu).astype(halves)
+
+        tiles(hidden, 256, one)
+
+    def partial_out(k):
+        rows = slice(k * two, (k + 1) * two)
+
+        def one(cols):
+            part_out[rows, cols] = dot_nn(hid[rows, :], w_d[:, cols]).astype(halves)
+
+        tiles(width, 256, one)
+
+    wait_weight(*weights[2])
+    wait_weight(*weights[3])
+    gather_one.wait_here()
+    activate(0)
+    partial_out(0)
+    gather_one.wait_there()
+    activate(1)
+    gather_one.finish()
+
+    def back_norm(k, put):
+        rows = slice(k * two, (k + 1) * two)
+        tiles(
+            width,
+            256,
+            lambda cols: put(
+                cols, dot_nt(dgate[rows, :], w_g[cols, :]) + dot_nt(dup[rows, :], w_u[cols, :])
+            ),
+        )
+
+    def outer(left, right, out):
+        def one(rows):
+            out[rows, :] = lax.dot_general(
+                left[:, rows], right[...], (((0,), (0,)), ((), ())), preferred_element_type=floats
+            ).astype(halves)
+
+        tiles(width, 256, one)
+
+    sum_two.run(back_norm)
+    partial_out(1)
+    outer(g_full, hid, down_out)
+    outer(m_full, dgate, gate_out)
+    gain_out[...] = jnp.zeros_like(gain_out)
+    for k in range(CHUNKS):
+        at = pl.ds(k * chunk, chunk)
+        back = sum_two.take(k)
+        res = res_out[at, :]
+        root = lax.rsqrt(jnp.mean(res * res, axis=-1, keepdims=True) + eps_norm)
+        weighted = back * gain_ref[...]
+        slope = jnp.mean(weighted * res, axis=-1, keepdims=True)
+        grad = g_full[at, :].astype(floats) + root * weighted - res * (root * root * root * slope)
+        gain_out[...] += jnp.sum(back * res * root, axis=0, keepdims=True)
+        gres_out[at, :] = grad
+        e_full[at, :] = grad.astype(halves)
+        gather_two.put(k)
+    sum_two.finish()
+    outer(m_full, dup, up_out)
+
+    def back_context(k):
+        lanes = slice(k * two, (k + 1) * two)
+        grad = dot_nt(w_o[...], e_full[lanes, :]).astype(halves)
+        dctx_out[:, lanes] = grad
+        prod = grad.astype(floats) * ctx_ref[:, lanes].astype(floats)
+        for hd in range(delta_out.shape[0]):
+            delta_out[hd : hd + 1, lanes] = VSCALE * jnp.sum(
+                prod[hd * HEAD_WIDTH : (hd + 1) * HEAD_WIDTH], axis=0, keepdims=True
+            )
+
+    gather_two.wait_here()
+    back_context(0)
+    gather_two.wait_there()
+    back_context(1)
+    gather_two.finish()
+
+
+def middle(context_t, tokens, gain, grads, weights):
+    q_cols, group = context_t.shape
+    block, width = tokens.shape
+    hidden = weights[2][0].shape[1]
+    flat = [ref for weight in weights for ref in weight]
+    shape = jax.ShapeDtypeStruct
+    out_shape = (
+        shape((block, width), floats),
+        shape((block, width), floats),
+        shape((group, width), halves),
+        shape((group, width), halves),
+        shape((width, hidden), halves),
+        shape((width, hidden), halves),
+        shape((width, hidden), halves),
+        shape((q_cols, group), halves),
+        shape((q_cols // HEAD_WIDTH, group), floats),
+        shape((1, width), floats),
+    )
+    copies = 2 * (GroupSum.copies + GroupGather.copies)
+    scratch = [
+        pltpu.VMEM((group, q_cols), halves),
+        pltpu.VMEM((group, width), halves),
+        pltpu.VMEM((group, width), halves),
+        pltpu.VMEM((group, hidden), halves),
+        pltpu.VMEM((group, hidden), halves),
+        pltpu.VMEM((group, hidden), halves),
+        pltpu.VMEM((group, hidden), halves),
+        *[pltpu.VMEM(weight[0].shape, halves) for weight in (weights[0], weights[2], weights[3], weights[1])],
+        *[pltpu.VMEM((block, width), floats)] * 2,
+        *[pltpu.VMEM((block, width), halves)] * 6,
+        pltpu.SemaphoreType.DMA((copies,)),
+        pltpu.SemaphoreType.DMA((copies,)),
+        pltpu.SemaphoreType.DMA((4, 4)),
+        pltpu.SemaphoreType.DMA((4,)),
+    ]
+
+    def kernel(*refs):
+        ctx_ref, tok_ref, gain_ref = refs[:3]
+        rest = refs[3:]
+        mid_kernel(
+            ctx_ref, tok_ref, gain_ref, rest[:4], rest[4 : 4 + len(flat)],
+            rest[4 + len(flat) : 14 + len(flat)], rest[14 + len(flat) :],
+        )
+
+    return pl.pallas_call(
+        kernel,
+        out_shape=out_shape,
+        in_specs=[VM] * 3 + [HB] * (4 + len(flat)),
+        out_specs=(VM,) * 10,
+        scratch_shapes=scratch,
+        compiler_params=pltpu.CompilerParams(
+            collective_id=1, has_side_effects=True, vmem_limit_bytes=62 << 20
+        ),
+        name="middle",
+    )(context_t, tokens, gain, *grads, *flat)
+
+
 def routes(target):
     pairs = []
     for index in range(32):
@@ -661,6 +1025,17 @@
     )(where, weight, *pieces)
 
 
+def fetch_pieces(weight, slot):
+    rows = weight.shape[0] // 4
+    part = send(lax.dynamic_slice_in_dim(weight, slot * rows, rows), "odd_far")
+    return weight, part, send(part, "odd_x"), send(part, "odd_y"), send(part, "odd_xy")
+
+
+def gather_blocks(block):
+    near = send(block, "near")
+    return block, send(block, "core"), near, send(near, "core")
+
+
 def gather_group(block):
     near = send(block, "near")
     beside = send(block, "core")
@@ -670,7 +1045,7 @@
 def scatter_group(here, there):
     rows = here.shape[0] // 2
     there_sum = there[:rows] + send(there[rows:].astype(halves), "core").astype(floats)
-    here_sum = here[:rows] + send(here[rows:].astype(halves), "core").astype(floats)
+    here_sum = here[:rows].astype(floats) + send(here[rows:].astype(halves), "core").astype(floats)
     return here_sum + send(there_sum.astype(halves), "near").astype(floats)
 
 
@@ -757,10 +1132,10 @@
     joined = fetch_quarter(
         jnp.concatenate([query_weight, key_matrix, value_matrix], axis=1), where, slot
     )
-    weight_o = fetch_quarter(output_weight, where, slot)
-    weight_gate = fetch_quarter(gate_weight, where, slot)
-    weight_up = fetch_quarter(up_weight, where, slot)
-    weight_down = fetch_quarter(down_weight, where, slot)
+    weights = [
+        fetch_pieces(weight, slot) for weight in (output_weight, down_weight, gate_weight, up_weight)
+    ]
+    grads_g = gather_blocks(out_grad)
 
     bases = [
         base(j, c, pair, side),
@@ -840,61 +1215,19 @@
     )
     context_t, log_total = attend_forward(sc, q_t, index_row, start_row, pieces)
 
-    def halves_of(product):
-        return product(slice(0, 2 * block)), product(slice(2 * block, 4 * block))
-
-    here_o, there_o = halves_of(
-        lambda lanes: lax.dot_general(
-            context_t[:, lanes], weight_o, (((0,), (0,)), ((), ())), preferred_element_type=floats
-        )
-    )
-    residual = tokens32 + scatter_group(here_o, there_o)
-
-    mlp_normed = rms_scale(residual, gain_mlp).astype(halves)
-    here_m, there_m = gather_group(mlp_normed)
-    here_g, there_g = gather_group(out_grad)
-    hiddens, d_gates, d_ups, outs, d_norms = [], [], [], [], []
-    for part, grad in ((here_m, here_g), (there_m, there_g)):
-        gate_pre = jnp.dot(part, weight_gate, preferred_element_type=floats)
-        up_pre = jnp.dot(part, weight_up, preferred_element_type=floats)
-        d_hidden = contract_cols(grad, weight_down)
-        sigma = jax.nn.sigmoid(gate_pre)
-        silu = gate_pre * sigma
-        hiddens.append((silu * up_pre).astype(halves))
-        d_gates.append(
-            (d_hidden * up_pre * (sigma * (1.0 + gate_pre * (1.0 - sigma)))).astype(halves)
-        )
-        d_ups.append((d_hidden * silu).astype(halves))
-    for n in range(2):
-        d_norms.append(contract_cols(d_gates[n], weight_gate) + contract_cols(d_ups[n], weight_up))
-    for n in range(2):
-        outs.append(jnp.dot(hiddens[n], weight_down, preferred_element_type=floats))
-    grad_mlp_normed = scatter_group(*d_norms)
-    output = residual + scatter_group(*outs)
-    mlp_full = jnp.concatenate([here_m, there_m])
-    grad_full = jnp.concatenate([here_g, there_g])
-    gate_grad = contract_rows(mlp_full, jnp.concatenate(d_gates)).astype(halves)
-    up_grad = contract_rows(mlp_full, jnp.concatenate(d_ups)).astype(halves)
-    down_grad = contract_rows(grad_full, jnp.concatenate(hiddens)).astype(halves)
+    (
+        residual, grad_residual, attn_grad_full, part_out, gate_grad, up_grad, down_grad,
+        d_context_t, delta, mlp_gain_part,
+    ) = middle(context_t, tokens, gain_mlp[None, :], grads_g, weights)
+    output = residual + scatter_group(part_out[: 2 * block], part_out[2 * block :])
     gate_sum = sum_rows_home(sum_rows_over_plane(gate_grad, x, y, True), odd)
     up_sum = sum_rows_home(sum_rows_over_plane(up_grad, x, y, False), odd)
     down_sum = sum_rows_home(sum_rows_over_plane(down_grad, x, y, True), odd)
 
-    grad_part, mlp_gain_part = norm_back(residual, gain_mlp, grad_mlp_normed)
-    grad_residual = out_grad.astype(floats) + grad_part
-    here_e, there_e = gather_group(grad_residual.astype(halves))
-
-    d_context_t = jnp.concatenate(
-        [contract_cols(weight_o, here_e), contract_cols(weight_o, there_e)], axis=1
-    ).astype(halves)
-    attn_grad_full = jnp.concatenate([here_e, there_e])
     output_grad = dot_tt(attn_grad_full, context_t).astype(halves)
     output_sum = sum_rows_home(sum_rows_over_plane(output_grad, x, y, False), odd)
-    delta = jnp.sum(
-        (d_context_t.astype(floats) * context_t.astype(floats)).reshape(heads, HEAD_WIDTH, -1), axis=1
-    )
     d_query_t, d_pieces = attend_backward(
-        sc, q_t, d_context_t, log_total, delta * VSCALE, index_row, start_row, pieces
+        sc, q_t, d_context_t, log_total, delta, index_row, start_row, pieces
     )
     d_halves = []
     for n in range(2):
@@ -913,7 +1246,8 @@
     d_turned = turn(jnp.concatenate([d_query_t, d_kv[:kv_cols]]), cosine, -sine)
     d_linear = jnp.concatenate([d_turned, d_kv[kv_cols:]]).astype(halves)
     normed_full = jnp.concatenate([here_n, there_n])
-    here_d, there_d = halves_of(lambda lanes: dot_tt(d_linear[:, lanes], joined))
+    here_d = dot_tt(d_linear[:, : 2 * block], joined)
+    there_d = dot_tt(d_linear[:, 2 * block :], joined)
     grad_normed = scatter_group(here_d, there_d)
     proj_grad = lax.dot_general(
         normed_full, d_linear, (((0,), (1,)), ((), ())), preferred_element_type=floats
@@ -922,7 +1256,7 @@
     grad_tokens_part, attn_gain_part = norm_back(tokens32, gain_attn, grad_normed)
     input_grad = grad_residual + grad_tokens_part
 
-    gains = jnp.stack([attn_gain_part, mlp_gain_part])
+    gains = jnp.stack([attn_gain_part, mlp_gain_part[0]])
     for way in ("core", "x", "y", "near", "far"):
         gains = gains + send(gains, way)
     per = gains.shape[1] // 8

time: 674 us -> 698 us (1.036)
  Pallas kernels: 77.4 us -> 186 us
  matrix products: 57.8 us -> 16.6 us
  other arithmetic: 44.7 us -> 30.4 us
  starting transfers between devices: 189 us -> 177 us
  local copies, waits for them, and re-layouts: 46.7 us -> 35.6 us
    pallas_call x0 -> x1, Pallas kernels: none -> 116 us  [middle(): pl.pallas_call(kernel, out_shape=out_shape, in_specs=[VM] * 3 + [HB] * (4...]
    dot_general x19 -> x0, matrix products: 43.1 us -> none  [the longest x3 14.4 us: contract_rows(): lax.dot_general(left_side, right_side, (((0,), (0,)), ((), ())), preferre...]
    ppermute x97 -> x85, starting transfers between devices: 189 us -> 177 us  [send(): return lax.ppermute(block, ('dp', 'tp'), ROUTES[way])]
    dynamic_slice x0 -> x4, local copies, waits for them, and re-layouts: none -> 7.11 us  [fetch_pieces(): part = send(lax.dynamic_slice_in_dim(weight, slot * rows, rows), 'odd_far')]
    unnamed x247 -> x170, local copies, waits for them, and re-layouts: 28.2 us -> 21.4 us
    ppermute x97 -> x85, waiting for transfers between devices: 244 us -> 239 us  [send(): return lax.ppermute(block, ('dp', 'tp'), ROUTES[way])]
  transfers between devices with their start and end apart: 97 -> 85, of which waited for: 30 -> 24; matrix products, arithmetic and copies ran while one was open for 17% -> 8% of each run, Pallas kernels for 5% -> 10%
where the time goes in v3:
time: 698 us; the launch traced here: 687 us
  waiting for transfers between devices  239 us (34%)
  Pallas kernels  186 us (27%)
  starting transfers between devices  177 us (25%)
  local copies, waits for them, and re-layouts  35.6 us (5%)
  other arithmetic  30.4 us (4%)
  matrix products  16.6 us (2%)
    ppermute x85, waiting for transfers between devices, send(): return lax.ppermute(block, ('dp', 'tp'), ROUTES[way])  239 us
    ppermute x85, starting transfers between devices, send(): return lax.ppermute(block, ('dp', 'tp'), ROUTES[way])  177 us
    pallas_call x1, Pallas kernels, middle(): pl.pallas_call(kernel, out_shape=out_shape, in_specs=[VM] * 3 + [HB] * (4...  116 us
    pallas_call x1, Pallas kernels, attend_backward(): pl.pallas_call(functools.partial(bwd_kernel, n, width, True), out_shape=(...  47.6 us
    unnamed x170, local copies, waits for them, and re-layouts  21.4 us
    pallas_call x1, Pallas kernels, attend_forward(): pl.pallas_call(functools.partial(fwd_kernel, n, width, first, last), out_...  20.8 us
  transfers between devices with their start and end apart: 85, of which 24 were waited for; matrix products, arithmetic and copies ran while one was open for 8% of the time, Pallas kernels for 10%

profile of v3, /device:TPU:3, one launch (start us, length us, event | category | flops | bytes accessed | tf_op | source)
XLA Modules:
  0.0 687.5 jit_solution(2439281817457172570)
XLA Ops:
  5.3 4.3 collective-permute-start
  20.7 2.6 subtract_convert_fusion.1
  25.6 3.2 collective-permute-start.2
  28.7 3.1 collective-permute-start.3
  33.3 3.4 collective-permute-done.24.refs_8_
  44.6 3.1 collective-permute-start.26
  48.6 3.1 collective-permute-start.27
  54.3 4.7 collective-permute-start.28
  61.0 4.3 collective-permute-start.36
  65.5 2.8 fusion.17
  69.4 24.3 %collective-permute-done.28.refs_13_ = bf16[256,1536]{1,0:T(8,128)(2,1)S(1)} collective-permute-done((bf16[256,1536]{1,0:T(8,128)(2,1)S(1)}, bf16[256,1536]{1,0:T(8,128)(2,1)S(1)}, u32[]{:S(2)}, u32[]{:S(2)}) %collective-permute-start.28) | collective-permute-done | bytes 786464 | tf_op jit(solution)/shard_map/ppermute | solution.py:980
  93.8 8.4 %collective-permute-done.32.refs_18_ = bf16[384,1024]{1,0:T(8,128)(2,1)S(1)} collective-permute-done((bf16[384,1024]{1,0:T(8,128)(2,1)S(1)}, bf16[384,1024]{1,0:T(8,128)(2,1)S(1)}, u32[]{:S(2)}, u32[]{:S(2)}) %collective-permute-start.32) | collective-permute-done | bytes 786464 | tf_op jit(solution)/shard_map/ppermute | solution.py:980
  104.3 6.3 collective-permute-done.36.refs_23_
  111.5 3.2 collective-permute-start.8
  116.0 2.6 fusion.21
  121.9 6.1 collective-permute-done.10.refs_4_
  127.9 3.1 collective-permute-start.31
  131.1 3.1 collective-permute-start.33
  136.6 3.2 collective-permute-start.15
  143.3 14.5 %collective-permute-done.33.refs_19_ = bf16[384,1024]{1,0:T(8,128)(2,1)S(1)} collective-permute-done((bf16[384,1024]{1,0:T(8,128)(2,1)S(1)}, bf16[384,1024]{1,0:T(8,128)(2,1)S(1)}, u32[]{:S(2)}, u32[]{:S(2)}) %collective-permute-start.33) | collective-permute-done | bytes 786464 | tf_op jit(solution)/shard_map/ppermute | solution.py:980
  157.8 4.0 collective-permute-start.12
  177.1 6.9 %collective-permute-start.35 = (bf16[384,1024]{1,0:T(8,128)(2,1)}, bf16[384,1024]{1,0:T(8,128)(2,1)S(1)}, u32[]{:S(2)}, u32[]{:S(2)}) collective-permute-start(bf16[384,1024]{1,0:T(8,128)(2,1)} %copy-done.41), channel_id=1, source_target_pairs={{4,28},{5,29},{6,30},{7,31},{12,20},{13,21},{14,22},{15,23},{20,12... | collective-permute-start | bytes 2359304 | tf_op jit(solution)/shard_map/ppermute | solution.py:980
  184.1 5.3 collective-permute-start.37
  191.5 3.2 collective-permute-start.39
  199.4 20.8 %attend_forward.1 = (bf16[384,1024]{1,0:T(8,128)(2,1)S(1)}, f32[4,1024]{1,0:T(4,128)S(1)}) custom-call(s32[4,32]{1,0:T(4,128)S(1)} %pad_add_fusion.2.sc, bf16[384,1024]{1,0:T(8,128)(2,1)S(1)} %pad_maximum_fusion.6.q_ref, s32[1,1024]{1,0:T(1,128)S(1)} %bitcast.123, s32[1,1024]{1,0:T(1,128)S(1)} %compare_select_fusion.2.start_ref, ...), custom_call_target="tpu_custom_call" | custom-call | tf_op jit(solution)/shard_map/attend_forward/pallas_call | solution.py:136
  223.7 116.5 %middle.1 = (f32[256,1536]{1,0:T(8,128)}, f32[256,1536]{1,0:T(8,128)}, bf16[1024,1536]{1,0:T(8,128)(2,1)}, bf16[1024,1536]{1,0:T(8,128)(2,1)}, bf16[1536,1024]{1...) custom-call(bf16[384,1024]{1,0:T(8,128)(2,1)} %copy-done.16, ...), custom_call_target="tpu_custom_call" | custom-call | tf_op jit(solution)/shard_map/middle/pallas_call | solution.py:933
  340.2 3.8 convolution_convert_fusion.1
  345.4 47.6 %attend_backward.1 = (f32[384,1024]{1,0:T(8,128)}, bf16[384,512]{1,0:T(8,128)(2,1)S(1)}, bf16[384,512]{1,0:T(8,128)(2,1)S(1)}, bf16[384,512]{1,0:T(8,128)(2,1)S(...) custom-call(s32[4,32]{1,0:T(4,128)S(1)} %pad_add_fusion.2.sc, ...), custom_call_target="tpu_custom_call" | custom-call | tf_op jit(solution)/shard_map/attend_backward/pallas_call | solution.py:247
  410.6 50.2 %collective-permute-done.55 = bf16[384,512]{1,0:T(8,128)(2,1)S(1)} collective-permute-done((bf16[384,512]{1,0:T(8,128)(2,1)S(1)}, bf16[384,512]{1,0:T(8,128)(2,1)S(1)}, u32[]{:S(2)}, u32[]{:S(2)}) %collective-permute-start.55) | collective-permute-done | bytes 393248 | tf_op jit(solution)/shard_map/ppermute | solution.py:980
  462.3 7.6 %collective-permute-start.56 = (bf16[384,512]{1,0:T(8,128)(2,1)S(1)}, bf16[384,512]{1,0:T(8,128)(2,1)S(1)}, u32[]{:S(2)}, u32[]{:S(2)}) collective-permute-start(bf16[384,512]{1,0:T(8,128)(2,1)S(1)} %add_convert_fusion.3), channel_id=1, source_target_pairs={{0,6},{1,7},{2,4},{3,5},{4,2},{5,3},{6,0},{7,1},{8,14},{9,15},{10,... | collective-permute-start | bytes 1179656 | tf_op jit(solution)/shard_map/ppermute | solution.py:980
  472.4 5.3 collective-permute-done.48
  482.5 13.7 %collective-permute-done.72 = bf16[192,384]{1,0:T(8,128)(2,1)S(1)} collective-permute-done((bf16[192,384]{1,0:T(8,128)(2,1)S(1)}, bf16[192,384]{1,0:T(8,128)(2,1)S(1)}, u32[]{:S(2)}, u32[]{:S(2)}) %collective-permute-start.72) | collective-permute-done | bytes 147488 | tf_op jit(solution)/shard_map/ppermute | solution.py:980
  499.9 9.1 %collective-permute-start.40 = (bf16[256,1536]{1,0:T(8,128)(2,1)}, bf16[256,1536]{1,0:T(8,128)(2,1)}, u32[]{:S(2)}, u32[]{:S(2)}) collective-permute-start(bf16[256,1536]{1,0:T(8,128)(2,1)} %get-tuple-element.78), channel_id=1, source_target_pairs={{0,4},{1,5},{2,6},{3,7},{4,0},{5,1},{6,2},{7,3},{8,12},{9,13},{10,... | collective-permute-start | bytes 2359304 | tf_op jit(solution)/shard_map/ppermute | solution.py:980
  509.0 6.4 collective-permute-done.49
  521.6 4.5 convolution_convert_fusion
  527.9 4.6 collective-permute-done.81
  536.2 2.6 add_convert_fusion
  542.0 24.1 %collective-permute-done.73 = bf16[2,384,1024]{2,1,0:T(8,128)(2,1)S(1)} collective-permute-done((bf16[2,384,1024]{2,1,0:T(8,128)(2,1)S(1)}, bf16[2,384,1024]{2,1,0:T(8,128)(2,1)S(1)}, u32[]{:S(2)}, u32[]{:S(2)}) %collective-permute-start.73) | collective-permute-done | bytes 1572896 | tf_op jit(solution)/shard_map/ppermute | solution.py:980
  567.4 4.9 collective-permute-start.59
  572.7 35.6 %collective-permute-done.78 = bf16[384,1024]{1,0:T(8,128)(2,1)S(1)} collective-permute-done((bf16[384,1024]{1,0:T(8,128)(2,1)S(1)}, bf16[384,1024]{1,0:T(8,128)(2,1)S(1)}, u32[]{:S(2)}, u32[]{:S(2)}) %collective-permute-start.78) | collective-permute-done | bytes 786464 | tf_op jit(solution)/shard_map/ppermute | solution.py:980
  608.2 6.3 collective-permute-start.83
  614.9 4.0 collective-permute-start.84
  627.5 16.8 %collective-permute-start.76 = (bf16[192,1024]{1,0:T(8,128)(2,1)S(1)}, bf16[192,1024]{1,0:T(8,128)(2,1)S(1)}, u32[]{:S(2)}, u32[]{:S(2)}) collective-permute-start(bf16[192,1024]{1,0:T(8,128)(2,1)S(1)} %get-tuple-element.86), channel_id=1, source_target_pairs={{4,6},{5,7},{6,4},{7,5},{12,14},{13,15},{14,12},{15,13},{20,22},{2... | collective-permute-start | bytes 1179656 | tf_op jit(solution)/shard_map/ppermute | solution.py:980
  644.3 7.0 %collective-permute-done.84 = bf16[192,1024]{1,0:T(8,128)(2,1)S(1)} collective-permute-done((bf16[192,1024]{1,0:T(8,128)(2,1)S(1)}, bf16[192,1024]{1,0:T(8,128)(2,1)S(1)}, u32[]{:S(2)}, u32[]{:S(2)}) %collective-permute-start.84) | collective-permute-done | bytes 393248 | tf_op jit(solution)/shard_map/ppermute | solution.py:980
  655.7 4.0 collective-permute-done.80
  660.7 3.3 collective-permute-done.62
  664.2 4.1 collective-permute-done.76
  675.5 10.1 %collective-permute-done.68 = bf16[192,768]{1,0:T(8,128)(2,1)S(1)} collective-permute-done((bf16[192,768]{1,0:T(8,128)(2,1)S(1)}, bf16[192,768]{1,0:T(8,128)(2,1)S(1)}, u32[]{:S(2)}, u32[]{:S(2)}) %collective-permute-start.68) | collective-permute-done | bytes 294944 | tf_op jit(solution)/shard_map/ppermute | solution.py:980
  (410 shorter events, 142.7 us)
Async XLA Ops:
  11.7 53.6 %collective-permute-start.5 = (bf16[256,1536]{1,0:T(8,128)(2,1)}, bf16[256,1536]{1,0:T(8,128)(2,1)}, u32[]{:S(2)}, u32[]{:S(2)}) collective-permute-start(bf16[256,1536]{1,0:T(8,128)(2,1)} %fusion.9), channel_id=1, source_target_pairs={{0,1},{1,0},{2,3},{3,2},{4,5},{5,4},{6,7},{7,6},{8,9},{9,8},{10,11... | collective-permute-start | bytes 2359304 | tf_op jit(solution)/shard_map/ppermute | solution.py:980
  14.7 21.9 %collective-permute-start.24 = (bf16[96,1536]{1,0:T(8,128)(2,1)}, bf16[96,1536]{1,0:T(8,128)(2,1)}, u32[]{:S(2)}, u32[]{:S(2)}) collective-permute-start(bf16[96,1536]{1,0:T(8,128)(2,1)} %constant_dynamic-slice_fusion.5), channel_id=1, source_target_pairs={{4,6},{5,7},{6,4},{7,5},{12,14},{13,15},{14,12},{15,13},{20,22},{2... | collective-permute-start | bytes 884744 | tf_op jit(solution)/shard_map/ppermute | solution.py:980
  36.6 28.7 %collective-permute-start.4 = (bf16[256,1536]{1,0:T(8,128)(2,1)}, bf16[256,1536]{1,0:T(8,128)(2,1)}, u32[]{:S(2)}, u32[]{:S(2)}) collective-permute-start(bf16[256,1536]{1,0:T(8,128)(2,1)} %fusion.9), channel_id=1, source_target_pairs={{0,4},{1,5},{2,6},{3,7},{4,0},{5,1},{6,2},{7,3},{8,12},{9,13},{10,... | collective-permute-start | bytes 2359304 | tf_op jit(solution)/shard_map/ppermute | solution.py:980
  54.3 39.4 %collective-permute-start.28 = (bf16[256,1536]{1,0:T(8,128)(2,1)S(1)}, bf16[256,1536]{1,0:T(8,128)(2,1)S(1)}, u32[]{:S(2)}, u32[]{:S(2)}) collective-permute-start(bf16[256,1536]{1,0:T(8,128)(2,1)S(1)} %constant_dynamic-slice_fusion.4), channel_id=1, source_target_pairs={{4,6},{5,7},{6,4},{7,5},{12,14},{13,15},{14,12},{15,13},{20,22},{2... | collective-permute-start | bytes 2359304 | tf_op jit(solution)/shard_map/ppermute | solution.py:980
  59.1 43.1 %collective-permute-start.32 = (bf16[384,1024]{1,0:T(8,128)(2,1)S(1)}, bf16[384,1024]{1,0:T(8,128)(2,1)S(1)}, u32[]{:S(2)}, u32[]{:S(2)}) collective-permute-start(bf16[384,1024]{1,0:T(8,128)(2,1)S(1)} %copy-done.56), channel_id=1, source_target_pairs={{4,6},{5,7},{6,4},{7,5},{12,14},{13,15},{14,12},{15,13},{20,22},{2... | collective-permute-start | bytes 2359304 | tf_op jit(solution)/shard_map/ppermute | solution.py:980
  61.0 49.6 %collective-permute-start.36 = (bf16[384,1024]{1,0:T(8,128)(2,1)S(1)}, bf16[384,1024]{1,0:T(8,128)(2,1)S(1)}, u32[]{:S(2)}, u32[]{:S(2)}) collective-permute-start(bf16[384,1024]{1,0:T(8,128)(2,1)S(1)} %copy-done.55), channel_id=1, source_target_pairs={{4,6},{5,7},{6,4},{7,5},{12,14},{13,15},{14,12},{15,13},{20,22},{2... | collective-permute-start | bytes 2359304 | tf_op jit(solution)/shard_map/ppermute | solution.py:980
  65.3 46.2 %collective-permute-start.22 = (bf16[256,1536]{1,0:T(8,128)(2,1)S(1)}, bf16[256,1536]{1,0:T(8,128)(2,1)S(1)}, u32[]{:S(2)}, u32[]{:S(2)}) collective-permute-start(bf16[256,1536]{1,0:T(8,128)(2,1)S(1)} %copy-done.39), channel_id=1, source_target_pairs={{0,1},{1,0},{2,3},{3,2},{4,5},{5,4},{6,7},{7,6},{8,9},{9,8},{10,11... | collective-permute-start | bytes 2359304 | tf_op jit(solution)/shard_map/ppermute | solution.py:980
  65.4 49.3 %collective-permute-start.6 = (bf16[256,1536]{1,0:T(8,128)(2,1)}, bf16[256,1536]{1,0:T(8,128)(2,1)S(1)}, u32[]{:S(2)}, u32[]{:S(2)}) collective-permute-start(bf16[256,1536]{1,0:T(8,128)(2,1)} %collective-permute-done.5), channel_id=1, source_target_pairs={{0,4},{1,5},{2,6},{3,7},{4,0},{5,1},{6,2},{7,3},{8,12},{9,13},{10,... | collective-permute-start | bytes 2359304 | tf_op jit(solution)/shard_map/ppermute | solution.py:980
  93.7 26.1 %collective-permute-start.21 = (bf16[256,1536]{1,0:T(8,128)(2,1)S(1)}, bf16[256,1536]{1,0:T(8,128)(2,1)S(1)}, u32[]{:S(2)}, u32[]{:S(2)}) collective-permute-start(bf16[256,1536]{1,0:T(8,128)(2,1)S(1)} %copy-done.39), channel_id=1, source_target_pairs={{0,4},{1,5},{2,6},{3,7},{4,0},{5,1},{6,2},{7,3},{8,12},{9,13},{10,... | collective-permute-start | bytes 2359304 | tf_op jit(solution)/shard_map/ppermute | solution.py:980
  102.2 34.3 %collective-permute-start.29 = (bf16[256,1536]{1,0:T(8,128)(2,1)S(1)}, bf16[256,1536]{1,0:T(8,128)(2,1)S(1)}, u32[]{:S(2)}, u32[]{:S(2)}) collective-permute-start(bf16[256,1536]{1,0:T(8,128)(2,1)S(1)} %collective-permute-done.28.refs_13_), channel_id=1, source_target_pairs={{4,12},{5,13},{6,14},{7,15},{12,4},{13,5},{14,6},{15,7},{20,28},{2... | collective-permute-start | bytes 2359304 | tf_op jit(solution)/shard_map/ppermute | solution.py:980
  111.5 19.6 %collective-permute-start.8 = (bf16[384,512]{1,0:T(8,128)(2,1)S(1)}, bf16[384,512]{1,0:T(8,128)(2,1)S(1)}, u32[]{:S(2)}, u32[]{:S(2)}) collective-permute-start(bf16[384,512]{1,0:T(8,128)(2,1)S(1)} %pad_maximum_fusion.7.refs_0_), channel_id=1, source_target_pairs={{0,16},{1,17},{2,18},{3,19},{4,20},{5,21},{6,22},{7,23},{8,24},{9,... | collective-permute-start | bytes 1179656 | tf_op jit(solution)/shard_map/ppermute | solution.py:980
  114.7 19.5 %collective-permute-start.7 = (bf16[384,512]{1,0:T(8,128)(2,1)S(1)}, bf16[384,512]{1,0:T(8,128)(2,1)S(1)}, u32[]{:S(2)}, u32[]{:S(2)}) collective-permute-start(bf16[384,512]{1,0:T(8,128)(2,1)S(1)} %pad_maximum_fusion.7.refs_0_), channel_id=1, source_target_pairs={{0,8},{1,9},{2,10},{3,11},{4,12},{5,13},{6,14},{7,15},{16,24},{17,... | collective-permute-start | bytes 1179656 | tf_op jit(solution)/shard_map/ppermute | solution.py:980
  131.1 26.7 %collective-permute-start.33 = (bf16[384,1024]{1,0:T(8,128)(2,1)S(1)}, bf16[384,1024]{1,0:T(8,128)(2,1)S(1)}, u32[]{:S(2)}, u32[]{:S(2)}) collective-permute-start(bf16[384,1024]{1,0:T(8,128)(2,1)S(1)} %collective-permute-done.32.refs_18_), channel_id=1, source_target_pairs={{4,12},{5,13},{6,14},{7,15},{12,4},{13,5},{14,6},{15,7},{20,28},{2... | collective-permute-start | bytes 2359304 | tf_op jit(solution)/shard_map/ppermute | solution.py:980
  134.2 27.6 %collective-permute-start.34 = (bf16[384,1024]{1,0:T(8,128)(2,1)S(1)}, bf16[384,1024]{1,0:T(8,128)(2,1)S(1)}, u32[]{:S(2)}, u32[]{:S(2)}) collective-permute-start(bf16[384,1024]{1,0:T(8,128)(2,1)S(1)} %collective-permute-done.32.refs_18_), channel_id=1, source_target_pairs={{4,20},{5,21},{6,22},{7,23},{12,28},{13,29},{14,30},{15,31},{20,4}... | collective-permute-start | bytes 2359304 | tf_op jit(solution)/shard_map/ppermute | solution.py:980
  136.5 26.6 %collective-permute-start.17 = (bf16[384,512]{1,0:T(8,128)(2,1)S(1)}, bf16[384,512]{1,0:T(8,128)(2,1)S(1)}, u32[]{:S(2)}, u32[]{:S(2)}) collective-permute-start(bf16[384,512]{1,0:T(8,128)(2,1)S(1)} %pad_maximum_fusion.8.refs_8_), channel_id=1, source_target_pairs={{0,6},{1,7},{2,4},{3,5},{4,2},{5,3},{6,0},{7,1},{8,14},{9,15},{10,... | collective-permute-start | bytes 1179656 | tf_op jit(solution)/shard_map/ppermute | solution.py:980
  136.6 29.5 %collective-permute-start.15 = (bf16[384,512]{1,0:T(8,128)(2,1)S(1)}, bf16[384,512]{1,0:T(8,128)(2,1)S(1)}, u32[]{:S(2)}, u32[]{:S(2)}) collective-permute-start(bf16[384,512]{1,0:T(8,128)(2,1)S(1)} %pad_maximum_fusion.8.refs_8_), channel_id=1, source_target_pairs={{0,16},{1,17},{2,18},{3,19},{4,20},{5,21},{6,22},{7,23},{8,24},{9,... | collective-permute-start | bytes 1179656 | tf_op jit(solution)/shard_map/ppermute | solution.py:980
  142.0 25.5 %collective-permute-start.14 = (bf16[384,512]{1,0:T(8,128)(2,1)S(1)}, bf16[384,512]{1,0:T(8,128)(2,1)S(1)}, u32[]{:S(2)}, u32[]{:S(2)}) collective-permute-start(bf16[384,512]{1,0:T(8,128)(2,1)S(1)} %pad_maximum_fusion.8.refs_8_), channel_id=1, source_target_pairs={{0,8},{1,9},{2,10},{3,11},{4,12},{5,13},{6,14},{7,15},{16,24},{17,... | collective-permute-start | bytes 1179656 | tf_op jit(solution)/shard_map/ppermute | solution.py:980
  174.7 20.0 %collective-permute-start.20 = (bf16[384,512]{1,0:T(8,128)(2,1)}, bf16[384,512]{1,0:T(8,128)(2,1)}, u32[]{:S(2)}, u32[]{:S(2)}) collective-permute-start(bf16[384,512]{1,0:T(8,128)(2,1)} %collective-permute-done.19.refs_14_), channel_id=1, source_target_pairs={{24,16},{25,17},{26,18},{27,19},{28,20},{29,21},{30,22},{31,23}} | collective-permute-start | bytes 1179656 | tf_op jit(solution)/shard_map/ppermute | solution.py:980
  177.1 44.0 %collective-permute-start.35 = (bf16[384,1024]{1,0:T(8,128)(2,1)}, bf16[384,1024]{1,0:T(8,128)(2,1)S(1)}, u32[]{:S(2)}, u32[]{:S(2)}) collective-permute-start(bf16[384,1024]{1,0:T(8,128)(2,1)} %copy-done.41), channel_id=1, source_target_pairs={{4,28},{5,29},{6,30},{7,31},{12,20},{13,21},{14,22},{15,23},{20,12... | collective-permute-start | bytes 2359304 | tf_op jit(solution)/shard_map/ppermute | solution.py:980
  184.1 37.1 %collective-permute-start.37 = (bf16[384,1024]{1,0:T(8,128)(2,1)}, bf16[384,1024]{1,0:T(8,128)(2,1)S(1)}, u32[]{:S(2)}, u32[]{:S(2)}) collective-permute-start(bf16[384,1024]{1,0:T(8,128)(2,1)} %copy-done.42), channel_id=1, source_target_pairs={{4,12},{5,13},{6,14},{7,15},{12,4},{13,5},{14,6},{15,7},{20,28},{2... | collective-permute-start | bytes 2359304 | tf_op jit(solution)/shard_map/ppermute | solution.py:980
  189.4 31.8 %collective-permute-start.38 = (bf16[384,1024]{1,0:T(8,128)(2,1)}, bf16[384,1024]{1,0:T(8,128)(2,1)S(1)}, u32[]{:S(2)}, u32[]{:S(2)}) collective-permute-start(bf16[384,1024]{1,0:T(8,128)(2,1)} %copy-done.42), channel_id=1, source_target_pairs={{4,20},{5,21},{6,22},{7,23},{12,28},{13,29},{14,30},{15,31},{20,4}... | collective-permute-start | bytes 2359304 | tf_op jit(solution)/shard_map/ppermute | solution.py:980
  191.5 29.7 %collective-permute-start.39 = (bf16[384,1024]{1,0:T(8,128)(2,1)}, bf16[384,1024]{1,0:T(8,128)(2,1)S(1)}, u32[]{:S(2)}, u32[]{:S(2)}) collective-permute-start(bf16[384,1024]{1,0:T(8,128)(2,1)} %copy-done.42), channel_id=1, source_target_pairs={{4,28},{5,29},{6,30},{7,31},{12,20},{13,21},{14,22},{15,23},{20,12... | collective-permute-start | bytes 2359304 | tf_op jit(solution)/shard_map/ppermute | solution.py:980
  194.7 26.5 %collective-permute-start.23 = (bf16[256,1536]{1,0:T(8,128)(2,1)}, bf16[256,1536]{1,0:T(8,128)(2,1)S(1)}, u32[]{:S(2)}, u32[]{:S(2)}) collective-permute-start(bf16[256,1536]{1,0:T(8,128)(2,1)} %copy-done.43), channel_id=1, source_target_pairs={{0,4},{1,5},{2,6},{3,7},{4,0},{5,1},{6,2},{7,3},{8,12},{9,13},{10,... | collective-permute-start | bytes 2359304 | tf_op jit(solution)/shard_map/ppermute | solution.py:980
  344.1 62.6 %collective-permute-start.69 = (bf16[2,384,384]{2,1,0:T(8,128)(2,1)S(1)}, bf16[2,384,384]{2,1,0:T(8,128)(2,1)S(1)}, u32[]{:S(2)}, u32[]{:S(2)}) collective-permute-start(bf16[2,384,384]{2,1,0:T(8,128)(2,1)S(1)} %dynamic-slice_bitcast_fusion.4), channel_id=1, source_target_pairs={{0,16},{1,17},{2,18},{3,19},{4,20},{5,21},{6,22},{7,23},{8,24},{9,... | collective-permute-start | bytes 1769480 | tf_op jit(solution)/shard_map/ppermute | solution.py:980
  395.7 84.0 %collective-permute-start.50 = (bf16[384,512]{1,0:T(8,128)(2,1)S(1)}, bf16[384,512]{1,0:T(8,128)(2,1)S(1)}, u32[]{:S(2)}, u32[]{:S(2)}) collective-permute-start(bf16[384,512]{1,0:T(8,128)(2,1)S(1)} %get-tuple-element.57), channel_id=1, source_target_pairs={{8,0},{9,1},{10,2},{11,3},{12,4},{13,5},{14,6},{15,7},{24,16},{25,... | collective-permute-start | bytes 1179656 | tf_op jit(solution)/shard_map/ppermute | solution.py:980
  405.2 64.8 %collective-permute-start.46 = (bf16[384,512]{1,0:T(8,128)(2,1)S(1)}, bf16[384,512]{1,0:T(8,128)(2,1)S(1)}, u32[]{:S(2)}, u32[]{:S(2)}) collective-permute-start(bf16[384,512]{1,0:T(8,128)(2,1)S(1)} %get-tuple-element.53), channel_id=1, source_target_pairs={{8,0},{9,1},{10,2},{11,3},{12,4},{13,5},{14,6},{15,7},{24,16},{25,... | collective-permute-start | bytes 1179656 | tf_op jit(solution)/shard_map/ppermute | solution.py:980
  406.7 54.2 %collective-permute-start.55 = (bf16[384,512]{1,0:T(8,128)(2,1)S(1)}, bf16[384,512]{1,0:T(8,128)(2,1)S(1)}, u32[]{:S(2)}, u32[]{:S(2)}) collective-permute-start(bf16[384,512]{1,0:T(8,128)(2,1)S(1)} %add_convert_fusion.4), channel_id=1, source_target_pairs={{16,0},{17,1},{18,2},{19,3},{20,4},{21,5},{22,6},{23,7},{24,8},{25... | collective-permute-start | bytes 1179656 | tf_op jit(solution)/shard_map/ppermute | solution.py:980
  408.2 54.1 %collective-permute-start.70 = (bf16[384,384]{1,0:T(8,128)(2,1)S(1)}, bf16[384,384]{1,0:T(8,128)(2,1)S(1)}, u32[]{:S(2)}, u32[]{:S(2)}) collective-permute-start(bf16[384,384]{1,0:T(8,128)(2,1)S(1)} %fusion.44), channel_id=1, source_target_pairs={{0,8},{1,9},{2,10},{3,11},{4,12},{5,13},{6,14},{7,15},{8,0},{9,1},... | collective-permute-start | bytes 884744 | tf_op jit(solution)/shard_map/ppermute | solution.py:980
  409.3 87.6 %collective-permute-start.52 = (bf16[384,512]{1,0:T(8,128)(2,1)S(1)}, bf16[384,512]{1,0:T(8,128)(2,1)S(1)}, u32[]{:S(2)}, u32[]{:S(2)}) collective-permute-start(bf16[384,512]{1,0:T(8,128)(2,1)S(1)} %add_convert_fusion.5), channel_id=1, source_target_pairs={{16,0},{17,1},{18,2},{19,3},{20,4},{21,5},{22,6},{23,7},{24,8},{25... | collective-permute-start | bytes 1179656 | tf_op jit(solution)/shard_map/ppermute | solution.py:980
  462.3 34.9 %collective-permute-start.56 = (bf16[384,512]{1,0:T(8,128)(2,1)S(1)}, bf16[384,512]{1,0:T(8,128)(2,1)S(1)}, u32[]{:S(2)}, u32[]{:S(2)}) collective-permute-start(bf16[384,512]{1,0:T(8,128)(2,1)S(1)} %add_convert_fusion.3), channel_id=1, source_target_pairs={{0,6},{1,7},{2,4},{3,5},{4,2},{5,3},{6,0},{7,1},{8,14},{9,15},{10,... | collective-permute-start | bytes 1179656 | tf_op jit(solution)/shard_map/ppermute | solution.py:980
  496.1 19.3 %collective-permute-start.49 = (bf16[384,512]{1,0:T(8,128)(2,1)S(1)}, bf16[384,512]{1,0:T(8,128)(2,1)S(1)}, u32[]{:S(2)}, u32[]{:S(2)}) collective-permute-start(bf16[384,512]{1,0:T(8,128)(2,1)S(1)} %add_convert_fusion.6), channel_id=1, source_target_pairs={{0,6},{1,7},{2,4},{3,5},{4,2},{5,3},{6,0},{7,1},{8,14},{9,15},{10,... | collective-permute-start | bytes 1179656 | tf_op jit(solution)/shard_map/ppermute | solution.py:980
  496.9 35.6 %collective-permute-start.81 = (bf16[2,384,1024]{2,1,0:T(8,128)(2,1)S(1)}, bf16[2,384,1024]{2,1,0:T(8,128)(2,1)S(1)}, u32[]{:S(2)}, u32[]{:S(2)}) collective-permute-start(bf16[2,384,1024]{2,1,0:T(8,128)(2,1)S(1)} %dynamic-slice_bitcast_fusion), channel_id=1, source_target_pairs={{0,8},{1,9},{2,10},{3,11},{4,12},{5,13},{6,14},{7,15},{8,0},{9,1},... | collective-permute-start | bytes 4718600 | tf_op jit(solution)/shard_map/ppermute | solution.py:980
  497.2 41.6 %collective-permute-start.77 = (bf16[2,384,1024]{2,1,0:T(8,128)(2,1)S(1)}, bf16[2,384,1024]{2,1,0:T(8,128)(2,1)S(1)}, u32[]{:S(2)}, u32[]{:S(2)}) collective-permute-start(bf16[2,384,1024]{2,1,0:T(8,128)(2,1)S(1)} %dynamic-slice_bitcast_fusion.1), channel_id=1, source_target_pairs={{0,16},{1,17},{2,18},{3,19},{4,20},{5,21},{6,22},{7,23},{8,24},{9,... | collective-permute-start | bytes 4718600 | tf_op jit(solution)/shard_map/ppermute | solution.py:980
  498.6 67.5 %collective-permute-start.73 = (bf16[2,384,1024]{2,1,0:T(8,128)(2,1)S(1)}, bf16[2,384,1024]{2,1,0:T(8,128)(2,1)S(1)}, u32[]{:S(2)}, u32[]{:S(2)}) collective-permute-start(bf16[2,384,1024]{2,1,0:T(8,128)(2,1)S(1)} %dynamic-slice_bitcast_fusion.2), channel_id=1, source_target_pairs={{0,8},{1,9},{2,10},{3,11},{4,12},{5,13},{6,14},{7,15},{8,0},{9,1},... | collective-permute-start | bytes 4718600 | tf_op jit(solution)/shard_map/ppermute | solution.py:980
  499.9 33.7 %collective-permute-start.40 = (bf16[256,1536]{1,0:T(8,128)(2,1)}, bf16[256,1536]{1,0:T(8,128)(2,1)}, u32[]{:S(2)}, u32[]{:S(2)}) collective-permute-start(bf16[256,1536]{1,0:T(8,128)(2,1)} %get-tuple-element.78), channel_id=1, source_target_pairs={{0,4},{1,5},{2,6},{3,7},{4,0},{5,1},{6,2},{7,3},{8,12},{9,13},{10,... | collective-permute-start | bytes 2359304 | tf_op jit(solution)/shard_map/ppermute | solution.py:980
  515.4 20.7 %collective-permute-start.42 = (bf16[256,1536]{1,0:T(8,128)(2,1)}, bf16[256,1536]{1,0:T(8,128)(2,1)}, u32[]{:S(2)}, u32[]{:S(2)}) collective-permute-start(bf16[256,1536]{1,0:T(8,128)(2,1)} %add_convert_fusion.1), channel_id=1, source_target_pairs={{0,1},{1,0},{2,3},{3,2},{4,5},{5,4},{6,7},{7,6},{8,9},{9,8},{10,11... | collective-permute-start | bytes 2359304 | tf_op jit(solution)/shard_map/ppermute | solution.py:980
  532.5 86.8 %collective-permute-start.65 = (bf16[2,384,768]{2,1,0:T(8,128)(2,1)S(1)}, bf16[2,384,768]{2,1,0:T(8,128)(2,1)S(1)}, u32[]{:S(2)}, u32[]{:S(2)}) collective-permute-start(bf16[2,384,768]{2,1,0:T(8,128)(2,1)S(1)} %dynamic-slice_bitcast_fusion.3), channel_id=1, source_target_pairs={{0,8},{1,9},{2,10},{3,11},{4,12},{5,13},{6,14},{7,15},{8,0},{9,1},... | collective-permute-start | bytes 3538952 | tf_op jit(solution)/shard_map/ppermute | solution.py:980
  533.6 86.4 %collective-permute-start.57 = (bf16[256,1536]{1,0:T(8,128)(2,1)S(1)}, bf16[256,1536]{1,0:T(8,128)(2,1)S(1)}, u32[]{:S(2)}, u32[]{:S(2)}) collective-permute-start(bf16[256,1536]{1,0:T(8,128)(2,1)S(1)} %slice.329), channel_id=1, source_target_pairs={{0,4},{1,5},{2,6},{3,7},{4,0},{5,1},{6,2},{7,3},{8,12},{9,13},{10,... | collective-permute-start | bytes 2359304 | tf_op jit(solution)/shard_map/ppermute | solution.py:980
  536.1 31.1 %collective-permute-start.58 = (bf16[256,1536]{1,0:T(8,128)(2,1)S(1)}, bf16[256,1536]{1,0:T(8,128)(2,1)S(1)}, u32[]{:S(2)}, u32[]{:S(2)}) collective-permute-start(bf16[256,1536]{1,0:T(8,128)(2,1)S(1)} %slice.328), channel_id=1, source_target_pairs={{0,4},{1,5},{2,6},{3,7},{4,0},{5,1},{6,2},{7,3},{8,12},{9,13},{10,... | collective-permute-start | bytes 2359304 | tf_op jit(solution)/shard_map/ppermute | solution.py:980
  538.8 28.6 %collective-permute-start.82 = (bf16[384,1024]{1,0:T(8,128)(2,1)S(1)}, bf16[384,1024]{1,0:T(8,128)(2,1)S(1)}, u32[]{:S(2)}, u32[]{:S(2)}) collective-permute-start(bf16[384,1024]{1,0:T(8,128)(2,1)S(1)} %fusion.31), channel_id=1, source_target_pairs={{0,16},{1,17},{2,18},{3,19},{4,20},{5,21},{6,22},{7,23},{8,24},{9,... | collective-permute-start | bytes 2359304 | tf_op jit(solution)/shard_map/ppermute | solution.py:980
  566.1 42.1 %collective-permute-start.78 = (bf16[384,1024]{1,0:T(8,128)(2,1)S(1)}, bf16[384,1024]{1,0:T(8,128)(2,1)S(1)}, u32[]{:S(2)}, u32[]{:S(2)}) collective-permute-start(bf16[384,1024]{1,0:T(8,128)(2,1)S(1)} %fusion.30), channel_id=1, source_target_pairs={{0,8},{1,9},{2,10},{3,11},{4,12},{5,13},{6,14},{7,15},{8,0},{9,1},... | collective-permute-start | bytes 2359304 | tf_op jit(solution)/shard_map/ppermute | solution.py:980
  567.2 47.7 %collective-permute-start.74 = (bf16[384,1024]{1,0:T(8,128)(2,1)S(1)}, bf16[384,1024]{1,0:T(8,128)(2,1)S(1)}, u32[]{:S(2)}, u32[]{:S(2)}) collective-permute-start(bf16[384,1024]{1,0:T(8,128)(2,1)S(1)} %fusion.29), channel_id=1, source_target_pairs={{0,16},{1,17},{2,18},{3,19},{4,20},{5,21},{6,22},{7,23},{8,24},{9,... | collective-permute-start | bytes 2359304 | tf_op jit(solution)/shard_map/ppermute | solution.py:980
  567.4 54.9 %collective-permute-start.59 = (bf16[256,1536]{1,0:T(8,128)(2,1)S(1)}, bf16[256,1536]{1,0:T(8,128)(2,1)S(1)}, u32[]{:S(2)}, u32[]{:S(2)}) collective-permute-start(bf16[256,1536]{1,0:T(8,128)(2,1)S(1)} %fusion.15), channel_id=1, source_target_pairs={{0,1},{1,0},{2,3},{3,2},{4,5},{5,4},{6,7},{7,6},{8,9},{9,8},{10,11... | collective-permute-start | bytes 2359304 | tf_op jit(solution)/shard_map/ppermute | solution.py:980
  614.9 36.4 %collective-permute-start.84 = (bf16[192,1024]{1,0:T(8,128)(2,1)S(1)}, bf16[192,1024]{1,0:T(8,128)(2,1)S(1)}, u32[]{:S(2)}, u32[]{:S(2)}) collective-permute-start(bf16[192,1024]{1,0:T(8,128)(2,1)S(1)} %get-tuple-element.82), channel_id=1, source_target_pairs={{4,6},{5,7},{6,4},{7,5},{12,14},{13,15},{14,12},{15,13},{20,22},{2... | collective-permute-start | bytes 1179656 | tf_op jit(solution)/shard_map/ppermute | solution.py:980
  619.3 36.0 %collective-permute-start.79 = (bf16[192,1024]{1,0:T(8,128)(2,1)S(1)}, bf16[192,1024]{1,0:T(8,128)(2,1)S(1)}, u32[]{:S(2)}, u32[]{:S(2)}) collective-permute-start(bf16[192,1024]{1,0:T(8,128)(2,1)S(1)} %get-tuple-element.85), channel_id=1, source_target_pairs={{0,4},{1,5},{2,6},{3,7},{4,2},{5,3},{6,0},{7,1},{8,12},{9,13},{10,... | collective-permute-start | bytes 1179656 | tf_op jit(solution)/shard_map/ppermute | solution.py:980
  620.0 39.7 %collective-permute-start.80 = (bf16[192,1024]{1,0:T(8,128)(2,1)S(1)}, bf16[192,1024]{1,0:T(8,128)(2,1)S(1)}, u32[]{:S(2)}, u32[]{:S(2)}) collective-permute-start(bf16[192,1024]{1,0:T(8,128)(2,1)S(1)} %get-tuple-element.84), channel_id=1, source_target_pairs={{4,6},{5,7},{6,4},{7,5},{12,14},{13,15},{14,12},{15,13},{20,22},{2... | collective-permute-start | bytes 1179656 | tf_op jit(solution)/shard_map/ppermute | solution.py:980
  625.0 39.2 %collective-permute-start.75 = (bf16[192,1024]{1,0:T(8,128)(2,1)S(1)}, bf16[192,1024]{1,0:T(8,128)(2,1)S(1)}, u32[]{:S(2)}, u32[]{:S(2)}) collective-permute-start(bf16[192,1024]{1,0:T(8,128)(2,1)S(1)} %get-tuple-element.87), channel_id=1, source_target_pairs={{0,4},{1,5},{2,6},{3,7},{4,2},{5,3},{6,0},{7,1},{8,12},{9,13},{10,... | collective-permute-start | bytes 1179656 | tf_op jit(solution)/shard_map/ppermute | solution.py:980
  627.5 40.8 %collective-permute-start.76 = (bf16[192,1024]{1,0:T(8,128)(2,1)S(1)}, bf16[192,1024]{1,0:T(8,128)(2,1)S(1)}, u32[]{:S(2)}, u32[]{:S(2)}) collective-permute-start(bf16[192,1024]{1,0:T(8,128)(2,1)S(1)} %get-tuple-element.86), channel_id=1, source_target_pairs={{4,6},{5,7},{6,4},{7,5},{12,14},{13,15},{14,12},{15,13},{20,22},{2... | collective-permute-start | bytes 1179656 | tf_op jit(solution)/shard_map/ppermute | solution.py:980
  (121 other events, 2245.5 us)

commit v4 on v3

--- a/solution.py
+++ b/solution.py
@@ -37,9 +37,7 @@
     return (keys <= tok_ref[0:1, lanes]) & (keys >= start_ref[0:1, lanes])
 
 
-def fwd_kernel(n, width, first, last, sc, q_ref, tok_ref, start_ref, *refs):
-    pieces = refs[:n]
-    refs = refs[n:]
+def fwd_kernel(n, width, first, last, sc, q_ref, tok_ref, start_ref, pieces, *refs):
     if not first:
         acc_in, sum_in = refs[:2]
         refs = refs[2:]
@@ -47,7 +45,7 @@
     kv, keys_nat, acc, total, q_wide, sem = refs[2:]
     per = width // BLK
     for i in range(n):
-        pltpu.make_async_copy(pieces[i], kv.at[i], sem.at[i]).start()
+        pltpu.make_async_copy(pieces.at[i], kv.at[i], sem.at[i]).start()
     if first:
         acc[...] = jnp.zeros_like(acc)
         total[...] = jnp.zeros_like(total)
@@ -55,8 +53,8 @@
         acc[...] = acc_in[...]
         total[...] = sum_in[...]
     for i in range(n):
-        pltpu.make_async_copy(pieces[i], kv.at[i], sem.at[i]).wait()
-    heads_kv = pieces[0].shape[0] // (2 * HEAD_WIDTH)
+        pltpu.make_async_copy(pieces.at[i], kv.at[i], sem.at[i]).wait()
+    heads_kv = pieces.shape[1] // (2 * HEAD_WIDTH)
     group = q_ref.shape[0] // (heads_kv * HEAD_WIDTH)
     v_off = heads_kv * HEAD_WIDTH
     places = [
@@ -124,9 +122,9 @@
 
 
 def attend_forward(sc, q_t, tok, start, pieces, state=None, last=True):
-    n, width = len(pieces), pieces[0].shape[1]
+    n, width = pieces.shape[0], pieces.shape[2]
     heads = q_t.shape[0] // HEAD_WIDTH
-    heads_kv = pieces[0].shape[0] // (2 * HEAD_WIDTH)
+    heads_kv = pieces.shape[1] // (2 * HEAD_WIDTH)
     first = state is None
     tokens = q_t.shape[1]
     out_shape = (
@@ -136,10 +134,10 @@
     return pl.pallas_call(
         functools.partial(fwd_kernel, n, width, first, last),
         out_shape=out_shape,
-        in_specs=[SM, VM, VM, VM] + [HB] * n + ([] if first else [VM, VM]),
+        in_specs=[SM, VM, VM, VM] + [HB] + ([] if first else [VM, VM]),
         out_specs=(VM, VM),
         scratch_shapes=[
-            pltpu.VMEM((n,) + pieces[0].shape, halves),
+            pltpu.VMEM(pieces.shape, halves),
             pltpu.VMEM((heads_kv, BLK, HEAD_WIDTH), halves),
             pltpu.VMEM((heads_kv * HEAD_WIDTH, tokens * heads // heads_kv), floats),
             pltpu.VMEM((heads_kv, tokens * heads // heads_kv), floats),
@@ -148,24 +146,22 @@
         ],
         compiler_params=pltpu.CompilerParams(vmem_limit_bytes=40 << 20),
         name="attend_forward",
-    )(sc, q_t, tok, start, *pieces, *(() if first else state))
-
-
-def bwd_kernel(n, width, first, sc, q_ref, do_ref, log_ref, delta_ref, tok_ref, start_ref, *refs):
-    pieces = refs[:n]
-    refs = refs[n:]
+    )(sc, q_t, tok, start, pieces, *(() if first else state))
+
+
+def bwd_kernel(n, width, first, sc, q_ref, do_ref, log_ref, delta_ref, tok_ref, start_ref, pieces, *refs):
     if not first:
         dq_in = refs[0]
         refs = refs[1:]
     dq_out = refs[0]
-    douts = refs[1 : 1 + n]
-    kv, dkv, keys_nat, vals_nat, acc, q_wide, do_wide, log_wide, delta_wide, dq_wide, sem, osem = refs[1 + n :]
+    dkv_out = refs[1]
+    kv, dkv, keys_nat, vals_nat, acc, q_wide, do_wide, log_wide, delta_wide, dq_wide, sem, osem = refs[2:]
     per = width // BLK
     for i in range(n):
-        pltpu.make_async_copy(pieces[i], kv.at[i], sem.at[i]).start()
+        pltpu.make_async_copy(pieces.at[i], kv.at[i], sem.at[i]).start()
     for i in range(n):
-        pltpu.make_async_copy(pieces[i], kv.at[i], sem.at[i]).wait()
-    heads_kv = pieces[0].shape[0] // (2 * HEAD_WIDTH)
+        pltpu.make_async_copy(pieces.at[i], kv.at[i], sem.at[i]).wait()
+    heads_kv = pieces.shape[1] // (2 * HEAD_WIDTH)
     group = q_ref.shape[0] // (heads_kv * HEAD_WIDTH)
     v_off = heads_kv * HEAD_WIDTH
     places = [
@@ -233,29 +229,31 @@
 
     lax.fori_loop(0, n * per, key_block, 0)
     for i in range(n):
-        pltpu.make_async_copy(dkv.at[i], douts[i], osem.at[i]).start()
+        pltpu.make_async_copy(dkv.at[i], dkv_out.at[i], osem.at[i]).start()
     for h, rows, lanes, wrows, wlanes, hd in places:
         dq_out[rows, lanes] = dq_wide[wrows, wlanes] * out_scale
     for i in range(n):
-        pltpu.make_async_copy(dkv.at[i], douts[i], osem.at[i]).wait()
+        pltpu.make_async_copy(dkv.at[i], dkv_out.at[i], osem.at[i]).wait()
 
 
 def attend_backward(sc, q_t, do_t, log_total, delta, tok, start, pieces):
-    n, width = len(pieces), pieces[0].shape[1]
-    heads_kv = pieces[0].shape[0] // (2 * HEAD_WIDTH)
+    n, width = pieces.shape[0], pieces.shape[2]
+    heads_kv = pieces.shape[1] // (2 * HEAD_WIDTH)
     wide = q_t.shape[0] // (heads_kv * HEAD_WIDTH) * q_t.shape[1]
     outs = pl.pallas_call(
         functools.partial(bwd_kernel, n, width, True),
-        out_shape=(jax.ShapeDtypeStruct(q_t.shape, floats),)
-        + tuple(jax.ShapeDtypeStruct(p.shape, halves) for p in pieces),
-        in_specs=[SM] + [VM] * 6 + [HB] * n,
-        out_specs=(VM,) + (HB,) * n,
+        out_shape=(
+            jax.ShapeDtypeStruct(q_t.shape, floats),
+            jax.ShapeDtypeStruct(pieces.shape, halves),
+        ),
+        in_specs=[SM] + [VM] * 6 + [HB],
+        out_specs=(VM, HB),
         scratch_shapes=[
-            pltpu.VMEM((n,) + pieces[0].shape, halves),
-            pltpu.VMEM((n,) + pieces[0].shape, halves),
+            pltpu.VMEM(pieces.shape, halves),
+            pltpu.VMEM(pieces.shape, halves),
             pltpu.VMEM((heads_kv, BLK, HEAD_WIDTH), halves),
             pltpu.VMEM((heads_kv, BLK, HEAD_WIDTH), halves),
-            pltpu.VMEM((pieces[0].shape[0], BLK), floats),
+            pltpu.VMEM((pieces.shape[1], BLK), floats),
             pltpu.VMEM((heads_kv * HEAD_WIDTH, wide), halves),
             pltpu.VMEM((heads_kv * HEAD_WIDTH, wide), halves),
             pltpu.VMEM((heads_kv, wide), floats),
@@ -266,8 +264,8 @@
         ],
         compiler_params=pltpu.CompilerParams(vmem_limit_bytes=44 << 20),
         name="attend_backward",
-    )(sc, q_t, do_t, log_total, delta, tok, start, *pieces)
-    return outs[0], list(outs[1:])
+    )(sc, q_t, do_t, log_total, delta, tok, start, pieces)
+    return outs
 
 
 eps_norm = 1e-05
@@ -582,13 +580,6 @@
 MESH = pl.DeviceIdType.MESH
 
 
-def group_devices():
-    dp, z = lax.axis_index("dp"), lax.axis_index("tp")
-    beside = (dp + 1 - 2 * lax.rem(dp, 2), z)
-    near = (dp, z + 1 - 2 * lax.rem(z, 2))
-    return beside, near
-
-
 def meet(devices):
     barrier = pltpu.get_barrier_semaphore()
     for device in devices:
@@ -608,18 +599,8 @@
 
 
 class GroupSum:
-    copies = 2 + CHUNKS
-
-    def __init__(self, first, sems, bufs, devices):
-        self.first, (self.ss, self.rs), self.bufs = first, sems, bufs
-        self.beside, self.near = devices
-
-    def remote(self, i, src, dst, device):
-        i = self.first + i
-        return pltpu.make_async_remote_copy(
-            src_ref=src, dst_ref=dst, send_sem=self.ss.at[i], recv_sem=self.rs.at[i],
-            device_id=device, device_id_type=MESH,
-        )
+    def __init__(self, copies, bufs, place):
+        self.copies, self.bufs, self.place = copies, bufs, place
 
     def run(self, product):
         part_near, part_own, out_far, out_beside, out_near, in_near, in_own, in_sum = self.bufs
@@ -635,10 +616,10 @@
             out_beside[:, cols] = value[rows:].astype(halves)
 
         product(1, put_there)
-        self.far = self.remote(0, out_far, in_near, self.beside)
+        self.far = self.copies.make(out_far, in_near, self.place.beside)
         self.far.start()
         product(0, put_here)
-        self.side = self.remote(1, out_beside, in_own, self.beside)
+        self.side = self.copies.make(out_beside, in_own, self.place.beside)
         self.side.start()
         self.far.wait_recv()
         rows = part_near.shape[0] // CHUNKS
@@ -646,7 +627,7 @@
         for k in range(CHUNKS):
             at = pl.ds(k * rows, rows)
             out_near[at, :] = (part_near[at, :] + in_near[at, :].astype(floats)).astype(halves)
-            copy = self.remote(2 + k, out_near.at[at], in_sum.at[at], self.near)
+            copy = self.copies.make(out_near.at[at], in_sum.at[at], self.place.near)
             copy.start()
             self.sums.append(copy)
 
@@ -665,27 +646,17 @@
 
 
 class GroupGather:
-    copies = 3 * CHUNKS
-
-    def __init__(self, first, sems, full, block, devices):
-        self.first, (self.ss, self.rs), self.full, self.block = first, sems, full, block
-        self.beside, self.near = devices
+    def __init__(self, copies, full, block, place):
+        self.copies, self.full, self.block, self.place = copies, full, block, place
         self.sent = []
-
-    def remote(self, i, src, dst, device):
-        i = self.first + i
-        return pltpu.make_async_remote_copy(
-            src_ref=src, dst_ref=dst, send_sem=self.ss.at[i], recv_sem=self.rs.at[i],
-            device_id=device, device_id_type=MESH,
-        )
 
     def slot(self, n, k):
         rows = self.block // CHUNKS
         return self.full.at[pl.ds(n * self.block + k * rows, rows)]
 
     def put(self, k):
-        for i, (n, device) in enumerate(((2, self.near), (1, self.beside))):
-            copy = self.remote(i * CHUNKS + k, self.slot(0, k), self.slot(n, k), device)
+        for i, (n, device) in enumerate(((2, self.place.near), (1, self.place.beside))):
+            copy = self.copies.make(self.slot(0, k), self.slot(n, k), device)
             copy.start()
             self.sent.append((i, copy))
 
@@ -700,7 +671,7 @@
         for i, copy in self.sent:
             if i == 0:
                 copy.wait_recv()
-                relay = self.remote(2 * CHUNKS + k, self.slot(2, k), self.slot(3, k), self.beside)
+                relay = self.copies.make(self.slot(2, k), self.slot(3, k), self.place.beside)
                 relay.start()
                 relays.append(relay)
                 k += 1
@@ -713,82 +684,362 @@
             copy.wait_send()
 
 
-def start_weight(odd, slots, own, pieces, out, sem):
-    rows = pieces[0].shape[0]
-
-    @pl.when(odd == 0)
+class Copies:
+    limit = 96
+
+    def __init__(self, send_sems, recv_sems):
+        self.send_sems, self.recv_sems, self.used = send_sems, recv_sems, 0
+
+    def make(self, src, dst, device):
+        i = self.used
+        self.used += 1
+        return pltpu.make_async_remote_copy(
+            src_ref=src,
+            dst_ref=dst,
+            send_sem=self.send_sems.at[i],
+            recv_sem=self.recv_sems.at[i],
+            device_id=device,
+            device_id_type=MESH,
+        )
+
+
+def copy_semaphores():
+    return [pltpu.SemaphoreType.DMA((Copies.limit,)), pltpu.SemaphoreType.DMA((Copies.limit,))]
+
+
+class Place:
+    def __init__(self):
+        dp, z = lax.axis_index("dp"), lax.axis_index("tp")
+        self.dp, self.z = dp, z
+        self.c = lax.rem(dp, 2)
+        self.x = lax.rem(dp // 2, 2)
+        self.y = dp // 4
+        far_z = lax.rem(z + 2, 4)
+        self.beside = (dp + 1 - 2 * self.c, z)
+        self.near = (dp, z + 1 - 2 * lax.rem(z, 2))
+        self.far = (dp, far_z)
+        self.cross = (self.beside[0], far_z)
+        self.over_x = (dp + 2 - 4 * self.x, z)
+        self.over_y = (dp + 4 - 8 * self.y, z)
+        self.slot = 2 * self.y + self.x
+        self.slot_x = 2 * self.y + 1 - self.x
+        self.slot_y = 2 - 2 * self.y + self.x
+        self.odd = self.c == 1
+        self.corner = (self.x == 1) & (self.y == 1)
+        self.turn = (self.x == 0) & (self.y == 1)
+
+
+class PlaneFetch:
+    def __init__(self, copies, place, out, own=None):
+        self.place, self.out = place, out
+        rows = out.shape[0] // 8
+
+        def part(slot, ch):
+            return pl.ds(slot * (2 * rows) + ch * rows, rows)
+
+        def remote(slot, ch, device):
+            at = part(slot, ch)
+            return copies.make(out.at[at], out.at[at], device)
+
+        p = place
+        self.hop = None
+        if own is not None:
+            self.hop = [
+                copies.make(own.at[part(p.slot, ch)], out.at[part(p.slot, ch)], p.far)
+                for ch in range(2)
+            ]
+        self.x = [remote(p.slot, ch, p.over_x) for ch in range(2)]
+        self.y = [remote(p.slot, ch, p.over_y) for ch in range(2)]
+        self.relay_y = remote(p.slot_x, 0, p.over_y)
+        self.relay_x = remote(p.slot_y, 1, p.over_x)
+
+    def start(self):
+        @pl.when(self.place.odd)
+        def _():
+            for copy in self.hop:
+                copy.start()
+
+    def forward(self):
+        @pl.when(self.place.odd)
+        def _():
+            for ch in range(2):
+                if self.hop is not None:
+                    self.hop[ch].wait_recv()
+                self.x[ch].start()
+                self.y[ch].start()
+
+    def relay(self):
+        @pl.when(self.place.odd)
+        def _():
+            self.x[0].wait_recv()
+            self.relay_y.start()
+            self.y[1].wait_recv()
+            self.relay_x.start()
+
+    def finish(self):
+        @pl.when(self.place.odd)
+        def _():
+            self.x[1].wait_recv()
+            self.y[0].wait_recv()
+            self.relay_y.wait_recv()
+            self.relay_x.wait_recv()
+
+    def drain(self):
+        @pl.when(self.place.odd)
+        def _():
+            for copy in (self.hop or []) + self.x + self.y + [self.relay_y, self.relay_x]:
+                copy.wait_send()
+
+
+class Spread:
+    def __init__(self, copies, place, source, slots):
+        self.place = place
+        self.to_x = copies.make(source, slots[1], place.over_x)
+        self.to_y = copies.make(source, slots[2], place.over_y)
+        self.relayed = copies.make(slots[2], slots[3], place.over_x)
+
+    def start(self):
+        pl.when(self.place.x == 0)(self.to_x.start)
+        pl.when(self.place.y == 0)(self.to_y.start)
+
+    def relay(self):
+        @pl.when(self.place.corner)
+        def _():
+            self.to_y.wait_recv()
+            self.relayed.start()
+
+    def finish(self):
+        p = self.place
+        pl.when(p.x == 1)(self.to_x.wait_recv)
+        pl.when((p.y == 1) & (p.x == 0))(self.to_y.wait_recv)
+        pl.when(p.turn)(self.relayed.wait_recv)
+        pl.when(p.x == 0)(self.to_x.wait_send)
+        pl.when(p.y == 0)(self.to_y.wait_send)
+        pl.when(p.corner)(self.relayed.wait_send)
+
+
+def first_kernel(
+    tok_ref, grad_ref, gain_ref, cos_ref, sin_ref, joined_in, wo_in, wd_in,
+    q_out, kv_out, n_full, g_full, joined, wo_out, wd_out,
+    linear, kv_own, ss, rs, lsem,
+):
+    place = Place()
+    copies = Copies(ss, rs)
+    block, width = tok_ref.shape
+    two = 2 * block
+    q_cols = q_out.shape[0]
+    kv_cols = kv_own.shape[1] // 2
+    local = [
+        pltpu.make_async_copy(src, dst, lsem.at[i])
+        for i, (src, dst) in enumerate(((joined_in, joined), (wo_in, wo_out), (wd_in, wd_out)))
+    ]
+
+    @pl.when(place.c == 0)
     def _():
-        pltpu.make_async_copy(own, out, sem.at[0]).start()
-
-    @pl.when(odd != 0)
+        for copy in local:
+            copy.start()
+
+    own_grad = pltpu.make_async_copy(grad_ref, g_full.at[pl.ds(0, block)], lsem.at[3])
+    own_grad.start()
+    meet((place.beside, place.near, place.far, place.cross, place.over_x, place.over_y))
+
+    fetch_joined = PlaneFetch(copies, place, joined, joined_in)
+    fetch_o = PlaneFetch(copies, place, wo_out, wo_in)
+    fetch_d = PlaneFetch(copies, place, wd_out, wd_in)
+    gather = GroupGather(copies, n_full, block, place)
+    gather_g = GroupGather(copies, g_full, block, place)
+    fetch_joined.start()
+    chunk = block // CHUNKS
+    for k in range(CHUNKS):
+        at = pl.ds(k * chunk, chunk)
+        tok = tok_ref[at, :].astype(floats)
+        root = lax.rsqrt(jnp.mean(tok * tok, axis=-1, keepdims=True) + eps_norm)
+        n_full[at, :] = (tok * root * gain_ref[...]).astype(halves)
+        gather.put(k)
+    fetch_joined.forward()
+    fetch_o.start()
+    fetch_d.start()
+    fetch_joined.relay()
+    gather.wait_here()
+    fetch_joined.finish()
+    pl.when(place.c == 0)(local[0].wait)
+
+    def project(k):
+        rows = slice(k * two, (k + 1) * two)
+
+        def one(cols):
+            linear[cols, :] = dot_nn(n_full[rows, :], joined[:, cols]).T
+
+        tiles(joined.shape[1], 256, one)
+        half_width = HEAD_WIDTH // 2
+        for head in range((q_cols + kv_cols) // HEAD_WIDTH):
+            low = slice(head * HEAD_WIDTH, head * HEAD_WIDTH + half_width)
+            high = slice(head * HEAD_WIDTH + half_width, (head + 1) * HEAD_WIDTH)
+            one_half, two_half = linear[low, :], linear[high, :]
+            cosine, sine = cos_ref[:, rows], sin_ref[:, rows]
+            first = (one_half * cosine - two_half * sine).astype(halves)
+            second = (two_half * cosine + one_half * sine).astype(halves)
+            if head * HEAD_WIDTH < q_cols:
+                q_out[low, rows] = first
+                q_out[high, rows] = second
+            else:
+                kv_own[k, low.start - q_cols : low.stop - q_cols, :] = first
+                kv_own[k, high.start - q_cols : high.stop - q_cols, :] = second
+        kv_own[k, kv_cols:, :] = (linear[q_cols + kv_cols :, :].astype(halves) * VSCALE).astype(halves)
+
+    crossings, spreads_a, spreads_b, kept = [], [], [], []
+
+    def share(k):
+        slots = [kv_out.at[8 * k + i] for i in range(8)]
+        keep = pltpu.make_async_copy(kv_own.at[k], slots[0], lsem.at[4 + k])
+        keep.start()
+        kept.append(keep)
+        crossing = copies.make(kv_own.at[k], slots[4], place.cross)
+        crossing.start()
+        crossings.append(crossing)
+        spread = Spread(copies, place, kv_own.at[k], slots[:4])
+        spread.start()
+        spreads_a.append(spread)
+        spreads_b.append(Spread(copies, place, slots[4], slots[4:]))
+
+    project(0)
+    share(0)
+    gather.wait_there()
+    project(1)
+    share(1)
+    own_grad.wait()
+    for k in range(CHUNKS):
+        gather_g.put(k)
+    fetch_o.forward()
+    fetch_d.forward()
+    spreads_a[0].relay()
+    spreads_a[1].relay()
+    fetch_o.relay()
+    fetch_d.relay()
+    crossings[0].wait_recv()
+    spreads_b[0].start()
+    gather_g.wait_there()
+    spreads_b[0].relay()
+    crossings[1].wait_recv()
+    spreads_b[1].start()
+    spreads_b[1].relay()
+    fetch_o.finish()
+    fetch_d.finish()
+    gather_g.wait_here()
+    for spread in spreads_a + spreads_b:
+        spread.finish()
+    for copy in kept:
+        copy.wait()
+
+    @pl.when(place.c == 0)
     def _():
-        for i in range(4):
-            pltpu.make_async_copy(pieces[i], out.at[pl.ds(slots[i] * rows, rows)], sem.at[i]).start()
-
-
-def wait_weight(odd, slots, own, pieces, out, sem):
-    rows = pieces[0].shape[0]
-
-    @pl.when(odd == 0)
-    def _():
-        pltpu.make_async_copy(own, out, sem.at[0]).wait()
-
-    @pl.when(odd != 0)
-    def _():
-        for i in range(4):
-            pltpu.make_async_copy(pieces[i], out.at[pl.ds(slots[i] * rows, rows)], sem.at[i]).wait()
-
-
-def mid_kernel(ctx_ref, tok_ref, gain_ref, grad_refs, weight_refs, outs, scratch):
+        for copy in local[1:]:
+            copy.wait()
+
+    for copy in crossings:
+        copy.wait_send()
+    for fetch in (fetch_joined, fetch_o, fetch_d):
+        fetch.drain()
+    gather.finish()
+    gather_g.finish()
+
+
+def first_part(tokens, out_grad, gain, cosine, sine, joined, weight_o, weight_d, q_cols, kv_cols):
+    block, width = tokens.shape
+    group = 4 * block
+    shape = jax.ShapeDtypeStruct
+    out_shape = (
+        shape((q_cols, group), halves),
+        shape((16, 2 * kv_cols, 2 * block), halves),
+        shape((group, width), halves),
+        shape((group, width), halves),
+        shape(joined.shape, halves),
+        shape(weight_o.shape, halves),
+        shape(weight_d.shape, halves),
+    )
+    return pl.pallas_call(
+        first_kernel,
+        out_shape=out_shape,
+        in_specs=[VM] * 5 + [HB] * 3,
+        out_specs=(VM, HB, VM, VM, VM, HB, HB),
+        scratch_shapes=[
+            pltpu.VMEM((joined.shape[1], 2 * block), floats),
+            pltpu.VMEM((2, 2 * kv_cols, 2 * block), halves),
+            *copy_semaphores(),
+            pltpu.SemaphoreType.DMA((6,)),
+        ],
+        compiler_params=pltpu.CompilerParams(
+            collective_id=2, has_side_effects=True, vmem_limit_bytes=40 << 20
+        ),
+        name="first",
+    )(tokens, out_grad, gain, cosine, sine, joined, weight_o, weight_d)
+
+
+def mid_kernel(ctx_ref, tok_ref, gain_ref, g_full, weight_refs, outs, scratch):
     (res_out, gres_out, e_full, part_out, gate_out, up_out, down_out, dctx_out, delta_out, gain_out) = outs
-    (ctx, g_full, m_full, dh, hid, dgate, dup, w_o, w_g, w_u, w_d, *bufs, ss, rs, wsem, gsem) = scratch
-    dp = lax.axis_index("dp")
-    odd = lax.rem(dp, 2)
-    x, y = lax.rem(dp // 2, 2), dp // 4
-    slots = (2 * y + x, 2 * y + 1 - x, 2 - 2 * y + x, 3 - 2 * y - x)
-    devices = group_devices()
+    (ctx, m_full, dh, hid, dgate, dup, w_o, w_d, w_g, w_u, *bufs, ss, rs, wsem) = scratch
+    place = Place()
+    copies = Copies(ss, rs)
     block, width = tok_ref.shape
     two = 2 * block
     hidden = w_g.shape[1]
-    weights = [
-        (odd, slots, weight_refs[5 * i], weight_refs[5 * i + 1 : 5 * i + 5], out, wsem.at[i])
-        for i, out in enumerate((w_o, w_d, w_g, w_u))
+    wo_ref, wd_ref, wg_ref, wu_ref, slice_g, slice_u = weight_refs
+    load_o = pltpu.make_async_copy(wo_ref, w_o, wsem.at[0])
+    load_d = pltpu.make_async_copy(wd_ref, w_d, wsem.at[1])
+    load_o.start()
+    load_d.start()
+    rows4 = slice_g.shape[0]
+    at_slot = pl.ds(place.slot * rows4, rows4)
+    loads = [
+        pltpu.make_async_copy(src, dst, wsem.at[2 + i])
+        for i, (src, dst) in enumerate(((wg_ref, w_g), (wu_ref, w_u)))
     ]
-    start_weight(*weights[0])
-    grads = [
-        pltpu.make_async_copy(grad_refs[i], g_full.at[pl.ds(i * block, block)], gsem.at[i])
-        for i in range(4)
+    loads_odd = [
+        pltpu.make_async_copy(src, dst.at[at_slot], wsem.at[2 + i])
+        for i, (src, dst) in enumerate(((slice_g, w_g), (slice_u, w_u)))
     ]
-    for copy in grads:
-        copy.start()
-    for weight in weights[1:]:
-        start_weight(*weight)
+
+    @pl.when(place.c == 0)
+    def _():
+        for copy in loads:
+            copy.start()
+
+    @pl.when(place.odd)
+    def _():
+        for copy in loads_odd:
+            copy.start()
+
     ctx[...] = ctx_ref[...].T
-    meet(devices)
-
-    sum_one = GroupSum(0, (ss, rs), bufs, devices)
-    first = GroupSum.copies
-    gather_one = GroupGather(first, (ss, rs), m_full, block, devices)
-    first += GroupGather.copies
-    sum_two = GroupSum(first, (ss, rs), bufs, devices)
-    first += GroupSum.copies
-    gather_two = GroupGather(first, (ss, rs), e_full, block, devices)
+    meet((place.beside, place.near, place.over_x, place.over_y))
+    fetches = [PlaneFetch(copies, place, w_g), PlaneFetch(copies, place, w_u)]
+
+    @pl.when(place.odd)
+    def _():
+        for copy in loads_odd:
+            copy.wait()
+
+    for fetch in fetches:
+        fetch.forward()
+    sum_one = GroupSum(copies, bufs, place)
+    gather_one = GroupGather(copies, m_full, block, place)
+    sum_two = GroupSum(copies, bufs, place)
+    gather_two = GroupGather(copies, e_full, block, place)
 
     def project(k, put):
         rows = slice(k * two, (k + 1) * two)
         tiles(width, 256, lambda cols: put(cols, dot_nn(ctx[rows, :], w_o[:, cols])))
 
-    wait_weight(*weights[0])
+    load_o.wait()
     sum_one.run(project)
-    wait_weight(*weights[1])
-    for copy in grads:
-        copy.wait()
+    load_d.wait()
 
     def back_hidden(cols):
         for rows in (slice(0, two), slice(two, 2 * two)):
             dh[rows, cols] = dot_nt(g_full[rows, :], w_d[cols, :]).astype(halves)
 
     tiles(hidden, 256, back_hidden)
+    for fetch in fetches:
+        fetch.relay()
     chunk = block // CHUNKS
     for k in range(CHUNKS):
         at = pl.ds(k * chunk, chunk)
@@ -822,8 +1073,14 @@
 
         tiles(width, 256, one)
 
-    wait_weight(*weights[2])
-    wait_weight(*weights[3])
+    for fetch in fetches:
+        fetch.finish()
+
+    @pl.when(place.c == 0)
+    def _():
+        for copy in loads:
+            copy.wait()
+
     gather_one.wait_here()
     activate(0)
     partial_out(0)
@@ -884,13 +1141,14 @@
     gather_two.wait_there()
     back_context(1)
     gather_two.finish()
-
-
-def middle(context_t, tokens, gain, grads, weights):
+    for fetch in fetches:
+        fetch.drain()
+
+
+def middle(context_t, tokens, gain, grad_full, weights):
     q_cols, group = context_t.shape
     block, width = tokens.shape
-    hidden = weights[2][0].shape[1]
-    flat = [ref for weight in weights for ref in weight]
+    hidden = weights[2].shape[1]
     shape = jax.ShapeDtypeStruct
     out_shape = (
         shape((block, width), floats),
@@ -904,43 +1162,31 @@
         shape((q_cols // HEAD_WIDTH, group), floats),
         shape((1, width), floats),
     )
-    copies = 2 * (GroupSum.copies + GroupGather.copies)
     scratch = [
         pltpu.VMEM((group, q_cols), halves),
         pltpu.VMEM((group, width), halves),
-        pltpu.VMEM((group, width), halves),
-        pltpu.VMEM((group, hidden), halves),
-        pltpu.VMEM((group, hidden), halves),
-        pltpu.VMEM((group, hidden), halves),
-        pltpu.VMEM((group, hidden), halves),
-        *[pltpu.VMEM(weight[0].shape, halves) for weight in (weights[0], weights[2], weights[3], weights[1])],
+        *[pltpu.VMEM((group, hidden), halves)] * 4,
+        *[pltpu.VMEM(weight.shape, halves) for weight in weights[:4]],
         *[pltpu.VMEM((block, width), floats)] * 2,
         *[pltpu.VMEM((block, width), halves)] * 6,
-        pltpu.SemaphoreType.DMA((copies,)),
-        pltpu.SemaphoreType.DMA((copies,)),
-        pltpu.SemaphoreType.DMA((4, 4)),
+        *copy_semaphores(),
         pltpu.SemaphoreType.DMA((4,)),
     ]
 
     def kernel(*refs):
-        ctx_ref, tok_ref, gain_ref = refs[:3]
-        rest = refs[3:]
-        mid_kernel(
-            ctx_ref, tok_ref, gain_ref, rest[:4], rest[4 : 4 + len(flat)],
-            rest[4 + len(flat) : 14 + len(flat)], rest[14 + len(flat) :],
-        )
+        mid_kernel(*refs[:4], refs[4:10], refs[10:20], refs[20:])
 
     return pl.pallas_call(
         kernel,
         out_shape=out_shape,
-        in_specs=[VM] * 3 + [HB] * (4 + len(flat)),
+        in_specs=[VM] * 4 + [HB] * 6,
         out_specs=(VM,) * 10,
         scratch_shapes=scratch,
         compiler_params=pltpu.CompilerParams(
             collective_id=1, has_side_effects=True, vmem_limit_bytes=62 << 20
         ),
         name="middle",
-    )(context_t, tokens, gain, *grads, *flat)
+    )(context_t, tokens, gain, grad_full, *weights)
 
 
 def routes(target):
@@ -978,68 +1224,6 @@
 
 def send(block, way):
     return lax.ppermute(block, ("dp", "tp"), ROUTES[way])
-
-
-def assemble_kernel(where, own_ref, a_ref, x_ref, y_ref, xy_ref, out_ref, sem):
-    odd, y, x = where[0], where[1], where[2]
-    rows = a_ref.shape[0]
-
-    @pl.when(odd == 0)
-    def _():
-        copy = pltpu.make_async_copy(own_ref, out_ref, sem.at[0])
-        copy.start()
-        copy.wait()
-
-    @pl.when(odd != 0)
-    def _():
-        copies = []
-        for i, (ref, slot) in enumerate(
-            (
-                (a_ref, 2 * y + x),
-                (x_ref, 2 * y + (1 - x)),
-                (y_ref, 2 * (1 - y) + x),
-                (xy_ref, 2 * (1 - y) + (1 - x)),
-            )
-        ):
-            copies.append(
-                pltpu.make_async_copy(ref, out_ref.at[pl.ds(slot * rows, rows)], sem.at[i])
-            )
-        for copy in copies:
-            copy.start()
-        for copy in copies:
-            copy.wait()
-
-
-def fetch_quarter(weight, where, slot):
-    rows = weight.shape[0] // 4
-    part = send(lax.dynamic_slice_in_dim(weight, slot * rows, rows), "odd_far")
-    pieces = (part, send(part, "odd_x"), send(part, "odd_y"), send(part, "odd_xy"))
-    return pl.pallas_call(
-        assemble_kernel,
-        out_shape=jax.ShapeDtypeStruct(weight.shape, weight.dtype),
-        in_specs=[SM] + [HB] * 5,
-        out_specs=HB,
-        scratch_shapes=[pltpu.SemaphoreType.DMA((4,))],
-        compiler_params=pltpu.CompilerParams(vmem_limit_bytes=4 << 20),
-        name="assemble",
-    )(where, weight, *pieces)
-
-
-def fetch_pieces(weight, slot):
-    rows = weight.shape[0] // 4
-    part = send(lax.dynamic_slice_in_dim(weight, slot * rows, rows), "odd_far")
-    return weight, part, send(part, "odd_x"), send(part, "odd_y"), send(part, "odd_xy")
-
-
-def gather_blocks(block):
-    near = send(block, "near")
-    return block, send(block, "core"), near, send(near, "core")
-
-
-def gather_group(block):
-    near = send(block, "near")
-    beside = send(block, "core")
-    return jnp.concatenate([block, beside]), jnp.concatenate([near, send(near, "core")])
 
 
 def scatter_group(here, there):
@@ -1127,16 +1311,6 @@
     def base(j_of, core, pair_of, side_of):
         return (2 * j_of + core) * row_len + (2 * pair_of + side_of) * block
 
-    where = jnp.stack([c, y, x]).astype(jnp.int32)
-    slot = 2 * y + x
-    joined = fetch_quarter(
-        jnp.concatenate([query_weight, key_matrix, value_matrix], axis=1), where, slot
-    )
-    weights = [
-        fetch_pieces(weight, slot) for weight in (output_weight, down_weight, gate_weight, up_weight)
-    ]
-    grads_g = gather_blocks(out_grad)
-
     bases = [
         base(j, c, pair, side),
         base(j, 1 - c, pair, side),
@@ -1154,50 +1328,34 @@
     starts4 = start.reshape(4, block)
 
     tokens32 = tokens.astype(floats)
-    normed = rms_scale(tokens32, gain_attn).astype(halves)
-    here_n, there_n = gather_group(normed)
-    qs, kvs = [], []
-    for n, part in enumerate((here_n, there_n)):
-        lanes = slice(2 * n * block, 2 * (n + 1) * block)
-        linear = dot_tt(joined, part)
-        cos_n, sin_n = cosine[:, lanes], sine[:, lanes]
-        turned = turn(linear[: q_cols + kv_cols], cos_n, sin_n)
-        qs.append(turned[:q_cols].astype(halves))
-        kvs.append(
-            jnp.concatenate(
-                [
-                    turned[q_cols:].astype(halves),
-                    (linear[q_cols + kv_cols :].astype(halves) * VSCALE).astype(halves),
-                ]
-            )
-        )
-    q_t = jnp.concatenate(qs, axis=1)
-
-    pieces, piece_bases = [], []
-
-    def there_or_far(present, value):
-        return jnp.where(present, value, FAR_BASE)
-
+    joined = jnp.concatenate([query_weight, key_matrix, value_matrix], axis=1)
+    q_t, pieces, normed_full, grad_full, joined, weight_o, weight_d = first_part(
+        tokens, out_grad, gain_attn[None, :], cosine, sine, joined, output_weight, down_weight,
+        q_cols, kv_cols,
+    )
+    slot = 2 * y + x
+    rows = gate_weight.shape[0] // 4
+    own_slices = [
+        lax.dynamic_slice_in_dim(weight, slot * rows, rows) for weight in (gate_weight, up_weight)
+    ]
+    own_slices, pieces = lax.optimization_barrier((own_slices, pieces))
+    slices = [send(part, "odd_far") for part in own_slices]
+
+    piece_bases = []
     for n in range(2):
         side_n = side if n == 0 else 1 - side
         for cross in range(2):
-            block_kv = kvs[n] if cross == 0 else send(kvs[n], "cross")
-            from_x = send(block_kv, "x_up")
-            from_y = send(block_kv, "y_up")
-            from_relay = send(from_y, "relay")
             cores = (c, 1 - c) if cross == 0 else (1 - c, c)
             pair_of = pair if cross == 0 else 1 - pair
-            for piece, j_of, present in (
-                (block_kv, j, None),
-                (from_x, j - 1, x == 1),
-                (from_y, j - 2, y == 1),
-                (from_relay, j - 1, (y == 1) & (x == 0)),
+            for j_of, present in (
+                (j, True),
+                (j - 1, x == 1),
+                (j - 2, y == 1),
+                (j - 1, (y == 1) & (x == 0)),
             ):
-                pieces.append(piece)
                 for core in cores:
-                    where_from = base(j_of, core, pair_of, side_n)
                     piece_bases.append(
-                        where_from if present is None else there_or_far(present, where_from)
+                        jnp.where(present, base(j_of, core, pair_of, side_n), FAR_BASE)
                     )
     total_blocks = len(piece_bases)
 
@@ -1218,7 +1376,10 @@
     (
         residual, grad_residual, attn_grad_full, part_out, gate_grad, up_grad, down_grad,
         d_context_t, delta, mlp_gain_part,
-    ) = middle(context_t, tokens, gain_mlp[None, :], grads_g, weights)
+    ) = middle(
+        context_t, tokens, gain_mlp[None, :], grad_full,
+        (weight_o, weight_d, gate_weight, up_weight, *slices),
+    )
     output = residual + scatter_group(part_out[: 2 * block], part_out[2 * block :])
     gate_sum = sum_rows_home(sum_rows_over_plane(gate_grad, x, y, True), odd)
     up_sum = sum_rows_home(sum_rows_over_plane(up_grad, x, y, False), odd)
@@ -1233,7 +1394,7 @@
     for n in range(2):
         sums = []
         for cross in range(2):
-            own, from_x, from_y, from_relay = d_pieces[8 * n + 4 * cross : 8 * n + 4 * cross + 4]
+            own, from_x, from_y, from_relay = (d_pieces[8 * n + 4 * cross + i] for i in range(4))
             back = send(from_relay, "unrelay").astype(floats)
             from_y = (from_y.astype(floats) + back).astype(halves)
             sums.append(
@@ -1245,7 +1406,6 @@
     d_kv = jnp.concatenate(d_halves, axis=1)
     d_turned = turn(jnp.concatenate([d_query_t, d_kv[:kv_cols]]), cosine, -sine)
     d_linear = jnp.concatenate([d_turned, d_kv[kv_cols:]]).astype(halves)
-    normed_full = jnp.concatenate([here_n, there_n])
     here_d = dot_tt(d_linear[:, : 2 * block], joined)
     there_d = dot_tt(d_linear[:, 2 * block :], joined)
     grad_normed = scatter_group(here_d, there_d)

time: 698 us -> 628 us (0.90)
  Pallas kernels: 186 us -> 276 us
  waiting for transfers between devices: 239 us -> 167 us
  starting transfers between devices: 177 us -> 115 us
  local copies, waits for them, and re-layouts: 35.6 us -> 24.8 us
  other arithmetic: 30.4 us -> 22.1 us
    pallas_call x2, Pallas kernels: 118 us -> 214 us  [the longest x1 116 us: middle(): pl.pallas_call(kernel, out_shape=out_shape, in_specs=[VM] * 4 + [HB] * 6,...]
    ppermute x85 -> x47, waiting for transfers between devices: 239 us -> 167 us  [send(): return lax.ppermute(block, ('dp', 'tp'), ROUTES[way])]
    ppermute x85 -> x47, starting transfers between devices: 177 us -> 115 us  [send(): return lax.ppermute(block, ('dp', 'tp'), ROUTES[way])]
    pallas_call x1, Pallas kernels: 47.6 us -> 38.4 us  [attend_backward(): pl.pallas_call(functools.partial(bwd_kernel, n, width, True), out_shape=(...]
    unnamed x170 -> x68, local copies, waits for them, and re-layouts: 21.4 us -> 15.5 us
  transfers between devices with their start and end apart: 85 -> 47, of which waited for: 24 -> 18; matrix products, arithmetic and copies ran while one was open for 8% -> 4% of each run, Pallas kernels for 10% -> 10%
where the time goes in v4:
time: 628 us; the launch traced here: 617 us
  Pallas kernels  276 us (44%)
  waiting for transfers between devices  167 us (27%)
  starting transfers between devices  115 us (18%)
  local copies, waits for them, and re-layouts  24.8 us (4%)
  other arithmetic  22.1 us (4%)
  matrix products  9.72 us (2%)
    ppermute x47, waiting for transfers between devices, send(): return lax.ppermute(block, ('dp', 'tp'), ROUTES[way])  167 us
    pallas_call x1, Pallas kernels, middle(): pl.pallas_call(kernel, out_shape=out_shape, in_specs=[VM] * 4 + [HB] * 6,...  116 us
    ppermute x47, starting transfers between devices, send(): return lax.ppermute(block, ('dp', 'tp'), ROUTES[way])  115 us
    pallas_call x1, Pallas kernels, first_part(): pl.pallas_call(first_kernel, out_shape=out_shape, in_specs=[VM] * 5 + [HB...  97.8 us
    pallas_call x1, Pallas kernels, attend_backward(): pl.pallas_call(functools.partial(bwd_kernel, n, width, True), out_shape=(...  38.4 us
    pallas_call x1, Pallas kernels, attend_forward(): pl.pallas_call(functools.partial(fwd_kernel, n, width, first, last), out_...  23.9 us
    unnamed x68, local copies, waits for them, and re-layouts  15.5 us
  transfers between devices with their start and end apart: 47, of which 18 were waited for; matrix products, arithmetic and copies ran while one was open for 4% of the time, Pallas kernels for 10%

profile of v4, /device:TPU:3, one launch (start us, length us, event | category | flops | bytes accessed | tf_op | source)
XLA Modules:
  0.0 617.0 jit_solution(388448832816604170)
XLA Ops:
  1.3 1.5 convert_reduce_fusion.2
  5.5 2.0 subtract_convert_fusion.1
  9.5 2.8 constant_dynamic-slice_fusion.2
  12.4 97.8 %first.1 = (bf16[384,1024]{1,0:T(8,128)(2,1)S(1)}, bf16[16,384,512]{2,1,0:T(8,128)(2,1)}, bf16[1024,1536]{1,0:T(8,128)(2,1)S(1)}, bf16[1024,1536]{1,0:T(8,128)(2...) custom-call(bf16[256,1536]{1,0:T(8,128)(2,1)S(1)} %copy-done.1, ...), custom_call_target="tpu_custom_call" | custom-call | tf_op jit(solution)/shard_map/first/pallas_call | solution.py:960
  111.2 1.7 copy-done.10
  114.3 1.9 collective-permute-start
  116.2 4.4 collective-permute-start.1
  121.9 1.9 compare_select_fusion.2.start_ref
  123.9 2.8 copy-done
  126.7 23.9 %attend_forward.1 = (bf16[384,1024]{1,0:T(8,128)(2,1)S(1)}, f32[4,1024]{1,0:T(4,128)S(1)}) custom-call(s32[4,32]{1,0:T(4,128)S(1)} %pad_add_fusion.2.sc, bf16[384,1024]{1,0:T(8,128)(2,1)S(1)} %get-tuple-element.35.q_ref, s32[1,1024]{1,0:T(1,128)S(1)} %bitcast.153, s32[1,1024]{1,0:T(1,128)S(1)} %compare_select_fusion.2.start_ref, ...), custom_call_target="tpu_custom_call" | custom-call | tf_op jit(solution)/shard_map/attend_forward/pallas_call | solution.py:134
  151.5 2.0 collective-permute-done.1.refs_9_
  153.5 115.9 %middle.1 = (f32[256,1536]{1,0:T(8,128)}, f32[256,1536]{1,0:T(8,128)}, bf16[1024,1536]{1,0:T(8,128)(2,1)}, bf16[1024,1536]{1,0:T(8,128)(2,1)}, bf16[1536,1024]{1...) custom-call(bf16[384,1024]{1,0:T(8,128)(2,1)} %copy-done.5, ...), custom_call_target="tpu_custom_call" | custom-call | tf_op jit(solution)/shard_map/middle/pallas_call | solution.py:1179
  269.5 3.9 convolution_convert_fusion.1
  274.7 6.3 %collective-permute-start.31 = (bf16[2,384,384]{2,1,0:T(8,128)(2,1)S(1)}, bf16[2,384,384]{2,1,0:T(8,128)(2,1)S(1)}, u32[]{:S(2)}, u32[]{:S(2)}) collective-permute-start(bf16[2,384,384]{2,1,0:T(8,128)(2,1)S(1)} %dynamic-slice_bitcast_fusion.4), channel_id=1, source_target_pairs={{0,16},{1,17},{2,18},{3,19},{4,20},{5,21},{6,22},{7,23},{8,24},{9,... | collective-permute-start | bytes 1769480 | tf_op jit(solution)/shard_map/ppermute | solution.py:1226
  281.0 38.4 %attend_backward.1 = (f32[384,1024]{1,0:T(8,128)S(1)}, bf16[16,384,512]{2,1,0:T(8,128)(2,1)S(1)}) custom-call(s32[4,32]{1,0:T(4,128)S(1)} %pad_add_fusion.2.sc, bf16[384,1024]{1,0:T(8,128)(2,1)S(1)} %get-tuple-element.35.q_ref, bf16[384,1024]{1,0:T(8,128)(2,1)S(1)} %copy-done.8, f32[4,1024]{1,0:T(4,128)S(1)} %get-tuple-element.48.log_ref, ...), custom_call_target="tpu_custom_call" | custom-call | tf_op jit(solution)/shard_map/attend_backward/pallas_call | solution.py:243
  323.9 1.7 copy-done.14
  326.1 1.5 copy-done.15
  329.1 16.5 %collective-permute-done.32 = bf16[384,384]{1,0:T(8,128)(2,1)S(1)} collective-permute-done((bf16[384,384]{1,0:T(8,128)(2,1)S(1)}, bf16[384,384]{1,0:T(8,128)(2,1)S(1)}, u32[]{:S(2)}, u32[]{:S(2)}) %collective-permute-start.32) | collective-permute-done | bytes 294944 | tf_op jit(solution)/shard_map/ppermute | solution.py:1226
  347.0 2.3 collective-permute-start.43
  350.0 4.0 collective-permute-start.33
  354.0 19.2 %collective-permute-done.17 = bf16[384,512]{1,0:T(8,128)(2,1)S(1)} collective-permute-done((bf16[384,512]{1,0:T(8,128)(2,1)S(1)}, bf16[384,512]{1,0:T(8,128)(2,1)S(1)}, u32[]{:S(2)}, u32[]{:S(2)}) %collective-permute-start.17) | collective-permute-done | bytes 393248 | tf_op jit(solution)/shard_map/ppermute | solution.py:1226
  373.1 1.9 collective-permute-start.34
  375.2 36.2 %collective-permute-start.39 = (bf16[2,384,1024]{2,1,0:T(8,128)(2,1)}, bf16[2,384,1024]{2,1,0:T(8,128)(2,1)S(1)}, u32[]{:S(2)}, u32[]{:S(2)}) collective-permute-start(bf16[2,384,1024]{2,1,0:T(8,128)(2,1)} %dynamic-slice_bitcast_fusion.1), channel_id=1, source_target_pairs={{0,16},{1,17},{2,18},{3,19},{4,20},{5,21},{6,22},{7,23},{8,24},{9,... | collective-permute-start | bytes 4718600 | tf_op jit(solution)/shard_map/ppermute | solution.py:1226
  413.8 40.5 %collective-permute-done.14 = bf16[384,512]{1,0:T(8,128)(2,1)S(1)} collective-permute-done((bf16[384,512]{1,0:T(8,128)(2,1)S(1)}, bf16[384,512]{1,0:T(8,128)(2,1)S(1)}, u32[]{:S(2)}, u32[]{:S(2)}) %collective-permute-start.14) | collective-permute-done | bytes 393248 | tf_op jit(solution)/shard_map/ppermute | solution.py:1226
  461.4 1.5 collective-permute-start.10
  465.2 8.6 %collective-permute-done.10 = bf16[384,512]{1,0:T(8,128)(2,1)S(1)} collective-permute-done((bf16[384,512]{1,0:T(8,128)(2,1)S(1)}, bf16[384,512]{1,0:T(8,128)(2,1)S(1)}, u32[]{:S(2)}, u32[]{:S(2)}) %collective-permute-start.10) | collective-permute-done | bytes 393248 | tf_op jit(solution)/shard_map/ppermute | solution.py:1226
  474.0 4.7 collective-permute-done.4
  480.0 2.2 collective-permute-done.7
  482.2 17.4 %collective-permute-done.11 = bf16[384,512]{1,0:T(8,128)(2,1)S(1)} collective-permute-done((bf16[384,512]{1,0:T(8,128)(2,1)S(1)}, bf16[384,512]{1,0:T(8,128)(2,1)S(1)}, u32[]{:S(2)}, u32[]{:S(2)}) %collective-permute-start.11) | collective-permute-done | bytes 393248 | tf_op jit(solution)/shard_map/ppermute | solution.py:1226
  502.1 2.9 convolution_convert_fusion
  505.2 1.5 copy-done.13
  506.7 1.5 fusion.17
  508.3 1.5 fusion.20
  510.8 4.2 collective-permute-start.46
  516.3 5.2 collective-permute-start.42
  521.7 11.6 %collective-permute-start.19 = (bf16[256,1536]{1,0:T(8,128)(2,1)S(1)}, bf16[256,1536]{1,0:T(8,128)(2,1)S(1)}, u32[]{:S(2)}, u32[]{:S(2)}) collective-permute-start(bf16[256,1536]{1,0:T(8,128)(2,1)S(1)} %slice.307), channel_id=1, source_target_pairs={{0,4},{1,5},{2,6},{3,7},{4,0},{5,1},{6,2},{7,3},{8,12},{9,13},{10,... | collective-permute-start | bytes 2359304 | tf_op jit(solution)/shard_map/ppermute | solution.py:1226
  533.3 3.5 collective-permute-done.46
  536.9 9.9 %collective-permute-start.38 = (bf16[192,1024]{1,0:T(8,128)(2,1)S(1)}, bf16[192,1024]{1,0:T(8,128)(2,1)S(1)}, u32[]{:S(2)}, u32[]{:S(2)}) collective-permute-start(bf16[192,1024]{1,0:T(8,128)(2,1)S(1)} %get-tuple-element.89), channel_id=1, source_target_pairs={{4,6},{5,7},{6,4},{7,5},{12,14},{13,15},{14,12},{15,13},{20,22},{2... | collective-permute-start | bytes 1179656 | tf_op jit(solution)/shard_map/ppermute | solution.py:1226
  546.8 2.7 collective-permute-done.42
  552.4 9.8 %collective-permute-done.38 = bf16[192,1024]{1,0:T(8,128)(2,1)S(1)} collective-permute-done((bf16[192,1024]{1,0:T(8,128)(2,1)S(1)}, bf16[192,1024]{1,0:T(8,128)(2,1)S(1)}, u32[]{:S(2)}, u32[]{:S(2)}) %collective-permute-start.38) | collective-permute-done | bytes 393248 | tf_op jit(solution)/shard_map/ppermute | solution.py:1226
  563.3 11.5 %collective-permute-done.21 = bf16[256,1536]{1,0:T(8,128)(2,1)S(1)} collective-permute-done((bf16[256,1536]{1,0:T(8,128)(2,1)S(1)}, bf16[256,1536]{1,0:T(8,128)(2,1)S(1)}, u32[]{:S(2)}, u32[]{:S(2)}) %collective-permute-start.21) | collective-permute-done | bytes 786464 | tf_op jit(solution)/shard_map/ppermute | solution.py:1226
  577.3 2.1 collective-permute-done.23
  579.5 12.5 %collective-permute-done.24 = f32[2,1536]{1,0:T(2,128)S(1)} collective-permute-done((f32[2,1536]{1,0:T(2,128)S(1)}, f32[2,1536]{1,0:T(2,128)S(1)}, u32[]{:S(2)}, u32[]{:S(2)}) %collective-permute-start.24) | collective-permute-done | bytes 12320 | tf_op jit(solution)/shard_map/ppermute | solution.py:1226
  592.1 1.7 fusion.3
  594.6 2.3 collective-permute-start.26
  597.1 2.8 collective-permute-start.29
  599.9 3.3 collective-permute-start.30
  603.9 11.0 %collective-permute-done.30 = bf16[192,768]{1,0:T(8,128)(2,1)S(1)} collective-permute-done((bf16[192,768]{1,0:T(8,128)(2,1)S(1)}, bf16[192,768]{1,0:T(8,128)(2,1)S(1)}, u32[]{:S(2)}, u32[]{:S(2)}) %collective-permute-start.30) | collective-permute-done | bytes 294944 | tf_op jit(solution)/shard_map/ppermute | solution.py:1226
  (207 shorter events, 47.5 us)
Async XLA Ops:
  114.3 37.2 %collective-permute-start = (bf16[384,1024]{1,0:T(8,128)(2,1)}, bf16[384,1024]{1,0:T(8,128)(2,1)S(1)}, u32[]{:S(2)}, u32[]{:S(2)}) collective-permute-start(bf16[384,1024]{1,0:T(8,128)(2,1)} %get-tuple-element.42), channel_id=1, source_target_pairs={{4,6},{5,7},{6,4},{7,5},{12,14},{13,15},{14,12},{15,13},{20,22},{2... | collective-permute-start | bytes 2359304 | tf_op jit(solution)/shard_map/ppermute | solution.py:1226
  116.2 37.3 %collective-permute-start.1 = (bf16[384,1024]{1,0:T(8,128)(2,1)}, bf16[384,1024]{1,0:T(8,128)(2,1)}, u32[]{:S(2)}, u32[]{:S(2)}) collective-permute-start(bf16[384,1024]{1,0:T(8,128)(2,1)} %get-tuple-element.43), channel_id=1, source_target_pairs={{4,6},{5,7},{6,4},{7,5},{12,14},{13,15},{14,12},{15,13},{20,22},{2... | collective-permute-start | bytes 2359304 | tf_op jit(solution)/shard_map/ppermute | solution.py:1226
  153.5 115.9 %copy-start.6 = (bf16[384,1024]{1,0:T(8,128)(2,1)S(1)}, bf16[384,1024]{1,0:T(8,128)(2,1)}, u32[]{:S(2)}) copy-start(bf16[384,1024]{1,0:T(8,128)(2,1)} %copy-done.5) | copy-start | bytes 2359300
  274.7 51.1 %collective-permute-start.31 = (bf16[2,384,384]{2,1,0:T(8,128)(2,1)S(1)}, bf16[2,384,384]{2,1,0:T(8,128)(2,1)S(1)}, u32[]{:S(2)}, u32[]{:S(2)}) collective-permute-start(bf16[2,384,384]{2,1,0:T(8,128)(2,1)S(1)} %dynamic-slice_bitcast_fusion.4), channel_id=1, source_target_pairs={{0,16},{1,17},{2,18},{3,19},{4,20},{5,21},{6,22},{7,23},{8,24},{9,... | collective-permute-start | bytes 1769480 | tf_op jit(solution)/shard_map/ppermute | solution.py:1226
  319.6 8.1 %collective-permute-start.13 = (bf16[384,512]{1,0:T(8,128)(2,1)S(1)}, bf16[384,512]{1,0:T(8,128)(2,1)S(1)}, u32[]{:S(2)}, u32[]{:S(2)}) collective-permute-start(bf16[384,512]{1,0:T(8,128)(2,1)S(1)} %get-tuple-element.74), channel_id=1, source_target_pairs={{16,24},{17,25},{18,26},{19,27},{20,28},{21,29},{22,30},{23,31}} | collective-permute-start | bytes 1179656 | tf_op jit(solution)/shard_map/ppermute | solution.py:1226
  320.4 8.0 %collective-permute-start.16 = (bf16[384,512]{1,0:T(8,128)(2,1)S(1)}, bf16[384,512]{1,0:T(8,128)(2,1)S(1)}, u32[]{:S(2)}, u32[]{:S(2)}) collective-permute-start(bf16[384,512]{1,0:T(8,128)(2,1)S(1)} %get-tuple-element.72), channel_id=1, source_target_pairs={{16,24},{17,25},{18,26},{19,27},{20,28},{21,29},{22,30},{23,31}} | collective-permute-start | bytes 1179656 | tf_op jit(solution)/shard_map/ppermute | solution.py:1226
  321.1 25.8 %collective-permute-start.15 = (bf16[384,512]{1,0:T(8,128)(2,1)S(1)}, bf16[384,512]{1,0:T(8,128)(2,1)S(1)}, u32[]{:S(2)}, u32[]{:S(2)}) collective-permute-start(bf16[384,512]{1,0:T(8,128)(2,1)S(1)} %get-tuple-element.73), channel_id=1, source_target_pairs={{8,0},{9,1},{10,2},{11,3},{12,4},{13,5},{14,6},{15,7},{24,16},{25,... | collective-permute-start | bytes 1179656 | tf_op jit(solution)/shard_map/ppermute | solution.py:1226
  322.4 26.8 %collective-permute-start.12 = (bf16[384,512]{1,0:T(8,128)(2,1)S(1)}, bf16[384,512]{1,0:T(8,128)(2,1)S(1)}, u32[]{:S(2)}, u32[]{:S(2)}) collective-permute-start(bf16[384,512]{1,0:T(8,128)(2,1)S(1)} %get-tuple-element.71), channel_id=1, source_target_pairs={{8,0},{9,1},{10,2},{11,3},{12,4},{13,5},{14,6},{15,7},{24,16},{25,... | collective-permute-start | bytes 1179656 | tf_op jit(solution)/shard_map/ppermute | solution.py:1226
  326.0 19.6 %collective-permute-start.32 = (bf16[384,384]{1,0:T(8,128)(2,1)S(1)}, bf16[384,384]{1,0:T(8,128)(2,1)S(1)}, u32[]{:S(2)}, u32[]{:S(2)}) collective-permute-start(bf16[384,384]{1,0:T(8,128)(2,1)S(1)} %fusion.39), channel_id=1, source_target_pairs={{0,8},{1,9},{2,10},{3,11},{4,12},{5,13},{6,14},{7,15},{8,0},{9,1},... | collective-permute-start | bytes 884744 | tf_op jit(solution)/shard_map/ppermute | solution.py:1226
  327.7 22.3 %collective-permute-start.6 = (bf16[384,512]{1,0:T(8,128)(2,1)S(1)}, bf16[384,512]{1,0:T(8,128)(2,1)S(1)}, u32[]{:S(2)}, u32[]{:S(2)}) collective-permute-start(bf16[384,512]{1,0:T(8,128)(2,1)S(1)} %get-tuple-element.77), channel_id=1, source_target_pairs={{16,24},{17,25},{18,26},{19,27},{20,28},{21,29},{22,30},{23,31}} | collective-permute-start | bytes 1179656 | tf_op jit(solution)/shard_map/ppermute | solution.py:1226
  328.4 83.0 %collective-permute-start.3 = (bf16[256,1536]{1,0:T(8,128)(2,1)S(1)}, bf16[256,1536]{1,0:T(8,128)(2,1)S(1)}, u32[]{:S(2)}, u32[]{:S(2)}) collective-permute-start(bf16[256,1536]{1,0:T(8,128)(2,1)S(1)} %get-tuple-element.82), channel_id=1, source_target_pairs={{0,4},{1,5},{2,6},{3,7},{4,0},{5,1},{6,2},{7,3},{8,12},{9,13},{10,... | collective-permute-start | bytes 2359304 | tf_op jit(solution)/shard_map/ppermute | solution.py:1226
  345.6 27.6 %collective-permute-start.17 = (bf16[384,512]{1,0:T(8,128)(2,1)S(1)}, bf16[384,512]{1,0:T(8,128)(2,1)S(1)}, u32[]{:S(2)}, u32[]{:S(2)}) collective-permute-start(bf16[384,512]{1,0:T(8,128)(2,1)S(1)} %get-tuple-element.80), channel_id=1, source_target_pairs={{16,0},{17,1},{18,2},{19,3},{20,4},{21,5},{22,6},{23,7},{24,8},{25... | collective-permute-start | bytes 1179656 | tf_op jit(solution)/shard_map/ppermute | solution.py:1226
  347.0 110.4 %collective-permute-start.43 = (bf16[2,384,1024]{2,1,0:T(8,128)(2,1)S(1)}, bf16[2,384,1024]{2,1,0:T(8,128)(2,1)S(1)}, u32[]{:S(2)}, u32[]{:S(2)}) collective-permute-start(bf16[2,384,1024]{2,1,0:T(8,128)(2,1)S(1)} %dynamic-slice_bitcast_fusion), channel_id=1, source_target_pairs={{0,8},{1,9},{2,10},{3,11},{4,12},{5,13},{6,14},{7,15},{8,0},{9,1},... | collective-permute-start | bytes 4718600 | tf_op jit(solution)/shard_map/ppermute | solution.py:1226
  349.2 26.0 %collective-permute-start.9 = (bf16[384,512]{1,0:T(8,128)(2,1)S(1)}, bf16[384,512]{1,0:T(8,128)(2,1)S(1)}, u32[]{:S(2)}, u32[]{:S(2)}) collective-permute-start(bf16[384,512]{1,0:T(8,128)(2,1)S(1)} %get-tuple-element.75), channel_id=1, source_target_pairs={{16,24},{17,25},{18,26},{19,27},{20,28},{21,29},{22,30},{23,31}} | collective-permute-start | bytes 1179656 | tf_op jit(solution)/shard_map/ppermute | solution.py:1226
  350.0 61.5 %collective-permute-start.33 = (bf16[192,384]{1,0:T(8,128)(2,1)S(1)}, bf16[192,384]{1,0:T(8,128)(2,1)S(1)}, u32[]{:S(2)}, u32[]{:S(2)}) collective-permute-start(bf16[192,384]{1,0:T(8,128)(2,1)S(1)} %get-tuple-element.94), channel_id=1, source_target_pairs={{0,4},{1,5},{2,6},{3,7},{4,2},{5,3},{6,0},{7,1},{8,12},{9,13},{10,... | collective-permute-start | bytes 442376 | tf_op jit(solution)/shard_map/ppermute | solution.py:1226
  373.1 39.6 %collective-permute-start.34 = (bf16[192,384]{1,0:T(8,128)(2,1)S(1)}, bf16[192,384]{1,0:T(8,128)(2,1)S(1)}, u32[]{:S(2)}, u32[]{:S(2)}) collective-permute-start(bf16[192,384]{1,0:T(8,128)(2,1)S(1)} %get-tuple-element.93), channel_id=1, source_target_pairs={{4,6},{5,7},{6,4},{7,5},{12,14},{13,15},{14,12},{15,13},{20,22},{2... | collective-permute-start | bytes 442376 | tf_op jit(solution)/shard_map/ppermute | solution.py:1226
  375.2 84.3 %collective-permute-start.39 = (bf16[2,384,1024]{2,1,0:T(8,128)(2,1)}, bf16[2,384,1024]{2,1,0:T(8,128)(2,1)S(1)}, u32[]{:S(2)}, u32[]{:S(2)}) collective-permute-start(bf16[2,384,1024]{2,1,0:T(8,128)(2,1)} %dynamic-slice_bitcast_fusion.1), channel_id=1, source_target_pairs={{0,16},{1,17},{2,18},{3,19},{4,20},{5,21},{6,22},{7,23},{8,24},{9,... | collective-permute-start | bytes 4718600 | tf_op jit(solution)/shard_map/ppermute | solution.py:1226
  411.5 49.9 %collective-permute-start.35 = (bf16[2,384,1024]{2,1,0:T(8,128)(2,1)S(1)}, bf16[2,384,1024]{2,1,0:T(8,128)(2,1)S(1)}, u32[]{:S(2)}, u32[]{:S(2)}) collective-permute-start(bf16[2,384,1024]{2,1,0:T(8,128)(2,1)S(1)} %dynamic-slice_bitcast_fusion.2), channel_id=1, source_target_pairs={{0,8},{1,9},{2,10},{3,11},{4,12},{5,13},{6,14},{7,15},{8,0},{9,1},... | collective-permute-start | bytes 4718600 | tf_op jit(solution)/shard_map/ppermute | solution.py:1226
  411.5 42.8 %collective-permute-start.14 = (bf16[384,512]{1,0:T(8,128)(2,1)S(1)}, bf16[384,512]{1,0:T(8,128)(2,1)S(1)}, u32[]{:S(2)}, u32[]{:S(2)}) collective-permute-start(bf16[384,512]{1,0:T(8,128)(2,1)S(1)} %get-tuple-element.79), channel_id=1, source_target_pairs={{16,0},{17,1},{18,2},{19,3},{20,4},{21,5},{22,6},{23,7},{24,8},{25... | collective-permute-start | bytes 1179656 | tf_op jit(solution)/shard_map/ppermute | solution.py:1226
  412.8 42.8 %collective-permute-start.18 = (bf16[384,512]{1,0:T(8,128)(2,1)S(1)}, bf16[384,512]{1,0:T(8,128)(2,1)S(1)}, u32[]{:S(2)}, u32[]{:S(2)}) collective-permute-start(bf16[384,512]{1,0:T(8,128)(2,1)S(1)} %fusion.25), channel_id=1, source_target_pairs={{0,6},{1,7},{2,4},{3,5},{4,2},{5,3},{6,0},{7,1},{8,14},{9,15},{10,... | collective-permute-start | bytes 1179656 | tf_op jit(solution)/shard_map/ppermute | solution.py:1226
  454.3 9.5 %collective-permute-start.8 = (bf16[384,512]{1,0:T(8,128)(2,1)S(1)}, bf16[384,512]{1,0:T(8,128)(2,1)S(1)}, u32[]{:S(2)}, u32[]{:S(2)}) collective-permute-start(bf16[384,512]{1,0:T(8,128)(2,1)S(1)} %get-tuple-element.76), channel_id=1, source_target_pairs={{8,0},{9,1},{10,2},{11,3},{12,4},{13,5},{14,6},{15,7},{24,16},{25,... | collective-permute-start | bytes 1179656 | tf_op jit(solution)/shard_map/ppermute | solution.py:1226
  455.6 24.4 %collective-permute-start.5 = (bf16[384,512]{1,0:T(8,128)(2,1)S(1)}, bf16[384,512]{1,0:T(8,128)(2,1)S(1)}, u32[]{:S(2)}, u32[]{:S(2)}) collective-permute-start(bf16[384,512]{1,0:T(8,128)(2,1)S(1)} %get-tuple-element.78), channel_id=1, source_target_pairs={{8,0},{9,1},{10,2},{11,3},{12,4},{13,5},{14,6},{15,7},{24,16},{25,... | collective-permute-start | bytes 1179656 | tf_op jit(solution)/shard_map/ppermute | solution.py:1226
  457.4 16.6 %collective-permute-start.2 = (bf16[256,1536]{1,0:T(8,128)(2,1)S(1)}, bf16[256,1536]{1,0:T(8,128)(2,1)S(1)}, u32[]{:S(2)}, u32[]{:S(2)}) collective-permute-start(bf16[256,1536]{1,0:T(8,128)(2,1)S(1)} %get-tuple-element.81), channel_id=1, source_target_pairs={{0,4},{1,5},{2,6},{3,7},{4,0},{5,1},{6,2},{7,3},{8,12},{9,13},{10,... | collective-permute-start | bytes 2359304 | tf_op jit(solution)/shard_map/ppermute | solution.py:1226
  459.5 19.2 %collective-permute-start.4 = (bf16[256,1536]{1,0:T(8,128)(2,1)S(1)}, bf16[256,1536]{1,0:T(8,128)(2,1)S(1)}, u32[]{:S(2)}, u32[]{:S(2)}) collective-permute-start(bf16[256,1536]{1,0:T(8,128)(2,1)S(1)} %add_convert_fusion.1), channel_id=1, source_target_pairs={{0,1},{1,0},{2,3},{3,2},{4,5},{5,4},{6,7},{7,6},{8,9},{9,8},{10,11... | collective-permute-start | bytes 2359304 | tf_op jit(solution)/shard_map/ppermute | solution.py:1226
  461.4 12.4 %collective-permute-start.10 = (bf16[384,512]{1,0:T(8,128)(2,1)S(1)}, bf16[384,512]{1,0:T(8,128)(2,1)S(1)}, u32[]{:S(2)}, u32[]{:S(2)}) collective-permute-start(bf16[384,512]{1,0:T(8,128)(2,1)S(1)} %get-tuple-element.69), channel_id=1, source_target_pairs={{16,0},{17,1},{18,2},{19,3},{20,4},{21,5},{22,6},{23,7},{24,8},{25... | collective-permute-start | bytes 1179656 | tf_op jit(solution)/shard_map/ppermute | solution.py:1226
  463.8 18.5 %collective-permute-start.7 = (bf16[384,512]{1,0:T(8,128)(2,1)S(1)}, bf16[384,512]{1,0:T(8,128)(2,1)S(1)}, u32[]{:S(2)}, u32[]{:S(2)}) collective-permute-start(bf16[384,512]{1,0:T(8,128)(2,1)S(1)} %get-tuple-element.70), channel_id=1, source_target_pairs={{16,0},{17,1},{18,2},{19,3},{20,4},{21,5},{22,6},{23,7},{24,8},{25... | collective-permute-start | bytes 1179656 | tf_op jit(solution)/shard_map/ppermute | solution.py:1226
  473.8 36.6 %collective-permute-start.44 = (bf16[384,1024]{1,0:T(8,128)(2,1)S(1)}, bf16[384,1024]{1,0:T(8,128)(2,1)S(1)}, u32[]{:S(2)}, u32[]{:S(2)}) collective-permute-start(bf16[384,1024]{1,0:T(8,128)(2,1)S(1)} %fusion.14), channel_id=1, source_target_pairs={{0,16},{1,17},{2,18},{3,19},{4,20},{5,21},{6,22},{7,23},{8,24},{9,... | collective-permute-start | bytes 2359304 | tf_op jit(solution)/shard_map/ppermute | solution.py:1226
  474.0 36.9 %collective-permute-start.40 = (bf16[384,1024]{1,0:T(8,128)(2,1)S(1)}, bf16[384,1024]{1,0:T(8,128)(2,1)S(1)}, u32[]{:S(2)}, u32[]{:S(2)}) collective-permute-start(bf16[384,1024]{1,0:T(8,128)(2,1)S(1)} %fusion.13), channel_id=1, source_target_pairs={{0,8},{1,9},{2,10},{3,11},{4,12},{5,13},{6,14},{7,15},{8,0},{9,1},... | collective-permute-start | bytes 2359304 | tf_op jit(solution)/shard_map/ppermute | solution.py:1226
  478.7 20.9 %collective-permute-start.11 = (bf16[384,512]{1,0:T(8,128)(2,1)S(1)}, bf16[384,512]{1,0:T(8,128)(2,1)S(1)}, u32[]{:S(2)}, u32[]{:S(2)}) collective-permute-start(bf16[384,512]{1,0:T(8,128)(2,1)S(1)} %fusion.31), channel_id=1, source_target_pairs={{0,6},{1,7},{2,4},{3,5},{4,2},{5,3},{6,0},{7,1},{8,14},{9,15},{10,... | collective-permute-start | bytes 1179656 | tf_op jit(solution)/shard_map/ppermute | solution.py:1226
  480.0 35.9 %collective-permute-start.36 = (bf16[384,1024]{1,0:T(8,128)(2,1)S(1)}, bf16[384,1024]{1,0:T(8,128)(2,1)S(1)}, u32[]{:S(2)}, u32[]{:S(2)}) collective-permute-start(bf16[384,1024]{1,0:T(8,128)(2,1)S(1)} %fusion.12), channel_id=1, source_target_pairs={{0,16},{1,17},{2,18},{3,19},{4,20},{5,21},{6,22},{7,23},{8,24},{9,... | collective-permute-start | bytes 2359304 | tf_op jit(solution)/shard_map/ppermute | solution.py:1226
  505.2 70.5 %collective-permute-start.27 = (bf16[2,384,768]{2,1,0:T(8,128)(2,1)S(1)}, bf16[2,384,768]{2,1,0:T(8,128)(2,1)S(1)}, u32[]{:S(2)}, u32[]{:S(2)}) collective-permute-start(bf16[2,384,768]{2,1,0:T(8,128)(2,1)S(1)} %dynamic-slice_bitcast_fusion.3), channel_id=1, source_target_pairs={{0,8},{1,9},{2,10},{3,11},{4,12},{5,13},{6,14},{7,15},{8,0},{9,1},... | collective-permute-start | bytes 3538952 | tf_op jit(solution)/shard_map/ppermute | solution.py:1226
  509.8 6.4 %collective-permute-start.20 = (bf16[256,1536]{1,0:T(8,128)(2,1)S(1)}, bf16[256,1536]{1,0:T(8,128)(2,1)S(1)}, u32[]{:S(2)}, u32[]{:S(2)}) collective-permute-start(bf16[256,1536]{1,0:T(8,128)(2,1)S(1)} %slice.306), channel_id=1, source_target_pairs={{0,4},{1,5},{2,6},{3,7},{4,0},{5,1},{6,2},{7,3},{8,12},{9,13},{10,... | collective-permute-start | bytes 2359304 | tf_op jit(solution)/shard_map/ppermute | solution.py:1226
  510.7 11.0 %collective-permute-start.45 = (bf16[192,1024]{1,0:T(8,128)(2,1)S(1)}, bf16[192,1024]{1,0:T(8,128)(2,1)S(1)}, u32[]{:S(2)}, u32[]{:S(2)}) collective-permute-start(bf16[192,1024]{1,0:T(8,128)(2,1)S(1)} %get-tuple-element.86), channel_id=1, source_target_pairs={{0,4},{1,5},{2,6},{3,7},{4,2},{5,3},{6,0},{7,1},{8,12},{9,13},{10,... | collective-permute-start | bytes 1179656 | tf_op jit(solution)/shard_map/ppermute | solution.py:1226
  510.8 26.0 %collective-permute-start.46 = (bf16[192,1024]{1,0:T(8,128)(2,1)S(1)}, bf16[192,1024]{1,0:T(8,128)(2,1)S(1)}, u32[]{:S(2)}, u32[]{:S(2)}) collective-permute-start(bf16[192,1024]{1,0:T(8,128)(2,1)S(1)} %get-tuple-element.85), channel_id=1, source_target_pairs={{4,6},{5,7},{6,4},{7,5},{12,14},{13,15},{14,12},{15,13},{20,22},{2... | collective-permute-start | bytes 1179656 | tf_op jit(solution)/shard_map/ppermute | solution.py:1226
  515.9 21.0 %collective-permute-start.41 = (bf16[192,1024]{1,0:T(8,128)(2,1)S(1)}, bf16[192,1024]{1,0:T(8,128)(2,1)S(1)}, u32[]{:S(2)}, u32[]{:S(2)}) collective-permute-start(bf16[192,1024]{1,0:T(8,128)(2,1)S(1)} %get-tuple-element.88), channel_id=1, source_target_pairs={{0,4},{1,5},{2,6},{3,7},{4,2},{5,3},{6,0},{7,1},{8,12},{9,13},{10,... | collective-permute-start | bytes 1179656 | tf_op jit(solution)/shard_map/ppermute | solution.py:1226
  516.3 33.2 %collective-permute-start.42 = (bf16[192,1024]{1,0:T(8,128)(2,1)S(1)}, bf16[192,1024]{1,0:T(8,128)(2,1)S(1)}, u32[]{:S(2)}, u32[]{:S(2)}) collective-permute-start(bf16[192,1024]{1,0:T(8,128)(2,1)S(1)} %get-tuple-element.87), channel_id=1, source_target_pairs={{4,6},{5,7},{6,4},{7,5},{12,14},{13,15},{14,12},{15,13},{20,22},{2... | collective-permute-start | bytes 1179656 | tf_op jit(solution)/shard_map/ppermute | solution.py:1226
  521.7 41.6 %collective-permute-start.19 = (bf16[256,1536]{1,0:T(8,128)(2,1)S(1)}, bf16[256,1536]{1,0:T(8,128)(2,1)S(1)}, u32[]{:S(2)}, u32[]{:S(2)}) collective-permute-start(bf16[256,1536]{1,0:T(8,128)(2,1)S(1)} %slice.307), channel_id=1, source_target_pairs={{0,4},{1,5},{2,6},{3,7},{4,0},{5,1},{6,2},{7,3},{8,12},{9,13},{10,... | collective-permute-start | bytes 2359304 | tf_op jit(solution)/shard_map/ppermute | solution.py:1226
  536.9 15.6 %collective-permute-start.37 = (bf16[192,1024]{1,0:T(8,128)(2,1)S(1)}, bf16[192,1024]{1,0:T(8,128)(2,1)S(1)}, u32[]{:S(2)}, u32[]{:S(2)}) collective-permute-start(bf16[192,1024]{1,0:T(8,128)(2,1)S(1)} %get-tuple-element.90), channel_id=1, source_target_pairs={{0,4},{1,5},{2,6},{3,7},{4,2},{5,3},{6,0},{7,1},{8,12},{9,13},{10,... | collective-permute-start | bytes 1179656 | tf_op jit(solution)/shard_map/ppermute | solution.py:1226
  536.9 25.3 %collective-permute-start.38 = (bf16[192,1024]{1,0:T(8,128)(2,1)S(1)}, bf16[192,1024]{1,0:T(8,128)(2,1)S(1)}, u32[]{:S(2)}, u32[]{:S(2)}) collective-permute-start(bf16[192,1024]{1,0:T(8,128)(2,1)S(1)} %get-tuple-element.89), channel_id=1, source_target_pairs={{4,6},{5,7},{6,4},{7,5},{12,14},{13,15},{14,12},{15,13},{20,22},{2... | collective-permute-start | bytes 1179656 | tf_op jit(solution)/shard_map/ppermute | solution.py:1226
  549.5 25.3 %collective-permute-start.21 = (bf16[256,1536]{1,0:T(8,128)(2,1)S(1)}, bf16[256,1536]{1,0:T(8,128)(2,1)S(1)}, u32[]{:S(2)}, u32[]{:S(2)}) collective-permute-start(bf16[256,1536]{1,0:T(8,128)(2,1)S(1)} %fusion.6), channel_id=1, source_target_pairs={{0,1},{1,0},{2,3},{3,2},{4,5},{5,4},{6,7},{7,6},{8,9},{9,8},{10,11... | collective-permute-start | bytes 2359304 | tf_op jit(solution)/shard_map/ppermute | solution.py:1226
  575.6 1.2 collective-permute-start.22
  576.8 2.6 collective-permute-start.23
  577.2 19.7 %collective-permute-start.28 = (bf16[384,768]{1,0:T(8,128)(2,1)S(1)}, bf16[384,768]{1,0:T(8,128)(2,1)S(1)}, u32[]{:S(2)}, u32[]{:S(2)}) collective-permute-start(bf16[384,768]{1,0:T(8,128)(2,1)S(1)} %fusion.36), channel_id=1, source_target_pairs={{0,16},{1,17},{2,18},{3,19},{4,20},{5,21},{6,22},{7,23},{8,24},{9,... | collective-permute-start | bytes 1769480 | tf_op jit(solution)/shard_map/ppermute | solution.py:1226
  579.5 12.5 %collective-permute-start.24 = (f32[2,1536]{1,0:T(2,128)S(1)}, f32[2,1536]{1,0:T(2,128)S(1)}, u32[]{:S(2)}, u32[]{:S(2)}) collective-permute-start(f32[2,1536]{1,0:T(2,128)S(1)} %fusion.61), channel_id=1, source_target_pairs={{0,16},{1,17},{2,18},{3,19},{4,20},{5,21},{6,22},{7,23},{8,24},{9,... | collective-permute-start | bytes 36872 | tf_op jit(solution)/shard_map/ppermute | solution.py:1226
  592.0 2.6 collective-permute-start.25
  594.6 8.6 %collective-permute-start.26 = (f32[2,1536]{1,0:T(2,128)S(1)}, f32[2,1536]{1,0:T(2,128)S(1)}, u32[]{:S(2)}, u32[]{:S(2)}) collective-permute-start(f32[2,1536]{1,0:T(2,128)S(1)} %add.526), channel_id=1, source_target_pairs={{0,2},{1,3},{2,0},{3,1},{4,6},{5,7},{6,4},{7,5},{8,10},{9,11},{10,... | collective-permute-start | bytes 36872 | tf_op jit(solution)/shard_map/ppermute | solution.py:1226
  597.1 6.7 %collective-permute-start.29 = (bf16[192,768]{1,0:T(8,128)(2,1)S(1)}, bf16[192,768]{1,0:T(8,128)(2,1)S(1)}, u32[]{:S(2)}, u32[]{:S(2)}) collective-permute-start(bf16[192,768]{1,0:T(8,128)(2,1)S(1)} %get-tuple-element.92), channel_id=1, source_target_pairs={{0,4},{1,5},{2,6},{3,7},{4,2},{5,3},{6,0},{7,1},{8,12},{9,13},{10,... | collective-permute-start | bytes 884744 | tf_op jit(solution)/shard_map/ppermute | solution.py:1226
  599.9 15.0 %collective-permute-start.30 = (bf16[192,768]{1,0:T(8,128)(2,1)S(1)}, bf16[192,768]{1,0:T(8,128)(2,1)S(1)}, u32[]{:S(2)}, u32[]{:S(2)}) collective-permute-start(bf16[192,768]{1,0:T(8,128)(2,1)S(1)} %get-tuple-element.91), channel_id=1, source_target_pairs={{4,6},{5,7},{6,4},{7,5},{12,14},{13,15},{14,12},{15,13},{20,22},{2... | collective-permute-start | bytes 884744 | tf_op jit(solution)/shard_map/ppermute | solution.py:1226
  (32 other events, 588.3 us)

commit v5 on v4

--- a/solution.py
+++ b/solution.py
@@ -975,9 +975,78 @@
     )(tokens, out_grad, gain, cosine, sine, joined, weight_o, weight_d)
 
 
+class PlaneSum:
+    def __init__(self, copies, place, x_first, bufs, sent=None, come=None):
+        self.place, self.bufs, self.x_first = place, bufs, x_first
+        half, keep, come_two, home_one, home_two = bufs
+        first, second = (place.over_x, place.over_y) if x_first else (place.over_y, place.over_x)
+        self.at = place.y if x_first else place.x
+        self.one = None if sent is None else copies.make(sent, come, first)
+        self.two = copies.make(half, come_two, second)
+        rows = home_one.shape[0]
+        c = place.c
+        home = (c * place.cross[0] + (1 - c) * place.beside[0], c * place.cross[1] + (1 - c) * place.beside[1])
+        self.to_home = copies.make(half.at[pl.ds((1 - c) * rows, rows)], home_one, home)
+        self.to_far = copies.make(half.at[pl.ds(rows, rows)], home_two, place.far)
+
+    def cross_second(self, kept, come):
+        if self.one is not None:
+            self.one.wait()
+        half, keep, come_two, home_one, home_two = self.bufs
+        at = self.at
+        half[...] = (kept[1 - at].astype(floats) + come[1 - at].astype(floats)).astype(halves)
+        self.two.start()
+        keep[...] = (kept[at].astype(floats) + come[at].astype(floats)).astype(halves)
+
+    def go_home(self):
+        half, keep, come_two, home_one, home_two = self.bufs
+        self.two.wait()
+        half[...] = (keep[...].astype(floats) + come_two[...].astype(floats)).astype(halves)
+        self.to_home.start()
+        pl.when(self.place.odd)(self.to_far.start)
+
+    def finish(self, out):
+        half, keep, come_two, home_one, home_two = self.bufs
+        rows = home_one.shape[0]
+        self.to_home.wait()
+
+        @pl.when(self.place.c == 0)
+        def _():
+            out[...] = half[:rows, :].astype(floats) + home_one[...].astype(floats)
+
+        @pl.when(self.place.odd)
+        def _():
+            self.to_far.wait()
+            out[...] = home_one[...].astype(floats) + home_two[...].astype(floats)
+
+
+def plane_buffers(rows, cols):
+    full = pltpu.VMEM((rows, cols), halves)
+    part = pltpu.VMEM((rows // 2, cols), halves)
+    return [full, full, full, part, part]
+
+
+def outer_blocks(place, x_first, left, right, send_ref, keep_ref, on_sent):
+    rows = left.shape[1] // 4
+    for kept in (False, True):
+        for i in range(2):
+            if x_first:
+                block = 2 * i + (place.x if kept else 1 - place.x)
+            else:
+                block = 2 * (place.y if kept else 1 - place.y) + i
+            cols = pl.ds(pl.multiple_of(block * rows, 128), rows)
+            value = lax.dot_general(
+                left[:, cols], right, (((0,), (0,)), ((), ())), preferred_element_type=floats
+            ).astype(halves)
+            (keep_ref if kept else send_ref)[i] = value
+        if not kept:
+            on_sent()
+
+
 def mid_kernel(ctx_ref, tok_ref, gain_ref, g_full, weight_refs, outs, scratch):
-    (res_out, gres_out, e_full, part_out, gate_out, up_out, down_out, dctx_out, delta_out, gain_out) = outs
-    (ctx, m_full, dh, hid, dgate, dup, w_o, w_d, w_g, w_u, *bufs, ss, rs, wsem) = scratch
+    (res_out, gres_out, e_full, part_out, down_keep, down_come, gate_keep, gate_send, up_keep, up_send,
+     dctx_out, delta_out, gain_out) = outs
+    (ctx, m_full, dh, hid, dgate, dup, w_o, w_d, w_g, w_u, down_send, *bufs, ss, rs, wsem) = scratch
     place = Place()
     copies = Copies(ss, rs)
     block, width = tok_ref.shape
@@ -1098,18 +1167,11 @@
             ),
         )
 
-    def outer(left, right, out):
-        def one(rows):
-            out[rows, :] = lax.dot_general(
-                left[:, rows], right[...], (((0,), (0,)), ((), ())), preferred_element_type=floats
-            ).astype(halves)
-
-        tiles(width, 256, one)
-
     sum_two.run(back_norm)
     partial_out(1)
-    outer(g_full, hid, down_out)
-    outer(m_full, dgate, gate_out)
+    down_over = copies.make(down_send, down_come, place.over_x)
+    outer_blocks(place, True, g_full, hid[...], down_send, down_keep, down_over.start)
+    outer_blocks(place, False, m_full, dgate[...], gate_send, gate_keep, lambda: None)
     gain_out[...] = jnp.zeros_like(gain_out)
     for k in range(CHUNKS):
         at = pl.ds(k * chunk, chunk)
@@ -1124,7 +1186,7 @@
         e_full[at, :] = grad.astype(halves)
         gather_two.put(k)
     sum_two.finish()
-    outer(m_full, dup, up_out)
+    outer_blocks(place, True, m_full, dup[...], up_send, up_keep, lambda: None)
 
     def back_context(k):
         lanes = slice(k * two, (k + 1) * two)
@@ -1143,6 +1205,7 @@
     gather_two.finish()
     for fetch in fetches:
         fetch.drain()
+    down_over.wait()
 
 
 def middle(context_t, tokens, gain, grad_full, weights):
@@ -1155,9 +1218,7 @@
         shape((block, width), floats),
         shape((group, width), halves),
         shape((group, width), halves),
-        shape((width, hidden), halves),
-        shape((width, hidden), halves),
-        shape((width, hidden), halves),
+        *[shape((2, width // 4, hidden), halves)] * 6,
         shape((q_cols, group), halves),
         shape((q_cols // HEAD_WIDTH, group), floats),
         shape((1, width), floats),
@@ -1167,6 +1228,7 @@
         pltpu.VMEM((group, width), halves),
         *[pltpu.VMEM((group, hidden), halves)] * 4,
         *[pltpu.VMEM(weight.shape, halves) for weight in weights[:4]],
+        pltpu.VMEM((2, width // 4, hidden), halves),
         *[pltpu.VMEM((block, width), floats)] * 2,
         *[pltpu.VMEM((block, width), halves)] * 6,
         *copy_semaphores(),
@@ -1174,19 +1236,294 @@
     ]
 
     def kernel(*refs):
-        mid_kernel(*refs[:4], refs[4:10], refs[10:20], refs[20:])
+        mid_kernel(*refs[:4], refs[4:10], refs[10:23], refs[23:])
 
     return pl.pallas_call(
         kernel,
         out_shape=out_shape,
         in_specs=[VM] * 4 + [HB] * 6,
-        out_specs=(VM,) * 10,
+        out_specs=(VM,) * 13,
         scratch_shapes=scratch,
         compiler_params=pltpu.CompilerParams(
             collective_id=1, has_side_effects=True, vmem_limit_bytes=62 << 20
         ),
         name="middle",
     )(context_t, tokens, gain, grad_full, *weights)
+
+
+def last_kernel(ins, outs, scratch):
+    (dq_ref, dkv_ref, cos_ref, sin_ref, n_ref, joined, tok_ref, gain_ref, gres_ref, e_ref, ctx_ref,
+     gain_mlp_ref, *mlp) = ins
+    (in_grad, gains_out, gate_out, up_out, down_out, q_out, kv_out, o_out) = outs
+    (full, ctx, d_lin, acc_a, acc_b, own, x_in, y_in, rel_in, cross_in, cross_out, kept, come,
+     gains, gains_in, *rest) = scratch
+    bufs_mlp = [rest[5 * i : 5 * i + 5] for i in range(3)]
+    rest = rest[15:]
+    bufs_attn = [rest[8 * i : 8 * i + 8] for i in range(3)]
+    rest = rest[24:]
+    sum_bufs, (ss, rs, lsem) = rest[:8], rest[8:]
+    place = Place()
+    copies = Copies(ss, rs)
+    block, width = tok_ref.shape
+    two = 2 * block
+    q_cols = dq_ref.shape[0]
+    kv_cols = own.shape[1] // 2
+    half_width = HEAD_WIDTH // 2
+
+    load_e = pltpu.make_async_copy(e_ref, full, lsem.at[0])
+    load_e.start()
+    order = (4, 12, 0, 8)
+    own_loads = [
+        pltpu.make_async_copy(dkv_ref.at[at], own.at[i], lsem.at[1 + i]) for i, at in enumerate(order)
+    ]
+    y_loads = [
+        pltpu.make_async_copy(dkv_ref.at[at + 2], y_in.at[i], lsem.at[5 + i])
+        for i, at in enumerate(order)
+    ]
+    for copy in own_loads:
+        copy.start()
+
+    @pl.when(place.corner)
+    def _():
+        for copy in y_loads:
+            copy.start()
+
+    def load_mlp(i):
+        return [
+            pltpu.make_async_copy(mlp[2 * i], kept, lsem.at[9]),
+            pltpu.make_async_copy(mlp[2 * i + 1], come, lsem.at[10]),
+        ]
+
+    loads = load_mlp(0)
+    for copy in loads:
+        copy.start()
+    gains[0, 0:1, :] = gain_mlp_ref[...]
+    gains[0, 1:2, :] = jnp.zeros_like(gain_mlp_ref)
+    meet((place.beside, place.near, place.far, place.cross, place.over_x, place.over_y))
+
+    back_rel = [copies.make(dkv_ref.at[at + 3], rel_in.at[i], place.over_x) for i, at in enumerate(order)]
+    back_x = [copies.make(dkv_ref.at[at + 1], x_in.at[i], place.over_x) for i, at in enumerate(order)]
+    back_y = [copies.make(dkv_ref.at[at + 2], y_in.at[i], place.over_y) for i, at in enumerate(order)]
+    back_sum = [copies.make(y_in.at[i], y_in.at[i], place.over_y) for i in range(4)]
+    crossing = [copies.make(cross_out.at[i], cross_in.at[i], place.cross) for i in range(2)]
+    for i in range(4):
+        pl.when(place.turn)(back_rel[i].start)
+        pl.when(place.x == 1)(back_x[i].start)
+        pl.when(place.turn)(back_y[i].start)
+
+    def corner_sum(i):
+        @pl.when(place.corner)
+        def _():
+            back_rel[i].wait_recv()
+            y_loads[i].wait()
+            y_in[i] = (y_in[i].astype(floats) + rel_in[i].astype(floats)).astype(halves)
+            back_sum[i].start()
+
+    def home_sum(i, put):
+        own_loads[i].wait()
+        acc_b[...] = own[i].astype(floats)
+
+        @pl.when(place.x == 0)
+        def _():
+            back_x[i].wait_recv()
+            acc_b[...] += x_in[i].astype(floats)
+
+        @pl.when((place.y == 0) & (place.x == 0))
+        def _():
+            back_y[i].wait_recv()
+            acc_b[...] += y_in[i].astype(floats)
+
+        @pl.when((place.y == 0) & (place.x == 1))
+        def _():
+            back_sum[i].wait_recv()
+            acc_b[...] += y_in[i].astype(floats)
+
+        put()
+
+    sums = []
+    for i, x_first in enumerate((True, False, True)):
+        sums.append(PlaneSum(copies, place, x_first, bufs_mlp[i]))
+    for i in range(3):
+        for copy in loads:
+            copy.wait()
+        sums[i].cross_second(kept, come)
+        if i < 2:
+            loads = load_mlp(i + 1)
+            for copy in loads:
+                copy.start()
+        if i == 1:
+            corner_sum(0)
+    ctx[...] = ctx_ref[...].T
+
+    attn_sums = []
+    for i, x_first in enumerate((False, True, False)):
+        sent, keep, got = bufs_attn[i][:3]
+        attn_sums.append(PlaneSum(copies, place, x_first, bufs_attn[i][3:], sent, got))
+
+    def attn_grad(i, left, right):
+        sent, keep, got = bufs_attn[i][:3]
+        outer_blocks(place, attn_sums[i].x_first, left, right, sent, keep, attn_sums[i].one.start)
+
+    corner_sum(1)
+    load_e.wait()
+    attn_grad(0, full, ctx[...])
+    load_n = pltpu.make_async_copy(n_ref, full, lsem.at[0])
+    load_n.start()
+
+    def cross_back(i):
+        def put():
+            cross_out[i] = acc_b[...].astype(halves)
+            crossing[i].start()
+
+        home_sum(i, put)
+
+    def unturn(value, at, first_row):
+        low, high = value[:half_width], value[half_width:]
+        cosine, sine = cos_ref[:, at], sin_ref[:, at]
+        turned = jnp.concatenate([low * cosine + high * sine, high * cosine - low * sine], axis=0)
+        d_lin[first_row : first_row + HEAD_WIDTH, at] = turned.astype(halves)
+
+    cross_back(0)
+    corner_sum(2)
+    everything = slice(0, 2 * two)
+    for head in range(q_cols // HEAD_WIDTH):
+        unturn(dq_ref[head * HEAD_WIDTH : (head + 1) * HEAD_WIDTH, :], everything, head * HEAD_WIDTH)
+    cross_back(1)
+    corner_sum(3)
+    load_n.wait()
+    attn_grad(1, full, d_lin[:q_cols, :].T)
+    for plane in sums:
+        plane.go_home()
+
+    def second(i):
+        sent, keep, got = bufs_attn[i][:3]
+        attn_sums[i].cross_second(keep, got)
+
+    second(0)
+
+    def keep_a(k):
+        def put():
+            acc_a[:, k * two : (k + 1) * two] = acc_b[...]
+
+        home_sum(2 + k, put)
+
+    keep_a(0)
+    keep_a(1)
+    second(1)
+    attn_sums[0].go_home()
+    for k in range(2):
+        crossing[k].wait_recv()
+        lanes = slice(k * two, (k + 1) * two)
+        total = acc_a[:, lanes] + cross_in[k].astype(floats)
+        for head in range(kv_cols // HEAD_WIDTH):
+            rows = slice(head * HEAD_WIDTH, (head + 1) * HEAD_WIDTH)
+            unturn(total[rows], lanes, q_cols + head * HEAD_WIDTH)
+        d_lin[q_cols + kv_cols :, lanes] = total[kv_cols:].astype(halves)
+
+    group_sum = GroupSum(copies, sum_bufs, place)
+
+    def back_norm(k, put):
+        rows = slice(k * two, (k + 1) * two)
+        left = d_lin[:, rows].T
+
+        def one(cols):
+            value = dot_nt(left, joined[cols, :])
+            put(cols, value)
+            gains[0, 1:2, cols] += jnp.sum(value * full[rows, cols].astype(floats), axis=0, keepdims=True)
+
+        tiles(width, 256, one)
+
+    group_sum.run(back_norm)
+    gains[0, 1:2, :] = gains[0, 1:2, :] / gain_ref[...]
+    attn_grad(2, full, d_lin[q_cols:, :].T)
+    attn_sums[1].go_home()
+    for stage, device in enumerate((place.beside, place.over_x, place.over_y, place.near, place.far)):
+        copy = copies.make(gains.at[stage], gains_in.at[stage], device)
+        copy.start()
+        copy.wait()
+        if stage < 4:
+            gains[stage + 1] = gains[stage] + gains_in[stage]
+        else:
+            gains_out[...] = gains[stage] + gains_in[stage]
+        if stage == 2:
+            second(2)
+    for plane, out in zip(sums, (down_out, gate_out, up_out)):
+        plane.finish(out)
+    attn_sums[2].go_home()
+    chunk = block // CHUNKS
+    for k in range(CHUNKS):
+        at = pl.ds(k * chunk, chunk)
+        back = group_sum.take(k)
+        tok = tok_ref[at, :].astype(floats)
+        root = lax.rsqrt(jnp.mean(tok * tok, axis=-1, keepdims=True) + eps_norm)
+        weighted = back * gain_ref[...]
+        slope = jnp.mean(weighted * tok, axis=-1, keepdims=True)
+        in_grad[at, :] = gres_ref[at, :] + root * weighted - tok * (root * root * root * slope)
+    for plane, out in zip(attn_sums, (o_out, q_out, kv_out)):
+        plane.finish(out)
+    group_sum.finish()
+    for i in range(4):
+        pl.when(place.turn)(back_rel[i].wait_send)
+        pl.when(place.x == 1)(back_x[i].wait_send)
+        pl.when(place.turn)(back_y[i].wait_send)
+        pl.when(place.corner)(back_sum[i].wait_send)
+    for copy in crossing:
+        copy.wait_send()
+
+
+def last_part(d_query_t, d_kv, cosine, sine, normed, joined, tokens, gain, gres, e_full, context_t, gain_mlp, mlp):
+    block, width = tokens.shape
+    group = 4 * block
+    q_cols, kv_all = d_query_t.shape[0], d_kv.shape[1]
+    kv_cols = kv_all // 2
+    hidden = mlp[0].shape[2]
+    per = width // 8
+    shape = jax.ShapeDtypeStruct
+    out_shape = (
+        shape((block, width), floats),
+        shape((2, width), floats),
+        *[shape((per, hidden), floats)] * 3,
+        shape((per, q_cols), floats),
+        shape((per, kv_all), floats),
+        shape((per, q_cols), floats),
+    )
+    piece = (kv_all, 2 * block)
+    scratch = [
+        pltpu.VMEM((group, width), halves),
+        pltpu.VMEM((group, q_cols), halves),
+        pltpu.VMEM((joined.shape[1], group), halves),
+        pltpu.VMEM((kv_all, group), floats),
+        pltpu.VMEM(piece, floats),
+        *[pltpu.VMEM((4,) + piece, halves)] * 4,
+        *[pltpu.VMEM((2,) + piece, halves)] * 2,
+        *[pltpu.VMEM((2, width // 4, hidden), halves)] * 2,
+        *[pltpu.VMEM((5, 2, width), floats)] * 2,
+    ]
+    for _ in range(3):
+        scratch += plane_buffers(width // 4, hidden)
+    for cols in (q_cols, q_cols, kv_all):
+        scratch += [pltpu.VMEM((2, width // 4, cols), halves)] * 3 + plane_buffers(width // 4, cols)
+    scratch += [
+        *[pltpu.VMEM((block, width), floats)] * 2,
+        *[pltpu.VMEM((block, width), halves)] * 6,
+        *copy_semaphores(),
+        pltpu.SemaphoreType.DMA((11,)),
+    ]
+
+    def kernel(*refs):
+        last_kernel(refs[:18], refs[18:26], refs[26:])
+
+    return pl.pallas_call(
+        kernel,
+        out_shape=out_shape,
+        in_specs=[VM, HB, VM, VM, HB, VM, VM, VM, VM, HB, VM, VM] + [HB] * 6,
+        out_specs=(VM,) * 8,
+        scratch_shapes=scratch,
+        compiler_params=pltpu.CompilerParams(
+            collective_id=3, has_side_effects=True, vmem_limit_bytes=63 << 20
+        ),
+        name="last",
+    )(d_query_t, d_kv, cosine, sine, normed, joined, tokens, gain, gres, e_full, context_t, gain_mlp, *mlp)
 
 
 def routes(target):
@@ -1233,52 +1570,11 @@
     return here_sum + send(there_sum.astype(halves), "near").astype(floats)
 
 
-def dot_tt(a, b):
-    return lax.dot_general(a, b, (((0,), (1,)), ((), ())), preferred_element_type=floats)
-
-
 def rope_tables(positions):
     half_width = HEAD_WIDTH // 2
     inverse = 1.0 / rope_base ** (jnp.arange(half_width, dtype=floats) * 2.0 / HEAD_WIDTH)
     angles = inverse[:, None] * positions.astype(floats)[None, :]
     return jnp.cos(angles), jnp.sin(angles)
-
-
-def turn(linear, cosine, sine):
-    shaped = linear.reshape(-1, 2, HEAD_WIDTH // 2, linear.shape[-1])
-    one, two = shaped[:, 0], shaped[:, 1]
-    turned = jnp.stack([one * cosine - two * sine, two * cosine + one * sine], axis=1)
-    return turned.reshape(linear.shape)
-
-
-def norm_back(vectors, gain, grad):
-    root = lax.rsqrt(jnp.mean(vectors * vectors, axis=-1, keepdims=True) + eps_norm)
-    weighted = grad * gain
-    slope = jnp.mean(weighted * vectors, axis=-1, keepdims=True)
-    back = root * weighted - vectors * (root * root * root * slope)
-    return back, jnp.sum(grad * vectors * root, axis=0)
-
-
-def sum_rows_over_plane(grad, x, y, x_first):
-    shaped = grad.reshape(2, 2, -1, grad.shape[-1])
-
-    def pick(array, at, axis):
-        return lax.dynamic_index_in_dim(array, at, axis, keepdims=False)
-
-    axes = (("x", x, 1), ("y", y, 0)) if x_first else (("y", y, 0), ("x", x, 1))
-    (way, at, axis), (way_two, at_two, _) = axes
-    come = send(pick(shaped, 1 - at, axis), way)
-    half = pick(shaped, at, axis).astype(floats) + come.astype(floats)
-    come = send(pick(half, 1 - at_two, 0).astype(halves), way_two)
-    return pick(half, at_two, 0) + come.astype(floats)
-
-
-def sum_rows_home(part, odd):
-    rows = part.shape[0] // 2
-    first, second = part[:rows], part[rows:]
-    one = send(jnp.where(odd, first, second).astype(halves), "home").astype(floats)
-    two = send(second.astype(halves), "odd_far").astype(floats)
-    return jnp.where(odd, one + two, first + one)
 
 
 def local_regrouped(
@@ -1374,62 +1670,36 @@
     context_t, log_total = attend_forward(sc, q_t, index_row, start_row, pieces)
 
     (
-        residual, grad_residual, attn_grad_full, part_out, gate_grad, up_grad, down_grad,
+        residual, grad_residual, attn_grad_full, part_out, down_keep, down_come, gate_keep, gate_send,
+        up_keep, up_send,
         d_context_t, delta, mlp_gain_part,
     ) = middle(
         context_t, tokens, gain_mlp[None, :], grad_full,
         (weight_o, weight_d, gate_weight, up_weight, *slices),
     )
     output = residual + scatter_group(part_out[: 2 * block], part_out[2 * block :])
-    gate_sum = sum_rows_home(sum_rows_over_plane(gate_grad, x, y, True), odd)
-    up_sum = sum_rows_home(sum_rows_over_plane(up_grad, x, y, False), odd)
-    down_sum = sum_rows_home(sum_rows_over_plane(down_grad, x, y, True), odd)
-
-    output_grad = dot_tt(attn_grad_full, context_t).astype(halves)
-    output_sum = sum_rows_home(sum_rows_over_plane(output_grad, x, y, False), odd)
+    gate_come = send(gate_send, "y")
+    up_come = send(up_send, "x")
+
     d_query_t, d_pieces = attend_backward(
         sc, q_t, d_context_t, log_total, delta, index_row, start_row, pieces
     )
-    d_halves = []
-    for n in range(2):
-        sums = []
-        for cross in range(2):
-            own, from_x, from_y, from_relay = (d_pieces[8 * n + 4 * cross + i] for i in range(4))
-            back = send(from_relay, "unrelay").astype(floats)
-            from_y = (from_y.astype(floats) + back).astype(halves)
-            sums.append(
-                own.astype(floats)
-                + send(from_x, "x_down").astype(floats)
-                + send(from_y, "y_down").astype(floats)
-            )
-        d_halves.append(sums[0] + send(sums[1].astype(halves), "cross").astype(floats))
-    d_kv = jnp.concatenate(d_halves, axis=1)
-    d_turned = turn(jnp.concatenate([d_query_t, d_kv[:kv_cols]]), cosine, -sine)
-    d_linear = jnp.concatenate([d_turned, d_kv[kv_cols:]]).astype(halves)
-    here_d = dot_tt(d_linear[:, : 2 * block], joined)
-    there_d = dot_tt(d_linear[:, 2 * block :], joined)
-    grad_normed = scatter_group(here_d, there_d)
-    proj_grad = lax.dot_general(
-        normed_full, d_linear, (((0,), (1,)), ((), ())), preferred_element_type=floats
-    ).astype(halves)
-    proj_sum = sum_rows_home(sum_rows_over_plane(proj_grad, x, y, True), odd)
-    grad_tokens_part, attn_gain_part = norm_back(tokens32, gain_attn, grad_normed)
-    input_grad = grad_residual + grad_tokens_part
-
-    gains = jnp.stack([attn_gain_part, mlp_gain_part[0]])
-    for way in ("core", "x", "y", "near", "far"):
-        gains = gains + send(gains, way)
+    input_grad, gains, gate_sum, up_sum, down_sum, query_sum, kv_sum, output_sum = last_part(
+        d_query_t, d_pieces, cosine, sine, normed_full, joined, tokens, gain_attn[None, :],
+        grad_residual, attn_grad_full, context_t, mlp_gain_part,
+        (down_keep, down_come, gate_keep, gate_come, up_keep, up_come),
+    )
     per = gains.shape[1] // 8
     gains = lax.dynamic_slice_in_dim(gains, dp * per, per, axis=1)
     return (
         output.astype(halves),
         input_grad,
+        gains[1],
+        query_sum,
+        kv_sum[:, :kv_cols],
+        kv_sum[:, kv_cols:],
+        output_sum.T,
         gains[0],
-        proj_sum[:, :q_cols],
-        proj_sum[:, q_cols : q_cols + kv_cols],
-        proj_sum[:, q_cols + kv_cols :],
-        output_sum.T,
-        gains[1],
         gate_sum,
         up_sum,
         down_sum.T,

time: 628 us -> 532 us (0.85)
  Pallas kernels: 276 us -> 463 us
  waiting for transfers between devices: 167 us -> 6.54 us
  starting transfers between devices: 115 us -> 12.9 us
  other arithmetic: 22.1 us -> 12 us
  matrix products: 9.72 us -> 0 us
    pallas_call x0 -> x1, Pallas kernels: none -> 196 us  [last_part(): pl.pallas_call(kernel, out_shape=out_shape, in_specs=[VM, HB, VM, VM, HB,...]
    ppermute x47 -> x7, waiting for transfers between devices: 167 us -> 6.54 us  [send(): return lax.ppermute(block, ('dp', 'tp'), ROUTES[way])]
    ppermute x47 -> x7, starting transfers between devices: 115 us -> 12.9 us  [send(): return lax.ppermute(block, ('dp', 'tp'), ROUTES[way])]
    dot_general x4 -> x0, matrix products: 9.72 us -> none  [the longest x3 6.8 us: dot_tt(): lax.dot_general(a, b, (((0,), (1,)), ((), ())), preferred_element_type=fl...]
    pallas_call x1, Pallas kernels: 38.4 us -> 30.4 us  [attend_backward(): pl.pallas_call(functools.partial(bwd_kernel, n, width, True), out_shape=(...]
    unnamed x68 -> x56, local copies, waits for them, and re-layouts: 15.5 us -> 19.6 us
  transfers between devices with their start and end apart: 47 -> 7, of which waited for: 18 -> 1; matrix products, arithmetic and copies ran while one was open for 4% -> 2% of each run, Pallas kernels for 10% -> 47%
where the time goes in v5:
time: 532 us; the launch traced here: 527 us
  Pallas kernels  463 us (87%)
  local copies, waits for them, and re-layouts  30.4 us (6%)
  starting transfers between devices  12.9 us (2%)
  other arithmetic  12 us (2%)
  waiting for transfers between devices  6.54 us (1%)
    pallas_call x1, Pallas kernels, last_part(): pl.pallas_call(kernel, out_shape=out_shape, in_specs=[VM, HB, VM, VM, HB,...  196 us
    pallas_call x1, Pallas kernels, middle(): pl.pallas_call(kernel, out_shape=out_shape, in_specs=[VM] * 4 + [HB] * 6,...  120 us
    pallas_call x1, Pallas kernels, first_part(): pl.pallas_call(first_kernel, out_shape=out_shape, in_specs=[VM] * 5 + [HB...  97.7 us
    pallas_call x1, Pallas kernels, attend_backward(): pl.pallas_call(functools.partial(bwd_kernel, n, width, True), out_shape=(...  30.4 us
    unnamed x56, local copies, waits for them, and re-layouts  19.6 us
    pallas_call x1, Pallas kernels, attend_forward(): pl.pallas_call(functools.partial(fwd_kernel, n, width, first, last), out_...  19.3 us
    ppermute x7, starting transfers between devices, send(): return lax.ppermute(block, ('dp', 'tp'), ROUTES[way])  12.9 us
  transfers between devices with their start and end apart: 7, of which 1 were waited for; matrix products, arithmetic and copies ran while one was open for 2% of the time, Pallas kernels for 47%

profile of v5, /device:TPU:3, one launch (start us, length us, event | category | flops | bytes accessed | tf_op | source)
XLA Modules:
  0.0 526.8 jit_solution(17449377281412230314)
XLA Ops:
  0.8 1.5 convert_reduce_fusion.2
  2.2 0.7 reshape.275.gain_ref.refs_7_
  2.9 1.4 copy.27
  4.4 1.3 copy.28
  5.8 0.9 fusion.2
  6.6 1.8 subtract_convert_fusion
  8.5 0.8 multiply_sine_fusion
  9.2 0.0 copy-start.7
  9.3 0.6 pad_maximum_fusion.joined_in
  9.9 0.0 copy-start.9
  9.9 0.0 copy-start.11
  9.9 2.8 constant_dynamic-slice_fusion.1
  12.7 97.7 %first.1 = (bf16[384,1024]{1,0:T(8,128)(2,1)S(1)}, bf16[16,384,512]{2,1,0:T(8,128)(2,1)}, bf16[1024,1536]{1,0:T(8,128)(2,1)S(1)}, bf16[1024,1536]{1,0:T(8,128)(2...) custom-call(bf16[256,1536]{1,0:T(8,128)(2,1)S(1)} %copy-done.1, ...), custom_call_target="tpu_custom_call" | custom-call | tf_op jit(solution)/shard_map/first/pallas_call | solution.py:960
  110.5 1.7 copy-done.4
  112.2 1.4 copy-done.5
  113.6 1.0 copy-done.10
  114.6 1.9 collective-permute-start
  116.5 4.8 collective-permute-start.1
  121.5 0.6 reshape.276.refs_2_
  122.0 0.1 stack.153
  122.2 0.1 pad_add_fusion.3
  122.3 0.2 slice_reduce_fusion.1
  122.5 1.8 compare_select_fusion.2.start_ref
  124.3 2.8 copy-done
  127.1 19.3 %attend_forward.1 = (bf16[384,1024]{1,0:T(8,128)(2,1)S(1)}, f32[4,1024]{1,0:T(4,128)S(1)}) custom-call(s32[4,32]{1,0:T(4,128)S(1)} %pad_add_fusion.2.sc, bf16[384,1024]{1,0:T(8,128)(2,1)S(1)} %get-tuple-element.46.q_ref, s32[1,1024]{1,0:T(1,128)S(1)} %bitcast.48, s32[1,1024]{1,0:T(1,128)S(1)} %compare_select_fusion.2.start_ref, bf16[16,384,512]{2,1,0:T(8,128)(2,1)S(1)} %copy-done), custom_call_target="tpu_custom_call" | custom-call | tf_op jit(solution)/shard_map/attend_forward/pallas_call | solution.py:134
  146.4 0.9 copy-done.3
  147.3 6.5 %collective-permute-done.1.refs_9_ = bf16[384,1024]{1,0:T(8,128)(2,1)} collective-permute-done((bf16[384,1024]{1,0:T(8,128)(2,1)}, bf16[384,1024]{1,0:T(8,128)(2,1)}, u32[]{:S(2)}, u32[]{:S(2)}) %collective-permute-start.1) | collective-permute-done | bytes 786464 | tf_op jit(solution)/shard_map/ppermute | solution.py:1563
  153.8 120.4 %middle.1 = (f32[256,1536]{1,0:T(8,128)}, f32[256,1536]{1,0:T(8,128)}, bf16[1024,1536]{1,0:T(8,128)(2,1)}, bf16[1024,1536]{1,0:T(8,128)(2,1)}, bf16[2,384,1024]{...) custom-call(bf16[384,1024]{1,0:T(8,128)(2,1)} %copy-done.3, ...), custom_call_target="tpu_custom_call" | custom-call | tf_op jit(solution)/shard_map/middle/pallas_call | solution.py:1241
  274.2 2.4 fusion
  276.5 0.7 collective-permute-start.3
  277.2 2.2 collective-permute-start.5
  279.4 2.2 collective-permute-start.6
  281.6 0.7 collective-permute-start.2
  282.3 2.2 add_convert_fusion.1
  284.5 0.5 collective-permute-start.4
  285.0 30.4 %attend_backward.1 = (f32[384,1024]{1,0:T(8,128)S(1)}, bf16[16,384,512]{2,1,0:T(8,128)(2,1)S(1)}) custom-call(s32[4,32]{1,0:T(4,128)S(1)} %pad_add_fusion.2.sc, bf16[384,1024]{1,0:T(8,128)(2,1)S(1)} %get-tuple-element.46.q_ref, bf16[384,1024]{1,0:T(8,128)(2,1)S(1)} %copy-done.12, f32[4,1024]{1,0:T(4,128)S(1)} %get-tuple-element.58.log_ref, ...), custom_call_target="tpu_custom_call" | custom-call | tf_op jit(solution)/shard_map/attend_backward/pallas_call | solution.py:243
  315.4 2.6 copy-done.2
  318.0 1.1 copy-done.8
  319.2 195.7 %last.1 = (f32[256,1536]{1,0:T(8,128)}, f32[2,1536]{1,0:T(2,128)}, f32[192,1024]{1,0:T(8,128)}, f32[192,1024]{1,0:T(8,128)}, f32[192,1024]{1,0:T(8,128)}, /*inde...) custom-call(f32[384,1024]{1,0:T(8,128)} %copy-done.8, bf16[16,384,512]{2,1,0:T(8,128)(2,1)} %copy-done.2, ...), custom_call_target="tpu_custom_call" | custom-call | tf_op jit(solution)/shard_map/last/pallas_call | solution.py:1516
  514.9 1.4 constant_dynamic-slice_fusion
  516.3 1.8 fusion.1
  518.1 3.2 add_convert_fusion
  521.3 1.1 copy.35
  522.5 0.7 copy.36
  523.2 0.7 copy.37
  523.9 0.9 copy.38
  524.8 0.9 copy.39
  525.7 0.9 copy.40
  (53 shorter events, 0.2 us)
Async XLA Ops:
  2.9 9.7 %copy-start.13 = (f32[1,1536]{1,0:T(1,128)}, f32[1,1536]{1,0:T(1,128)S(1)}, u32[]{:S(2)}) copy-start(f32[1,1536]{1,0:T(1,128)S(1)} %reshape.275.gain_ref.refs_7_) | copy-start | bytes 18436
  2.9 6.3 %copy-start.16 = (bf16[1536,384]{1,0:T(8,128)(2,1)S(1)}, bf16[1536,384]{1,0:T(8,128)(2,1)}, u32[]{:S(2)}) copy-start(bf16[1536,384]{1,0:T(8,128)(2,1)} %param.16) | copy-start | bytes 3538948
  9.2 3.5 copy-start.6
  9.2 3.4 copy-start.7
  9.9 2.8 copy-start.1
  9.9 2.8 copy-start.9
  9.9 2.8 copy-start.11
  12.7 108.7 %copy-start.23 = (bf16[1536]{0:T(1024)(128)(2,1)S(1)}, bf16[1536]{0:T(1024)(128)(2,1)}, u32[]{:S(2)}) copy-start(bf16[1536]{0:T(1024)(128)(2,1)} %param.20) | copy-start | bytes 9220
  110.5 1.7 copy-start.4
  112.2 1.4 copy-start.5
  113.6 1.0 copy-start.10
  114.6 32.7 %collective-permute-start = (bf16[384,1024]{1,0:T(8,128)(2,1)}, bf16[384,1024]{1,0:T(8,128)(2,1)S(1)}, u32[]{:S(2)}, u32[]{:S(2)}) collective-permute-start(bf16[384,1024]{1,0:T(8,128)(2,1)} %get-tuple-element.53), channel_id=1, source_target_pairs={{4,6},{5,7},{6,4},{7,5},{12,14},{13,15},{14,12},{15,13},{20,22},{2... | collective-permute-start | bytes 2359304 | tf_op jit(solution)/shard_map/ppermute | solution.py:1563
  116.5 37.3 %collective-permute-start.1 = (bf16[384,1024]{1,0:T(8,128)(2,1)}, bf16[384,1024]{1,0:T(8,128)(2,1)}, u32[]{:S(2)}, u32[]{:S(2)}) collective-permute-start(bf16[384,1024]{1,0:T(8,128)(2,1)} %get-tuple-element.54), channel_id=1, source_target_pairs={{4,6},{5,7},{6,4},{7,5},{12,14},{13,15},{14,12},{15,13},{20,22},{2... | collective-permute-start | bytes 2359304 | tf_op jit(solution)/shard_map/ppermute | solution.py:1563
  124.3 2.8 copy-start
  146.4 0.9 copy-start.3
  147.3 6.5 %copy-start.17 = (bf16[384,1024]{1,0:T(8,128)(2,1)}, bf16[384,1024]{1,0:T(8,128)(2,1)S(1)}, u32[]{:S(2)}) copy-start(bf16[384,1024]{1,0:T(8,128)(2,1)S(1)} %collective-permute-done.refs_8_) | copy-start | bytes 2359300
  276.5 8.4 %copy-start.12 = (bf16[384,1024]{1,0:T(8,128)(2,1)S(1)}, bf16[384,1024]{1,0:T(8,128)(2,1)}, u32[]{:S(2)}) copy-start(bf16[384,1024]{1,0:T(8,128)(2,1)} %get-tuple-element.57.do_ref) | copy-start | bytes 2359300
  276.5 8.4 %copy-start.14 = (f32[4,1024]{1,0:T(4,128)S(1)}, f32[4,1024]{1,0:T(4,128)}, u32[]{:S(2)}) copy-start(f32[4,1024]{1,0:T(4,128)} %get-tuple-element.59.delta_ref) | copy-start | bytes 49156
  276.5 5.7 %collective-permute-start.3 = (bf16[256,1536]{1,0:T(8,128)(2,1)S(1)}, bf16[256,1536]{1,0:T(8,128)(2,1)S(1)}, u32[]{:S(2)}, u32[]{:S(2)}) collective-permute-start(bf16[256,1536]{1,0:T(8,128)(2,1)S(1)} %get-tuple-element.89), channel_id=1, source_target_pairs={{0,4},{1,5},{2,6},{3,7},{4,0},{5,1},{6,2},{7,3},{8,12},{9,13},{10,... | collective-permute-start | bytes 2359304 | tf_op jit(solution)/shard_map/ppermute | solution.py:1563
  277.2 42.0 %collective-permute-start.5 = (bf16[2,384,1024]{2,1,0:T(8,128)(2,1)}, bf16[2,384,1024]{2,1,0:T(8,128)(2,1)}, u32[]{:S(2)}, u32[]{:S(2)}) collective-permute-start(bf16[2,384,1024]{2,1,0:T(8,128)(2,1)} %get-tuple-element.70), channel_id=1, source_target_pairs={{0,16},{1,17},{2,18},{3,19},{4,20},{5,21},{6,22},{7,23},{8,24},{9,... | collective-permute-start | bytes 4718600 | tf_op jit(solution)/shard_map/ppermute | solution.py:1563
  279.4 39.8 %collective-permute-start.6 = (bf16[2,384,1024]{2,1,0:T(8,128)(2,1)}, bf16[2,384,1024]{2,1,0:T(8,128)(2,1)}, u32[]{:S(2)}, u32[]{:S(2)}) collective-permute-start(bf16[2,384,1024]{2,1,0:T(8,128)(2,1)} %get-tuple-element.72), channel_id=1, source_target_pairs={{0,8},{1,9},{2,10},{3,11},{4,12},{5,13},{6,14},{7,15},{8,0},{9,1},... | collective-permute-start | bytes 4718600 | tf_op jit(solution)/shard_map/ppermute | solution.py:1563
  281.6 236.5 %collective-permute-start.2 = (bf16[256,1536]{1,0:T(8,128)(2,1)}, bf16[256,1536]{1,0:T(8,128)(2,1)S(1)}, u32[]{:S(2)}, u32[]{:S(2)}) collective-permute-start(bf16[256,1536]{1,0:T(8,128)(2,1)} %get-tuple-element.88), channel_id=1, source_target_pairs={{0,4},{1,5},{2,6},{3,7},{4,0},{5,1},{6,2},{7,3},{8,12},{9,13},{10,... | collective-permute-start | bytes 2359304 | tf_op jit(solution)/shard_map/ppermute | solution.py:1563
  284.5 233.6 %collective-permute-start.4 = (bf16[256,1536]{1,0:T(8,128)(2,1)}, bf16[256,1536]{1,0:T(8,128)(2,1)}, u32[]{:S(2)}, u32[]{:S(2)}) collective-permute-start(bf16[256,1536]{1,0:T(8,128)(2,1)} %add_convert_fusion.1), channel_id=1, source_target_pairs={{0,1},{1,0},{2,3},{3,2},{4,5},{5,4},{6,7},{7,6},{8,9},{9,8},{10,11... | collective-permute-start | bytes 2359304 | tf_op jit(solution)/shard_map/ppermute | solution.py:1563
  315.4 2.6 copy-start.2
  318.0 1.1 copy-start.8
  518.1 3.2 copy-start.15
  521.3 1.2 copy-start.22
  521.3 1.9 copy-start.21
  521.3 2.6 copy-start.20
  522.5 2.3 copy-start.19
  523.9 1.8 copy-start.18

commit v6 on v5

--- a/solution.py
+++ b/solution.py
@@ -12,6 +12,7 @@
 LOG2E = 1.4426950408889634
 SCORE = LOG2E * HEAD_WIDTH ** (-0.5)
 VSCALE = 2.0 ** -9
+FAR_BASE = 1 << 24
 floats = jnp.float32
 halves = jnp.bfloat16
 
@@ -22,6 +23,51 @@
 
 def dot_nt(a, b):
     return lax.dot_general(a, b, (((1,), (1,)), ((), ())), preferred_element_type=floats)
+
+
+def token_base(j, core, pair, side):
+    return ((2 * j + core) * 4 + 2 * pair + side) * BLK
+
+
+def group_bases():
+    dp, z = lax.axis_index("dp"), lax.axis_index("tp")
+    j, c, pair, side = dp // 2, lax.rem(dp, 2), z // 2, lax.rem(z, 2)
+    return [
+        token_base(j, core, pair, at) for at in (side, 1 - side) for core in (c, 1 - c)
+    ]
+
+
+def item_start(counts_ref, token):
+    start = jnp.zeros_like(token)
+    for i in range(3):
+        start = jnp.where(token >= counts_ref[i], counts_ref[i], start)
+    return start
+
+
+def group_index():
+    lanes = lax.broadcasted_iota(jnp.int32, (1, BLK), 1)
+    return jnp.concatenate([lanes + base for base in group_bases()], axis=1)
+
+
+def fill_places(counts_ref, sc, tok_ref, start_ref):
+    dp, z = lax.axis_index("dp"), lax.axis_index("tp")
+    j, c, pair, side = dp // 2, lax.rem(dp, 2), z // 2, lax.rem(z, 2)
+    x, y = lax.rem(j, 2), j // 2
+    kb = 0
+    for side_of in (side, 1 - side):
+        for cores, pair_of in (((c, 1 - c), pair), ((1 - c, c), 1 - pair)):
+            for j_of, present in ((j, None), (j - 1, x), (j - 2, y), (j - 1, y * (1 - x))):
+                for core in cores:
+                    base = token_base(j_of, core, pair_of, side_of)
+                    sc[0, kb] = base if present is None else jnp.where(present == 1, base, FAR_BASE)
+                    kb += 1
+    for qb, base in enumerate(group_bases()):
+        sc[1, qb] = base
+        sc[2, qb] = item_start(counts_ref, base)
+        sc[3, qb] = item_start(counts_ref, base + (BLK - 1))
+    index = group_index()
+    tok_ref[...] = index
+    start_ref[...] = item_start(counts_ref, index)
 
 
 def pair_state(sc, kb, qb):
@@ -37,21 +83,15 @@
     return (keys <= tok_ref[0:1, lanes]) & (keys >= start_ref[0:1, lanes])
 
 
-def fwd_kernel(n, width, first, last, sc, q_ref, tok_ref, start_ref, pieces, *refs):
-    if not first:
-        acc_in, sum_in = refs[:2]
-        refs = refs[2:]
+def fwd_kernel(n, width, counts, q_ref, pieces, *refs):
     out_acc, out_sum = refs[:2]
-    kv, keys_nat, acc, total, q_wide, sem = refs[2:]
+    kv, keys_nat, acc, total, q_wide, sc, tok_ref, start_ref, sem = refs[2:]
     per = width // BLK
     for i in range(n):
         pltpu.make_async_copy(pieces.at[i], kv.at[i], sem.at[i]).start()
-    if first:
-        acc[...] = jnp.zeros_like(acc)
-        total[...] = jnp.zeros_like(total)
-    else:
-        acc[...] = acc_in[...]
-        total[...] = sum_in[...]
+    acc[...] = jnp.zeros_like(acc)
+    total[...] = jnp.zeros_like(total)
+    fill_places(counts, sc, tok_ref, start_ref)
     for i in range(n):
         pltpu.make_async_copy(pieces.at[i], kv.at[i], sem.at[i]).wait()
     heads_kv = pieces.shape[1] // (2 * HEAD_WIDTH)
@@ -106,59 +146,62 @@
         return lax.fori_loop(0, q_ref.shape[1] // BLK, query_block, carry)
 
     lax.fori_loop(0, n * per, key_block, 0)
-    if last:
-        for h, rows, lanes, wrows, wlanes, hd in places:
-            row = total[h : h + 1, wlanes]
-            out_acc[rows, lanes] = (acc[wrows, wlanes] * ((1.0 / VSCALE) / row)).astype(halves)
-            out_sum[hd : hd + 1, lanes] = jnp.log2(row)
-    else:
-        out_acc[...] = acc[...]
-        out_sum[...] = total[...]
+    for h, rows, lanes, wrows, wlanes, hd in places:
+        row = total[h : h + 1, wlanes]
+        out_acc[rows, lanes] = (acc[wrows, wlanes] * ((1.0 / VSCALE) / row)).astype(halves)
+        out_sum[hd : hd + 1, lanes] = jnp.log2(row)
 
 
 VM = pl.BlockSpec(memory_space=pltpu.VMEM)
 SM = pl.BlockSpec(memory_space=pltpu.SMEM)
 HB = pl.BlockSpec(memory_space=pl.ANY)
-
-
-def attend_forward(sc, q_t, tok, start, pieces, state=None, last=True):
+HM = pl.BlockSpec(memory_space=pltpu.HBM)
+
+
+def place_scratch(blocks, tokens):
+    return [
+        pltpu.SMEM((4, blocks), jnp.int32),
+        pltpu.VMEM((1, tokens), jnp.int32),
+        pltpu.VMEM((1, tokens), jnp.int32),
+    ]
+
+
+def attend_forward(counts, q_t, pieces):
     n, width = pieces.shape[0], pieces.shape[2]
     heads = q_t.shape[0] // HEAD_WIDTH
     heads_kv = pieces.shape[1] // (2 * HEAD_WIDTH)
-    first = state is None
     tokens = q_t.shape[1]
-    out_shape = (
-        jax.ShapeDtypeStruct(q_t.shape, halves if last else floats),
-        jax.ShapeDtypeStruct((heads, tokens), floats),
-    )
+    wide = tokens * heads // heads_kv
     return pl.pallas_call(
-        functools.partial(fwd_kernel, n, width, first, last),
-        out_shape=out_shape,
-        in_specs=[SM, VM, VM, VM] + [HB] + ([] if first else [VM, VM]),
+        functools.partial(fwd_kernel, n, width),
+        out_shape=(
+            jax.ShapeDtypeStruct(q_t.shape, halves),
+            jax.ShapeDtypeStruct((heads, tokens), floats),
+        ),
+        in_specs=[SM, VM, HM],
         out_specs=(VM, VM),
         scratch_shapes=[
             pltpu.VMEM(pieces.shape, halves),
             pltpu.VMEM((heads_kv, BLK, HEAD_WIDTH), halves),
-            pltpu.VMEM((heads_kv * HEAD_WIDTH, tokens * heads // heads_kv), floats),
-            pltpu.VMEM((heads_kv, tokens * heads // heads_kv), floats),
-            pltpu.VMEM((heads_kv * HEAD_WIDTH, tokens * heads // heads_kv), halves),
+            pltpu.VMEM((heads_kv * HEAD_WIDTH, wide), floats),
+            pltpu.VMEM((heads_kv, wide), floats),
+            pltpu.VMEM((heads_kv * HEAD_WIDTH, wide), halves),
+            *place_scratch(n * width // BLK, tokens),
             pltpu.SemaphoreType.DMA((n,)),
         ],
-        compiler_params=pltpu.CompilerParams(vmem_limit_bytes=40 << 20),
+        compiler_params=pltpu.CompilerParams(vmem_limit_bytes=63 << 20),
         name="attend_forward",
-    )(sc, q_t, tok, start, pieces, *(() if first else state))
-
-
-def bwd_kernel(n, width, first, sc, q_ref, do_ref, log_ref, delta_ref, tok_ref, start_ref, pieces, *refs):
-    if not first:
-        dq_in = refs[0]
-        refs = refs[1:]
+    )(counts, q_t, pieces)
+
+
+def bwd_kernel(n, width, counts, q_ref, do_ref, log_ref, delta_ref, pieces, *refs):
     dq_out = refs[0]
     dkv_out = refs[1]
-    kv, dkv, keys_nat, vals_nat, acc, q_wide, do_wide, log_wide, delta_wide, dq_wide, sem, osem = refs[2:]
+    kv, dkv, keys_nat, vals_nat, acc, q_wide, do_wide, log_wide, delta_wide, dq_wide, sc, tok_ref, start_ref, sem, osem = refs[2:]
     per = width // BLK
     for i in range(n):
         pltpu.make_async_copy(pieces.at[i], kv.at[i], sem.at[i]).start()
+    fill_places(counts, sc, tok_ref, start_ref)
     for i in range(n):
         pltpu.make_async_copy(pieces.at[i], kv.at[i], sem.at[i]).wait()
     heads_kv = pieces.shape[1] // (2 * HEAD_WIDTH)
@@ -174,7 +217,7 @@
         do_wide[wrows, wlanes] = do_ref[rows, lanes]
         log_wide[h : h + 1, wlanes] = log_ref[hd : hd + 1, lanes]
         delta_wide[h : h + 1, wlanes] = delta_ref[hd : hd + 1, lanes]
-        dq_wide[wrows, wlanes] = jnp.zeros((HEAD_WIDTH, BLK), floats) if first else dq_in[rows, lanes]
+        dq_wide[wrows, wlanes] = jnp.zeros((HEAD_WIDTH, BLK), floats)
     out_scale = (1.0 / VSCALE) * HEAD_WIDTH ** (-0.5)
 
     def key_block(kb, carry):
@@ -236,18 +279,18 @@
         pltpu.make_async_copy(dkv.at[i], dkv_out.at[i], osem.at[i]).wait()
 
 
-def attend_backward(sc, q_t, do_t, log_total, delta, tok, start, pieces):
+def attend_backward(counts, q_t, do_t, log_total, delta, pieces):
     n, width = pieces.shape[0], pieces.shape[2]
     heads_kv = pieces.shape[1] // (2 * HEAD_WIDTH)
     wide = q_t.shape[0] // (heads_kv * HEAD_WIDTH) * q_t.shape[1]
     outs = pl.pallas_call(
-        functools.partial(bwd_kernel, n, width, True),
+        functools.partial(bwd_kernel, n, width),
         out_shape=(
             jax.ShapeDtypeStruct(q_t.shape, floats),
             jax.ShapeDtypeStruct(pieces.shape, halves),
         ),
-        in_specs=[SM] + [VM] * 6 + [HB],
-        out_specs=(VM, HB),
+        in_specs=[SM] + [VM] * 4 + [HM],
+        out_specs=(VM, HM),
         scratch_shapes=[
             pltpu.VMEM(pieces.shape, halves),
             pltpu.VMEM(pieces.shape, halves),
@@ -259,12 +302,13 @@
             pltpu.VMEM((heads_kv, wide), floats),
             pltpu.VMEM((heads_kv, wide), floats),
             pltpu.VMEM((heads_kv * HEAD_WIDTH, wide), floats),
+            *place_scratch(n * width // BLK, q_t.shape[1]),
             pltpu.SemaphoreType.DMA((n,)),
             pltpu.SemaphoreType.DMA((n,)),
         ],
-        compiler_params=pltpu.CompilerParams(vmem_limit_bytes=44 << 20),
+        compiler_params=pltpu.CompilerParams(vmem_limit_bytes=63 << 20),
         name="attend_backward",
-    )(sc, q_t, do_t, log_total, delta, tok, start, pieces)
+    )(counts, q_t, do_t, log_total, delta, pieces)
     return outs
 
 
@@ -729,8 +773,16 @@
         self.turn = (self.x == 0) & (self.y == 1)
 
 
+def rope_tables(counts_ref, inverse_ref, cos_ref, sin_ref):
+    index = group_index()
+    positions = (index - item_start(counts_ref, index)).astype(floats)
+    angles = inverse_ref[...] * positions
+    cos_ref[...] = jnp.cos(angles)
+    sin_ref[...] = jnp.sin(angles)
+
+
 class PlaneFetch:
-    def __init__(self, copies, place, out, own=None):
+    def __init__(self, copies, place, out, own=None, own_slice=None):
         self.place, self.out = place, out
         rows = out.shape[0] // 8
 
@@ -746,6 +798,11 @@
         if own is not None:
             self.hop = [
                 copies.make(own.at[part(p.slot, ch)], out.at[part(p.slot, ch)], p.far)
+                for ch in range(2)
+            ]
+        if own_slice is not None:
+            self.hop = [
+                copies.make(own_slice.at[part(0, ch)], out.at[part(p.slot, ch)], p.far)
                 for ch in range(2)
             ]
         self.x = [remote(p.slot, ch, p.over_x) for ch in range(2)]
@@ -819,9 +876,9 @@
 
 
 def first_kernel(
-    tok_ref, grad_ref, gain_ref, cos_ref, sin_ref, joined_in, wo_in, wd_in,
-    q_out, kv_out, n_full, g_full, joined, wo_out, wd_out,
-    linear, kv_own, ss, rs, lsem,
+    counts, inverse_ref, tok_ref, grad_ref, gain_ref, wq_in, wk_ref, wv_ref, wo_in, wd_in, wg_in, wu_in,
+    q_out, kv_out, n_out, g_full, joined_out, wo_out, wd_out, slice_g, slice_u,
+    n_full, joined, own_slice, slices, cos_ref, sin_ref, linear, kv_own, ss, rs, lsem,
 ):
     place = Place()
     copies = Copies(ss, rs)
@@ -829,21 +886,39 @@
     two = 2 * block
     q_cols = q_out.shape[0]
     kv_cols = kv_own.shape[1] // 2
-    local = [
-        pltpu.make_async_copy(src, dst, lsem.at[i])
-        for i, (src, dst) in enumerate(((joined_in, joined), (wo_in, wo_out), (wd_in, wd_out)))
+    q_lanes = pl.ds(0, q_cols)
+    slice_rows = pl.ds(place.slot * own_slice.shape[0], own_slice.shape[0])
+    load_q = pltpu.make_async_copy(wq_in, joined.at[:, q_lanes], lsem.at[0])
+    load_q_odd = pltpu.make_async_copy(
+        wq_in.at[slice_rows], own_slice.at[:, q_lanes], lsem.at[0]
+    )
+    pl.when(place.c == 0)(load_q.start)
+    pl.when(place.odd)(load_q_odd.start)
+    rows4 = slice_g.shape[0]
+    at_slot = pl.ds(place.slot * rows4, rows4)
+    slice_loads = [
+        pltpu.make_async_copy(src.at[at_slot], slices.at[i], lsem.at[1 + i])
+        for i, src in enumerate((wg_in, wu_in))
     ]
-
-    @pl.when(place.c == 0)
-    def _():
-        for copy in local:
-            copy.start()
+    slice_stores = [
+        pltpu.make_async_copy(slices.at[i], dst, lsem.at[6 + i])
+        for i, dst in enumerate((slice_g, slice_u))
+    ]
+    for copy in slice_loads:
+        copy.start()
 
     own_grad = pltpu.make_async_copy(grad_ref, g_full.at[pl.ds(0, block)], lsem.at[3])
     own_grad.start()
     meet((place.beside, place.near, place.far, place.cross, place.over_x, place.over_y))
 
-    fetch_joined = PlaneFetch(copies, place, joined, joined_in)
+    @pl.when(place.odd)
+    def _():
+        lanes = pl.ds(pl.multiple_of(place.slot * own_slice.shape[0], 128), own_slice.shape[0])
+        own_slice[:, q_cols : q_cols + kv_cols] = wk_ref[:, lanes].T
+        own_slice[:, q_cols + kv_cols :] = wv_ref[:, lanes].T
+        load_q_odd.wait()
+
+    fetch_joined = PlaneFetch(copies, place, joined, own_slice=own_slice)
     fetch_o = PlaneFetch(copies, place, wo_out, wo_in)
     fetch_d = PlaneFetch(copies, place, wd_out, wd_in)
     gather = GroupGather(copies, n_full, block, place)
@@ -859,10 +934,21 @@
     fetch_joined.forward()
     fetch_o.start()
     fetch_d.start()
+    @pl.when(place.c == 0)
+    def _():
+        joined[:, q_cols : q_cols + kv_cols] = wk_ref[...].T
+        joined[:, q_cols + kv_cols :] = wv_ref[...].T
+
+    rope_tables(counts, inverse_ref, cos_ref, sin_ref)
+    for load, store in zip(slice_loads, slice_stores):
+        load.wait()
+        store.start()
     fetch_joined.relay()
     gather.wait_here()
     fetch_joined.finish()
-    pl.when(place.c == 0)(local[0].wait)
+    pl.when(place.c == 0)(load_q.wait)
+    keep_joined = pltpu.make_async_copy(joined, joined_out, lsem.at[8])
+    keep_joined.start()
 
     def project(k):
         rows = slice(k * two, (k + 1) * two)
@@ -905,19 +991,21 @@
     project(0)
     share(0)
     gather.wait_there()
-    project(1)
-    share(1)
     own_grad.wait()
     for k in range(CHUNKS):
         gather_g.put(k)
+    project(1)
+    share(1)
+    keep_n = pltpu.make_async_copy(n_full, n_out, lsem.at[9])
+    keep_n.start()
     fetch_o.forward()
     fetch_d.forward()
     spreads_a[0].relay()
     spreads_a[1].relay()
+    crossings[0].wait_recv()
+    spreads_b[0].start()
     fetch_o.relay()
     fetch_d.relay()
-    crossings[0].wait_recv()
-    spreads_b[0].start()
     gather_g.wait_there()
     spreads_b[0].relay()
     crossings[1].wait_recv()
@@ -928,14 +1016,8 @@
     gather_g.wait_here()
     for spread in spreads_a + spreads_b:
         spread.finish()
-    for copy in kept:
+    for copy in kept + slice_stores + [keep_joined, keep_n]:
         copy.wait()
-
-    @pl.when(place.c == 0)
-    def _():
-        for copy in local[1:]:
-            copy.wait()
-
     for copy in crossings:
         copy.wait_send()
     for fetch in (fetch_joined, fetch_o, fetch_d):
@@ -944,35 +1026,48 @@
     gather_g.finish()
 
 
-def first_part(tokens, out_grad, gain, cosine, sine, joined, weight_o, weight_d, q_cols, kv_cols):
+def first_part(counts, inverse, tokens, out_grad, gain, projections, weights):
     block, width = tokens.shape
     group = 4 * block
     shape = jax.ShapeDtypeStruct
+    hidden = weights[2].shape[1]
+    part = (width // 4, hidden)
+    half_width = HEAD_WIDTH // 2
+    q_cols, kv_cols = projections[0].shape[1], projections[1].shape[0]
+    joined_cols = q_cols + 2 * kv_cols
     out_shape = (
         shape((q_cols, group), halves),
         shape((16, 2 * kv_cols, 2 * block), halves),
         shape((group, width), halves),
         shape((group, width), halves),
-        shape(joined.shape, halves),
-        shape(weight_o.shape, halves),
-        shape(weight_d.shape, halves),
+        shape((width, joined_cols), halves),
+        shape(weights[0].shape, halves),
+        shape(weights[1].shape, halves),
+        shape(part, halves),
+        shape(part, halves),
     )
     return pl.pallas_call(
         first_kernel,
         out_shape=out_shape,
-        in_specs=[VM] * 5 + [HB] * 3,
-        out_specs=(VM, HB, VM, VM, VM, HB, HB),
+        in_specs=[SM] + [VM] * 4 + [HB, VM, VM] + [HB] * 4,
+        out_specs=(VM, HM, HM, VM, HM, HM, HM, HM, HM),
         scratch_shapes=[
-            pltpu.VMEM((joined.shape[1], 2 * block), floats),
+            pltpu.VMEM((group, width), halves),
+            pltpu.VMEM((width, joined_cols), halves),
+            pltpu.VMEM((width // 4, joined_cols), halves),
+            pltpu.VMEM((2,) + part, halves),
+            pltpu.VMEM((half_width, group), floats),
+            pltpu.VMEM((half_width, group), floats),
+            pltpu.VMEM((joined_cols, 2 * block), floats),
             pltpu.VMEM((2, 2 * kv_cols, 2 * block), halves),
             *copy_semaphores(),
-            pltpu.SemaphoreType.DMA((6,)),
+            pltpu.SemaphoreType.DMA((10,)),
         ],
         compiler_params=pltpu.CompilerParams(
-            collective_id=2, has_side_effects=True, vmem_limit_bytes=40 << 20
+            collective_id=2, has_side_effects=True, vmem_limit_bytes=63 << 20
         ),
         name="first",
-    )(tokens, out_grad, gain, cosine, sine, joined, weight_o, weight_d)
+    )(counts, inverse, tokens, out_grad, gain, *projections, *weights)
 
 
 class PlaneSum:
@@ -1044,19 +1139,28 @@
 
 
 def mid_kernel(ctx_ref, tok_ref, gain_ref, g_full, weight_refs, outs, scratch):
-    (res_out, gres_out, e_full, part_out, down_keep, down_come, gate_keep, gate_send, up_keep, up_send,
+    (res_out, gres_out, e_full, near_out, down_keep, down_come, gate_keep, gate_send, up_keep, up_send,
      dctx_out, delta_out, gain_out) = outs
-    (ctx, m_full, dh, hid, dgate, dup, w_o, w_d, w_g, w_u, down_send, *bufs, ss, rs, wsem) = scratch
+    (ctx, m_full, dh, hid, dgate, dup, w_o, w_d, w_g, w_u, down_send, part_out, far_in, own_in, *bufs, ss, rs, wsem) = scratch
     place = Place()
     copies = Copies(ss, rs)
     block, width = tok_ref.shape
     two = 2 * block
     hidden = w_g.shape[1]
-    wo_ref, wd_ref, wg_ref, wu_ref, slice_g, slice_u = weight_refs
-    load_o = pltpu.make_async_copy(wo_ref, w_o, wsem.at[0])
-    load_d = pltpu.make_async_copy(wd_ref, w_d, wsem.at[1])
-    load_o.start()
-    load_d.start()
+    wo_ref, wd_ref, wg_ref, wu_ref, wo_got, wd_got, slice_g, slice_u = weight_refs
+    first_loads = [
+        pltpu.make_async_copy(src, dst, wsem.at[i])
+        for i, (src, dst) in enumerate(((wo_ref, w_o), (wd_ref, w_d)))
+    ]
+    first_loads_odd = [
+        pltpu.make_async_copy(src, dst, wsem.at[i])
+        for i, (src, dst) in enumerate(((wo_got, w_o), (wd_got, w_d)))
+    ]
+
+    def wait_first(i):
+        pl.when(place.c == 0)(first_loads[i].wait)
+        pl.when(place.odd)(first_loads_odd[i].wait)
+
     rows4 = slice_g.shape[0]
     at_slot = pl.ds(place.slot * rows4, rows4)
     loads = [
@@ -1070,12 +1174,12 @@
 
     @pl.when(place.c == 0)
     def _():
-        for copy in loads:
+        for copy in first_loads + loads:
             copy.start()
 
     @pl.when(place.odd)
     def _():
-        for copy in loads_odd:
+        for copy in first_loads_odd + loads_odd:
             copy.start()
 
     ctx[...] = ctx_ref[...].T
@@ -1098,9 +1202,9 @@
         rows = slice(k * two, (k + 1) * two)
         tiles(width, 256, lambda cols: put(cols, dot_nn(ctx[rows, :], w_o[:, cols])))
 
-    load_o.wait()
+    wait_first(0)
     sum_one.run(project)
-    load_d.wait()
+    wait_first(1)
 
     def back_hidden(cols):
         for rows in (slice(0, two), slice(two, 2 * two)):
@@ -1169,6 +1273,12 @@
 
     sum_two.run(back_norm)
     partial_out(1)
+    to_side = [
+        copies.make(part_out.at[pl.ds(3 * block, block)], far_in, place.beside),
+        copies.make(part_out.at[pl.ds(block, block)], own_in, place.beside),
+    ]
+    for copy in to_side:
+        copy.start()
     down_over = copies.make(down_send, down_come, place.over_x)
     outer_blocks(place, True, g_full, hid[...], down_send, down_keep, down_over.start)
     outer_blocks(place, False, m_full, dgate[...], gate_send, gate_keep, lambda: None)
@@ -1198,6 +1308,13 @@
                 prod[hd * HEAD_WIDTH : (hd + 1) * HEAD_WIDTH], axis=0, keepdims=True
             )
 
+    for copy in to_side:
+        copy.wait()
+    for k in range(CHUNKS):
+        at = pl.ds(k * chunk, chunk)
+        near = pl.ds(two + k * chunk, chunk)
+        near_out[at, :] = (part_out[near, :].astype(floats) + far_in[at, :].astype(floats)).astype(halves)
+        res_out[at, :] += part_out[at, :].astype(floats) + own_in[at, :].astype(floats)
     gather_two.wait_here()
     back_context(0)
     gather_two.wait_there()
@@ -1217,7 +1334,7 @@
         shape((block, width), floats),
         shape((block, width), floats),
         shape((group, width), halves),
-        shape((group, width), halves),
+        shape((block, width), halves),
         *[shape((2, width // 4, hidden), halves)] * 6,
         shape((q_cols, group), halves),
         shape((q_cols // HEAD_WIDTH, group), floats),
@@ -1229,6 +1346,8 @@
         *[pltpu.VMEM((group, hidden), halves)] * 4,
         *[pltpu.VMEM(weight.shape, halves) for weight in weights[:4]],
         pltpu.VMEM((2, width // 4, hidden), halves),
+        pltpu.VMEM((group, width), halves),
+        *[pltpu.VMEM((block, width), halves)] * 2,
         *[pltpu.VMEM((block, width), floats)] * 2,
         *[pltpu.VMEM((block, width), halves)] * 6,
         *copy_semaphores(),
@@ -1236,27 +1355,27 @@
     ]
 
     def kernel(*refs):
-        mid_kernel(*refs[:4], refs[4:10], refs[10:23], refs[23:])
+        mid_kernel(*refs[:4], refs[4:12], refs[12:25], refs[25:])
 
     return pl.pallas_call(
         kernel,
         out_shape=out_shape,
-        in_specs=[VM] * 4 + [HB] * 6,
+        in_specs=[VM] * 4 + [HB] * 8,
         out_specs=(VM,) * 13,
         scratch_shapes=scratch,
         compiler_params=pltpu.CompilerParams(
-            collective_id=1, has_side_effects=True, vmem_limit_bytes=62 << 20
+            collective_id=1, has_side_effects=True, vmem_limit_bytes=63 << 20
         ),
         name="middle",
     )(context_t, tokens, gain, grad_full, *weights)
 
 
 def last_kernel(ins, outs, scratch):
-    (dq_ref, dkv_ref, cos_ref, sin_ref, n_ref, joined, tok_ref, gain_ref, gres_ref, e_ref, ctx_ref,
+    (counts, inverse_ref, dq_ref, dkv_ref, n_ref, joined_ref, tok_ref, gain_ref, gres_ref, e_ref, ctx_ref,
      gain_mlp_ref, *mlp) = ins
     (in_grad, gains_out, gate_out, up_out, down_out, q_out, kv_out, o_out) = outs
     (full, ctx, d_lin, acc_a, acc_b, own, x_in, y_in, rel_in, cross_in, cross_out, kept, come,
-     gains, gains_in, *rest) = scratch
+     gains, gains_in, cos_ref, sin_ref, joined, *rest) = scratch
     bufs_mlp = [rest[5 * i : 5 * i + 5] for i in range(3)]
     rest = rest[15:]
     bufs_attn = [rest[8 * i : 8 * i + 8] for i in range(3)]
@@ -1272,6 +1391,8 @@
 
     load_e = pltpu.make_async_copy(e_ref, full, lsem.at[0])
     load_e.start()
+    load_joined = pltpu.make_async_copy(joined_ref, joined, lsem.at[11])
+    load_joined.start()
     order = (4, 12, 0, 8)
     own_loads = [
         pltpu.make_async_copy(dkv_ref.at[at], own.at[i], lsem.at[1 + i]) for i, at in enumerate(order)
@@ -1306,10 +1427,13 @@
     back_y = [copies.make(dkv_ref.at[at + 2], y_in.at[i], place.over_y) for i, at in enumerate(order)]
     back_sum = [copies.make(y_in.at[i], y_in.at[i], place.over_y) for i in range(4)]
     crossing = [copies.make(cross_out.at[i], cross_in.at[i], place.cross) for i in range(2)]
-    for i in range(4):
+    def start_back(i):
         pl.when(place.turn)(back_rel[i].start)
         pl.when(place.x == 1)(back_x[i].start)
         pl.when(place.turn)(back_y[i].start)
+
+    start_back(0)
+    start_back(1)
 
     def corner_sum(i):
         @pl.when(place.corner)
@@ -1353,7 +1477,10 @@
                 copy.start()
         if i == 1:
             corner_sum(0)
+            start_back(2)
+            start_back(3)
     ctx[...] = ctx_ref[...].T
+    rope_tables(counts, inverse_ref, cos_ref, sin_ref)
 
     attn_sums = []
     for i, x_first in enumerate((False, True, False)):
@@ -1421,6 +1548,7 @@
         d_lin[q_cols + kv_cols :, lanes] = total[kv_cols:].astype(halves)
 
     group_sum = GroupSum(copies, sum_bufs, place)
+    load_joined.wait()
 
     def back_norm(k, put):
         rows = slice(k * two, (k + 1) * two)
@@ -1471,7 +1599,7 @@
         copy.wait_send()
 
 
-def last_part(d_query_t, d_kv, cosine, sine, normed, joined, tokens, gain, gres, e_full, context_t, gain_mlp, mlp):
+def last_part(counts, inverse, d_query_t, d_kv, normed, joined, tokens, gain, gres, e_full, context_t, gain_mlp, mlp):
     block, width = tokens.shape
     group = 4 * block
     q_cols, kv_all = d_query_t.shape[0], d_kv.shape[1]
@@ -1498,6 +1626,8 @@
         *[pltpu.VMEM((2,) + piece, halves)] * 2,
         *[pltpu.VMEM((2, width // 4, hidden), halves)] * 2,
         *[pltpu.VMEM((5, 2, width), floats)] * 2,
+        *[pltpu.VMEM((HEAD_WIDTH // 2, group), floats)] * 2,
+        pltpu.VMEM(joined.shape, halves),
     ]
     for _ in range(3):
         scratch += plane_buffers(width // 4, hidden)
@@ -1507,7 +1637,7 @@
         *[pltpu.VMEM((block, width), floats)] * 2,
         *[pltpu.VMEM((block, width), halves)] * 6,
         *copy_semaphores(),
-        pltpu.SemaphoreType.DMA((11,)),
+        pltpu.SemaphoreType.DMA((12,)),
     ]
 
     def kernel(*refs):
@@ -1516,14 +1646,60 @@
     return pl.pallas_call(
         kernel,
         out_shape=out_shape,
-        in_specs=[VM, HB, VM, VM, HB, VM, VM, VM, VM, HB, VM, VM] + [HB] * 6,
+        in_specs=[SM, VM, VM, HM, HM, HM, VM, VM, VM, HM, VM, VM] + [HM] * 6,
         out_specs=(VM,) * 8,
         scratch_shapes=scratch,
         compiler_params=pltpu.CompilerParams(
             collective_id=3, has_side_effects=True, vmem_limit_bytes=63 << 20
         ),
         name="last",
-    )(d_query_t, d_kv, cosine, sine, normed, joined, tokens, gain, gres, e_full, context_t, gain_mlp, *mlp)
+    )(counts, inverse, d_query_t, d_kv, normed, joined, tokens, gain, gres, e_full, context_t, gain_mlp, *mlp)
+
+
+def finish_kernel(*refs):
+    base, near, kv_sum, *ready = refs[:9]
+    output, k_out, v_out, *outs = refs[9:18]
+    out_buf, k_buf, v_buf, sem = refs[18:]
+    copies = [pltpu.make_async_copy(src, dst, sem.at[i]) for i, (src, dst) in enumerate(zip(ready, outs))]
+    for copy in copies:
+        copy.start()
+    out_buf[...] = (base[...] + near[...].astype(floats)).astype(halves)
+    kv_cols = k_buf.shape[1]
+    k_buf[...] = kv_sum[:, :kv_cols]
+    v_buf[...] = kv_sum[:, kv_cols:]
+    more = [
+        pltpu.make_async_copy(src, dst, sem.at[len(copies) + i])
+        for i, (src, dst) in enumerate(((out_buf, output), (k_buf, k_out), (v_buf, v_out)))
+    ]
+    for copy in more:
+        copy.start()
+    for copy in copies + more:
+        copy.wait()
+
+
+def finish(base, near, kv_sum, *ready):
+    shape = jax.ShapeDtypeStruct
+    rows, cols = kv_sum.shape
+    small = (rows, cols // 2)
+    return pl.pallas_call(
+        finish_kernel,
+        out_shape=(
+            shape(base.shape, halves),
+            shape(small, floats),
+            shape(small, floats),
+            *[shape(a.shape, a.dtype) for a in ready],
+        ),
+        in_specs=[VM] * (3 + len(ready)),
+        out_specs=(HM,) * (3 + len(ready)),
+        scratch_shapes=[
+            pltpu.VMEM(base.shape, halves),
+            pltpu.VMEM(small, floats),
+            pltpu.VMEM(small, floats),
+            pltpu.SemaphoreType.DMA((3 + len(ready),)),
+        ],
+        compiler_params=pltpu.CompilerParams(vmem_limit_bytes=63 << 20),
+        name="finish",
+    )(base, near, kv_sum, *ready)
 
 
 def routes(target):
@@ -1556,25 +1732,10 @@
     "relay": routes(lambda y, x, c, z: (1, 0, c, z) if x and y else None),
     "unrelay": routes(lambda y, x, c, z: (1, 1, c, z) if y and not x else None),
 }
-FAR_BASE = 1 << 24
 
 
 def send(block, way):
     return lax.ppermute(block, ("dp", "tp"), ROUTES[way])
-
-
-def scatter_group(here, there):
-    rows = here.shape[0] // 2
-    there_sum = there[:rows] + send(there[rows:].astype(halves), "core").astype(floats)
-    here_sum = here[:rows].astype(floats) + send(here[rows:].astype(halves), "core").astype(floats)
-    return here_sum + send(there_sum.astype(halves), "near").astype(floats)
-
-
-def rope_tables(positions):
-    half_width = HEAD_WIDTH // 2
-    inverse = 1.0 / rope_base ** (jnp.arange(half_width, dtype=floats) * 2.0 / HEAD_WIDTH)
-    angles = inverse[:, None] * positions.astype(floats)[None, :]
-    return jnp.cos(angles), jnp.sin(angles)
 
 
 def local_regrouped(
@@ -1592,112 +1753,49 @@
     down_weight,
 ):
     block = tokens.shape[0]
-    row_len = 4 * block
-    dp, z = lax.axis_index("dp"), lax.axis_index("tp")
-    y, x, c = dp // 4, dp // 2 % 2, dp % 2
-    j = dp // 2
-    odd = c == 1
-    pair, side = z // 2, z % 2
-    q_cols, kv_cols = query_weight.shape[1], key_matrix.shape[1]
-    heads = q_cols // HEAD_WIDTH
-    group_width = q_cols // kv_cols
-    ff_cols = gate_weight.shape[1]
-    gain_attn, gain_mlp = attn_gain.astype(floats), mlp_gain.astype(floats)
-
-    def base(j_of, core, pair_of, side_of):
-        return (2 * j_of + core) * row_len + (2 * pair_of + side_of) * block
-
-    bases = [
-        base(j, c, pair, side),
-        base(j, 1 - c, pair, side),
-        base(j, c, pair, 1 - side),
-        base(j, 1 - c, pair, 1 - side),
-    ]
-    counts = [jnp.sum((segment_ids < item).astype(jnp.int32)) for item in range(1, 4)]
-    segs = jnp.concatenate([lax.dynamic_slice_in_dim(segment_ids, b, block) for b in bases])
-    index = jnp.concatenate([b + jnp.arange(block, dtype=jnp.int32) for b in bases])
-    start = jnp.zeros_like(segs)
-    for item in range(1, 4):
-        start = jnp.where(segs == item, counts[item - 1], start)
-    cosine, sine = rope_tables(index - start)
-    index_row, start_row = index[None, :], start[None, :]
-    starts4 = start.reshape(4, block)
-
-    tokens32 = tokens.astype(floats)
-    joined = jnp.concatenate([query_weight, key_matrix, value_matrix], axis=1)
-    q_t, pieces, normed_full, grad_full, joined, weight_o, weight_d = first_part(
-        tokens, out_grad, gain_attn[None, :], cosine, sine, joined, output_weight, down_weight,
-        q_cols, kv_cols,
-    )
-    slot = 2 * y + x
-    rows = gate_weight.shape[0] // 4
-    own_slices = [
-        lax.dynamic_slice_in_dim(weight, slot * rows, rows) for weight in (gate_weight, up_weight)
-    ]
-    own_slices, pieces = lax.optimization_barrier((own_slices, pieces))
-    slices = [send(part, "odd_far") for part in own_slices]
-
-    piece_bases = []
-    for n in range(2):
-        side_n = side if n == 0 else 1 - side
-        for cross in range(2):
-            cores = (c, 1 - c) if cross == 0 else (1 - c, c)
-            pair_of = pair if cross == 0 else 1 - pair
-            for j_of, present in (
-                (j, True),
-                (j - 1, x == 1),
-                (j - 2, y == 1),
-                (j - 1, (y == 1) & (x == 0)),
-            ):
-                for core in cores:
-                    piece_bases.append(
-                        jnp.where(present, base(j_of, core, pair_of, side_n), FAR_BASE)
-                    )
-    total_blocks = len(piece_bases)
-
-    def padded(values):
-        values = jnp.stack(values).astype(jnp.int32)
-        return jnp.pad(values, (0, total_blocks - values.shape[0]))
-
-    sc = jnp.stack(
-        [
-            padded(piece_bases),
-            padded(bases),
-            jnp.pad(starts4[:, 0], (0, total_blocks - 4)),
-            jnp.pad(starts4[:, -1], (0, total_blocks - 4)),
-        ]
-    )
-    context_t, log_total = attend_forward(sc, q_t, index_row, start_row, pieces)
-
+    dp = lax.axis_index("dp")
+    half_width = HEAD_WIDTH // 2
+    gain_attn, gain_mlp = attn_gain.astype(floats)[None, :], mlp_gain.astype(floats)[None, :]
+    counts = jnp.sum(
+        (segment_ids[None, :] < jnp.arange(1, 4, dtype=jnp.int32)[:, None]).astype(jnp.int32), axis=1
+    )
+    inverse = 1.0 / rope_base ** (jnp.arange(half_width, dtype=floats) * 2.0 / HEAD_WIDTH)
+    inverse = inverse[:, None]
+    q_t, pieces, normed_full, grad_full, joined, weight_o, weight_d, slice_g, slice_u = first_part(
+        counts, inverse, tokens, out_grad, gain_attn,
+        (query_weight, key_matrix.T, value_matrix.T),
+        (output_weight, down_weight, gate_weight, up_weight),
+    )
+    slices = [send(part, "odd_far") for part in (slice_g, slice_u)]
+    context_t, log_total = attend_forward(counts, q_t, pieces)
     (
-        residual, grad_residual, attn_grad_full, part_out, down_keep, down_come, gate_keep, gate_send,
-        up_keep, up_send,
-        d_context_t, delta, mlp_gain_part,
+        out_base, grad_residual, attn_grad_full, out_near, down_keep, down_come, gate_keep, gate_send,
+        up_keep, up_send, d_context_t, delta, mlp_gain_part,
     ) = middle(
-        context_t, tokens, gain_mlp[None, :], grad_full,
-        (weight_o, weight_d, gate_weight, up_weight, *slices),
-    )
-    output = residual + scatter_group(part_out[: 2 * block], part_out[2 * block :])
+        context_t, tokens, gain_mlp, grad_full,
+        (output_weight, down_weight, gate_weight, up_weight, weight_o, weight_d, *slices),
+    )
     gate_come = send(gate_send, "y")
     up_come = send(up_send, "x")
-
-    d_query_t, d_pieces = attend_backward(
-        sc, q_t, d_context_t, log_total, delta, index_row, start_row, pieces
-    )
+    out_near = send(out_near, "near")
+    d_query_t, d_pieces = attend_backward(counts, q_t, d_context_t, log_total, delta, pieces)
     input_grad, gains, gate_sum, up_sum, down_sum, query_sum, kv_sum, output_sum = last_part(
-        d_query_t, d_pieces, cosine, sine, normed_full, joined, tokens, gain_attn[None, :],
+        counts, inverse, d_query_t, d_pieces, normed_full, joined, tokens, gain_attn,
         grad_residual, attn_grad_full, context_t, mlp_gain_part,
         (down_keep, down_come, gate_keep, gate_come, up_keep, up_come),
     )
     per = gains.shape[1] // 8
     gains = lax.dynamic_slice_in_dim(gains, dp * per, per, axis=1)
+    output, key_sum, value_sum, input_grad, query_sum, output_sum, gate_sum, up_sum, down_sum = finish(
+        out_base, out_near, kv_sum, input_grad, query_sum, output_sum, gate_sum, up_sum, down_sum
+    )
     return (
-        output.astype(halves),
+        output,
         input_grad,
         gains[1],
         query_sum,
-        kv_sum[:, :kv_cols],
-        kv_sum[:, kv_cols:],
+        key_sum,
+        value_sum,
         output_sum.T,
         gains[0],
         gate_sum,

time: 532 us -> 487 us (0.915)
  local copies, waits for them, and re-layouts: 30.4 us -> 5.04 us
  other arithmetic: 12 us -> 2.15 us
  waiting for transfers between devices: 6.54 us -> 0.01 us
  Pallas kernels: 463 us -> 457 us
    unnamed x56 -> x6, local copies, waits for them, and re-layouts: 19.6 us -> 1.75 us
    convert_element_type x3 -> x0, other arithmetic: 7.26 us -> none  [the longest x1 3.22 us: local_regrouped(): output.astype(halves)]
    ppermute x7 -> x5, waiting for transfers between devices: 6.54 us -> 0.01 us  [send(): return lax.ppermute(block, ('dp', 'tp'), ROUTES[way])]
    pallas_call x5 -> x6, Pallas kernels: 463 us -> 457 us  [the longest x1 164 us: last_part(): pl.pallas_call(kernel, out_shape=out_shape, in_specs=[SM, VM, VM, HM, HM,...]
    ppermute x7 -> x5, starting transfers between devices: 12.9 us -> 12.9 us  [send(): return lax.ppermute(block, ('dp', 'tp'), ROUTES[way])]
  transfers between devices with their start and end apart: 7 -> 5, of which waited for: 1 -> 0; matrix products, arithmetic and copies ran while one was open for 2% -> 0% of each run, Pallas kernels for 47% -> 52%
where the time goes in v6:
time: 487 us; the launch traced here: 479 us
  Pallas kernels  457 us (94%)
  starting transfers between devices  12.9 us (3%)
  local copies, waits for them, and re-layouts  5.04 us (1%)
    pallas_call x1, Pallas kernels, last_part(): pl.pallas_call(kernel, out_shape=out_shape, in_specs=[SM, VM, VM, HM, HM,...  164 us
    pallas_call x1, Pallas kernels, middle(): pl.pallas_call(kernel, out_shape=out_shape, in_specs=[VM] * 4 + [HB] * 8,...  111 us
    pallas_call x1, Pallas kernels, first_part(): pl.pallas_call(first_kernel, out_shape=out_shape, in_specs=[SM] + [VM] *...  93 us
    pallas_call x1, Pallas kernels, attend_backward(): pl.pallas_call(functools.partial(bwd_kernel, n, width), out_shape=(jax.Sh...  51.9 us
    pallas_call x1, Pallas kernels, attend_forward(): pl.pallas_call(functools.partial(fwd_kernel, n, width), out_shape=(jax.Sh...  32 us
    ppermute x5, starting transfers between devices, send(): return lax.ppermute(block, ('dp', 'tp'), ROUTES[way])  12.9 us
  transfers between devices with their start and end apart: 5, of which 0 were waited for; matrix products, arithmetic and copies ran while one was open for 0% of the time, Pallas kernels for 52%

profile of v6, /device:TPU:3, one launch (start us, length us, event | category | flops | bytes accessed | tf_op | source)
XLA Modules:
  0.0 478.7 jit_solution(2469985726455896792)
XLA Ops:
  0.7 0.6 negate_power_fusion.inverse_ref.refs_1_
  1.3 1.3 reshape.40.gain_ref.refs_7_
  2.6 1.5 convert_reduce_fusion.counts.refs_0_
  4.1 0.0 copy-start.2
  4.1 93.0 %first.1 = (bf16[384,1024]{1,0:T(8,128)(2,1)}, bf16[16,384,512]{2,1,0:T(8,128)(2,1)}, bf16[1024,1536]{1,0:T(8,128)(2,1)}, bf16[1024,1536]{1,0:T(8,128)(2,1)}, bf...) custom-call(s32[3]{0:T(128)} %convert_reduce_fusion.counts.refs_0_, ...), custom_call_target="tpu_custom_call" | custom-call | tf_op jit(solution)/shard_map/first/pallas_call | solution.py:1049
  97.1 1.9 collective-permute-start
  99.1 4.3 collective-permute-start.1
  103.3 0.0 copy-done.2
  103.3 0.6 reshape.41.refs_2_
  103.9 32.0 %attend_forward.1 = (bf16[384,1024]{1,0:T(8,128)(2,1)}, f32[4,1024]{1,0:T(4,128)}) custom-call(s32[3]{0:T(128)} %convert_reduce_fusion.counts.refs_0_, bf16[384,1024]{1,0:T(8,128)(2,1)} %get-tuple-element.54.q_ref, bf16[16,384,512]{2,1,0:T(8,128)(2,1)} %get-tuple-element.55.pieces), custom_call_target="tpu_custom_call" | custom-call | tf_op jit(solution)/shard_map/attend_forward/pallas_call | solution.py:175
  136.0 0.0 collective-permute-done.refs_10_
  136.0 0.0 copy-start
  136.0 0.0 collective-permute-done.1.refs_11_
  136.0 0.9 copy-done
  136.8 111.0 %middle.1 = (f32[256,1536]{1,0:T(8,128)}, f32[256,1536]{1,0:T(8,128)}, bf16[1024,1536]{1,0:T(8,128)(2,1)}, bf16[256,1536]{1,0:T(8,128)(2,1)}, bf16[2,384,1024]{2...) custom-call(bf16[384,1024]{1,0:T(8,128)(2,1)} %get-tuple-element.56., ...), custom_call_target="tpu_custom_call" | custom-call | tf_op jit(solution)/shard_map/middle/pallas_call | solution.py:1360
  247.9 4.2 collective-permute-start.3
  252.1 0.0 collective-permute-start.4
  252.1 2.5 collective-permute-start.2
  254.6 51.9 %attend_backward.1 = (f32[384,1024]{1,0:T(8,128)}, bf16[16,384,512]{2,1,0:T(8,128)(2,1)}) custom-call(s32[3]{0:T(128)} %convert_reduce_fusion.counts.refs_0_, bf16[384,1024]{1,0:T(8,128)(2,1)} %get-tuple-element.54.q_ref, bf16[384,1024]{1,0:T(8,128)(2,1)} %get-tuple-element.64.do_ref, f32[4,1024]{1,0:T(4,128)} %get-tuple-element.65.log_ref, ...), custom_call_target="tpu_custom_call" | custom-call | tf_op jit(solution)/shard_map/attend_backward/pallas_call | solution.py:286
  306.5 0.0 collective-permute-done.3.refs_15_
  306.5 0.0 collective-permute-done.4.refs_17_
  306.5 163.9 %last.1 = (f32[256,1536]{1,0:T(8,128)}, f32[2,1536]{1,0:T(2,128)}, f32[192,1024]{1,0:T(8,128)}, f32[192,1024]{1,0:T(8,128)}, f32[192,1024]{1,0:T(8,128)}, /*inde...) custom-call(s32[3]{0:T(128)} %convert_reduce_fusion.counts.refs_0_, ...), custom_call_target="tpu_custom_call" | custom-call | tf_op jit(solution)/shard_map/last/pallas_call | solution.py:1646
  470.4 1.4 constant_dynamic-slice_fusion
  471.8 0.0 collective-permute-done.2.refs_1_
  471.8 0.0 copy-start.1
  471.8 0.9 copy-done.1
  472.7 5.6 %finish.1 = (bf16[256,1536]{1,0:T(8,128)(2,1)}, f32[192,192]{1,0:T(8,128)}, f32[192,192]{1,0:T(8,128)}, f32[256,1536]{1,0:T(8,128)}, f32[192,384]{1,0:T(8,128)},...) custom-call(f32[256,1536]{1,0:T(8,128)} %get-tuple-element.62.refs_0_, ...), custom_call_target="tpu_custom_call" | custom-call | tf_op jit(solution)/shard_map/finish/pallas_call | solution.py:1684
  (1 shorter events, 0.0 us)
Async XLA Ops:
  4.1 99.3 %copy-start.2 = (bf16[1536]{0:T(1024)(128)(2,1)S(1)}, bf16[1536]{0:T(1024)(128)(2,1)}, u32[]{:S(2)}) copy-start(bf16[1536]{0:T(1024)(128)(2,1)} %param.20) | copy-start | bytes 9220
  97.1 38.8 %collective-permute-start = (bf16[384,1024]{1,0:T(8,128)(2,1)}, bf16[384,1024]{1,0:T(8,128)(2,1)S(1)}, u32[]{:S(2)}, u32[]{:S(2)}) collective-permute-start(bf16[384,1024]{1,0:T(8,128)(2,1)} %get-tuple-element.60), channel_id=1, source_target_pairs={{4,6},{5,7},{6,4},{7,5},{12,14},{13,15},{14,12},{15,13},{20,22},{2... | collective-permute-start | bytes 2359304 | tf_op jit(solution)/shard_map/ppermute | solution.py:1738
  99.1 36.9 %collective-permute-start.1 = (bf16[384,1024]{1,0:T(8,128)(2,1)}, bf16[384,1024]{1,0:T(8,128)(2,1)}, u32[]{:S(2)}, u32[]{:S(2)}) collective-permute-start(bf16[384,1024]{1,0:T(8,128)(2,1)} %get-tuple-element.61), channel_id=1, source_target_pairs={{4,6},{5,7},{6,4},{7,5},{12,14},{13,15},{14,12},{15,13},{20,22},{2... | collective-permute-start | bytes 2359304 | tf_op jit(solution)/shard_map/ppermute | solution.py:1738
  136.0 0.9 copy-start
  247.9 58.6 %collective-permute-start.3 = (bf16[2,384,1024]{2,1,0:T(8,128)(2,1)}, bf16[2,384,1024]{2,1,0:T(8,128)(2,1)}, u32[]{:S(2)}, u32[]{:S(2)}) collective-permute-start(bf16[2,384,1024]{2,1,0:T(8,128)(2,1)} %get-tuple-element.77), channel_id=1, source_target_pairs={{0,16},{1,17},{2,18},{3,19},{4,20},{5,21},{6,22},{7,23},{8,24},{9,... | collective-permute-start | bytes 4718600 | tf_op jit(solution)/shard_map/ppermute | solution.py:1738
  252.1 54.4 %collective-permute-start.4 = (bf16[2,384,1024]{2,1,0:T(8,128)(2,1)}, bf16[2,384,1024]{2,1,0:T(8,128)(2,1)}, u32[]{:S(2)}, u32[]{:S(2)}) collective-permute-start(bf16[2,384,1024]{2,1,0:T(8,128)(2,1)} %get-tuple-element.79), channel_id=1, source_target_pairs={{0,8},{1,9},{2,10},{3,11},{4,12},{5,13},{6,14},{7,15},{8,0},{9,1},... | collective-permute-start | bytes 4718600 | tf_op jit(solution)/shard_map/ppermute | solution.py:1738
  252.1 219.7 %collective-permute-start.2 = (bf16[256,1536]{1,0:T(8,128)(2,1)}, bf16[256,1536]{1,0:T(8,128)(2,1)S(1)}, u32[]{:S(2)}, u32[]{:S(2)}) collective-permute-start(bf16[256,1536]{1,0:T(8,128)(2,1)} %get-tuple-element.63), channel_id=1, source_target_pairs={{0,1},{1,0},{2,3},{3,2},{4,5},{5,4},{6,7},{7,6},{8,9},{9,8},{10,11... | collective-permute-start | bytes 2359304 | tf_op jit(solution)/shard_map/ppermute | solution.py:1738
  471.8 0.9 copy-start.1

commit v7 on v6

--- a/solution.py
+++ b/solution.py
@@ -646,34 +646,49 @@
     def __init__(self, copies, bufs, place):
         self.copies, self.bufs, self.place = copies, bufs, place
 
-    def run(self, product):
-        part_near, part_own, out_far, out_beside, out_near, in_near, in_own, in_sum = self.bufs
-
-        def put_there(cols, value):
-            rows = value.shape[0] // 2
-            part_near[:, cols] = value[:rows]
-            out_far[:, cols] = value[rows:].astype(halves)
-
-        def put_here(cols, value):
-            rows = value.shape[0] // 2
-            part_own[:, cols] = value[:rows]
-            out_beside[:, cols] = value[rows:].astype(halves)
-
-        product(1, put_there)
-        self.far = self.copies.make(out_far, in_near, self.place.beside)
-        self.far.start()
-        product(0, put_here)
+        self.far, self.sums = [], []
+
+    def put_there(self, at, cols, value):
+        part_near, _, out_far = self.bufs[:3]
+        rows = value.shape[0] // 2
+        part_near[at, cols] = value[:rows]
+        out_far[at, cols] = value[rows:].astype(halves)
+
+    def put_here(self, cols, value):
+        _, part_own, _, out_beside = self.bufs[:4]
+        rows = value.shape[0] // 2
+        part_own[:, cols] = value[:rows]
+        out_beside[:, cols] = value[rows:].astype(halves)
+
+    def send_far(self, at):
+        _, _, out_far, _, _, in_near = self.bufs[:6]
+        copy = self.copies.make(out_far.at[at], in_near.at[at], self.place.beside)
+        copy.start()
+        self.far.append(copy)
+
+    def send_beside(self):
+        _, _, _, out_beside, _, _, in_own = self.bufs[:7]
         self.side = self.copies.make(out_beside, in_own, self.place.beside)
         self.side.start()
-        self.far.wait_recv()
+
+    def send_near(self, count):
+        part_near, _, _, _, out_near, in_near, _, in_sum = self.bufs
+        self.far[-1].wait_recv()
         rows = part_near.shape[0] // CHUNKS
-        self.sums = []
-        for k in range(CHUNKS):
-            at = pl.ds(k * rows, rows)
+        for _ in range(count):
+            at = pl.ds(len(self.sums) * rows, rows)
             out_near[at, :] = (part_near[at, :] + in_near[at, :].astype(floats)).astype(halves)
             copy = self.copies.make(out_near.at[at], in_sum.at[at], self.place.near)
             copy.start()
             self.sums.append(copy)
+
+    def run(self, product):
+        everything = pl.ds(0, self.bufs[0].shape[0])
+        product(1, lambda cols, value: self.put_there(everything, cols, value))
+        self.send_far(everything)
+        product(0, self.put_here)
+        self.send_beside()
+        self.send_near(CHUNKS)
 
     def take(self, k):
         part_near, part_own, out_far, out_beside, out_near, in_near, in_own, in_sum = self.bufs
@@ -685,7 +700,7 @@
         return part_own[at, :] + in_own[at, :].astype(floats) + in_sum[at, :].astype(floats)
 
     def finish(self):
-        for copy in (self.far, self.side, *self.sums):
+        for copy in (*self.far, self.side, *self.sums):
             copy.wait_send()
 
 
@@ -709,16 +724,15 @@
             if i == 1:
                 copy.wait_recv()
 
-    def wait_there(self):
+    def wait_there(self, part=0, parts=1):
+        near = [copy for i, copy in self.sent if i == 0]
+        count = CHUNKS // parts
         relays = []
-        k = 0
-        for i, copy in self.sent:
-            if i == 0:
-                copy.wait_recv()
-                relay = self.copies.make(self.slot(2, k), self.slot(3, k), self.place.beside)
-                relay.start()
-                relays.append(relay)
-                k += 1
+        for k in range(part * count, (part + 1) * count):
+            near[k].wait_recv()
+            relay = self.copies.make(self.slot(2, k), self.slot(3, k), self.place.beside)
+            relay.start()
+            relays.append(relay)
         for relay in relays:
             relay.wait_recv()
         self.sent += [(2, relay) for relay in relays]
@@ -1093,9 +1107,10 @@
         self.two.start()
         keep[...] = (kept[at].astype(floats) + come[at].astype(floats)).astype(halves)
 
-    def go_home(self):
+    def go_home(self, exchanged=True):
         half, keep, come_two, home_one, home_two = self.bufs
-        self.two.wait()
+        if exchanged:
+            self.two.wait()
         half[...] = (keep[...].astype(floats) + come_two[...].astype(floats)).astype(halves)
         self.to_home.start()
         pl.when(self.place.odd)(self.to_far.start)
@@ -1139,9 +1154,9 @@
 
 
 def mid_kernel(ctx_ref, tok_ref, gain_ref, g_full, weight_refs, outs, scratch):
-    (res_out, gres_out, e_full, near_out, down_keep, down_come, gate_keep, gate_send, up_keep, up_send,
+    (res_out, gres_out, e_full, near_out, down_half, down_mine, gate_keep, gate_send, up_keep, up_send,
      dctx_out, delta_out, gain_out) = outs
-    (ctx, m_full, dh, hid, dgate, dup, w_o, w_d, w_g, w_u, down_send, part_out, far_in, own_in, *bufs, ss, rs, wsem) = scratch
+    (ctx, m_full, dh, hid, dgate, dup, w_o, w_d, w_g, w_u, down_send, down_keep, down_come, part_out, far_in, own_in, *bufs, ss, rs, wsem) = scratch
     place = Place()
     copies = Copies(ss, rs)
     block, width = tok_ref.shape
@@ -1211,8 +1226,6 @@
             dh[rows, cols] = dot_nt(g_full[rows, :], w_d[cols, :]).astype(halves)
 
     tiles(hidden, 256, back_hidden)
-    for fetch in fetches:
-        fetch.relay()
     chunk = block // CHUNKS
     for k in range(CHUNKS):
         at = pl.ds(k * chunk, chunk)
@@ -1221,28 +1234,48 @@
         root = lax.rsqrt(jnp.mean(res * res, axis=-1, keepdims=True) + eps_norm)
         m_full[at, :] = (res * root * gain_ref[...]).astype(halves)
         gather_one.put(k)
+        if k == 1:
+            for fetch in fetches:
+                fetch.relay()
     sum_one.finish()
 
-    def activate(k):
-        rows = slice(k * two, (k + 1) * two)
-
+    def there(h):
+        rows = block // 2
+        return [slice(two + h * rows, two + (h + 1) * rows), slice(3 * block + h * rows, 3 * block + (h + 1) * rows)]
+
+    def read(ref, parts):
+        values = [ref[rows, :] for rows in parts]
+        return values[0] if len(values) == 1 else jnp.concatenate(values, axis=0)
+
+    def write(ref, parts, cols, value):
+        rows = value.shape[0] // len(parts)
+        for i, part in enumerate(parts):
+            ref[part, cols] = value[i * rows : (i + 1) * rows]
+
+    def activate(parts):
         def one(cols):
-            gate_pre = dot_nn(m_full[rows, :], w_g[:, cols])
-            up_pre = dot_nn(m_full[rows, :], w_u[:, cols])
-            back = dh[rows, cols].astype(floats)
+            left = read(m_full, parts)
+            gate_pre = dot_nn(left, w_g[:, cols])
+            up_pre = dot_nn(left, w_u[:, cols])
+            back = [dh[rows, cols] for rows in parts]
+            back = (back[0] if len(back) == 1 else jnp.concatenate(back, axis=0)).astype(floats)
             sigma = 1.0 / (1.0 + jnp.exp(-gate_pre))
             silu = gate_pre * sigma
-            hid[rows, cols] = (silu * up_pre).astype(halves)
-            dgate[rows, cols] = (back * up_pre * (sigma + silu * (1.0 - sigma))).astype(halves)
-            dup[rows, cols] = (back * silu).astype(halves)
+            write(hid, parts, cols, (silu * up_pre).astype(halves))
+            write(dgate, parts, cols, (back * up_pre * (sigma + silu * (1.0 - sigma))).astype(halves))
+            write(dup, parts, cols, (back * silu).astype(halves))
 
         tiles(hidden, 256, one)
 
-    def partial_out(k):
-        rows = slice(k * two, (k + 1) * two)
-
+    def partial_out(parts):
         def one(cols):
-            part_out[rows, cols] = dot_nn(hid[rows, :], w_d[:, cols]).astype(halves)
+            write(part_out, parts, cols, dot_nn(read(hid, parts), w_d[:, cols]).astype(halves))
+
+        tiles(width, 256, one)
+
+    def back_norm(parts, put):
+        def one(cols):
+            put(cols, dot_nt(read(dgate, parts), w_g[cols, :]) + dot_nt(read(dup, parts), w_u[cols, :]))
 
         tiles(width, 256, one)
 
@@ -1254,25 +1287,21 @@
         for copy in loads:
             copy.wait()
 
+    here = [slice(0, two)]
     gather_one.wait_here()
-    activate(0)
-    partial_out(0)
+    activate(here)
+    partial_out(here)
+    whole = [slice(two, 2 * two)]
     gather_one.wait_there()
-    activate(1)
+    at = pl.ds(0, block)
+    activate(whole)
+    back_norm(whole, lambda cols, value: sum_two.put_there(at, cols, value))
+    sum_two.send_far(at)
     gather_one.finish()
-
-    def back_norm(k, put):
-        rows = slice(k * two, (k + 1) * two)
-        tiles(
-            width,
-            256,
-            lambda cols: put(
-                cols, dot_nt(dgate[rows, :], w_g[cols, :]) + dot_nt(dup[rows, :], w_u[cols, :])
-            ),
-        )
-
-    sum_two.run(back_norm)
-    partial_out(1)
+    back_norm(here, sum_two.put_here)
+    sum_two.send_beside()
+    sum_two.send_near(CHUNKS)
+    partial_out(whole)
     to_side = [
         copies.make(part_out.at[pl.ds(3 * block, block)], far_in, place.beside),
         copies.make(part_out.at[pl.ds(block, block)], own_in, place.beside),
@@ -1298,15 +1327,17 @@
     sum_two.finish()
     outer_blocks(place, True, m_full, dup[...], up_send, up_keep, lambda: None)
 
-    def back_context(k):
-        lanes = slice(k * two, (k + 1) * two)
-        grad = dot_nt(w_o[...], e_full[lanes, :]).astype(halves)
-        dctx_out[:, lanes] = grad
-        prod = grad.astype(floats) * ctx_ref[:, lanes].astype(floats)
-        for hd in range(delta_out.shape[0]):
-            delta_out[hd : hd + 1, lanes] = VSCALE * jnp.sum(
-                prod[hd * HEAD_WIDTH : (hd + 1) * HEAD_WIDTH], axis=0, keepdims=True
-            )
+    def back_context(parts):
+        grad = dot_nt(w_o[...], read(e_full, parts)).astype(halves)
+        rows = grad.shape[1] // len(parts)
+        for i, part in enumerate(parts):
+            piece = grad[:, i * rows : (i + 1) * rows]
+            dctx_out[:, part] = piece
+            prod = piece.astype(floats) * ctx_ref[:, part].astype(floats)
+            for hd in range(delta_out.shape[0]):
+                delta_out[hd : hd + 1, part] = VSCALE * jnp.sum(
+                    prod[hd * HEAD_WIDTH : (hd + 1) * HEAD_WIDTH], axis=0, keepdims=True
+                )
 
     for copy in to_side:
         copy.wait()
@@ -1316,13 +1347,18 @@
         near_out[at, :] = (part_out[near, :].astype(floats) + far_in[at, :].astype(floats)).astype(halves)
         res_out[at, :] += part_out[at, :].astype(floats) + own_in[at, :].astype(floats)
     gather_two.wait_here()
-    back_context(0)
-    gather_two.wait_there()
-    back_context(1)
+    back_context(here)
+    gather_two.wait_there(0, 2)
+    back_context(there(0))
+    down_over.wait()
+    at = place.y
+    down_half[...] = (down_keep[1 - at].astype(floats) + down_come[1 - at].astype(floats)).astype(halves)
+    down_mine[...] = (down_keep[at].astype(floats) + down_come[at].astype(floats)).astype(halves)
+    gather_two.wait_there(1, 2)
+    back_context(there(1))
     gather_two.finish()
     for fetch in fetches:
         fetch.drain()
-    down_over.wait()
 
 
 def middle(context_t, tokens, gain, grad_full, weights):
@@ -1335,7 +1371,8 @@
         shape((block, width), floats),
         shape((group, width), halves),
         shape((block, width), halves),
-        *[shape((2, width // 4, hidden), halves)] * 6,
+        *[shape((width // 4, hidden), halves)] * 2,
+        *[shape((2, width // 4, hidden), halves)] * 4,
         shape((q_cols, group), halves),
         shape((q_cols // HEAD_WIDTH, group), floats),
         shape((1, width), floats),
@@ -1345,7 +1382,7 @@
         pltpu.VMEM((group, width), halves),
         *[pltpu.VMEM((group, hidden), halves)] * 4,
         *[pltpu.VMEM(weight.shape, halves) for weight in weights[:4]],
-        pltpu.VMEM((2, width // 4, hidden), halves),
+        *[pltpu.VMEM((2, width // 4, hidden), halves)] * 3,
         pltpu.VMEM((group, width), halves),
         *[pltpu.VMEM((block, width), halves)] * 2,
         *[pltpu.VMEM((block, width), floats)] * 2,
@@ -1415,8 +1452,11 @@
             pltpu.make_async_copy(mlp[2 * i + 1], come, lsem.at[10]),
         ]
 
-    loads = load_mlp(0)
-    for copy in loads:
+    down_loads = [
+        pltpu.make_async_copy(mlp[i], bufs_mlp[0][1 + i], lsem.at[12 + i]) for i in range(2)
+    ]
+    loads = load_mlp(1)
+    for copy in down_loads + loads:
         copy.start()
     gains[0, 0:1, :] = gain_mlp_ref[...]
     gains[0, 1:2, :] = jnp.zeros_like(gain_mlp_ref)
@@ -1467,15 +1507,17 @@
     sums = []
     for i, x_first in enumerate((True, False, True)):
         sums.append(PlaneSum(copies, place, x_first, bufs_mlp[i]))
-    for i in range(3):
+    for copy in down_loads:
+        copy.wait()
+    sums[0].go_home(exchanged=False)
+    for i in (1, 2):
         for copy in loads:
             copy.wait()
         sums[i].cross_second(kept, come)
-        if i < 2:
-            loads = load_mlp(i + 1)
+        if i == 1:
+            loads = load_mlp(2)
             for copy in loads:
                 copy.start()
-        if i == 1:
             corner_sum(0)
             start_back(2)
             start_back(3)
@@ -1519,7 +1561,7 @@
     corner_sum(3)
     load_n.wait()
     attn_grad(1, full, d_lin[:q_cols, :].T)
-    for plane in sums:
+    for plane in sums[1:]:
         plane.go_home()
 
     def second(i):
@@ -1604,7 +1646,7 @@
     group = 4 * block
     q_cols, kv_all = d_query_t.shape[0], d_kv.shape[1]
     kv_cols = kv_all // 2
-    hidden = mlp[0].shape[2]
+    hidden = mlp[0].shape[1]
     per = width // 8
     shape = jax.ShapeDtypeStruct
     out_shape = (
@@ -1637,7 +1679,7 @@
         *[pltpu.VMEM((block, width), floats)] * 2,
         *[pltpu.VMEM((block, width), halves)] * 6,
         *copy_semaphores(),
-        pltpu.SemaphoreType.DMA((12,)),
+        pltpu.SemaphoreType.DMA((14,)),
     ]
 
     def kernel(*refs):
@@ -1769,7 +1811,7 @@
     slices = [send(part, "odd_far") for part in (slice_g, slice_u)]
     context_t, log_total = attend_forward(counts, q_t, pieces)
     (
-        out_base, grad_residual, attn_grad_full, out_near, down_keep, down_come, gate_keep, gate_send,
+        out_base, grad_residual, attn_grad_full, out_near, down_half, down_mine, gate_keep, gate_send,
         up_keep, up_send, d_context_t, delta, mlp_gain_part,
     ) = middle(
         context_t, tokens, gain_mlp, grad_full,
@@ -1777,12 +1819,13 @@
     )
     gate_come = send(gate_send, "y")
     up_come = send(up_send, "x")
+    down_come = send(down_half, "y")
     out_near = send(out_near, "near")
     d_query_t, d_pieces = attend_backward(counts, q_t, d_context_t, log_total, delta, pieces)
     input_grad, gains, gate_sum, up_sum, down_sum, query_sum, kv_sum, output_sum = last_part(
         counts, inverse, d_query_t, d_pieces, normed_full, joined, tokens, gain_attn,
         grad_residual, attn_grad_full, context_t, mlp_gain_part,
-        (down_keep, down_come, gate_keep, gate_come, up_keep, up_come),
+        (down_mine, down_come, gate_keep, gate_come, up_keep, up_come),
     )
     per = gains.shape[1] // 8
     gains = lax.dynamic_slice_in_dim(gains, dp * per, per, axis=1)

time: 487 us -> 474 us (0.973); the launches traced: 479 us -> 471 us
  Pallas kernels: 457 us -> 429 us
  waiting for transfers between devices: 0.01 us -> 25.6 us
    ppermute x5 -> x6, waiting for transfers between devices: 0.01 us -> 25.6 us  [send(): return lax.ppermute(block, ('dp', 'tp'), ROUTES[way])]
    pallas_call x1, Pallas kernels: 51.9 us -> 34.3 us  [attend_backward(): pl.pallas_call(functools.partial(bwd_kernel, n, width), out_shape=(jax.Sh...]
    pallas_call x1, Pallas kernels: 32 us -> 22.1 us  [attend_forward(): pl.pallas_call(functools.partial(fwd_kernel, n, width), out_shape=(jax.Sh...]
    pallas_call x1, Pallas kernels: 164 us -> 155 us  [last_part(): pl.pallas_call(kernel, out_shape=out_shape, in_specs=[SM, VM, VM, HM, HM,...]
    pallas_call x1, Pallas kernels: 111 us -> 119 us  [middle(): pl.pallas_call(kernel, out_shape=out_shape, in_specs=[VM] * 4 + [HB] * 8,...]
    ppermute x5 -> x6, starting transfers between devices: 12.9 us -> 9.67 us  [send(): return lax.ppermute(block, ('dp', 'tp'), ROUTES[way])]
  transfers between devices with their start and end apart: 5 -> 6, of which waited for: 0 -> 3; matrix products, arithmetic and copies ran while one was open for 0% -> 0% of each run, Pallas kernels for 52% -> 45%
where the time goes in v7:
time: 474 us; the launch traced here: 471 us
  Pallas kernels  429 us (91%)
  waiting for transfers between devices  25.6 us (5%)
  starting transfers between devices  9.67 us (2%)
    pallas_call x1, Pallas kernels, last_part(): pl.pallas_call(kernel, out_shape=out_shape, in_specs=[SM, VM, VM, HM, HM,...  155 us
    pallas_call x1, Pallas kernels, middle(): pl.pallas_call(kernel, out_shape=out_shape, in_specs=[VM] * 4 + [HB] * 8,...  119 us
    pallas_call x1, Pallas kernels, first_part(): pl.pallas_call(first_kernel, out_shape=out_shape, in_specs=[SM] + [VM] *...  93.1 us
    pallas_call x1, Pallas kernels, attend_backward(): pl.pallas_call(functools.partial(bwd_kernel, n, width), out_shape=(jax.Sh...  34.3 us
    ppermute x6, waiting for transfers between devices, send(): return lax.ppermute(block, ('dp', 'tp'), ROUTES[way])  25.6 us
    pallas_call x1, Pallas kernels, attend_forward(): pl.pallas_call(functools.partial(fwd_kernel, n, width), out_shape=(jax.Sh...  22.1 us
    ppermute x6, starting transfers between devices, send(): return lax.ppermute(block, ('dp', 'tp'), ROUTES[way])  9.67 us
  transfers between devices with their start and end apart: 6, of which 3 were waited for; matrix products, arithmetic and copies ran while one was open for 0% of the time, Pallas kernels for 45%

profile of v7, /device:TPU:3, one launch (start us, length us, event | category | flops | bytes accessed | tf_op | source)
XLA Modules:
  0.0 471.4 jit_solution(2571885767977352385)
XLA Ops:
  0.7 0.6 negate_power_fusion.inverse_ref.refs_1_
  1.3 1.3 reshape.40.gain_ref.refs_7_
  2.6 1.5 convert_reduce_fusion.counts.refs_0_
  4.1 0.0 copy-start.2
  4.1 93.1 %first.1 = (bf16[384,1024]{1,0:T(8,128)(2,1)}, bf16[16,384,512]{2,1,0:T(8,128)(2,1)}, bf16[1024,1536]{1,0:T(8,128)(2,1)}, bf16[1024,1536]{1,0:T(8,128)(2,1)}, bf...) custom-call(s32[3]{0:T(128)} %convert_reduce_fusion.counts.refs_0_, ...), custom_call_target="tpu_custom_call" | custom-call | tf_op jit(solution)/shard_map/first/pallas_call | solution.py:1063
  97.1 1.9 collective-permute-start
  99.1 4.3 collective-permute-start.1
  103.3 0.0 copy-done.2
  103.4 0.6 reshape.41.refs_2_
  104.0 22.1 %attend_forward.1 = (bf16[384,1024]{1,0:T(8,128)(2,1)}, f32[4,1024]{1,0:T(4,128)}) custom-call(s32[3]{0:T(128)} %convert_reduce_fusion.counts.refs_0_, bf16[384,1024]{1,0:T(8,128)(2,1)} %get-tuple-element.54.q_ref, bf16[16,384,512]{2,1,0:T(8,128)(2,1)} %get-tuple-element.55.pieces), custom_call_target="tpu_custom_call" | custom-call | tf_op jit(solution)/shard_map/attend_forward/pallas_call | solution.py:175
  126.0 0.8 collective-permute-done.refs_10_
  126.8 0.0 copy-start.1
  126.8 8.5 %collective-permute-done.1.refs_11_ = bf16[384,1024]{1,0:T(8,128)(2,1)} collective-permute-done((bf16[384,1024]{1,0:T(8,128)(2,1)}, bf16[384,1024]{1,0:T(8,128)(2,1)}, u32[]{:S(2)}, u32[]{:S(2)}) %collective-permute-start.1) | collective-permute-done | bytes 786464 | tf_op jit(solution)/shard_map/ppermute | solution.py:1780
  135.3 0.0 copy-done.1
  135.3 119.1 %middle.1 = (f32[256,1536]{1,0:T(8,128)}, f32[256,1536]{1,0:T(8,128)}, bf16[1024,1536]{1,0:T(8,128)(2,1)}, bf16[256,1536]{1,0:T(8,128)(2,1)}, bf16[384,1024]{1,0...) custom-call(bf16[384,1024]{1,0:T(8,128)(2,1)} %get-tuple-element.56., ...), custom_call_target="tpu_custom_call" | custom-call | tf_op jit(solution)/shard_map/middle/pallas_call | solution.py:1397
  254.4 2.5 collective-permute-start.4
  256.9 0.0 collective-permute-start.5
  256.9 0.2 collective-permute-start.3
  257.0 0.9 collective-permute-start.2
  257.9 34.3 %attend_backward.1 = (f32[384,1024]{1,0:T(8,128)}, bf16[16,384,512]{2,1,0:T(8,128)(2,1)}) custom-call(s32[3]{0:T(128)} %convert_reduce_fusion.counts.refs_0_, bf16[384,1024]{1,0:T(8,128)(2,1)} %get-tuple-element.54.q_ref, bf16[384,1024]{1,0:T(8,128)(2,1)} %get-tuple-element.64.do_ref, f32[4,1024]{1,0:T(4,128)} %get-tuple-element.65.log_ref, ...), custom_call_target="tpu_custom_call" | custom-call | tf_op jit(solution)/shard_map/attend_backward/pallas_call | solution.py:286
  292.3 16.3 %collective-permute-done.3.refs_13_ = bf16[384,1024]{1,0:T(8,128)(2,1)S(1)} collective-permute-done((bf16[384,1024]{1,0:T(8,128)(2,1)}, bf16[384,1024]{1,0:T(8,128)(2,1)S(1)}, u32[]{:S(2)}, u32[]{:S(2)}) %collective-permute-start.3) | collective-permute-done | bytes 786464 | tf_op jit(solution)/shard_map/ppermute | solution.py:1780
  308.6 0.0 copy-start
  308.6 0.0 collective-permute-done.4.refs_15_
  308.6 0.0 collective-permute-done.5.refs_17_
  308.6 0.9 copy-done
  309.4 154.5 %last.1 = (f32[256,1536]{1,0:T(8,128)}, f32[2,1536]{1,0:T(2,128)}, f32[192,1024]{1,0:T(8,128)}, f32[192,1024]{1,0:T(8,128)}, f32[192,1024]{1,0:T(8,128)}, /*inde...) custom-call(s32[3]{0:T(128)} %convert_reduce_fusion.counts.refs_0_, ...), custom_call_target="tpu_custom_call" | custom-call | tf_op jit(solution)/shard_map/last/pallas_call | solution.py:1688
  464.0 1.4 constant_dynamic-slice_fusion
  465.4 0.0 collective-permute-done.2.refs_1_
  465.4 5.6 %finish.1 = (bf16[256,1536]{1,0:T(8,128)(2,1)}, f32[192,192]{1,0:T(8,128)}, f32[192,192]{1,0:T(8,128)}, f32[256,1536]{1,0:T(8,128)}, f32[192,384]{1,0:T(8,128)},...) custom-call(f32[256,1536]{1,0:T(8,128)} %get-tuple-element.62.refs_0_, ...), custom_call_target="tpu_custom_call" | custom-call | tf_op jit(solution)/shard_map/finish/pallas_call | solution.py:1726
  (1 shorter events, 0.0 us)
Async XLA Ops:
  4.1 99.3 %copy-start.2 = (bf16[1536]{0:T(1024)(128)(2,1)S(1)}, bf16[1536]{0:T(1024)(128)(2,1)}, u32[]{:S(2)}) copy-start(bf16[1536]{0:T(1024)(128)(2,1)} %param.20) | copy-start | bytes 9220
  97.1 29.6 %collective-permute-start = (bf16[384,1024]{1,0:T(8,128)(2,1)}, bf16[384,1024]{1,0:T(8,128)(2,1)S(1)}, u32[]{:S(2)}, u32[]{:S(2)}) collective-permute-start(bf16[384,1024]{1,0:T(8,128)(2,1)} %get-tuple-element.60), channel_id=1, source_target_pairs={{4,6},{5,7},{6,4},{7,5},{12,14},{13,15},{14,12},{15,13},{20,22},{2... | collective-permute-start | bytes 2359304 | tf_op jit(solution)/shard_map/ppermute | solution.py:1780
  99.1 36.2 %collective-permute-start.1 = (bf16[384,1024]{1,0:T(8,128)(2,1)}, bf16[384,1024]{1,0:T(8,128)(2,1)}, u32[]{:S(2)}, u32[]{:S(2)}) collective-permute-start(bf16[384,1024]{1,0:T(8,128)(2,1)} %get-tuple-element.61), channel_id=1, source_target_pairs={{4,6},{5,7},{6,4},{7,5},{12,14},{13,15},{14,12},{15,13},{20,22},{2... | collective-permute-start | bytes 2359304 | tf_op jit(solution)/shard_map/ppermute | solution.py:1780
  126.8 8.5 %copy-start.1 = (bf16[384,1024]{1,0:T(8,128)(2,1)}, bf16[384,1024]{1,0:T(8,128)(2,1)S(1)}, u32[]{:S(2)}) copy-start(bf16[384,1024]{1,0:T(8,128)(2,1)S(1)} %collective-permute-done.refs_10_) | copy-start | bytes 2359300
  254.4 54.2 %collective-permute-start.4 = (bf16[2,384,1024]{2,1,0:T(8,128)(2,1)}, bf16[2,384,1024]{2,1,0:T(8,128)(2,1)}, u32[]{:S(2)}, u32[]{:S(2)}) collective-permute-start(bf16[2,384,1024]{2,1,0:T(8,128)(2,1)} %get-tuple-element.77), channel_id=1, source_target_pairs={{0,16},{1,17},{2,18},{3,19},{4,20},{5,21},{6,22},{7,23},{8,24},{9,... | collective-permute-start | bytes 4718600 | tf_op jit(solution)/shard_map/ppermute | solution.py:1780
  256.9 51.7 %collective-permute-start.5 = (bf16[2,384,1024]{2,1,0:T(8,128)(2,1)}, bf16[2,384,1024]{2,1,0:T(8,128)(2,1)}, u32[]{:S(2)}, u32[]{:S(2)}) collective-permute-start(bf16[2,384,1024]{2,1,0:T(8,128)(2,1)} %get-tuple-element.79), channel_id=1, source_target_pairs={{0,8},{1,9},{2,10},{3,11},{4,12},{5,13},{6,14},{7,15},{8,0},{9,1},... | collective-permute-start | bytes 4718600 | tf_op jit(solution)/shard_map/ppermute | solution.py:1780
  256.9 51.7 %collective-permute-start.3 = (bf16[384,1024]{1,0:T(8,128)(2,1)}, bf16[384,1024]{1,0:T(8,128)(2,1)S(1)}, u32[]{:S(2)}, u32[]{:S(2)}) collective-permute-start(bf16[384,1024]{1,0:T(8,128)(2,1)} %get-tuple-element.75), channel_id=1, source_target_pairs={{0,16},{1,17},{2,18},{3,19},{4,20},{5,21},{6,22},{7,23},{8,24},{9,... | collective-permute-start | bytes 2359304 | tf_op jit(solution)/shard_map/ppermute | solution.py:1780
  257.0 208.3 %collective-permute-start.2 = (bf16[256,1536]{1,0:T(8,128)(2,1)}, bf16[256,1536]{1,0:T(8,128)(2,1)}, u32[]{:S(2)}, u32[]{:S(2)}) collective-permute-start(bf16[256,1536]{1,0:T(8,128)(2,1)} %get-tuple-element.63), channel_id=1, source_target_pairs={{0,1},{1,0},{2,3},{3,2},{4,5},{5,4},{6,7},{7,6},{8,9},{9,8},{10,11... | collective-permute-start | bytes 2359304 | tf_op jit(solution)/shard_map/ppermute | solution.py:1780
  308.6 0.9 copy-start

commit v8 on v7

--- a/solution.py
+++ b/solution.py
@@ -78,22 +78,41 @@
     return key_base, needed, whole
 
 
-def allowed_mask(key_base, tok_ref, start_ref, lanes):
-    keys = key_base + lax.broadcasted_iota(jnp.int32, (BLK, BLK), 0)
-    return (keys <= tok_ref[0:1, lanes]) & (keys >= start_ref[0:1, lanes])
+def allowed_mask(key_bases, tok_ref, start_ref, lanes):
+    masks = []
+    for key_base in key_bases:
+        keys = key_base + lax.broadcasted_iota(jnp.int32, (BLK, BLK), 0)
+        masks.append((keys <= tok_ref[0:1, lanes]) & (keys >= start_ref[0:1, lanes]))
+    return masks[0] if len(masks) == 1 else jnp.concatenate(masks, axis=0)
+
+
+def piece_used(sc, piece, blocks):
+    used = False
+    for kb in range(2):
+        for qb in range(blocks):
+            used = used | pair_state(sc, 2 * piece + kb, qb)[1]
+    return used
+
+
+def for_piece(sc, piece, qb, unit):
+    one_base, one, one_whole = pair_state(sc, 2 * piece, qb)
+    two_base, two, two_whole = pair_state(sc, 2 * piece + 1, qb)
+    both, free = one & two, one_whole & two_whole
+    bases = (one_base, two_base)
+    pl.when(both & free)(lambda: unit((0, 1), bases, False))
+    pl.when(both & jnp.logical_not(free))(lambda: unit((0, 1), bases, True))
+    pl.when(one & jnp.logical_not(two))(lambda: unit((0,), bases[:1], True))
+    pl.when(two & jnp.logical_not(one))(lambda: unit((1,), bases[1:], True))
 
 
 def fwd_kernel(n, width, counts, q_ref, pieces, *refs):
     out_acc, out_sum = refs[:2]
     kv, keys_nat, acc, total, q_wide, sc, tok_ref, start_ref, sem = refs[2:]
-    per = width // BLK
     for i in range(n):
         pltpu.make_async_copy(pieces.at[i], kv.at[i], sem.at[i]).start()
     acc[...] = jnp.zeros_like(acc)
     total[...] = jnp.zeros_like(total)
     fill_places(counts, sc, tok_ref, start_ref)
-    for i in range(n):
-        pltpu.make_async_copy(pieces.at[i], kv.at[i], sem.at[i]).wait()
     heads_kv = pieces.shape[1] // (2 * HEAD_WIDTH)
     group = q_ref.shape[0] // (heads_kv * HEAD_WIDTH)
     v_off = heads_kv * HEAD_WIDTH
@@ -105,23 +124,19 @@
     for h, rows, lanes, wrows, wlanes, hd in places:
         q_wide[wrows, wlanes] = q_ref[rows, lanes]
 
-    def key_block(kb, carry):
-        piece = kb // per
-        klanes = pl.ds(pl.multiple_of((kb % per) * BLK, BLK), BLK)
-        for h in range(heads_kv):
-            keys_nat[h] = kv[piece, h * HEAD_WIDTH : (h + 1) * HEAD_WIDTH, klanes].T
-
+    def key_piece(piece, carry):
+        pltpu.make_async_copy(pieces.at[piece], kv.at[piece], sem.at[piece]).wait()
         def query_block(qb, carry):
-            key_base, needed, whole = pair_state(sc, kb, qb)
             lanes = pl.ds(pl.multiple_of(qb * BLK, BLK), BLK)
-
-            def unit(masked):
-                wide = pl.ds(pl.multiple_of(qb * (group * BLK), group * BLK), group * BLK)
+            wide = pl.ds(pl.multiple_of(qb * (group * BLK), group * BLK), group * BLK)
+
+            def unit(subs, bases, masked):
+                keys = slice(subs[0] * BLK, (subs[-1] + 1) * BLK)
                 if masked:
-                    allowed = allowed_mask(key_base, tok_ref, start_ref, lanes)
+                    allowed = allowed_mask(bases, tok_ref, start_ref, lanes)
                     allowed = jnp.concatenate([allowed] * group, axis=1)
                 scores = [
-                    dot_nn(keys_nat[h], q_wide[h * HEAD_WIDTH : (h + 1) * HEAD_WIDTH, wide])
+                    dot_nn(keys_nat[h, keys], q_wide[h * HEAD_WIDTH : (h + 1) * HEAD_WIDTH, wide])
                     for h in range(heads_kv)
                 ]
                 weights = [jnp.exp2(s * SCORE) for s in scores]
@@ -130,7 +145,7 @@
                 sums = [jnp.sum(w, axis=0, keepdims=True) for w in weights]
                 parts = [
                     dot_nn(
-                        kv[piece, v_off + h * HEAD_WIDTH : v_off + (h + 1) * HEAD_WIDTH, klanes],
+                        kv[piece, v_off + h * HEAD_WIDTH : v_off + (h + 1) * HEAD_WIDTH, keys],
                         weights[h].astype(halves),
                     )
                     for h in range(heads_kv)
@@ -139,13 +154,18 @@
                     total[h : h + 1, wide] += sums[h]
                     acc[h * HEAD_WIDTH : (h + 1) * HEAD_WIDTH, wide] += parts[h]
 
-            pl.when(needed & whole)(lambda: unit(False))
-            pl.when(needed & jnp.logical_not(whole))(lambda: unit(True))
+            for_piece(sc, piece, qb, unit)
             return carry
 
-        return lax.fori_loop(0, q_ref.shape[1] // BLK, query_block, carry)
-
-    lax.fori_loop(0, n * per, key_block, 0)
+        @pl.when(piece_used(sc, piece, q_ref.shape[1] // BLK))
+        def _():
+            for h in range(heads_kv):
+                keys_nat[h] = kv[piece, h * HEAD_WIDTH : (h + 1) * HEAD_WIDTH, :].T
+            lax.fori_loop(0, q_ref.shape[1] // BLK, query_block, 0)
+
+        return carry
+
+    lax.fori_loop(0, n, key_piece, 0)
     for h, rows, lanes, wrows, wlanes, hd in places:
         row = total[h : h + 1, wlanes]
         out_acc[rows, lanes] = (acc[wrows, wlanes] * ((1.0 / VSCALE) / row)).astype(halves)
@@ -182,7 +202,7 @@
         out_specs=(VM, VM),
         scratch_shapes=[
             pltpu.VMEM(pieces.shape, halves),
-            pltpu.VMEM((heads_kv, BLK, HEAD_WIDTH), halves),
+            pltpu.VMEM((heads_kv, width, HEAD_WIDTH), halves),
             pltpu.VMEM((heads_kv * HEAD_WIDTH, wide), floats),
             pltpu.VMEM((heads_kv, wide), floats),
             pltpu.VMEM((heads_kv * HEAD_WIDTH, wide), halves),
@@ -198,12 +218,9 @@
     dq_out = refs[0]
     dkv_out = refs[1]
     kv, dkv, keys_nat, vals_nat, acc, q_wide, do_wide, log_wide, delta_wide, dq_wide, sc, tok_ref, start_ref, sem, osem = refs[2:]
-    per = width // BLK
     for i in range(n):
         pltpu.make_async_copy(pieces.at[i], kv.at[i], sem.at[i]).start()
     fill_places(counts, sc, tok_ref, start_ref)
-    for i in range(n):
-        pltpu.make_async_copy(pieces.at[i], kv.at[i], sem.at[i]).wait()
     heads_kv = pieces.shape[1] // (2 * HEAD_WIDTH)
     group = q_ref.shape[0] // (heads_kv * HEAD_WIDTH)
     v_off = heads_kv * HEAD_WIDTH
@@ -220,30 +237,24 @@
         dq_wide[wrows, wlanes] = jnp.zeros((HEAD_WIDTH, BLK), floats)
     out_scale = (1.0 / VSCALE) * HEAD_WIDTH ** (-0.5)
 
-    def key_block(kb, carry):
-        piece = kb // per
-        klanes = pl.ds(pl.multiple_of((kb % per) * BLK, BLK), BLK)
-        for h in range(heads_kv):
-            keys_nat[h] = kv[piece, h * HEAD_WIDTH : (h + 1) * HEAD_WIDTH, klanes].T
-            vals_nat[h] = kv[piece, v_off + h * HEAD_WIDTH : v_off + (h + 1) * HEAD_WIDTH, klanes].T
-        acc[...] = jnp.zeros_like(acc)
-
+    def key_piece(piece, carry):
+        pltpu.make_async_copy(pieces.at[piece], kv.at[piece], sem.at[piece]).wait()
         def query_block(qb, carry):
-            key_base, needed, whole = pair_state(sc, kb, qb)
             lanes = pl.ds(pl.multiple_of(qb * BLK, BLK), BLK)
-
-            def unit(masked):
-                wide = pl.ds(pl.multiple_of(qb * (group * BLK), group * BLK), group * BLK)
+            wide = pl.ds(pl.multiple_of(qb * (group * BLK), group * BLK), group * BLK)
+
+            def unit(subs, bases, masked):
+                keys = slice(subs[0] * BLK, (subs[-1] + 1) * BLK)
                 if masked:
-                    allowed = allowed_mask(key_base, tok_ref, start_ref, lanes)
+                    allowed = allowed_mask(bases, tok_ref, start_ref, lanes)
                     allowed = jnp.concatenate([allowed] * group, axis=1)
                 heads = range(heads_kv)
                 krows = [slice(h * HEAD_WIDTH, (h + 1) * HEAD_WIDTH) for h in heads]
                 vrows = [slice(v_off + h * HEAD_WIDTH, v_off + (h + 1) * HEAD_WIDTH) for h in heads]
                 qt = [q_wide[krows[h], wide] for h in heads]
                 dot = [do_wide[krows[h], wide] for h in heads]
-                scores = [dot_nn(keys_nat[h], qt[h]) for h in heads]
-                dprobs = [dot_nn(vals_nat[h], dot[h]) for h in heads]
+                scores = [dot_nn(keys_nat[h, keys], qt[h]) for h in heads]
+                dprobs = [dot_nn(vals_nat[h, keys], dot[h]) for h in heads]
                 weights = [
                     jnp.exp2(scores[h] * SCORE - log_wide[h : h + 1, wide]) for h in heads
                 ]
@@ -255,24 +266,37 @@
                 ]
                 dv = [dot_nt(dot[h], weights[h].astype(halves)) for h in heads]
                 dk = [dot_nt(qt[h], ds[h]) for h in heads]
-                dq = [dot_nn(kv[piece, krows[h], klanes], ds[h]) for h in heads]
+                dq = [dot_nn(kv[piece, krows[h], keys], ds[h]) for h in heads]
                 for h in heads:
-                    acc[vrows[h], :] += dv[h]
-                    acc[krows[h], :] += dk[h]
+                    acc[vrows[h], keys] += dv[h]
+                    acc[krows[h], keys] += dk[h]
                     dq_wide[krows[h], wide] += dq[h]
 
-            pl.when(needed & whole)(lambda: unit(False))
-            pl.when(needed & jnp.logical_not(whole))(lambda: unit(True))
+            for_piece(sc, piece, qb, unit)
             return carry
 
-        carry = lax.fori_loop(0, q_ref.shape[1] // BLK, query_block, carry)
-        dkv[piece, 0:v_off, klanes] = (acc[0:v_off, :] * out_scale).astype(halves)
-        dkv[piece, v_off:, klanes] = acc[v_off:, :].astype(halves)
+        used = piece_used(sc, piece, q_ref.shape[1] // BLK)
+
+        @pl.when(used)
+        def _():
+            for h in range(heads_kv):
+                rows = slice(h * HEAD_WIDTH, (h + 1) * HEAD_WIDTH)
+                vals = slice(v_off + h * HEAD_WIDTH, v_off + (h + 1) * HEAD_WIDTH)
+                keys_nat[h] = kv[piece, rows, :].T
+                vals_nat[h] = kv[piece, vals, :].T
+            acc[...] = jnp.zeros_like(acc)
+            lax.fori_loop(0, q_ref.shape[1] // BLK, query_block, 0)
+            dkv[piece, 0:v_off, :] = (acc[0:v_off, :] * out_scale).astype(halves)
+            dkv[piece, v_off:, :] = acc[v_off:, :].astype(halves)
+
+        @pl.when(jnp.logical_not(used))
+        def _():
+            dkv[piece] = jnp.zeros(dkv.shape[1:], halves)
+
+        pltpu.make_async_copy(dkv.at[piece], dkv_out.at[piece], osem.at[piece]).start()
         return carry
 
-    lax.fori_loop(0, n * per, key_block, 0)
-    for i in range(n):
-        pltpu.make_async_copy(dkv.at[i], dkv_out.at[i], osem.at[i]).start()
+    lax.fori_loop(0, n, key_piece, 0)
     for h, rows, lanes, wrows, wlanes, hd in places:
         dq_out[rows, lanes] = dq_wide[wrows, wlanes] * out_scale
     for i in range(n):
@@ -294,9 +318,9 @@
         scratch_shapes=[
             pltpu.VMEM(pieces.shape, halves),
             pltpu.VMEM(pieces.shape, halves),
-            pltpu.VMEM((heads_kv, BLK, HEAD_WIDTH), halves),
-            pltpu.VMEM((heads_kv, BLK, HEAD_WIDTH), halves),
-            pltpu.VMEM((pieces.shape[1], BLK), floats),
+            pltpu.VMEM((heads_kv, width, HEAD_WIDTH), halves),
+            pltpu.VMEM((heads_kv, width, HEAD_WIDTH), halves),
+            pltpu.VMEM(pieces.shape[1:], floats),
             pltpu.VMEM((heads_kv * HEAD_WIDTH, wide), halves),
             pltpu.VMEM((heads_kv * HEAD_WIDTH, wide), halves),
             pltpu.VMEM((heads_kv, wide), floats),

time: 474 us -> 460 us (0.970)
  Pallas kernels: 429 us -> 400 us
  waiting for transfers between devices: 25.6 us -> 36.5 us
    pallas_call x1, Pallas kernels: 155 us -> 141 us  [last_part(): pl.pallas_call(kernel, out_shape=out_shape, in_specs=[SM, VM, VM, HM, HM,...]
    ppermute x6, waiting for transfers between devices: 25.6 us -> 36.5 us  [send(): return lax.ppermute(block, ('dp', 'tp'), ROUTES[way])]
    pallas_call x1, Pallas kernels: 34.3 us -> 26.9 us  [attend_backward(): pl.pallas_call(functools.partial(bwd_kernel, n, width), out_shape=(jax.Sh...]
    pallas_call x1, Pallas kernels: 22.1 us -> 16.9 us  [attend_forward(): pl.pallas_call(functools.partial(fwd_kernel, n, width), out_shape=(jax.Sh...]
  transfers between devices with their start and end apart: 6 -> 6, of which waited for: 3 -> 3; matrix products, arithmetic and copies ran while one was open for 0% -> 0% of each run, Pallas kernels for 45% -> 41%
where the time goes in v8:
time: 460 us; the launch traced here: 455 us
  Pallas kernels  400 us (87%)
  waiting for transfers between devices  36.5 us (8%)
  starting transfers between devices  11.5 us (2%)
    pallas_call x1, Pallas kernels, last_part(): pl.pallas_call(kernel, out_shape=out_shape, in_specs=[SM, VM, VM, HM, HM,...  141 us
    pallas_call x1, Pallas kernels, middle(): pl.pallas_call(kernel, out_shape=out_shape, in_specs=[VM] * 4 + [HB] * 8,...  117 us
    pallas_call x1, Pallas kernels, first_part(): pl.pallas_call(first_kernel, out_shape=out_shape, in_specs=[SM] + [VM] *...  93.1 us
    ppermute x6, waiting for transfers between devices, send(): return lax.ppermute(block, ('dp', 'tp'), ROUTES[way])  36.5 us
    pallas_call x1, Pallas kernels, attend_backward(): pl.pallas_call(functools.partial(bwd_kernel, n, width), out_shape=(jax.Sh...  26.9 us
    pallas_call x1, Pallas kernels, attend_forward(): pl.pallas_call(functools.partial(fwd_kernel, n, width), out_shape=(jax.Sh...  16.9 us
    ppermute x6, starting transfers between devices, send(): return lax.ppermute(block, ('dp', 'tp'), ROUTES[way])  11.5 us
  transfers between devices with their start and end apart: 6, of which 3 were waited for; matrix products, arithmetic and copies ran while one was open for 0% of the time, Pallas kernels for 41%

profile of v8, /device:TPU:3, one launch (start us, length us, event | category | flops | bytes accessed | tf_op | source)
XLA Modules:
  0.0 455.3 jit_solution(10020632000917869361)
XLA Ops:
  0.7 0.6 negate_power_fusion.inverse_ref.refs_1_
  1.3 1.3 reshape.40.gain_ref.refs_7_
  2.6 1.5 convert_reduce_fusion.counts.refs_0_
  4.1 0.0 copy-start.2
  4.1 93.1 %first.1 = (bf16[384,1024]{1,0:T(8,128)(2,1)}, bf16[16,384,512]{2,1,0:T(8,128)(2,1)}, bf16[1024,1536]{1,0:T(8,128)(2,1)}, bf16[1024,1536]{1,0:T(8,128)(2,1)}, bf...) custom-call(s32[3]{0:T(128)} %convert_reduce_fusion.counts.refs_0_, ...), custom_call_target="tpu_custom_call" | custom-call | tf_op jit(solution)/shard_map/first/pallas_call | solution.py:1087
  97.1 1.9 collective-permute-start
  99.1 4.4 collective-permute-start.1
  103.5 0.0 copy-done.2
  103.5 0.6 reshape.41.refs_2_
  104.1 16.9 %attend_forward.1 = (bf16[384,1024]{1,0:T(8,128)(2,1)}, f32[4,1024]{1,0:T(4,128)}) custom-call(s32[3]{0:T(128)} %convert_reduce_fusion.counts.refs_0_, bf16[384,1024]{1,0:T(8,128)(2,1)} %get-tuple-element.54.q_ref, bf16[16,384,512]{2,1,0:T(8,128)(2,1)} %get-tuple-element.55.pieces), custom_call_target="tpu_custom_call" | custom-call | tf_op jit(solution)/shard_map/attend_forward/pallas_call | solution.py:195
  121.0 5.8 %collective-permute-done.refs_10_ = bf16[384,1024]{1,0:T(8,128)(2,1)S(1)} collective-permute-done((bf16[384,1024]{1,0:T(8,128)(2,1)}, bf16[384,1024]{1,0:T(8,128)(2,1)S(1)}, u32[]{:S(2)}, u32[]{:S(2)}) %collective-permute-start) | collective-permute-done | bytes 786464 | tf_op jit(solution)/shard_map/ppermute | solution.py:1804
  126.8 0.0 copy-start.1
  126.8 8.5 %collective-permute-done.1.refs_11_ = bf16[384,1024]{1,0:T(8,128)(2,1)} collective-permute-done((bf16[384,1024]{1,0:T(8,128)(2,1)}, bf16[384,1024]{1,0:T(8,128)(2,1)}, u32[]{:S(2)}, u32[]{:S(2)}) %collective-permute-start.1) | collective-permute-done | bytes 786464 | tf_op jit(solution)/shard_map/ppermute | solution.py:1804
  135.3 0.0 copy-done.1
  135.3 116.8 %middle.1 = (f32[256,1536]{1,0:T(8,128)}, f32[256,1536]{1,0:T(8,128)}, bf16[1024,1536]{1,0:T(8,128)(2,1)}, bf16[256,1536]{1,0:T(8,128)(2,1)}, bf16[384,1024]{1,0...) custom-call(bf16[384,1024]{1,0:T(8,128)(2,1)} %get-tuple-element.56., ...), custom_call_target="tpu_custom_call" | custom-call | tf_op jit(solution)/shard_map/middle/pallas_call | solution.py:1421
  252.1 2.5 collective-permute-start.4
  254.6 0.0 collective-permute-start.5
  254.7 0.2 collective-permute-start.3
  254.8 2.4 collective-permute-start.2
  257.3 26.9 %attend_backward.1 = (f32[384,1024]{1,0:T(8,128)}, bf16[16,384,512]{2,1,0:T(8,128)(2,1)}) custom-call(s32[3]{0:T(128)} %convert_reduce_fusion.counts.refs_0_, bf16[384,1024]{1,0:T(8,128)(2,1)} %get-tuple-element.54.q_ref, bf16[384,1024]{1,0:T(8,128)(2,1)} %get-tuple-element.64.do_ref, f32[4,1024]{1,0:T(4,128)} %get-tuple-element.65.log_ref, ...), custom_call_target="tpu_custom_call" | custom-call | tf_op jit(solution)/shard_map/attend_backward/pallas_call | solution.py:310
  284.2 22.2 %collective-permute-done.3.refs_13_ = bf16[384,1024]{1,0:T(8,128)(2,1)S(1)} collective-permute-done((bf16[384,1024]{1,0:T(8,128)(2,1)}, bf16[384,1024]{1,0:T(8,128)(2,1)S(1)}, u32[]{:S(2)}, u32[]{:S(2)}) %collective-permute-start.3) | collective-permute-done | bytes 786464 | tf_op jit(solution)/shard_map/ppermute | solution.py:1804
  306.4 0.0 copy-start
  306.4 0.0 collective-permute-done.4.refs_15_
  306.4 0.0 collective-permute-done.5.refs_17_
  306.4 0.9 copy-done
  307.2 140.8 %last.1 = (f32[256,1536]{1,0:T(8,128)}, f32[2,1536]{1,0:T(2,128)}, f32[192,1024]{1,0:T(8,128)}, f32[192,1024]{1,0:T(8,128)}, f32[192,1024]{1,0:T(8,128)}, /*inde...) custom-call(s32[3]{0:T(128)} %convert_reduce_fusion.counts.refs_0_, ...), custom_call_target="tpu_custom_call" | custom-call | tf_op jit(solution)/shard_map/last/pallas_call | solution.py:1712
  448.1 1.4 constant_dynamic-slice_fusion
  449.5 0.0 collective-permute-done.2.refs_1_
  449.5 5.6 %finish.1 = (bf16[256,1536]{1,0:T(8,128)(2,1)}, f32[192,192]{1,0:T(8,128)}, f32[192,192]{1,0:T(8,128)}, f32[256,1536]{1,0:T(8,128)}, f32[192,384]{1,0:T(8,128)},...) custom-call(f32[256,1536]{1,0:T(8,128)} %get-tuple-element.62.refs_0_, ...), custom_call_target="tpu_custom_call" | custom-call | tf_op jit(solution)/shard_map/finish/pallas_call | solution.py:1750
  (1 shorter events, 0.0 us)
Async XLA Ops:
  4.1 99.4 %copy-start.2 = (bf16[1536]{0:T(1024)(128)(2,1)S(1)}, bf16[1536]{0:T(1024)(128)(2,1)}, u32[]{:S(2)}) copy-start(bf16[1536]{0:T(1024)(128)(2,1)} %param.20) | copy-start | bytes 9220
  97.1 29.6 %collective-permute-start = (bf16[384,1024]{1,0:T(8,128)(2,1)}, bf16[384,1024]{1,0:T(8,128)(2,1)S(1)}, u32[]{:S(2)}, u32[]{:S(2)}) collective-permute-start(bf16[384,1024]{1,0:T(8,128)(2,1)} %get-tuple-element.60), channel_id=1, source_target_pairs={{4,6},{5,7},{6,4},{7,5},{12,14},{13,15},{14,12},{15,13},{20,22},{2... | collective-permute-start | bytes 2359304 | tf_op jit(solution)/shard_map/ppermute | solution.py:1804
  99.1 36.2 %collective-permute-start.1 = (bf16[384,1024]{1,0:T(8,128)(2,1)}, bf16[384,1024]{1,0:T(8,128)(2,1)}, u32[]{:S(2)}, u32[]{:S(2)}) collective-permute-start(bf16[384,1024]{1,0:T(8,128)(2,1)} %get-tuple-element.61), channel_id=1, source_target_pairs={{4,6},{5,7},{6,4},{7,5},{12,14},{13,15},{14,12},{15,13},{20,22},{2... | collective-permute-start | bytes 2359304 | tf_op jit(solution)/shard_map/ppermute | solution.py:1804
  126.8 8.5 %copy-start.1 = (bf16[384,1024]{1,0:T(8,128)(2,1)}, bf16[384,1024]{1,0:T(8,128)(2,1)S(1)}, u32[]{:S(2)}) copy-start(bf16[384,1024]{1,0:T(8,128)(2,1)S(1)} %collective-permute-done.refs_10_) | copy-start | bytes 2359300
  252.1 54.2 %collective-permute-start.4 = (bf16[2,384,1024]{2,1,0:T(8,128)(2,1)}, bf16[2,384,1024]{2,1,0:T(8,128)(2,1)}, u32[]{:S(2)}, u32[]{:S(2)}) collective-permute-start(bf16[2,384,1024]{2,1,0:T(8,128)(2,1)} %get-tuple-element.77), channel_id=1, source_target_pairs={{0,16},{1,17},{2,18},{3,19},{4,20},{5,21},{6,22},{7,23},{8,24},{9,... | collective-permute-start | bytes 4718600 | tf_op jit(solution)/shard_map/ppermute | solution.py:1804
  254.6 51.7 %collective-permute-start.5 = (bf16[2,384,1024]{2,1,0:T(8,128)(2,1)}, bf16[2,384,1024]{2,1,0:T(8,128)(2,1)}, u32[]{:S(2)}, u32[]{:S(2)}) collective-permute-start(bf16[2,384,1024]{2,1,0:T(8,128)(2,1)} %get-tuple-element.79), channel_id=1, source_target_pairs={{0,8},{1,9},{2,10},{3,11},{4,12},{5,13},{6,14},{7,15},{8,0},{9,1},... | collective-permute-start | bytes 4718600 | tf_op jit(solution)/shard_map/ppermute | solution.py:1804
  254.7 51.7 %collective-permute-start.3 = (bf16[384,1024]{1,0:T(8,128)(2,1)}, bf16[384,1024]{1,0:T(8,128)(2,1)S(1)}, u32[]{:S(2)}, u32[]{:S(2)}) collective-permute-start(bf16[384,1024]{1,0:T(8,128)(2,1)} %get-tuple-element.75), channel_id=1, source_target_pairs={{0,16},{1,17},{2,18},{3,19},{4,20},{5,21},{6,22},{7,23},{8,24},{9,... | collective-permute-start | bytes 2359304 | tf_op jit(solution)/shard_map/ppermute | solution.py:1804
  254.8 194.7 %collective-permute-start.2 = (bf16[256,1536]{1,0:T(8,128)(2,1)}, bf16[256,1536]{1,0:T(8,128)(2,1)}, u32[]{:S(2)}, u32[]{:S(2)}) collective-permute-start(bf16[256,1536]{1,0:T(8,128)(2,1)} %get-tuple-element.63), channel_id=1, source_target_pairs={{0,1},{1,0},{2,3},{3,2},{4,5},{5,4},{6,7},{7,6},{8,9},{9,8},{10,11... | collective-permute-start | bytes 2359304 | tf_op jit(solution)/shard_map/ppermute | solution.py:1804
  306.4 0.9 copy-start

commit v9 on v8

--- a/solution.py
+++ b/solution.py
@@ -1160,6 +1160,20 @@
     return [full, full, full, part, part]
 
 
+class RowBlocks:
+    def __init__(self, ref, rows):
+        self.ref, self.rows = ref, rows
+
+    def at(self, i):
+        return pl.ds(pl.multiple_of(i * self.rows, 128), self.rows)
+
+    def __getitem__(self, i):
+        return self.ref[self.at(i), :]
+
+    def __setitem__(self, i, value):
+        self.ref[self.at(i), :] = value
+
+
 def outer_blocks(place, x_first, left, right, send_ref, keep_ref, on_sent):
     rows = left.shape[1] // 4
     for kept in (False, True):
@@ -1178,9 +1192,9 @@
 
 
 def mid_kernel(ctx_ref, tok_ref, gain_ref, g_full, weight_refs, outs, scratch):
-    (res_out, gres_out, e_full, near_out, down_half, down_mine, gate_keep, gate_send, up_keep, up_send,
+    (res_out, gres_out, e_full, near_out, down_half, down_mine, gate_half, gate_mine, up_keep, up_send,
      dctx_out, delta_out, gain_out) = outs
-    (ctx, m_full, dh, hid, dgate, dup, w_o, w_d, w_g, w_u, down_send, down_keep, down_come, part_out, far_in, own_in, *bufs, ss, rs, wsem) = scratch
+    (ctx, m_full, dh, hid, dgate, dup, w_o, w_d, w_g, w_u, down_send, down_keep, down_come, gate_send, gate_come, part_out, far_in, own_in, *bufs, ss, rs, wsem) = scratch
     place = Place()
     copies = Copies(ss, rs)
     block, width = tok_ref.shape
@@ -1334,7 +1348,9 @@
         copy.start()
     down_over = copies.make(down_send, down_come, place.over_x)
     outer_blocks(place, True, g_full, hid[...], down_send, down_keep, down_over.start)
-    outer_blocks(place, False, m_full, dgate[...], gate_send, gate_keep, lambda: None)
+    gate_keep = RowBlocks(dh, width // 4)
+    gate_over = copies.make(gate_send, gate_come, place.over_y)
+    outer_blocks(place, False, m_full, dgate[...], gate_send, gate_keep, gate_over.start)
     gain_out[...] = jnp.zeros_like(gain_out)
     for k in range(CHUNKS):
         at = pl.ds(k * chunk, chunk)
@@ -1383,6 +1399,10 @@
     gather_two.finish()
     for fetch in fetches:
         fetch.drain()
+    gate_over.wait()
+    at = place.x
+    gate_half[...] = (gate_keep[1 - at].astype(floats) + gate_come[1 - at].astype(floats)).astype(halves)
+    gate_mine[...] = (gate_keep[at].astype(floats) + gate_come[at].astype(floats)).astype(halves)
 
 
 def middle(context_t, tokens, gain, grad_full, weights):
@@ -1395,8 +1415,8 @@
         shape((block, width), floats),
         shape((group, width), halves),
         shape((block, width), halves),
-        *[shape((width // 4, hidden), halves)] * 2,
-        *[shape((2, width // 4, hidden), halves)] * 4,
+        *[shape((width // 4, hidden), halves)] * 4,
+        *[shape((2, width // 4, hidden), halves)] * 2,
         shape((q_cols, group), halves),
         shape((q_cols // HEAD_WIDTH, group), floats),
         shape((1, width), floats),
@@ -1406,7 +1426,7 @@
         pltpu.VMEM((group, width), halves),
         *[pltpu.VMEM((group, hidden), halves)] * 4,
         *[pltpu.VMEM(weight.shape, halves) for weight in weights[:4]],
-        *[pltpu.VMEM((2, width // 4, hidden), halves)] * 3,
+        *[pltpu.VMEM((2, width // 4, hidden), halves)] * 5,
         pltpu.VMEM((group, width), halves),
         *[pltpu.VMEM((block, width), halves)] * 2,
         *[pltpu.VMEM((block, width), floats)] * 2,
@@ -1479,8 +1499,11 @@
     down_loads = [
         pltpu.make_async_copy(mlp[i], bufs_mlp[0][1 + i], lsem.at[12 + i]) for i in range(2)
     ]
-    loads = load_mlp(1)
-    for copy in down_loads + loads:
+    gate_loads = [
+        pltpu.make_async_copy(mlp[2 + i], bufs_mlp[1][1 + i], lsem.at[14 + i]) for i in range(2)
+    ]
+    loads = load_mlp(2)
+    for copy in down_loads + gate_loads + loads:
         copy.start()
     gains[0, 0:1, :] = gain_mlp_ref[...]
     gains[0, 1:2, :] = jnp.zeros_like(gain_mlp_ref)
@@ -1534,17 +1557,12 @@
     for copy in down_loads:
         copy.wait()
     sums[0].go_home(exchanged=False)
-    for i in (1, 2):
-        for copy in loads:
-            copy.wait()
-        sums[i].cross_second(kept, come)
-        if i == 1:
-            loads = load_mlp(2)
-            for copy in loads:
-                copy.start()
-            corner_sum(0)
-            start_back(2)
-            start_back(3)
+    corner_sum(0)
+    for copy in loads:
+        copy.wait()
+    sums[2].cross_second(kept, come)
+    start_back(2)
+    start_back(3)
     ctx[...] = ctx_ref[...].T
     rope_tables(counts, inverse_ref, cos_ref, sin_ref)
 
@@ -1585,8 +1603,10 @@
     corner_sum(3)
     load_n.wait()
     attn_grad(1, full, d_lin[:q_cols, :].T)
-    for plane in sums[1:]:
-        plane.go_home()
+    for copy in gate_loads:
+        copy.wait()
+    sums[1].go_home(exchanged=False)
+    sums[2].go_home()
 
     def second(i):
         sent, keep, got = bufs_attn[i][:3]
@@ -1703,7 +1723,7 @@
         *[pltpu.VMEM((block, width), floats)] * 2,
         *[pltpu.VMEM((block, width), halves)] * 6,
         *copy_semaphores(),
-        pltpu.SemaphoreType.DMA((14,)),
+        pltpu.SemaphoreType.DMA((16,)),
     ]
 
     def kernel(*refs):
@@ -1835,13 +1855,13 @@
     slices = [send(part, "odd_far") for part in (slice_g, slice_u)]
     context_t, log_total = attend_forward(counts, q_t, pieces)
     (
-        out_base, grad_residual, attn_grad_full, out_near, down_half, down_mine, gate_keep, gate_send,
+        out_base, grad_residual, attn_grad_full, out_near, down_half, down_mine, gate_half, gate_mine,
         up_keep, up_send, d_context_t, delta, mlp_gain_part,
     ) = middle(
         context_t, tokens, gain_mlp, grad_full,
         (output_weight, down_weight, gate_weight, up_weight, weight_o, weight_d, *slices),
     )
-    gate_come = send(gate_send, "y")
+    gate_come = send(gate_half, "x")
     up_come = send(up_send, "x")
     down_come = send(down_half, "y")
     out_near = send(out_near, "near")
@@ -1849,7 +1869,7 @@
     input_grad, gains, gate_sum, up_sum, down_sum, query_sum, kv_sum, output_sum = last_part(
         counts, inverse, d_query_t, d_pieces, normed_full, joined, tokens, gain_attn,
         grad_residual, attn_grad_full, context_t, mlp_gain_part,
-        (down_mine, down_come, gate_keep, gate_come, up_keep, up_come),
+        (down_mine, down_come, gate_mine, gate_come, up_keep, up_come),
     )
     per = gains.shape[1] // 8
     gains = lax.dynamic_slice_in_dim(gains, dp * per, per, axis=1)

time: 460 us -> 457 us (level)
  waiting for transfers between devices: 36.5 us -> 21.5 us
  Pallas kernels: 400 us -> 414 us
    ppermute x6, waiting for transfers between devices: 36.5 us -> 21.5 us  [send(): return lax.ppermute(block, ('dp', 'tp'), ROUTES[way])]
    pallas_call x1, Pallas kernels: 26.9 us -> 36.7 us  [attend_backward(): pl.pallas_call(functools.partial(bwd_kernel, n, width), out_shape=(jax.Sh...]
  transfers between devices with their start and end apart: 6 -> 6, of which waited for: 3 -> 3; matrix products, arithmetic and copies ran while one was open for 0% -> 0% of each run, Pallas kernels for 41% -> 44%
where the time goes in v9:
time: 457 us; the launch traced here: 453 us
  Pallas kernels  414 us (91%)
  waiting for transfers between devices  21.5 us (5%)
  starting transfers between devices  11.6 us (3%)
    pallas_call x1, Pallas kernels, last_part(): pl.pallas_call(kernel, out_shape=out_shape, in_specs=[SM, VM, VM, HM, HM,...  140 us
    pallas_call x1, Pallas kernels, middle(): pl.pallas_call(kernel, out_shape=out_shape, in_specs=[VM] * 4 + [HB] * 8,...  118 us
    pallas_call x1, Pallas kernels, first_part(): pl.pallas_call(first_kernel, out_shape=out_shape, in_specs=[SM] + [VM] *...  93.1 us
    pallas_call x1, Pallas kernels, attend_backward(): pl.pallas_call(functools.partial(bwd_kernel, n, width), out_shape=(jax.Sh...  36.7 us
    ppermute x6, waiting for transfers between devices, send(): return lax.ppermute(block, ('dp', 'tp'), ROUTES[way])  21.5 us
    pallas_call x1, Pallas kernels, attend_forward(): pl.pallas_call(functools.partial(fwd_kernel, n, width), out_shape=(jax.Sh...  21.3 us
    ppermute x6, starting transfers between devices, send(): return lax.ppermute(block, ('dp', 'tp'), ROUTES[way])  11.6 us
  transfers between devices with their start and end apart: 6, of which 3 were waited for; matrix products, arithmetic and copies ran while one was open for 0% of the time, Pallas kernels for 44%

profile of v9, /device:TPU:3, one launch (start us, length us, event | category | flops | bytes accessed | tf_op | source)
XLA Modules:
  0.0 453.4 jit_solution(14085480509249644292)
XLA Ops:
  0.7 0.6 negate_power_fusion.inverse_ref.refs_1_
  1.3 1.3 reshape.40.gain_ref.refs_7_
  2.6 1.5 convert_reduce_fusion.counts.refs_0_
  4.1 0.0 copy-start.2
  4.1 93.1 %first.1 = (bf16[384,1024]{1,0:T(8,128)(2,1)}, bf16[16,384,512]{2,1,0:T(8,128)(2,1)}, bf16[1024,1536]{1,0:T(8,128)(2,1)}, bf16[1024,1536]{1,0:T(8,128)(2,1)}, bf...) custom-call(s32[3]{0:T(128)} %convert_reduce_fusion.counts.refs_0_, ...), custom_call_target="tpu_custom_call" | custom-call | tf_op jit(solution)/shard_map/first/pallas_call | solution.py:1087
  97.2 1.9 collective-permute-start
  99.1 4.4 collective-permute-start.1
  103.5 0.0 copy-done.2
  103.5 0.6 reshape.41.refs_2_
  104.1 21.3 %attend_forward.1 = (bf16[384,1024]{1,0:T(8,128)(2,1)}, f32[4,1024]{1,0:T(4,128)}) custom-call(s32[3]{0:T(128)} %convert_reduce_fusion.counts.refs_0_, bf16[384,1024]{1,0:T(8,128)(2,1)} %get-tuple-element.54.q_ref, bf16[16,384,512]{2,1,0:T(8,128)(2,1)} %get-tuple-element.55.pieces), custom_call_target="tpu_custom_call" | custom-call | tf_op jit(solution)/shard_map/attend_forward/pallas_call | solution.py:195
  125.4 1.4 collective-permute-done.refs_10_
  126.8 0.0 copy-start.1
  126.8 8.5 %collective-permute-done.1.refs_11_ = bf16[384,1024]{1,0:T(8,128)(2,1)} collective-permute-done((bf16[384,1024]{1,0:T(8,128)(2,1)}, bf16[384,1024]{1,0:T(8,128)(2,1)}, u32[]{:S(2)}, u32[]{:S(2)}) %collective-permute-start.1) | collective-permute-done | bytes 786464 | tf_op jit(solution)/shard_map/ppermute | solution.py:1824
  135.3 0.0 copy-done.1
  135.3 117.7 %middle.1 = (f32[256,1536]{1,0:T(8,128)}, f32[256,1536]{1,0:T(8,128)}, bf16[1024,1536]{1,0:T(8,128)(2,1)}, bf16[256,1536]{1,0:T(8,128)(2,1)}, bf16[384,1024]{1,0...) custom-call(bf16[384,1024]{1,0:T(8,128)(2,1)} %get-tuple-element.56., ...), custom_call_target="tpu_custom_call" | custom-call | tf_op jit(solution)/shard_map/middle/pallas_call | solution.py:1441
  253.0 2.0 collective-permute-start.5
  255.0 0.0 collective-permute-start.3
  255.0 0.8 collective-permute-start.4
  255.8 2.4 collective-permute-start.2
  258.3 36.7 %attend_backward.1 = (f32[384,1024]{1,0:T(8,128)}, bf16[16,384,512]{2,1,0:T(8,128)(2,1)}) custom-call(s32[3]{0:T(128)} %convert_reduce_fusion.counts.refs_0_, bf16[384,1024]{1,0:T(8,128)(2,1)} %get-tuple-element.54.q_ref, bf16[384,1024]{1,0:T(8,128)(2,1)} %get-tuple-element.64.do_ref, f32[4,1024]{1,0:T(4,128)} %get-tuple-element.65.log_ref, ...), custom_call_target="tpu_custom_call" | custom-call | tf_op jit(solution)/shard_map/attend_backward/pallas_call | solution.py:310
  295.0 0.0 collective-permute-done.3.refs_13_
  295.0 0.0 copy-start
  295.0 11.6 %collective-permute-done.4.refs_15_ = bf16[384,1024]{1,0:T(8,128)(2,1)} collective-permute-done((bf16[384,1024]{1,0:T(8,128)(2,1)}, bf16[384,1024]{1,0:T(8,128)(2,1)}, u32[]{:S(2)}, u32[]{:S(2)}) %collective-permute-start.4) | collective-permute-done | bytes 786464 | tf_op jit(solution)/shard_map/ppermute | solution.py:1824
  306.6 0.0 collective-permute-done.5.refs_17_
  306.6 0.0 copy-done
  306.6 139.6 %last.1 = (f32[256,1536]{1,0:T(8,128)}, f32[2,1536]{1,0:T(2,128)}, f32[192,1024]{1,0:T(8,128)}, f32[192,1024]{1,0:T(8,128)}, f32[192,1024]{1,0:T(8,128)}, /*inde...) custom-call(s32[3]{0:T(128)} %convert_reduce_fusion.counts.refs_0_, ...), custom_call_target="tpu_custom_call" | custom-call | tf_op jit(solution)/shard_map/last/pallas_call | solution.py:1732
  446.2 1.4 constant_dynamic-slice_fusion
  447.6 0.0 collective-permute-done.2.refs_1_
  447.6 5.6 %finish.1 = (bf16[256,1536]{1,0:T(8,128)(2,1)}, f32[192,192]{1,0:T(8,128)}, f32[192,192]{1,0:T(8,128)}, f32[256,1536]{1,0:T(8,128)}, f32[192,384]{1,0:T(8,128)},...) custom-call(f32[256,1536]{1,0:T(8,128)} %get-tuple-element.62.refs_0_, ...), custom_call_target="tpu_custom_call" | custom-call | tf_op jit(solution)/shard_map/finish/pallas_call | solution.py:1770
  (1 shorter events, 0.0 us)
Async XLA Ops:
  4.1 99.5 %copy-start.2 = (bf16[1536]{0:T(1024)(128)(2,1)S(1)}, bf16[1536]{0:T(1024)(128)(2,1)}, u32[]{:S(2)}) copy-start(bf16[1536]{0:T(1024)(128)(2,1)} %param.20) | copy-start | bytes 9220
  97.2 29.6 %collective-permute-start = (bf16[384,1024]{1,0:T(8,128)(2,1)}, bf16[384,1024]{1,0:T(8,128)(2,1)S(1)}, u32[]{:S(2)}, u32[]{:S(2)}) collective-permute-start(bf16[384,1024]{1,0:T(8,128)(2,1)} %get-tuple-element.60), channel_id=1, source_target_pairs={{4,6},{5,7},{6,4},{7,5},{12,14},{13,15},{14,12},{15,13},{20,22},{2... | collective-permute-start | bytes 2359304 | tf_op jit(solution)/shard_map/ppermute | solution.py:1824
  99.1 36.2 %collective-permute-start.1 = (bf16[384,1024]{1,0:T(8,128)(2,1)}, bf16[384,1024]{1,0:T(8,128)(2,1)}, u32[]{:S(2)}, u32[]{:S(2)}) collective-permute-start(bf16[384,1024]{1,0:T(8,128)(2,1)} %get-tuple-element.61), channel_id=1, source_target_pairs={{4,6},{5,7},{6,4},{7,5},{12,14},{13,15},{14,12},{15,13},{20,22},{2... | collective-permute-start | bytes 2359304 | tf_op jit(solution)/shard_map/ppermute | solution.py:1824
  126.8 8.5 %copy-start.1 = (bf16[384,1024]{1,0:T(8,128)(2,1)}, bf16[384,1024]{1,0:T(8,128)(2,1)S(1)}, u32[]{:S(2)}) copy-start(bf16[384,1024]{1,0:T(8,128)(2,1)S(1)} %collective-permute-done.refs_10_) | copy-start | bytes 2359300
  253.0 53.6 %collective-permute-start.5 = (bf16[2,384,1024]{2,1,0:T(8,128)(2,1)}, bf16[2,384,1024]{2,1,0:T(8,128)(2,1)}, u32[]{:S(2)}, u32[]{:S(2)}) collective-permute-start(bf16[2,384,1024]{2,1,0:T(8,128)(2,1)} %get-tuple-element.79), channel_id=1, source_target_pairs={{0,8},{1,9},{2,10},{3,11},{4,12},{5,13},{6,14},{7,15},{8,0},{9,1},... | collective-permute-start | bytes 4718600 | tf_op jit(solution)/shard_map/ppermute | solution.py:1824
  255.0 40.0 %collective-permute-start.3 = (bf16[384,1024]{1,0:T(8,128)(2,1)}, bf16[384,1024]{1,0:T(8,128)(2,1)S(1)}, u32[]{:S(2)}, u32[]{:S(2)}) collective-permute-start(bf16[384,1024]{1,0:T(8,128)(2,1)} %get-tuple-element.75), channel_id=1, source_target_pairs={{0,16},{1,17},{2,18},{3,19},{4,20},{5,21},{6,22},{7,23},{8,24},{9,... | collective-permute-start | bytes 2359304 | tf_op jit(solution)/shard_map/ppermute | solution.py:1824
  255.0 51.6 %collective-permute-start.4 = (bf16[384,1024]{1,0:T(8,128)(2,1)}, bf16[384,1024]{1,0:T(8,128)(2,1)}, u32[]{:S(2)}, u32[]{:S(2)}) collective-permute-start(bf16[384,1024]{1,0:T(8,128)(2,1)} %get-tuple-element.77), channel_id=1, source_target_pairs={{0,8},{1,9},{2,10},{3,11},{4,12},{5,13},{6,14},{7,15},{8,0},{9,1},... | collective-permute-start | bytes 2359304 | tf_op jit(solution)/shard_map/ppermute | solution.py:1824
  255.8 191.8 %collective-permute-start.2 = (bf16[256,1536]{1,0:T(8,128)(2,1)}, bf16[256,1536]{1,0:T(8,128)(2,1)}, u32[]{:S(2)}, u32[]{:S(2)}) collective-permute-start(bf16[256,1536]{1,0:T(8,128)(2,1)} %get-tuple-element.63), channel_id=1, source_target_pairs={{0,1},{1,0},{2,3},{3,2},{4,5},{5,4},{6,7},{7,6},{8,9},{9,8},{10,11... | collective-permute-start | bytes 2359304 | tf_op jit(solution)/shard_map/ppermute | solution.py:1824
  295.0 11.6 %copy-start = (bf16[384,1024]{1,0:T(8,128)(2,1)}, bf16[384,1024]{1,0:T(8,128)(2,1)S(1)}, u32[]{:S(2)}) copy-start(bf16[384,1024]{1,0:T(8,128)(2,1)S(1)} %collective-permute-done.3.refs_13_) | copy-start | bytes 2359300

commit v10 on v9

--- a/solution.py
+++ b/solution.py
@@ -1743,12 +1743,22 @@
 
 
 def finish_kernel(*refs):
-    base, near, kv_sum, *ready = refs[:9]
+    sources = refs[:9]
     output, k_out, v_out, *outs = refs[9:18]
-    out_buf, k_buf, v_buf, sem = refs[18:]
+    out_buf, k_buf, v_buf, sem, load_sem = refs[18:23]
+    base, near, kv_sum, *ready = refs[23:]
+    loads = [
+        pltpu.make_async_copy(src, dst, load_sem.at[i])
+        for i, (src, dst) in enumerate(zip(sources, refs[23:]))
+    ]
+    for load in loads:
+        load.start()
     copies = [pltpu.make_async_copy(src, dst, sem.at[i]) for i, (src, dst) in enumerate(zip(ready, outs))]
-    for copy in copies:
+    for load, copy in zip(loads[3:], copies):
+        load.wait()
         copy.start()
+    for load in loads[:3]:
+        load.wait()
     out_buf[...] = (base[...] + near[...].astype(floats)).astype(halves)
     kv_cols = k_buf.shape[1]
     k_buf[...] = kv_sum[:, :kv_cols]
@@ -1775,13 +1785,15 @@
             shape(small, floats),
             *[shape(a.shape, a.dtype) for a in ready],
         ),
-        in_specs=[VM] * (3 + len(ready)),
+        in_specs=[HM] * (3 + len(ready)),
         out_specs=(HM,) * (3 + len(ready)),
         scratch_shapes=[
             pltpu.VMEM(base.shape, halves),
             pltpu.VMEM(small, floats),
             pltpu.VMEM(small, floats),
             pltpu.SemaphoreType.DMA((3 + len(ready),)),
+            pltpu.SemaphoreType.DMA((3 + len(ready),)),
+            *[pltpu.VMEM(a.shape, a.dtype) for a in (base, near, kv_sum, *ready)],
         ],
         compiler_params=pltpu.CompilerParams(vmem_limit_bytes=63 << 20),
         name="finish",

time: 457 us -> 457 us (level)
  Pallas kernels: 414 us -> 390 us
  waiting for transfers between devices: 21.5 us -> 45 us
    ppermute x6, waiting for transfers between devices: 21.5 us -> 45 us  [send(): return lax.ppermute(block, ('dp', 'tp'), ROUTES[way])]
    pallas_call x1, Pallas kernels: 36.7 us -> 21.2 us  [attend_backward(): pl.pallas_call(functools.partial(bwd_kernel, n, width), out_shape=(jax.Sh...]
    pallas_call x1, Pallas kernels: 21.3 us -> 13.2 us  [attend_forward(): pl.pallas_call(functools.partial(fwd_kernel, n, width), out_shape=(jax.Sh...]
  transfers between devices with their start and end apart: 6 -> 6, of which waited for: 3 -> 3; matrix products, arithmetic and copies ran while one was open for 0% -> 0% of each run, Pallas kernels for 44% -> 38%
where the time goes in v10:
time: 457 us; the launch traced here: 453 us
  Pallas kernels  390 us (85%)
  waiting for transfers between devices  45 us (10%)
  starting transfers between devices  11.6 us (3%)
    pallas_call x1, Pallas kernels, last_part(): pl.pallas_call(kernel, out_shape=out_shape, in_specs=[SM, VM, VM, HM, HM,...  140 us
    pallas_call x1, Pallas kernels, middle(): pl.pallas_call(kernel, out_shape=out_shape, in_specs=[VM] * 4 + [HB] * 8,...  118 us
    pallas_call x1, Pallas kernels, first_part(): pl.pallas_call(first_kernel, out_shape=out_shape, in_specs=[SM] + [VM] *...  93.1 us
    ppermute x6, waiting for transfers between devices, send(): return lax.ppermute(block, ('dp', 'tp'), ROUTES[way])  45 us
    pallas_call x1, Pallas kernels, attend_backward(): pl.pallas_call(functools.partial(bwd_kernel, n, width), out_shape=(jax.Sh...  21.2 us
    pallas_call x1, Pallas kernels, attend_forward(): pl.pallas_call(functools.partial(fwd_kernel, n, width), out_shape=(jax.Sh...  13.2 us
    ppermute x6, starting transfers between devices, send(): return lax.ppermute(block, ('dp', 'tp'), ROUTES[way])  11.6 us
  transfers between devices with their start and end apart: 6, of which 3 were waited for; matrix products, arithmetic and copies ran while one was open for 0% of the time, Pallas kernels for 38%

profile of v10, /device:TPU:3, one launch (start us, length us, event | category | flops | bytes accessed | tf_op | source)
XLA Modules:
  0.0 452.6 jit_solution(7695935578197136502)
XLA Ops:
  0.7 0.6 negate_power_fusion.inverse_ref.refs_1_
  1.3 1.3 reshape.40.gain_ref.refs_7_
  2.6 1.5 convert_reduce_fusion.counts.refs_0_
  4.1 0.0 copy-start.2
  4.1 93.1 %first.1 = (bf16[384,1024]{1,0:T(8,128)(2,1)}, bf16[16,384,512]{2,1,0:T(8,128)(2,1)}, bf16[1024,1536]{1,0:T(8,128)(2,1)}, bf16[1024,1536]{1,0:T(8,128)(2,1)}, bf...) custom-call(s32[3]{0:T(128)} %convert_reduce_fusion.counts.refs_0_, ...), custom_call_target="tpu_custom_call" | custom-call | tf_op jit(solution)/shard_map/first/pallas_call | solution.py:1087
  97.2 1.9 collective-permute-start
  99.1 4.4 collective-permute-start.1
  103.5 0.0 copy-done.2
  103.5 0.6 reshape.41.refs_2_
  104.1 13.2 %attend_forward.1 = (bf16[384,1024]{1,0:T(8,128)(2,1)}, f32[4,1024]{1,0:T(4,128)}) custom-call(s32[3]{0:T(128)} %convert_reduce_fusion.counts.refs_0_, bf16[384,1024]{1,0:T(8,128)(2,1)} %get-tuple-element.54.q_ref, bf16[16,384,512]{2,1,0:T(8,128)(2,1)} %get-tuple-element.55.pieces), custom_call_target="tpu_custom_call" | custom-call | tf_op jit(solution)/shard_map/attend_forward/pallas_call | solution.py:195
  117.4 9.4 %collective-permute-done.refs_10_ = bf16[384,1024]{1,0:T(8,128)(2,1)S(1)} collective-permute-done((bf16[384,1024]{1,0:T(8,128)(2,1)}, bf16[384,1024]{1,0:T(8,128)(2,1)S(1)}, u32[]{:S(2)}, u32[]{:S(2)}) %collective-permute-start) | collective-permute-done | bytes 786464 | tf_op jit(solution)/shard_map/ppermute | solution.py:1836
  126.8 0.0 copy-start.1
  126.8 8.5 %collective-permute-done.1.refs_11_ = bf16[384,1024]{1,0:T(8,128)(2,1)} collective-permute-done((bf16[384,1024]{1,0:T(8,128)(2,1)}, bf16[384,1024]{1,0:T(8,128)(2,1)}, u32[]{:S(2)}, u32[]{:S(2)}) %collective-permute-start.1) | collective-permute-done | bytes 786464 | tf_op jit(solution)/shard_map/ppermute | solution.py:1836
  135.3 0.0 copy-done.1
  135.3 117.7 %middle.1 = (f32[256,1536]{1,0:T(8,128)}, f32[256,1536]{1,0:T(8,128)}, bf16[1024,1536]{1,0:T(8,128)(2,1)}, bf16[256,1536]{1,0:T(8,128)(2,1)}, bf16[384,1024]{1,0...) custom-call(bf16[384,1024]{1,0:T(8,128)(2,1)} %get-tuple-element.56., ...), custom_call_target="tpu_custom_call" | custom-call | tf_op jit(solution)/shard_map/middle/pallas_call | solution.py:1441
  253.0 2.0 collective-permute-start.5
  255.0 0.0 collective-permute-start.3
  255.0 0.8 collective-permute-start.4
  255.8 2.4 collective-permute-start.2
  258.3 21.2 %attend_backward.1 = (f32[384,1024]{1,0:T(8,128)}, bf16[16,384,512]{2,1,0:T(8,128)(2,1)}) custom-call(s32[3]{0:T(128)} %convert_reduce_fusion.counts.refs_0_, bf16[384,1024]{1,0:T(8,128)(2,1)} %get-tuple-element.54.q_ref, bf16[384,1024]{1,0:T(8,128)(2,1)} %get-tuple-element.64.do_ref, f32[4,1024]{1,0:T(4,128)} %get-tuple-element.65.log_ref, ...), custom_call_target="tpu_custom_call" | custom-call | tf_op jit(solution)/shard_map/attend_backward/pallas_call | solution.py:310
  279.5 0.0 collective-permute-done.3.refs_13_
  279.5 0.0 copy-start
  279.5 27.1 %collective-permute-done.4.refs_15_ = bf16[384,1024]{1,0:T(8,128)(2,1)} collective-permute-done((bf16[384,1024]{1,0:T(8,128)(2,1)}, bf16[384,1024]{1,0:T(8,128)(2,1)}, u32[]{:S(2)}, u32[]{:S(2)}) %collective-permute-start.4) | collective-permute-done | bytes 786464 | tf_op jit(solution)/shard_map/ppermute | solution.py:1836
  306.6 0.0 collective-permute-done.5.refs_17_
  306.6 0.0 copy-done
  306.6 139.6 %last.1 = (f32[256,1536]{1,0:T(8,128)}, f32[2,1536]{1,0:T(2,128)}, f32[192,1024]{1,0:T(8,128)}, f32[192,1024]{1,0:T(8,128)}, f32[192,1024]{1,0:T(8,128)}, /*inde...) custom-call(s32[3]{0:T(128)} %convert_reduce_fusion.counts.refs_0_, ...), custom_call_target="tpu_custom_call" | custom-call | tf_op jit(solution)/shard_map/last/pallas_call | solution.py:1732
  446.2 1.4 constant_dynamic-slice_fusion
  447.6 0.0 collective-permute-done.2.refs_1_
  447.6 4.8 %finish.1 = (bf16[256,1536]{1,0:T(8,128)(2,1)}, f32[192,192]{1,0:T(8,128)}, f32[192,192]{1,0:T(8,128)}, f32[256,1536]{1,0:T(8,128)}, f32[192,384]{1,0:T(8,128)},...) custom-call(f32[256,1536]{1,0:T(8,128)} %get-tuple-element.62.refs_0_, ...), custom_call_target="tpu_custom_call" | custom-call | tf_op jit(solution)/shard_map/finish/pallas_call | solution.py:1780
  (1 shorter events, 0.0 us)
Async XLA Ops:
  4.1 99.5 %copy-start.2 = (bf16[1536]{0:T(1024)(128)(2,1)S(1)}, bf16[1536]{0:T(1024)(128)(2,1)}, u32[]{:S(2)}) copy-start(bf16[1536]{0:T(1024)(128)(2,1)} %param.20) | copy-start | bytes 9220
  97.2 29.6 %collective-permute-start = (bf16[384,1024]{1,0:T(8,128)(2,1)}, bf16[384,1024]{1,0:T(8,128)(2,1)S(1)}, u32[]{:S(2)}, u32[]{:S(2)}) collective-permute-start(bf16[384,1024]{1,0:T(8,128)(2,1)} %get-tuple-element.60), channel_id=1, source_target_pairs={{4,6},{5,7},{6,4},{7,5},{12,14},{13,15},{14,12},{15,13},{20,22},{2... | collective-permute-start | bytes 2359304 | tf_op jit(solution)/shard_map/ppermute | solution.py:1836
  99.1 36.2 %collective-permute-start.1 = (bf16[384,1024]{1,0:T(8,128)(2,1)}, bf16[384,1024]{1,0:T(8,128)(2,1)}, u32[]{:S(2)}, u32[]{:S(2)}) collective-permute-start(bf16[384,1024]{1,0:T(8,128)(2,1)} %get-tuple-element.61), channel_id=1, source_target_pairs={{4,6},{5,7},{6,4},{7,5},{12,14},{13,15},{14,12},{15,13},{20,22},{2... | collective-permute-start | bytes 2359304 | tf_op jit(solution)/shard_map/ppermute | solution.py:1836
  126.8 8.5 %copy-start.1 = (bf16[384,1024]{1,0:T(8,128)(2,1)}, bf16[384,1024]{1,0:T(8,128)(2,1)S(1)}, u32[]{:S(2)}) copy-start(bf16[384,1024]{1,0:T(8,128)(2,1)S(1)} %collective-permute-done.refs_10_) | copy-start | bytes 2359300
  253.0 53.6 %collective-permute-start.5 = (bf16[2,384,1024]{2,1,0:T(8,128)(2,1)}, bf16[2,384,1024]{2,1,0:T(8,128)(2,1)}, u32[]{:S(2)}, u32[]{:S(2)}) collective-permute-start(bf16[2,384,1024]{2,1,0:T(8,128)(2,1)} %get-tuple-element.79), channel_id=1, source_target_pairs={{0,8},{1,9},{2,10},{3,11},{4,12},{5,13},{6,14},{7,15},{8,0},{9,1},... | collective-permute-start | bytes 4718600 | tf_op jit(solution)/shard_map/ppermute | solution.py:1836
  255.0 24.5 %collective-permute-start.3 = (bf16[384,1024]{1,0:T(8,128)(2,1)}, bf16[384,1024]{1,0:T(8,128)(2,1)S(1)}, u32[]{:S(2)}, u32[]{:S(2)}) collective-permute-start(bf16[384,1024]{1,0:T(8,128)(2,1)} %get-tuple-element.75), channel_id=1, source_target_pairs={{0,16},{1,17},{2,18},{3,19},{4,20},{5,21},{6,22},{7,23},{8,24},{9,... | collective-permute-start | bytes 2359304 | tf_op jit(solution)/shard_map/ppermute | solution.py:1836
  255.0 51.6 %collective-permute-start.4 = (bf16[384,1024]{1,0:T(8,128)(2,1)}, bf16[384,1024]{1,0:T(8,128)(2,1)}, u32[]{:S(2)}, u32[]{:S(2)}) collective-permute-start(bf16[384,1024]{1,0:T(8,128)(2,1)} %get-tuple-element.77), channel_id=1, source_target_pairs={{0,8},{1,9},{2,10},{3,11},{4,12},{5,13},{6,14},{7,15},{8,0},{9,1},... | collective-permute-start | bytes 2359304 | tf_op jit(solution)/shard_map/ppermute | solution.py:1836
  255.8 191.8 %collective-permute-start.2 = (bf16[256,1536]{1,0:T(8,128)(2,1)}, bf16[256,1536]{1,0:T(8,128)(2,1)}, u32[]{:S(2)}, u32[]{:S(2)}) collective-permute-start(bf16[256,1536]{1,0:T(8,128)(2,1)} %get-tuple-element.63), channel_id=1, source_target_pairs={{0,1},{1,0},{2,3},{3,2},{4,5},{5,4},{6,7},{7,6},{8,9},{9,8},{10,11... | collective-permute-start | bytes 2359304 | tf_op jit(solution)/shard_map/ppermute | solution.py:1836
  279.5 27.1 %copy-start = (bf16[384,1024]{1,0:T(8,128)(2,1)}, bf16[384,1024]{1,0:T(8,128)(2,1)S(1)}, u32[]{:S(2)}) copy-start(bf16[384,1024]{1,0:T(8,128)(2,1)S(1)} %collective-permute-done.3.refs_13_) | copy-start | bytes 2359300
